TPU v7x, 512 devices: a whole 4x8x8 slice. The times are simulated.
512 devices in a mesh: dp: 64 (over y_hi, z, core), group: 8 (over y_lo, x).
Axes of the slice: x: 4, y: 8 (y_hi: 4, y_lo: 2; y = y_hi * 2 + y_lo), z: 8, core: 2. Of those that a mesh axis runs over, the one named last changes fastest.
Arguments:
- activations: bfloat16 [1024, 6144], P('dp', 'group'), may hold values from -6 to 6
- out_grads: bfloat16 [1024, 6144], P('dp', 'group'), may hold values from -6 to 6
- counts: int32 [64], P('dp'), may hold values from 1 to 16, 768 in all
- owners: int32 [64], P('dp'), may hold values from 0 to 63, each once
- rotated_grad: bfloat16 [6144, 6144], P('dp'), may hold values from -6 to 6
- basis: bfloat16 [6144, 6144], P('dp', 'group'), may hold values from -0.078125 to 0.078125
- input_eigs: float32 [6144], P('group'), may hold values from 0.5 to 2
- output_eigs: float32 [6144], P('dp'), may hold values from 0.5 to 2
Outputs:
- cov_in: float32 [6144, 6144], P('group', 'dp')
- cov_out: float32 [6144, 6144], P('group', 'dp')
- preconditioned: float32 [6144, 6144], P('dp', 'group')
Inputs may be any that keep to these rules, and one draw needn't show every extreme that they name: counts[i] live slots lead replica i's 16 slots; the counts sum to 768 and the largest equals 16. owners is a permutation.
All inputs are finite; a program needn't handle non-finite values. No bound on the sum of `counts` on one device may be relied on, other than what follows from the above.
Results may differ from a plain program's by a relative error of at most 0.0022.
Values may be sent and summed in bfloat16 or wider, within the bound.
No kernel may reach another device: no remote copies, remote signals or barrier semaphores. Data moves between devices by JAX's collectives and lax.ppermute only.
A program may use at most 64 MiB of HBM per device.

v0:
```python
import jax
import jax.numpy as jnp
from jax import lax
from jax.sharding import PartitionSpec as P

DAMPING = 0.1


def from_root(array, axis, root):
    mine = lax.axis_index(axis) == root
    return lax.psum(jnp.where(mine, array, jnp.zeros_like(array)), axis)


def shards(activations, out_grads, counts, owners, rotated_grad, basis, input_eigs, output_eigs):
    dp_count = lax.axis_size("dp")
    group_count = lax.axis_size("group")
    slots_here = activations.shape[0]
    owned_width = basis.shape[0]
    blocks_per = dp_count // group_count
    is_live = lax.broadcasted_iota(jnp.int32, (slots_here, 1), 0) < counts[0]
    kept_in = jnp.where(is_live, activations, jnp.zeros_like(activations))
    kept_out = jnp.where(is_live, out_grads, jnp.zeros_like(out_grads))
    all_in, all_out, all_counts = (
        lax.all_gather(kept_in, "dp", axis=0, tiled=True),
        lax.all_gather(kept_out, "dp", axis=0, tiled=True),
        lax.all_gather(counts.astype(jnp.bfloat16), "dp", axis=0, tiled=True),
    )
    live_total = jnp.sum(all_counts.astype(jnp.float32))
    owner_idx = owners[0]
    offset = owner_idx % blocks_per * owned_width
    owned_in = lax.dynamic_slice_in_dim(all_in, offset, owned_width, 1)
    owned_out = lax.dynamic_slice_in_dim(all_out, offset, owned_width, 1)
    owned_in, owned_out = (
        from_root(owned_in, "group", owner_idx // blocks_per),
        from_root(owned_out, "group", owner_idx // blocks_per),
    )
    contract_rows = (((0,), (0,)), ((), ()))
    cov_in = (
        lax.dot_general(all_in, owned_in, contract_rows, preferred_element_type=jnp.float32)
        / live_total
    )
    cov_out = (
        lax.dot_general(all_out, owned_out, contract_rows, preferred_element_type=jnp.float32)
        / live_total
    )
    contract_cols = (((1,), (1,)), ((), ()))
    denominator = output_eigs[:, None] * input_eigs[None, :] + DAMPING
    full_basis = lax.all_gather(basis, "dp", axis=0, tiled=True)
    projected = jnp.dot(rotated_grad, full_basis, preferred_element_type=jnp.float32)
    scaled = (projected / denominator).astype(jnp.bfloat16)
    terms = lax.dot_general(scaled, full_basis, contract_cols, preferred_element_type=jnp.float32)
    preconditioned = lax.psum_scatter(terms, "group", scatter_dimension=1, tiled=True)
    return (cov_in, cov_out, preconditioned)


def solution(mesh):
    placed = (
        P("dp", "group"),
        P("dp", "group"),
        P("dp"),
        P("dp"),
        P("dp", None),
        P("dp", "group"),
        P("group"),
        P("dp"),
    )
    return jax.shard_map(
        shards,
        mesh=mesh,
        in_specs=placed,
        out_specs=(P("group", "dp"), P("group", "dp"), P("dp", "group")),
        check_vma=False,
    )
```

profile of v0, /device:TPU:1, one launch (start us, length us, event | category | flops | bytes accessed | tf_op | source)
XLA Modules:
  0.0 459.3 jit_solution(14841034539233761723)
XLA Ops:
  7.2 0.0 copy-start
  7.2 0.0 copy-start.3
  7.2 0.0 copy-start.2
  7.2 0.0 all-gather.4.cloned.1.call-start
  8.0 1.4 broadcast_select_fusion
  9.4 0.0 all-gather.4.cloned.1.call-update
  9.5 0.0 all-gather.6.cloned.1.call-start
  9.5 0.7 all-gather.6.cloned.1.call-update
  10.2 0.0 all-gather.8.cloned.1.call-start
  10.3 0.7 all-gather.8.cloned.1.call-update
  10.9 0.0 all-reduce.4.cloned.1.call-start
  11.7 89.9 %all-gather.4.cloned.1.call-done = bf16[1024,768]{1,0:T(8,128)(2,1)} async-done(((bf16[16,768]{1,0:T(8,128)(2,1)}), bf16[1024,768]{1,0:T(8,128)(2,1)}) %all-gather.4.cloned.1.call-update) | async-done | bytes 1572880 | tf_op jit(solution)/shard_map/all_gather | solution.py:24
  101.6 1.9 dynamic-slice_select_fusion.1
  103.5 81.9 %all-gather.6.cloned.1.call-done = bf16[1024,768]{1,0:T(8,128)(2,1)} async-done(((bf16[16,768]{1,0:T(8,128)(2,1)}), bf16[1024,768]{1,0:T(8,128)(2,1)}) %all-gather.6.cloned.1.call-update) | async-done | bytes 1572880 | tf_op jit(solution)/shard_map/all_gather | solution.py:25
  185.4 1.9 dynamic-slice_select_fusion
  187.3 0.0 all-reduce.4.cloned.1.call-update
  187.3 0.0 reduce-scatter.2.cloned.1.call-start
  187.4 106.2 %all-gather.8.cloned.1.call-done = bf16[6144,768]{1,0:T(8,128)(2,1)} async-done(((bf16[96,768]{1,0:T(8,128)(2,1)}), bf16[6144,768]{1,0:T(8,128)(2,1)}) %all-gather.8.cloned.1.call-update) | async-done | bytes 9437200 | tf_op jit(solution)/shard_map/all_gather | solution.py:48
  293.6 0.0 copy-done
  293.6 0.0 copy-done.3
  293.7 0.0 copy-done.2
  293.7 12.7 %fusion.1 = f32[96,6144]{1,0:T(8,128)} fusion(bf16[6144,768]{1,0:T(8,128)(2,1)} %all-gather.8.cloned.1.call-done, bf16[96,6144]{1,0:T(8,128)(2,1)S(1)} %copy-done, f32[768]{0:T(1024)S(1)} %copy-done.2, f32[96]{0:T(128)S(1)} %copy-done.3), kind=kOutput, calls=%fused_computation.4 | convolution fusion | flops 1812234240 | bytes 12979584 | tf_op jit(solution)/shard_map/dot_general | solution.py:51
  306.3 0.0 reduce-scatter.2.cloned.1.call-update
  306.4 0.0 copy-start.1
  306.4 1.4 dynamic-slice
  307.8 0.7 dynamic-update-slice
  308.6 138.5 %all-reduce = bf16[64]{0:T(256)(128)(2,1)S(1)} all-reduce(bf16[64]{0:T(256)(128)(2,1)S(1)} %dynamic-update-slice), channel_id=1, replica_groups=mesh['dp'=64,'group'=8] {'dp'}, use_global_device_ids=true, to_apply=%add | all-reduce | flops 64 | bytes 256
  447.1 0.7 convert_reduce_fusion
  447.7 0.0 all-reduce.4.cloned.1.call-done
  447.7 0.0 copy-start.4
  447.7 3.2 convolution_divide_fusion
  451.0 0.0 copy-done.1
  451.0 0.0 copy-done.4
  451.0 1.8 convolution_divide_fusion.1
  452.7 0.0 reduce-scatter.2.cloned.1.call-done
  (2 shorter events, 0.0 us)
Async XLA Ops:
  7.2 286.5 %copy-start = (bf16[96,6144]{1,0:T(8,128)(2,1)S(1)}, bf16[96,6144]{1,0:T(8,128)(2,1)}, u32[]{:S(2)}) copy-start(bf16[96,6144]{1,0:T(8,128)(2,1)} %param.12) | copy-start | bytes 3538948
  7.2 286.5 %copy-start.3 = (f32[96]{0:T(128)S(1)}, f32[96]{0:T(128)}, u32[]{:S(2)}) copy-start(f32[96]{0:T(128)} %param.15) | copy-start | bytes 1156
  7.2 286.5 %copy-start.2 = (f32[768]{0:T(1024)S(1)}, f32[768]{0:T(1024)}, u32[]{:S(2)}) copy-start(f32[768]{0:T(1024)} %param.14) | copy-start | bytes 9220
  7.2 94.4 %all-gather.4.cloned.1.call-start = ((), (), s32[]{:S(2)}) async-start(), calls=%async_computation.1 | async-start | bytes 1597440 | tf_op jit(solution)/shard_map/all_gather | solution.py:24
  9.5 176.0 %all-gather.6.cloned.1.call-start = ((), (), s32[]{:S(2)}) async-start(), calls=%async_computation.2 | async-start | bytes 1597440 | tf_op jit(solution)/shard_map/all_gather | solution.py:25
  10.2 283.4 %all-gather.8.cloned.1.call-start = ((), (), s32[]{:S(2)}) async-start(), calls=%async_computation.3 | async-start | bytes 9584640 | tf_op jit(solution)/shard_map/all_gather | solution.py:48
  10.9 436.8 %all-reduce.4.cloned.1.call-start = ((), (), s32[]{:S(2)}) async-start(), calls=%async_computation.5 | async-start | bytes 1048576 | tf_op jit(solution)/shard_map/psum | solution.py:11
  187.3 265.4 %reduce-scatter.2.cloned.1.call-start = ((), (), s32[]{:S(2)}) async-start(), calls=%async_computation.4 | async-start | bytes 2654208 | tf_op jit(solution)/shard_map/reduce_scatter | solution.py:52
  306.4 144.6 %copy-start.1 = (bf16[1024,768]{1,0:T(8,128)(2,1)S(1)}, bf16[1024,768]{1,0:T(8,128)(2,1)}, u32[]{:S(2)}) copy-start(bf16[1024,768]{1,0:T(8,128)(2,1)} %all-gather.4.cloned.1.call-done) | copy-start | bytes 4718596
  447.7 3.2 copy-start.4
Sparse Core Ops, SparseCore 0:
  11.9 89.6 all-gather.3
  105.5 79.8 all-gather.5
  188.8 104.8 all-gather.7
  297.0 75.9 all-reduce.3
  376.5 48.6 reduce-scatter.1
where the time goes:
time: 462 us; the launch traced here: 459 us
  waiting for transfers between devices  280 us (61%)
  blocking collectives  138 us (30%)
  matrix products  17.7 us (4%)
  between operations  15.3 us (3%)
  other arithmetic  5.89 us (1%)
    unnamed x1, blocking collectives  138 us
    all_gather x1, waiting for transfers between devices, shards(): full_basis = lax.all_gather(basis, 'dp', axis=0, tiled=True)  106 us
    all_gather x1, waiting for transfers between devices, shards(): lax.all_gather(kept_in, 'dp', axis=0, tiled=True)  89.9 us
    all_gather x1, waiting for transfers between devices, shards(): lax.all_gather(kept_out, 'dp', axis=0, tiled=True)  81.9 us
    dot_general x1, matrix products, shards(): lax.dot_general(scaled, full_basis, contract_cols, preferred_element_type...  12.7 us
  transfers between devices with their start and end apart: 5, of which 3 were waited for; matrix products, arithmetic and copies ran while one was open for 5% of the time, Pallas kernels for 0%

commit v1 on v0

v1 whole, which is shorter than its diff:
```python
import jax
import jax.numpy as jnp
from jax import lax
from jax.sharding import Mesh, PartitionSpec as P

DAMPING = 0.1
SAMPLED = 768
DP = ("yh", "z", "core")
GROUP = ("yl", "x")


def shift(value, axis, by):
    size = lax.axis_size(axis)
    return lax.ppermute(value, axis, [((i + by) % size, i) for i in range(size)])


def gather_y(block):
    return [block] + [shift(block, "yh", k) for k in range(1, 4)]


def gather_z(block):
    chunks = [block]
    up = down = block
    for step in range(4):
        up = shift(up, "z", 1)
        chunks.append(up)
        if step < 3:
            down = shift(down, "z", -1)
            chunks.append(down)
    return chunks


def shards(activations, out_grads, counts, owners, rotated_grad, basis, input_eigs, output_eigs):
    slots, width = activations.shape
    owned_width = basis.shape[0]
    blocks_per = width // owned_width
    group_count = lax.axis_size("yl") * lax.axis_size("x")
    full_basis = lax.all_gather(basis, DP, axis=0, tiled=True)

    is_live = lax.broadcasted_iota(jnp.int32, (slots, 1), 0) < counts[0]
    kept = jnp.stack([jnp.where(is_live, v, jnp.zeros_like(v)) for v in (activations, out_grads)])
    kept = jnp.concatenate(gather_y(kept), axis=1)
    kept = jnp.concatenate(gather_z(kept), axis=1)
    both = jnp.concatenate([kept, shift(kept, "core", 1)], axis=1)
    samples = both.shape[1]
    owner_idx = owners[0]
    offset = owner_idx % blocks_per * owned_width
    owned = lax.dynamic_slice_in_dim(both, offset, owned_width, 2)
    pieces = owned.reshape(group_count, 2 * samples // group_count, owned_width)
    pieces = lax.all_to_all(pieces, GROUP, 0, 0, tiled=True)
    piece = lax.dynamic_index_in_dim(pieces, owner_idx // blocks_per, 0, keepdims=False)
    spread = jnp.broadcast_to(piece[None], pieces.shape)
    owned = lax.all_to_all(spread, GROUP, 0, 0, tiled=True).reshape(2, samples, owned_width)
    contract_rows = (((0,), (0,)), ((), ()))
    cov_in, cov_out = (
        lax.dot_general(both[k], owned[k], contract_rows, preferred_element_type=jnp.float32)
        / jnp.float32(SAMPLED)
        for k in range(2)
    )

    contract_cols = (((1,), (1,)), ((), ()))
    denominator = output_eigs[:, None] * input_eigs[None, :] + DAMPING
    projected = jnp.dot(rotated_grad, full_basis, preferred_element_type=jnp.float32)
    scaled = (projected / denominator).astype(jnp.bfloat16)
    wide = full_basis.reshape(group_count, width, width)
    terms = lax.dot_general(
        wide, scaled, (((2,), (1,)), ((), ())), preferred_element_type=jnp.float32
    )
    terms = jnp.swapaxes(terms, 1, 2)
    terms = lax.all_to_all(terms, GROUP, 0, 0, tiled=True)
    preconditioned = jnp.sum(terms, axis=0)
    return (cov_in, cov_out, preconditioned)


def solution(mesh):
    devices = mesh.devices.reshape(4, 8, 2, 2, 4)
    fine = Mesh(devices, DP + GROUP)
    placed = (
        P(DP, GROUP),
        P(DP, GROUP),
        P(DP),
        P(DP),
        P(DP, None),
        P(DP, GROUP),
        P(GROUP),
        P(DP),
    )
    return jax.shard_map(
        shards,
        mesh=fine,
        in_specs=placed,
        out_specs=(P(GROUP, DP), P(GROUP, DP), P(DP, GROUP)),
        check_vma=False,
    )
```

time: 462 us -> 186 us (0.40)
  waiting for transfers between devices: 280 us -> 66.6 us
  blocking collectives: 138 us -> 0 us
  starting transfers between devices: 0.2 us -> 69.4 us
  local copies, waits for them, and re-layouts: 2.21 us -> 15 us
    all_gather x3 -> x1, waiting for transfers between devices: 278 us -> 11.7 us  [shards(): full_basis = lax.all_gather(basis, DP, axis=0, tiled=True)]
    unnamed x1 -> x0, blocking collectives: 138 us -> none
    ppermute x0 -> x11, starting transfers between devices: none -> 54.2 us  [shift(): lax.ppermute(value, axis, [((i + by) % size, i) for i in range(size)])]
    all_to_all x0 -> x3, waiting for transfers between devices: none -> 46.2 us  [the longest x1 24.1 us: shards(): terms = lax.all_to_all(terms, GROUP, 0, 0, tiled=True)]
    all_to_all x0 -> x3, starting transfers between devices: none -> 15.2 us  [the longest x1 6.67 us: shards(): pieces = lax.all_to_all(pieces, GROUP, 0, 0, tiled=True)]
    ppermute x0 -> x11, waiting for transfers between devices: none -> 8.02 us  [shift(): lax.ppermute(value, axis, [((i + by) % size, i) for i in range(size)])]
    unnamed x13 -> x22, local copies, waits for them, and re-layouts: 2.21 us -> 9.75 us
    select_n x3 -> x0, other arithmetic: 5.22 us -> none  [the longest x2 3.77 us: from_root(): return lax.psum(jnp.where(mine, array, jnp.zeros_like(array)), axis)]
  transfers between devices with their start and end apart: 5 -> 15, of which waited for: 3 -> 9; matrix products, arithmetic and copies ran while one was open for 5% -> 16% of each run, Pallas kernels for 0% -> 0%
where the time goes in v1:
time: 186 us; the launch traced here: 185 us
  starting transfers between devices  69.4 us (37%)
  waiting for transfers between devices  66.6 us (36%)
  matrix products  16.3 us (9%)
  between operations  15.5 us (8%)
  local copies, waits for them, and re-layouts  15 us (8%)
  other arithmetic  2.34 us (1%)
    ppermute x11, starting transfers between devices, shift(): lax.ppermute(value, axis, [((i + by) % size, i) for i in range(size)])  54.2 us
    all_to_all x1, waiting for transfers between devices, shards(): terms = lax.all_to_all(terms, GROUP, 0, 0, tiled=True)  24.1 us
    all_to_all x1, waiting for transfers between devices, shards(): pieces = lax.all_to_all(pieces, GROUP, 0, 0, tiled=True)  22.1 us
    dot_general x1, matrix products, shards(): lax.dot_general(wide, scaled, (((2,), (1,)), ((), ())), preferred_element...  12.7 us
    all_gather x1, waiting for transfers between devices, shards(): full_basis = lax.all_gather(basis, DP, axis=0, tiled=True)  11.7 us
    unnamed x22, local copies, waits for them, and re-layouts  9.75 us
    ppermute x11, waiting for transfers between devices, shift(): lax.ppermute(value, axis, [((i + by) % size, i) for i in range(size)])  8.02 us
    all_to_all x1, starting transfers between devices, shards(): pieces = lax.all_to_all(pieces, GROUP, 0, 0, tiled=True)  6.67 us
  transfers between devices with their start and end apart: 15, of which 9 were waited for; matrix products, arithmetic and copies ran while one was open for 16% of the time, Pallas kernels for 0%

profile of v1, /device:TPU:1, one launch (start us, length us, event | category | flops | bytes accessed | tf_op | source)
XLA Modules:
  0.0 185.2 jit_solution(1641183977435931244)
XLA Ops:
  7.2 0.0 all-gather.2.cloned.1.call-start
  7.2 0.7 all-gather.2.cloned.1.call-update
  8.6 0.8 select_bitcast_fusion.1
  9.4 0.6 constant_dynamic-update-slice_fusion.10
  10.0 8.3 %collective-permute-start.1 = (bf16[2,16,768]{2,1,0:T(8,128)(2,1)S(1)}, bf16[2,16,768]{2,1,0:T(8,128)(2,1)S(1)}, u32[]{:S(2)}, u32[]{:S(2)}) collective-permute-start(bf16[2,16,768]{2,1,0:T(8,128)(2,1)S(1)} %get-tuple-element.27), channel_id=1, source_target_pairs={{256,0},{384,128},{0,256},{128,384},{257,1},{385,129},{1,257},{129... | collective-permute-start | bytes 147464 | tf_op jit(solution)/shard_map/ppermute | solution.py:14
  18.3 2.0 %collective-permute-start = (bf16[2,16,768]{2,1,0:T(8,128)(2,1)S(1)}, bf16[2,16,768]{2,1,0:T(8,128)(2,1)S(1)}, u32[]{:S(2)}, u32[]{:S(2)}) collective-permute-start(bf16[2,16,768]{2,1,0:T(8,128)(2,1)S(1)} %get-tuple-element.27), channel_id=1, source_target_pairs={{128,0},{256,128},{384,256},{0,384},{129,1},{257,129},{385,257},{1... | collective-permute-start | bytes 147464 | tf_op jit(solution)/shard_map/ppermute | solution.py:14
  20.3 4.2 %collective-permute-start.2 = (bf16[2,16,768]{2,1,0:T(8,128)(2,1)S(1)}, bf16[2,16,768]{2,1,0:T(8,128)(2,1)S(1)}, u32[]{:S(2)}, u32[]{:S(2)}) collective-permute-start(bf16[2,16,768]{2,1,0:T(8,128)(2,1)S(1)} %get-tuple-element.27), channel_id=1, source_target_pairs={{384,0},{0,128},{128,256},{256,384},{385,1},{1,129},{129,257},{257... | collective-permute-start | bytes 147464 | tf_op jit(solution)/shard_map/ppermute | solution.py:14
  24.5 0.2 collective-permute-done
  24.7 2.6 %collective-permute-done.2 = bf16[2,16,768]{2,1,0:T(8,128)(2,1)S(1)} collective-permute-done((bf16[2,16,768]{2,1,0:T(8,128)(2,1)S(1)}, bf16[2,16,768]{2,1,0:T(8,128)(2,1)S(1)}, u32[]{:S(2)}, u32[]{:S(2)}) %collective-permute-start.2) | collective-permute-done | bytes 49184 | tf_op jit(solution)/shard_map/ppermute | solution.py:14
  27.3 4.0 %collective-permute-start.4 = (bf16[2,64,768]{2,1,0:T(8,128)(2,1)S(1)}, bf16[2,64,768]{2,1,0:T(8,128)(2,1)S(1)}, u32[]{:S(2)}, u32[]{:S(2)}) collective-permute-start(bf16[2,64,768]{2,1,0:T(8,128)(2,1)S(1)} %pad_maximum_fusion), channel_id=1, source_target_pairs={{112,0},{0,16},{16,32},{32,48},{48,64},{64,80},{80,96},{96,112},{1... | collective-permute-start | bytes 589832 | tf_op jit(solution)/shard_map/ppermute | solution.py:14
  31.3 8.6 %collective-permute-start.3 = (bf16[2,64,768]{2,1,0:T(8,128)(2,1)S(1)}, bf16[2,64,768]{2,1,0:T(8,128)(2,1)S(1)}, u32[]{:S(2)}, u32[]{:S(2)}) collective-permute-start(bf16[2,64,768]{2,1,0:T(8,128)(2,1)S(1)} %pad_maximum_fusion), channel_id=1, source_target_pairs={{16,0},{32,16},{48,32},{64,48},{80,64},{96,80},{112,96},{0,112},{1... | collective-permute-start | bytes 589832 | tf_op jit(solution)/shard_map/ppermute | solution.py:14
  39.9 0.6 constant_dynamic-update-slice_fusion.9
  40.5 0.6 constant_dynamic-update-slice_fusion.8
  41.1 0.6 constant_dynamic-update-slice_fusion.7
  41.8 1.9 %collective-permute-start.6 = (bf16[2,64,768]{2,1,0:T(8,128)(2,1)S(1)}, bf16[2,64,768]{2,1,0:T(8,128)(2,1)S(1)}, u32[]{:S(2)}, u32[]{:S(2)}) collective-permute-start(bf16[2,64,768]{2,1,0:T(8,128)(2,1)S(1)} %collective-permute-done.4), channel_id=1, source_target_pairs={{112,0},{0,16},{16,32},{32,48},{48,64},{64,80},{80,96},{96,112},{1... | collective-permute-start | bytes 589832 | tf_op jit(solution)/shard_map/ppermute | solution.py:14
  43.7 4.6 %collective-permute-start.5 = (bf16[2,64,768]{2,1,0:T(8,128)(2,1)S(1)}, bf16[2,64,768]{2,1,0:T(8,128)(2,1)S(1)}, u32[]{:S(2)}, u32[]{:S(2)}) collective-permute-start(bf16[2,64,768]{2,1,0:T(8,128)(2,1)S(1)} %collective-permute-done.3), channel_id=1, source_target_pairs={{16,0},{32,16},{48,32},{64,48},{80,64},{96,80},{112,96},{0,112},{1... | collective-permute-start | bytes 589832 | tf_op jit(solution)/shard_map/ppermute | solution.py:14
  48.3 0.7 constant_dynamic-update-slice_fusion.6
  49.0 0.7 constant_dynamic-update-slice_fusion.5
  49.7 0.1 collective-permute-done.6
  49.8 1.9 %collective-permute-start.8 = (bf16[2,64,768]{2,1,0:T(8,128)(2,1)S(1)}, bf16[2,64,768]{2,1,0:T(8,128)(2,1)S(1)}, u32[]{:S(2)}, u32[]{:S(2)}) collective-permute-start(bf16[2,64,768]{2,1,0:T(8,128)(2,1)S(1)} %collective-permute-done.6), channel_id=1, source_target_pairs={{112,0},{0,16},{16,32},{32,48},{48,64},{64,80},{80,96},{96,112},{1... | collective-permute-start | bytes 589832 | tf_op jit(solution)/shard_map/ppermute | solution.py:14
  51.8 4.7 %collective-permute-start.7 = (bf16[2,64,768]{2,1,0:T(8,128)(2,1)S(1)}, bf16[2,64,768]{2,1,0:T(8,128)(2,1)S(1)}, u32[]{:S(2)}, u32[]{:S(2)}) collective-permute-start(bf16[2,64,768]{2,1,0:T(8,128)(2,1)S(1)} %collective-permute-done.5), channel_id=1, source_target_pairs={{16,0},{32,16},{48,32},{64,48},{80,64},{96,80},{112,96},{0,112},{1... | collective-permute-start | bytes 589832 | tf_op jit(solution)/shard_map/ppermute | solution.py:14
  56.5 0.7 constant_dynamic-update-slice_fusion.4
  57.2 0.7 constant_dynamic-update-slice_fusion.3
  57.9 1.4 collective-permute-done.7
  59.3 4.9 %collective-permute-start.9 = (bf16[2,64,768]{2,1,0:T(8,128)(2,1)S(1)}, bf16[2,64,768]{2,1,0:T(8,128)(2,1)S(1)}, u32[]{:S(2)}, u32[]{:S(2)}) collective-permute-start(bf16[2,64,768]{2,1,0:T(8,128)(2,1)S(1)} %collective-permute-done.7), channel_id=1, source_target_pairs={{16,0},{32,16},{48,32},{64,48},{80,64},{96,80},{112,96},{0,112},{1... | collective-permute-start | bytes 589832 | tf_op jit(solution)/shard_map/ppermute | solution.py:14
  64.2 0.7 constant_dynamic-update-slice_fusion.2
  64.9 0.7 constant_dynamic-update-slice_fusion.1
  65.6 1.2 collective-permute-done.9
  66.8 0.7 constant_dynamic-update-slice_fusion
  67.5 1.7 copy-done.2
  69.2 9.1 %collective-permute-start.10 = (bf16[2,512,768]{2,1,0:T(8,128)(2,1)}, bf16[2,512,768]{2,1,0:T(8,128)(2,1)S(1)}, u32[]{:S(2)}, u32[]{:S(2)}) collective-permute-start(bf16[2,512,768]{2,1,0:T(8,128)(2,1)} %get-tuple-element.5), channel_id=1, source_target_pairs={{8,0},{0,8},{9,1},{1,9},{10,2},{2,10},{11,3},{3,11},{12,4},{4,12},... | collective-permute-start | bytes 4718600 | tf_op jit(solution)/shard_map/ppermute | solution.py:14
  78.9 2.6 %collective-permute-done.10 = bf16[2,512,768]{2,1,0:T(8,128)(2,1)S(1)} collective-permute-done((bf16[2,512,768]{2,1,0:T(8,128)(2,1)}, bf16[2,512,768]{2,1,0:T(8,128)(2,1)S(1)}, u32[]{:S(2)}, u32[]{:S(2)}) %collective-permute-start.10) | collective-permute-done | bytes 1572896 | tf_op jit(solution)/shard_map/ppermute | solution.py:14
  81.5 1.3 constant_dynamic-update-slice_fusion.11
  82.8 1.5 constant_dynamic-slice_fusion
  84.2 1.0 copy.12
  85.3 6.7 %all-to-all-start = ((bf16[8,256,96]{1,2,0:T(8,128)(2,1)}), bf16[8,256,96]{1,2,0:T(8,128)(2,1)S(1)}, u32[]{:S(2)}, u32[]{:S(2)}) async-start(bf16[8,256,96]{1,2,0:T(8,128)(2,1)} %copy.12), calls=%async_computation | async-start | bytes 786432 | tf_op jit(solution)/shard_map/all_to_all | solution.py:50
  91.9 22.1 %all-to-all-done = bf16[8,256,96]{1,2,0:T(8,128)(2,1)S(1)} async-done(((bf16[8,256,96]{1,2,0:T(8,128)(2,1)}), bf16[8,256,96]{1,2,0:T(8,128)(2,1)S(1)}, u32[]{:S(2)}, u32[]{:S(2)}) %all-to-all-start) | async-done | bytes 393248 | tf_op jit(solution)/shard_map/all_to_all | solution.py:50
  114.0 0.8 broadcast_in_dim.23
  114.8 4.6 %all-to-all-start.1 = ((bf16[8,256,96]{1,2,0:T(8,128)(2,1)}), bf16[8,256,96]{1,2,0:T(8,128)(2,1)S(1)}, u32[]{:S(2)}, u32[]{:S(2)}) async-start(bf16[8,256,96]{1,2,0:T(8,128)(2,1)} %broadcast_in_dim.23), calls=%async_computation.1 | async-start | bytes 786432 | tf_op jit(solution)/shard_map/all_to_all | solution.py:53
  119.4 11.7 %all-gather.2.cloned.1.call-done = bf16[6144,768]{1,0:T(8,128)(2,1)} async-done(((bf16[96,768]{1,0:T(8,128)(2,1)}), bf16[6144,768]{1,0:T(8,128)(2,1)}) %all-gather.2.cloned.1.call-update) | async-done | bytes 9437200 | tf_op jit(solution)/shard_map/all_gather | solution.py:38
  131.1 12.7 %convolution_bitcast_fusion = f32[8,96,768]{2,1,0:T(8,128)} fusion(bf16[8,768,768]{2,1,0:T(8,128)(2,1)} %bitcast.42, bf16[96,6144]{1,0:T(8,128)(2,1)S(1)} %copy-done, bf16[6144,768]{1,0:T(8,128)(2,1)} %all-gather.2.cloned.1.call-done, f32[768]{0:T(1024)S(1)} %copy-done.4, f32[96]{0:T(128)S(1)} %copy-done.5), kind=kOutput, calls=%fused_computation | convolution fusion | flops 1812234240 | bytes 22416768 | tf_op jit(solution)/shard_map/dot_general | solution.py:66
  143.8 0.7 copy-done.1
  144.5 3.9 %all-to-all-start.2 = ((f32[8,96,768]{2,1,0:T(8,128)}), f32[8,96,768]{2,1,0:T(8,128)S(1)}, u32[]{:S(2)}, u32[]{:S(2)}) async-start(f32[8,96,768]{2,1,0:T(8,128)} %convolution_bitcast_fusion), calls=%async_computation.2 | async-start | bytes 4718592 | tf_op jit(solution)/shard_map/all_to_all | solution.py:70
  148.5 1.2 slice_bitcast_fusion.8
  149.7 2.5 %fusion.3 = f32[768,96]{0,1:T(8,128)} fusion(bf16[1024,96]{0,1:T(8,128)(2,1)S(1)} %bitcast.44, bf16[2,1024,768]{2,1,0:T(8,128)(2,1)} %constant_dynamic-update-slice_fusion.11), kind=kOutput, calls=%fused_computation.6 | convolution fusion | flops 151068672 | bytes 2064384 | tf_op jit(solution)/shard_map/dot_general | solution.py:56
  152.2 1.1 fusion.2
  153.4 24.1 %all-to-all-done.2 = f32[8,96,768]{2,1,0:T(8,128)S(1)} async-done(((f32[8,96,768]{2,1,0:T(8,128)}), f32[8,96,768]{2,1,0:T(8,128)S(1)}, u32[]{:S(2)}, u32[]{:S(2)}) %all-to-all-start.2) | async-done | bytes 2359328 | tf_op jit(solution)/shard_map/all_to_all | solution.py:70
  177.5 0.8 reduce_sum.9
  (21 shorter events, 0.1 us)
Async XLA Ops:
  7.2 123.9 %copy-start = (bf16[96,6144]{1,0:T(8,128)(2,1)S(1)}, bf16[96,6144]{1,0:T(8,128)(2,1)}, u32[]{:S(2)}) copy-start(bf16[96,6144]{1,0:T(8,128)(2,1)} %param.12) | copy-start | bytes 3538948
  7.2 123.9 %all-gather.2.cloned.1.call-start = ((), (), s32[]{:S(2)}) async-start(), calls=%async_computation.3 | async-start | bytes 9584640 | tf_op jit(solution)/shard_map/all_gather | solution.py:38
  10.0 14.5 %collective-permute-start.1 = (bf16[2,16,768]{2,1,0:T(8,128)(2,1)S(1)}, bf16[2,16,768]{2,1,0:T(8,128)(2,1)S(1)}, u32[]{:S(2)}, u32[]{:S(2)}) collective-permute-start(bf16[2,16,768]{2,1,0:T(8,128)(2,1)S(1)} %get-tuple-element.27), channel_id=1, source_target_pairs={{256,0},{384,128},{0,256},{128,384},{257,1},{385,129},{1,257},{129... | collective-permute-start | bytes 147464 | tf_op jit(solution)/shard_map/ppermute | solution.py:14
  18.3 6.4 %collective-permute-start = (bf16[2,16,768]{2,1,0:T(8,128)(2,1)S(1)}, bf16[2,16,768]{2,1,0:T(8,128)(2,1)S(1)}, u32[]{:S(2)}, u32[]{:S(2)}) collective-permute-start(bf16[2,16,768]{2,1,0:T(8,128)(2,1)S(1)} %get-tuple-element.27), channel_id=1, source_target_pairs={{128,0},{256,128},{384,256},{0,384},{129,1},{257,129},{385,257},{1... | collective-permute-start | bytes 147464 | tf_op jit(solution)/shard_map/ppermute | solution.py:14
  20.3 7.0 %collective-permute-start.2 = (bf16[2,16,768]{2,1,0:T(8,128)(2,1)S(1)}, bf16[2,16,768]{2,1,0:T(8,128)(2,1)S(1)}, u32[]{:S(2)}, u32[]{:S(2)}) collective-permute-start(bf16[2,16,768]{2,1,0:T(8,128)(2,1)S(1)} %get-tuple-element.27), channel_id=1, source_target_pairs={{384,0},{0,128},{128,256},{256,384},{385,1},{1,129},{129,257},{257... | collective-permute-start | bytes 147464 | tf_op jit(solution)/shard_map/ppermute | solution.py:14
  27.3 14.5 %collective-permute-start.4 = (bf16[2,64,768]{2,1,0:T(8,128)(2,1)S(1)}, bf16[2,64,768]{2,1,0:T(8,128)(2,1)S(1)}, u32[]{:S(2)}, u32[]{:S(2)}) collective-permute-start(bf16[2,64,768]{2,1,0:T(8,128)(2,1)S(1)} %pad_maximum_fusion), channel_id=1, source_target_pairs={{112,0},{0,16},{16,32},{32,48},{48,64},{64,80},{80,96},{96,112},{1... | collective-permute-start | bytes 589832 | tf_op jit(solution)/shard_map/ppermute | solution.py:14
  31.3 12.4 %collective-permute-start.3 = (bf16[2,64,768]{2,1,0:T(8,128)(2,1)S(1)}, bf16[2,64,768]{2,1,0:T(8,128)(2,1)S(1)}, u32[]{:S(2)}, u32[]{:S(2)}) collective-permute-start(bf16[2,64,768]{2,1,0:T(8,128)(2,1)S(1)} %pad_maximum_fusion), channel_id=1, source_target_pairs={{16,0},{32,16},{48,32},{64,48},{80,64},{96,80},{112,96},{0,112},{1... | collective-permute-start | bytes 589832 | tf_op jit(solution)/shard_map/ppermute | solution.py:14
  41.8 8.0 %collective-permute-start.6 = (bf16[2,64,768]{2,1,0:T(8,128)(2,1)S(1)}, bf16[2,64,768]{2,1,0:T(8,128)(2,1)S(1)}, u32[]{:S(2)}, u32[]{:S(2)}) collective-permute-start(bf16[2,64,768]{2,1,0:T(8,128)(2,1)S(1)} %collective-permute-done.4), channel_id=1, source_target_pairs={{112,0},{0,16},{16,32},{32,48},{48,64},{64,80},{80,96},{96,112},{1... | collective-permute-start | bytes 589832 | tf_op jit(solution)/shard_map/ppermute | solution.py:14
  43.7 8.0 %collective-permute-start.5 = (bf16[2,64,768]{2,1,0:T(8,128)(2,1)S(1)}, bf16[2,64,768]{2,1,0:T(8,128)(2,1)S(1)}, u32[]{:S(2)}, u32[]{:S(2)}) collective-permute-start(bf16[2,64,768]{2,1,0:T(8,128)(2,1)S(1)} %collective-permute-done.3), channel_id=1, source_target_pairs={{16,0},{32,16},{48,32},{64,48},{80,64},{96,80},{112,96},{0,112},{1... | collective-permute-start | bytes 589832 | tf_op jit(solution)/shard_map/ppermute | solution.py:14
  49.8 15.1 %collective-permute-start.8 = (bf16[2,64,768]{2,1,0:T(8,128)(2,1)S(1)}, bf16[2,64,768]{2,1,0:T(8,128)(2,1)S(1)}, u32[]{:S(2)}, u32[]{:S(2)}) collective-permute-start(bf16[2,64,768]{2,1,0:T(8,128)(2,1)S(1)} %collective-permute-done.6), channel_id=1, source_target_pairs={{112,0},{0,16},{16,32},{32,48},{48,64},{64,80},{80,96},{96,112},{1... | collective-permute-start | bytes 589832 | tf_op jit(solution)/shard_map/ppermute | solution.py:14
  51.8 7.5 %collective-permute-start.7 = (bf16[2,64,768]{2,1,0:T(8,128)(2,1)S(1)}, bf16[2,64,768]{2,1,0:T(8,128)(2,1)S(1)}, u32[]{:S(2)}, u32[]{:S(2)}) collective-permute-start(bf16[2,64,768]{2,1,0:T(8,128)(2,1)S(1)} %collective-permute-done.5), channel_id=1, source_target_pairs={{16,0},{32,16},{48,32},{64,48},{80,64},{96,80},{112,96},{0,112},{1... | collective-permute-start | bytes 589832 | tf_op jit(solution)/shard_map/ppermute | solution.py:14
  59.3 7.5 %collective-permute-start.9 = (bf16[2,64,768]{2,1,0:T(8,128)(2,1)S(1)}, bf16[2,64,768]{2,1,0:T(8,128)(2,1)S(1)}, u32[]{:S(2)}, u32[]{:S(2)}) collective-permute-start(bf16[2,64,768]{2,1,0:T(8,128)(2,1)S(1)} %collective-permute-done.7), channel_id=1, source_target_pairs={{16,0},{32,16},{48,32},{64,48},{80,64},{96,80},{112,96},{0,112},{1... | collective-permute-start | bytes 589832 | tf_op jit(solution)/shard_map/ppermute | solution.py:14
  67.5 1.7 copy-start.2
  69.2 12.3 %collective-permute-start.10 = (bf16[2,512,768]{2,1,0:T(8,128)(2,1)}, bf16[2,512,768]{2,1,0:T(8,128)(2,1)S(1)}, u32[]{:S(2)}, u32[]{:S(2)}) collective-permute-start(bf16[2,512,768]{2,1,0:T(8,128)(2,1)} %get-tuple-element.5), channel_id=1, source_target_pairs={{8,0},{0,8},{9,1},{1,9},{10,2},{2,10},{11,3},{3,11},{12,4},{4,12},... | collective-permute-start | bytes 4718600 | tf_op jit(solution)/shard_map/ppermute | solution.py:14
  81.5 49.6 %copy-start.4 = (f32[768]{0:T(1024)S(1)}, f32[768]{0:T(1024)}, u32[]{:S(2)}) copy-start(f32[768]{0:T(1024)} %param.14) | copy-start | bytes 9220
  81.5 49.6 %copy-start.5 = (f32[96]{0:T(128)S(1)}, f32[96]{0:T(128)}, u32[]{:S(2)}) copy-start(f32[96]{0:T(128)} %param.15) | copy-start | bytes 1156
  85.3 28.7 %all-to-all-start = ((bf16[8,256,96]{1,2,0:T(8,128)(2,1)}), bf16[8,256,96]{1,2,0:T(8,128)(2,1)S(1)}, u32[]{:S(2)}, u32[]{:S(2)}) async-start(bf16[8,256,96]{1,2,0:T(8,128)(2,1)} %copy.12), calls=%async_computation | async-start | bytes 786432 | tf_op jit(solution)/shard_map/all_to_all | solution.py:50
  114.8 29.0 %all-to-all-start.1 = ((bf16[8,256,96]{1,2,0:T(8,128)(2,1)}), bf16[8,256,96]{1,2,0:T(8,128)(2,1)S(1)}, u32[]{:S(2)}, u32[]{:S(2)}) async-start(bf16[8,256,96]{1,2,0:T(8,128)(2,1)} %broadcast_in_dim.23), calls=%async_computation.1 | async-start | bytes 786432 | tf_op jit(solution)/shard_map/all_to_all | solution.py:53
  143.8 0.7 copy-start.1
  144.5 32.9 %all-to-all-start.2 = ((f32[8,96,768]{2,1,0:T(8,128)}), f32[8,96,768]{2,1,0:T(8,128)S(1)}, u32[]{:S(2)}, u32[]{:S(2)}) async-start(f32[8,96,768]{2,1,0:T(8,128)} %convolution_bitcast_fusion), calls=%async_computation.2 | async-start | bytes 4718592 | tf_op jit(solution)/shard_map/all_to_all | solution.py:70
  148.5 3.8 %copy-start.3 = (bf16[2,1024,768]{2,1,0:T(8,128)(2,1)S(1)}, bf16[2,1024,768]{2,1,0:T(8,128)(2,1)}, u32[]{:S(2)}) copy-start(bf16[2,1024,768]{2,1,0:T(8,128)(2,1)} %constant_dynamic-update-slice_fusion.11) | copy-start | bytes 9437188
Sparse Core Ops, SparseCore 0:
  11.3 119.7 all-gather.1

commit v2 on v1

v2 whole, which is shorter than its diff:
```python
import functools

import jax
import jax.numpy as jnp
from jax import lax
from jax.experimental import pallas as pl
from jax.experimental.pallas import tpu as pltpu
from jax.sharding import Mesh, PartitionSpec as P

DAMPING = 0.1
SAMPLED = 768
DP = ("yh", "z", "core")
GROUP = ("yl", "x")
GATHERED = 384


def shift(value, axis, by):
    size = lax.axis_size(axis)
    return lax.ppermute(value, axis, [((i + by) % size, i) for i in range(size)])


def spread(block, axis):
    size = lax.axis_size(axis)
    return lax.all_to_all(jnp.broadcast_to(block[None], (size,) + block.shape), axis, 0, 0, tiled=True)


def ring_z(block):
    chunks = [(0, block)]
    up = down = block
    for step in range(1, 5):
        up = shift(up, "z", 1)
        chunks.append((step, up))
        if step < 4:
            down = shift(down, "z", -1)
            chunks.append((-step, down))
    return chunks


def precondition_kernel(
    near, place, gathered, gathered_other, *refs
):
    ring_refs, (grad, in_eigs, out_eigs, terms, basis, sems) = refs[:-6], refs[-6:]
    z, core = place[0], place[1]
    copies = []

    def bring(src, z_at, core_at, start, width):
        copy = pltpu.make_async_copy(
            src, basis.at[:, z_at, core_at, :, pl.ds(start, width)], sems.at[len(copies)]
        )
        copy.start()
        copies.append(copy)

    left = gathered.shape[-1]
    right = grad.shape[1] // 8 - left
    for k in range(8):
        bring(gathered.at[k], k, core, 0, left)
        bring(gathered_other.at[k], k, 1 - core, 0, left)
    half = len(ring_refs) // 2
    for side in range(2):
        at = 0
        for ref in ring_refs[side * half : (side + 1) * half]:
            for k in range(ref.shape[0]):
                z_at = lax.rem(z + (near[at] + 8), 8)
                bring(ref.at[k], z_at, core if side == 0 else 1 - core, left, right)
                at += 1
    for copy in copies:
        copy.wait()

    width = left + right
    projected = jnp.zeros((grad.shape[0], width), jnp.float32)
    for k in range(8):
        rows = basis[k // 2, (k % 2) * 4 : (k % 2) * 4 + 4].reshape(width, width)
        projected += jnp.dot(
            grad[:, k * width : (k + 1) * width], rows, preferred_element_type=jnp.float32
        )
    denominator = out_eigs[...] * in_eigs[...] + DAMPING
    scaled = (projected / denominator).astype(jnp.bfloat16)
    for k in range(8):
        rows = basis[k // 2, (k % 2) * 4 : (k % 2) * 4 + 4].reshape(width, width)
        terms[k] = lax.dot_general(
            scaled, rows, (((1,), (1,)), ((), ())), preferred_element_type=jnp.float32
        )


def precondition(near, gathered, gathered_other, ring, ring_other, grad, in_eigs, out_eigs):
    place = jnp.stack([lax.axis_index("z"), lax.axis_index("core")]).astype(jnp.int32)
    rows = grad.shape[0]
    width = in_eigs.shape[0]
    anywhere = pl.BlockSpec(memory_space=pl.ANY)
    vmem = pl.BlockSpec(memory_space=pltpu.VMEM)
    return pl.pallas_call(
        functools.partial(precondition_kernel, near),
        out_shape=jax.ShapeDtypeStruct((8, rows, width), jnp.float32),
        in_specs=[pl.BlockSpec(memory_space=pltpu.SMEM)]
        + [anywhere] * (2 + len(ring) + len(ring_other))
        + [vmem] * 3,
        out_specs=vmem,
        scratch_shapes=[
            pltpu.VMEM((4, 8, 2, rows, width), jnp.bfloat16),
            pltpu.SemaphoreType.DMA((32,)),
        ],
        compiler_params=pltpu.CompilerParams(vmem_limit_bytes=36 << 20),
        cost_estimate=pl.CostEstimate(
            flops=4 * rows * 8 * width * width, bytes_accessed=24 * width * width, transcendentals=0
        ),
    )(place, gathered, gathered_other, *ring, *ring_other, grad, in_eigs[None, :], out_eigs[:, None])


def shards(activations, out_grads, counts, owners, rotated_grad, basis, input_eigs, output_eigs):
    slots, width = activations.shape
    owned_width = basis.shape[0]
    blocks_per = width // owned_width
    group_count = lax.axis_size("yl") * lax.axis_size("x")

    first = spread(basis[:, :GATHERED], "yh")
    second = spread(basis[:, GATHERED:], "yh")
    gathered = lax.all_gather(first, "z", axis=0)
    gathered_other = shift(gathered, "core", 1)
    chunks = ring_z(second)
    near = [distance for distance, _ in chunks]
    early = jnp.stack([value for _, value in chunks[:5]])
    late = jnp.stack([value for _, value in chunks[5:]])
    ring = [early, late]
    ring_other = [shift(v, "core", 1) for v in ring]

    is_live = lax.broadcasted_iota(jnp.int32, (slots, 1), 0) < counts[0]
    kept = jnp.stack([jnp.where(is_live, v, jnp.zeros_like(v)) for v in (activations, out_grads)])
    kept = spread(spread(kept, "z"), "yh")
    kept = jnp.moveaxis(kept, 2, 0).reshape(2, -1, width)
    both = jnp.concatenate([kept, shift(kept, "core", 1)], axis=1)
    samples = both.shape[1]
    owner_idx = owners[0]
    offset = owner_idx % blocks_per * owned_width
    owned = lax.dynamic_slice_in_dim(both, offset, owned_width, 2)
    pieces = owned.reshape(group_count, 2 * samples // group_count, owned_width)
    pieces = lax.all_to_all(pieces, GROUP, 0, 0, tiled=True)
    piece = lax.dynamic_index_in_dim(pieces, owner_idx // blocks_per, 0, keepdims=False)
    owned = spread(piece, GROUP).reshape(2, samples, owned_width)
    contract_rows = (((0,), (0,)), ((), ()))
    cov_in, cov_out = (
        lax.dot_general(both[k], owned[k], contract_rows, preferred_element_type=jnp.float32)
        / jnp.float32(SAMPLED)
        for k in range(2)
    )

    terms = precondition(
        near, gathered, gathered_other, ring, ring_other, rotated_grad, input_eigs, output_eigs
    )
    terms = lax.all_to_all(terms, GROUP, 0, 0, tiled=True)
    preconditioned = jnp.sum(terms, axis=0)
    return (cov_in, cov_out, preconditioned)


def solution(mesh):
    devices = mesh.devices.reshape(4, 8, 2, 2, 4)
    fine = Mesh(devices, DP + GROUP)
    placed = (
        P(DP, GROUP),
        P(DP, GROUP),
        P(DP),
        P(DP),
        P(DP, None),
        P(DP, GROUP),
        P(GROUP),
        P(DP),
    )
    return jax.shard_map(
        shards,
        mesh=fine,
        in_specs=placed,
        out_specs=(P(GROUP, DP), P(GROUP, DP), P(DP, GROUP)),
        check_vma=False,
    )
```

time: 186 us -> 227 us (1.22)
  blocking collectives: 0 us -> 64.8 us
  waiting for transfers between devices: 66.6 us -> 44.6 us
  matrix products: 16.3 us -> 3.47 us
  Pallas kernels: 0 us -> 10.1 us
  starting transfers between devices: 69.4 us -> 66.7 us
  local copies, waits for them, and re-layouts: 15 us -> 17.6 us
    all_to_all x0 -> x2, blocking collectives: none -> 64.8 us  [spread(): lax.all_to_all(jnp.broadcast_to(block[None], (size,) + block.shape), axis...]
    all_to_all x1, waiting for transfers between devices: 22.1 us -> 0.01 us  [shards(): pieces = lax.all_to_all(pieces, GROUP, 0, 0, tiled=True)]
    ppermute x11, starting transfers between devices: 54.2 us -> 39.3 us  [shift(): lax.ppermute(value, axis, [((i + by) % size, i) for i in range(size)])]
    all_to_all x1 -> x3, waiting for transfers between devices: 0.01 us -> 13.3 us  [spread(): lax.all_to_all(jnp.broadcast_to(block[None], (size,) + block.shape), axis...]
    dot_general x1 -> x0, matrix products: 12.7 us -> none  [shards(): lax.dot_general(wide, scaled, (((2,), (1,)), ((), ())), preferred_element...]
    all_to_all x1 -> x3, starting transfers between devices: 4.64 us -> 16.4 us  [spread(): lax.all_to_all(jnp.broadcast_to(block[None], (size,) + block.shape), axis...]
    all_gather x1, waiting for transfers between devices: 11.7 us -> 0.02 us  [shards(): gathered = lax.all_gather(first, 'z', axis=0)]
    pallas_call x0 -> x1, Pallas kernels: none -> 10.1 us  [precondition(): pl.pallas_call(functools.partial(precondition_kernel, near), out_shape=ja...]
  transfers between devices with their start and end apart: 15 -> 17, of which waited for: 9 -> 6; matrix products, arithmetic and copies ran while one was open for 16% -> 8% of each run, Pallas kernels for 0% -> 4%
where the time goes in v2:
time: 227 us; the launch traced here: 225 us
  starting transfers between devices  66.7 us (29%)
  blocking collectives  64.8 us (29%)
  waiting for transfers between devices  44.6 us (20%)
  local copies, waits for them, and re-layouts  17.6 us (8%)
  between operations  15.7 us (7%)
  Pallas kernels  10.1 us (4%)
  matrix products  3.47 us (2%)
  other arithmetic  2.54 us (1%)
    all_to_all x2, blocking collectives, spread(): lax.all_to_all(jnp.broadcast_to(block[None], (size,) + block.shape), axis...  64.8 us
    ppermute x11, starting transfers between devices, shift(): lax.ppermute(value, axis, [((i + by) % size, i) for i in range(size)])  39.3 us
    all_to_all x1, waiting for transfers between devices, shards(): terms = lax.all_to_all(terms, GROUP, 0, 0, tiled=True)  23.9 us
    all_to_all x3, starting transfers between devices, spread(): lax.all_to_all(jnp.broadcast_to(block[None], (size,) + block.shape), axis...  16.4 us
    all_to_all x3, waiting for transfers between devices, spread(): lax.all_to_all(jnp.broadcast_to(block[None], (size,) + block.shape), axis...  13.3 us
    pallas_call x1, Pallas kernels, precondition(): pl.pallas_call(functools.partial(precondition_kernel, near), out_shape=ja...  10.1 us
    unnamed x27, local copies, waits for them, and re-layouts  9.45 us
    ppermute x11, waiting for transfers between devices, shift(): lax.ppermute(value, axis, [((i + by) % size, i) for i in range(size)])  7.31 us
  transfers between devices with their start and end apart: 17, of which 6 were waited for; matrix products, arithmetic and copies ran while one was open for 8% of the time, Pallas kernels for 4%

profile of v2, /device:TPU:1, one launch (start us, length us, event | category | flops | bytes accessed | tf_op | source)
XLA Modules:
  0.0 225.4 jit_solution(4464036175957356978)
XLA Ops:
  7.2 0.9 fusion.17
  8.1 0.7 broadcast_in_dim.54
  8.9 7.6 %all-to-all-start.4 = ((bf16[4,96,384]{2,1,0:T(8,128)(2,1)}), bf16[4,96,384]{2,1,0:T(8,128)(2,1)S(1)}, u32[]{:S(2)}, u32[]{:S(2)}) async-start(bf16[4,96,384]{2,1,0:T(8,128)(2,1)} %broadcast_in_dim.54), calls=%async_computation.4 | async-start | bytes 589824 | tf_op jit(solution)/shard_map/all_to_all | solution.py:24
  17.2 8.4 %all-to-all-done.4 = bf16[4,96,384]{2,1,0:T(8,128)(2,1)S(1)} async-done(((bf16[4,96,384]{2,1,0:T(8,128)(2,1)}), bf16[4,96,384]{2,1,0:T(8,128)(2,1)S(1)}, u32[]{:S(2)}, u32[]{:S(2)}) %all-to-all-start.4) | async-done | bytes 294944 | tf_op jit(solution)/shard_map/all_to_all | solution.py:24
  25.6 0.7 copy-done.6
  26.5 21.0 %all_to_all.35 = bf16[8,2,16,768]{3,2,1,0:T(8,128)(2,1)S(1)} all-to-all(bf16[8,2,16,768]{3,2,1,0:T(8,128)(2,1)S(1)} %broadcast_in_dim.50), channel_id=1, replica_groups=mesh['yh'=4,'z'=8,'core'=2,'yl'=2,'x'=4] {'z'}, dimensions={0} | all-to-all | bytes 786432 | tf_op jit(solution)/shard_map/all_to_all | solution.py:24
  47.5 0.1 broadcast_in_dim.51
  47.7 43.8 %all_to_all.36 = bf16[4,8,2,16,768]{4,3,1,2,0:T(8,128)(2,1)S(1)} all-to-all(bf16[4,8,2,16,768]{4,3,1,2,0:T(8,128)(2,1)S(1)} %broadcast_in_dim.51), channel_id=1, replica_groups=mesh['yh'=4,'z'=8,'core'=2,'yl'=2,'x'=4] {'yh'}, dimensions={0} | all-to-all | bytes 3145728 | tf_op jit(solution)/shard_map/all_to_all | solution.py:24
  91.5 0.7 broadcast_in_dim.55
  92.2 3.5 %all-to-all-start.5 = ((bf16[4,96,384]{2,1,0:T(8,128)(2,1)}), bf16[4,96,384]{2,1,0:T(8,128)(2,1)S(1)}, u32[]{:S(2)}, u32[]{:S(2)}) async-start(bf16[4,96,384]{2,1,0:T(8,128)(2,1)} %broadcast_in_dim.55), calls=%async_computation.5 | async-start | bytes 589824 | tf_op jit(solution)/shard_map/all_to_all | solution.py:24
  95.7 0.1 copy.17
  95.8 3.2 %collective-permute-start = (bf16[2,512,768]{2,1,0:T(8,128)(2,1)S(1)}, bf16[2,512,768]{2,1,0:T(8,128)(2,1)S(1)}, u32[]{:S(2)}, u32[]{:S(2)}) collective-permute-start(bf16[2,512,768]{2,1,0:T(8,128)(2,1)S(1)} %bitcast.54), channel_id=1, source_target_pairs={{8,0},{0,8},{9,1},{1,9},{10,2},{2,10},{11,3},{3,11},{12,4},{4,12},... | collective-permute-start | bytes 4718600 | tf_op jit(solution)/shard_map/ppermute | solution.py:19
  99.0 4.9 %all-to-all-done.5 = bf16[4,96,384]{2,1,0:T(8,128)(2,1)S(1)} async-done(((bf16[4,96,384]{2,1,0:T(8,128)(2,1)}), bf16[4,96,384]{2,1,0:T(8,128)(2,1)S(1)}, u32[]{:S(2)}, u32[]{:S(2)}) %all-to-all-start.5) | async-done | bytes 294944 | tf_op jit(solution)/shard_map/all_to_all | solution.py:24
  103.8 1.9 collective-permute-start.3
  105.7 4.6 %collective-permute-start.2 = (bf16[4,96,384]{2,1,0:T(8,128)(2,1)S(1)}, bf16[4,96,384]{2,1,0:T(8,128)(2,1)}, u32[]{:S(2)}, u32[]{:S(2)}) collective-permute-start(bf16[4,96,384]{2,1,0:T(8,128)(2,1)S(1)} %all-to-all-done.5), channel_id=1, source_target_pairs={{16,0},{32,16},{48,32},{64,48},{80,64},{96,80},{112,96},{0,112},{1... | collective-permute-start | bytes 884744 | tf_op jit(solution)/shard_map/ppermute | solution.py:19
  110.3 0.8 bitcast_dynamic-update-slice_fusion.4
  111.1 1.5 collective-permute-done.3
  112.6 1.9 collective-permute-start.5
  114.5 4.6 %collective-permute-start.4 = (bf16[4,96,384]{2,1,0:T(8,128)(2,1)}, bf16[4,96,384]{2,1,0:T(8,128)(2,1)}, u32[]{:S(2)}, u32[]{:S(2)}) collective-permute-start(bf16[4,96,384]{2,1,0:T(8,128)(2,1)} %collective-permute-done.2), channel_id=1, source_target_pairs={{16,0},{32,16},{48,32},{64,48},{80,64},{96,80},{112,96},{0,112},{1... | collective-permute-start | bytes 884744 | tf_op jit(solution)/shard_map/ppermute | solution.py:19
  119.1 6.6 %collective-permute-start.1 = (bf16[8,4,96,384]{3,2,1,0:T(8,128)(2,1)}, bf16[8,4,96,384]{3,2,1,0:T(8,128)(2,1)}, u32[]{:S(2)}, u32[]{:S(2)}) collective-permute-start(bf16[8,4,96,384]{3,2,1,0:T(8,128)(2,1)} %bitcast.52), channel_id=1, source_target_pairs={{8,0},{0,8},{9,1},{1,9},{10,2},{2,10},{11,3},{3,11},{12,4},{4,12},... | collective-permute-start | bytes 7077896 | tf_op jit(solution)/shard_map/ppermute | solution.py:19
  125.7 1.7 bitcast_dynamic-update-slice_fusion.3
  127.4 1.7 bitcast_dynamic-update-slice_fusion.2
  129.2 1.9 collective-permute-start.6
  131.1 1.7 bitcast_dynamic-update-slice_fusion.1
  132.8 1.7 bitcast_dynamic-update-slice_fusion.refs_0_
  134.5 4.7 %collective-permute-start.9 = (bf16[5,4,96,384]{3,2,1,0:T(8,128)(2,1)}, bf16[5,4,96,384]{3,2,1,0:T(8,128)(2,1)}, u32[]{:S(2)}, u32[]{:S(2)}) collective-permute-start(bf16[5,4,96,384]{3,2,1,0:T(8,128)(2,1)} %bitcast_dynamic-update-slice_fusion.refs_0_), channel_id=1, source_target_pairs={{8,0},{0,8},{9,1},{1,9},{10,2},{2,10},{11,3},{3,11},{12,4},{4,12},... | collective-permute-start | bytes 4423688 | tf_op jit(solution)/shard_map/ppermute | solution.py:19
  139.9 1.4 fusion.14
  141.3 2.0 copy.19
  143.3 5.8 %all-to-all-start.2 = ((bf16[8,256,96]{1,2,0:T(8,128)(2,1)}), bf16[8,256,96]{1,2,0:T(8,128)(2,1)}, u32[]{:S(2)}, u32[]{:S(2)}) async-start(bf16[8,256,96]{1,2,0:T(8,128)(2,1)} %copy.19), calls=%async_computation.2 | async-start | bytes 786432 | tf_op jit(solution)/shard_map/all_to_all | solution.py:136
  149.2 1.9 collective-permute-start.7
  151.1 4.6 %collective-permute-start.8 = (bf16[4,96,384]{2,1,0:T(8,128)(2,1)S(1)}, bf16[4,96,384]{2,1,0:T(8,128)(2,1)S(1)}, u32[]{:S(2)}, u32[]{:S(2)}) collective-permute-start(bf16[4,96,384]{2,1,0:T(8,128)(2,1)S(1)} %collective-permute-done.6), channel_id=1, source_target_pairs={{16,0},{32,16},{48,32},{64,48},{80,64},{96,80},{112,96},{0,112},{1... | collective-permute-start | bytes 884744 | tf_op jit(solution)/shard_map/ppermute | solution.py:19
  155.7 5.1 %collective-permute-done.7 = bf16[4,96,384]{2,1,0:T(8,128)(2,1)S(1)} collective-permute-done((bf16[4,96,384]{2,1,0:T(8,128)(2,1)}, bf16[4,96,384]{2,1,0:T(8,128)(2,1)S(1)}, u32[]{:S(2)}, u32[]{:S(2)}) %collective-permute-start.7) | collective-permute-done | bytes 294944 | tf_op jit(solution)/shard_map/ppermute | solution.py:19
  160.8 0.7 collective-permute-done.8
  161.5 0.1 pad_maximum_fusion.1.refs_1_
  161.6 3.5 %collective-permute-start.10 = (bf16[3,4,96,384]{3,2,1,0:T(8,128)(2,1)S(1)}, bf16[3,4,96,384]{3,2,1,0:T(8,128)(2,1)}, u32[]{:S(2)}, u32[]{:S(2)}) collective-permute-start(bf16[3,4,96,384]{3,2,1,0:T(8,128)(2,1)S(1)} %pad_maximum_fusion.1.refs_1_), channel_id=1, source_target_pairs={{8,0},{0,8},{9,1},{1,9},{10,2},{2,10},{11,3},{3,11},{12,4},{4,12},... | collective-permute-start | bytes 2654216 | tf_op jit(solution)/shard_map/ppermute | solution.py:19
  165.1 0.8 dynamic-slice_bitcast_fusion
  165.9 0.8 broadcast_in_dim.53
  166.7 5.3 %all-to-all-start.3 = ((bf16[8,256,96]{1,2,0:T(8,128)(2,1)}), bf16[8,256,96]{1,2,0:T(8,128)(2,1)}, u32[]{:S(2)}, u32[]{:S(2)}) async-start(bf16[8,256,96]{1,2,0:T(8,128)(2,1)} %broadcast_in_dim.53), calls=%async_computation.3 | async-start | bytes 786432 | tf_op jit(solution)/shard_map/all_to_all | solution.py:24
  172.0 0.1 copy.22.refs_6_
  172.2 1.3 copy-done.1
  173.5 10.1 %shard_map.103 = f32[8,96,768]{2,1,0:T(8,128)} custom-call(s32[2]{0:T(128)S(1)} %pad_add_fusion.place, bf16[8,4,96,384]{3,2,1,0:T(8,128)(2,1)S(1)} %bitcast.53, bf16[8,4,96,384]{3,2,1,0:T(8,128)(2,1)} %collective-permute-done.1.gathered_other, bf16[5,4,96,384]{3,2,1,0:T(8,128)(2,1)} %bitcast_dynamic-update-slice_fusion.refs_0_, ...), custom_call_target="tpu_custom_call" | custom-call | flops 1811939328 | bytes 14155776 | tf_op jit(solution)/shard_map/pallas_call | solution.py:91
  183.6 5.1 %all-to-all-start.6 = ((f32[8,96,768]{2,1,0:T(8,128)}), f32[8,96,768]{2,1,0:T(8,128)S(1)}, u32[]{:S(2)}, u32[]{:S(2)}) async-start(f32[8,96,768]{2,1,0:T(8,128)} %shard_map.103), calls=%async_computation.6 | async-start | bytes 4718592 | tf_op jit(solution)/shard_map/all_to_all | solution.py:149
  188.8 1.2 slice_bitcast_fusion
  190.0 0.4 copy-done.3
  190.4 2.4 %fusion.11 = f32[768,96]{0,1:T(8,128)} fusion(bf16[1024,96]{0,1:T(8,128)(2,1)S(1)} %bitcast.59, bf16[2,512,768]{2,1,0:T(8,128)(2,1)} %copy-done.4, bf16[2,512,768]{2,1,0:T(8,128)(2,1)S(1)} %bitcast.56), kind=kOutput, calls=%fused_computation.12 | convolution fusion | flops 154214400 | bytes 3637248 | tf_op jit(solution)/shard_map/dot_general | solution.py:141
  192.7 1.1 fusion.8
  193.8 23.9 %all-to-all-done.6 = f32[8,96,768]{2,1,0:T(8,128)S(1)} async-done(((f32[8,96,768]{2,1,0:T(8,128)}), f32[8,96,768]{2,1,0:T(8,128)S(1)}, u32[]{:S(2)}, u32[]{:S(2)}) %all-to-all-start.6) | async-done | bytes 2359328 | tf_op jit(solution)/shard_map/all_to_all | solution.py:149
  217.7 0.8 reduce_sum.9
  (41 shorter events, 0.4 us)
Async XLA Ops:
  7.2 19.2 %copy-start.8 = (bf16[16,768]{1,0:T(8,128)(2,1)S(1)}, bf16[16,768]{1,0:T(8,128)(2,1)}, u32[]{:S(2)}) copy-start(bf16[16,768]{1,0:T(8,128)(2,1)} %param.9) | copy-start | bytes 73732
  7.2 19.2 %copy-start.7 = (bf16[16,768]{1,0:T(8,128)(2,1)S(1)}, bf16[16,768]{1,0:T(8,128)(2,1)}, u32[]{:S(2)}) copy-start(bf16[16,768]{1,0:T(8,128)(2,1)} %param.8) | copy-start | bytes 73732
  8.9 16.7 %all-to-all-start.4 = ((bf16[4,96,384]{2,1,0:T(8,128)(2,1)}), bf16[4,96,384]{2,1,0:T(8,128)(2,1)S(1)}, u32[]{:S(2)}, u32[]{:S(2)}) async-start(bf16[4,96,384]{2,1,0:T(8,128)(2,1)} %broadcast_in_dim.54), calls=%async_computation.4 | async-start | bytes 589824 | tf_op jit(solution)/shard_map/all_to_all | solution.py:24
  16.5 102.6 %all-gather.3.cloned.1.call-start = ((), (), s32[]{:S(2)}) async-start(), calls=%async_computation.7 | async-start | bytes 2654208 | tf_op jit(solution)/shard_map/all_gather | solution.py:117
  25.6 0.7 copy-start.6
  92.2 11.6 %all-to-all-start.5 = ((bf16[4,96,384]{2,1,0:T(8,128)(2,1)}), bf16[4,96,384]{2,1,0:T(8,128)(2,1)S(1)}, u32[]{:S(2)}, u32[]{:S(2)}) async-start(bf16[4,96,384]{2,1,0:T(8,128)(2,1)} %broadcast_in_dim.55), calls=%async_computation.5 | async-start | bytes 589824 | tf_op jit(solution)/shard_map/all_to_all | solution.py:24
  95.8 45.6 %copy-start.2 = (bf16[4,8,2,16,768]{4,3,1,0,2:T(8,128)(2,1)}, bf16[4,8,2,16,768]{4,3,1,0,2:T(8,128)(2,1)S(1)}, u32[]{:S(2)}) copy-start(bf16[4,8,2,16,768]{4,3,1,0,2:T(8,128)(2,1)S(1)} %copy.17) | copy-start | bytes 4718596
  95.8 44.1 %collective-permute-start = (bf16[2,512,768]{2,1,0:T(8,128)(2,1)S(1)}, bf16[2,512,768]{2,1,0:T(8,128)(2,1)S(1)}, u32[]{:S(2)}, u32[]{:S(2)}) collective-permute-start(bf16[2,512,768]{2,1,0:T(8,128)(2,1)S(1)} %bitcast.54), channel_id=1, source_target_pairs={{8,0},{0,8},{9,1},{1,9},{10,2},{2,10},{11,3},{3,11},{12,4},{4,12},... | collective-permute-start | bytes 4718600 | tf_op jit(solution)/shard_map/ppermute | solution.py:19
  103.8 8.8 %collective-permute-start.3 = (bf16[4,96,384]{2,1,0:T(8,128)(2,1)S(1)}, bf16[4,96,384]{2,1,0:T(8,128)(2,1)}, u32[]{:S(2)}, u32[]{:S(2)}) collective-permute-start(bf16[4,96,384]{2,1,0:T(8,128)(2,1)S(1)} %all-to-all-done.5), channel_id=1, source_target_pairs={{112,0},{0,16},{16,32},{32,48},{48,64},{64,80},{80,96},{96,112},{1... | collective-permute-start | bytes 884744 | tf_op jit(solution)/shard_map/ppermute | solution.py:19
  105.7 8.8 %collective-permute-start.2 = (bf16[4,96,384]{2,1,0:T(8,128)(2,1)S(1)}, bf16[4,96,384]{2,1,0:T(8,128)(2,1)}, u32[]{:S(2)}, u32[]{:S(2)}) collective-permute-start(bf16[4,96,384]{2,1,0:T(8,128)(2,1)S(1)} %all-to-all-done.5), channel_id=1, source_target_pairs={{16,0},{32,16},{48,32},{64,48},{80,64},{96,80},{112,96},{0,112},{1... | collective-permute-start | bytes 884744 | tf_op jit(solution)/shard_map/ppermute | solution.py:19
  112.6 20.2 %collective-permute-start.5 = (bf16[4,96,384]{2,1,0:T(8,128)(2,1)}, bf16[4,96,384]{2,1,0:T(8,128)(2,1)}, u32[]{:S(2)}, u32[]{:S(2)}) collective-permute-start(bf16[4,96,384]{2,1,0:T(8,128)(2,1)} %collective-permute-done.3), channel_id=1, source_target_pairs={{112,0},{0,16},{16,32},{32,48},{48,64},{64,80},{80,96},{96,112},{1... | collective-permute-start | bytes 884744 | tf_op jit(solution)/shard_map/ppermute | solution.py:19
  114.5 14.6 %collective-permute-start.4 = (bf16[4,96,384]{2,1,0:T(8,128)(2,1)}, bf16[4,96,384]{2,1,0:T(8,128)(2,1)}, u32[]{:S(2)}, u32[]{:S(2)}) collective-permute-start(bf16[4,96,384]{2,1,0:T(8,128)(2,1)} %collective-permute-done.2), channel_id=1, source_target_pairs={{16,0},{32,16},{48,32},{64,48},{80,64},{96,80},{112,96},{0,112},{1... | collective-permute-start | bytes 884744 | tf_op jit(solution)/shard_map/ppermute | solution.py:19
  119.1 53.0 %collective-permute-start.1 = (bf16[8,4,96,384]{3,2,1,0:T(8,128)(2,1)}, bf16[8,4,96,384]{3,2,1,0:T(8,128)(2,1)}, u32[]{:S(2)}, u32[]{:S(2)}) collective-permute-start(bf16[8,4,96,384]{3,2,1,0:T(8,128)(2,1)} %bitcast.52), channel_id=1, source_target_pairs={{8,0},{0,8},{9,1},{1,9},{10,2},{2,10},{11,3},{3,11},{12,4},{4,12},... | collective-permute-start | bytes 7077896 | tf_op jit(solution)/shard_map/ppermute | solution.py:19
  129.2 22.0 %collective-permute-start.6 = (bf16[4,96,384]{2,1,0:T(8,128)(2,1)}, bf16[4,96,384]{2,1,0:T(8,128)(2,1)S(1)}, u32[]{:S(2)}, u32[]{:S(2)}) collective-permute-start(bf16[4,96,384]{2,1,0:T(8,128)(2,1)} %collective-permute-done.4), channel_id=1, source_target_pairs={{16,0},{32,16},{48,32},{64,48},{80,64},{96,80},{112,96},{0,112},{1... | collective-permute-start | bytes 884744 | tf_op jit(solution)/shard_map/ppermute | solution.py:19
  134.5 37.7 %collective-permute-start.9 = (bf16[5,4,96,384]{3,2,1,0:T(8,128)(2,1)}, bf16[5,4,96,384]{3,2,1,0:T(8,128)(2,1)}, u32[]{:S(2)}, u32[]{:S(2)}) collective-permute-start(bf16[5,4,96,384]{3,2,1,0:T(8,128)(2,1)} %bitcast_dynamic-update-slice_fusion.refs_0_), channel_id=1, source_target_pairs={{8,0},{0,8},{9,1},{1,9},{10,2},{2,10},{11,3},{3,11},{12,4},{4,12},... | collective-permute-start | bytes 4423688 | tf_op jit(solution)/shard_map/ppermute | solution.py:19
  139.9 1.4 copy-start.4
  143.3 21.8 %all-to-all-start.2 = ((bf16[8,256,96]{1,2,0:T(8,128)(2,1)}), bf16[8,256,96]{1,2,0:T(8,128)(2,1)}, u32[]{:S(2)}, u32[]{:S(2)}) async-start(bf16[8,256,96]{1,2,0:T(8,128)(2,1)} %copy.19), calls=%async_computation.2 | async-start | bytes 786432 | tf_op jit(solution)/shard_map/all_to_all | solution.py:136
  149.2 22.8 %copy-start.9 = (f32[768]{0:T(1024)S(1)}, f32[768]{0:T(1024)}, u32[]{:S(2)}) copy-start(f32[768]{0:T(1024)} %param.14) | copy-start | bytes 9220
  149.2 11.6 %collective-permute-start.7 = (bf16[4,96,384]{2,1,0:T(8,128)(2,1)}, bf16[4,96,384]{2,1,0:T(8,128)(2,1)S(1)}, u32[]{:S(2)}, u32[]{:S(2)}) collective-permute-start(bf16[4,96,384]{2,1,0:T(8,128)(2,1)} %collective-permute-done.5), channel_id=1, source_target_pairs={{112,0},{0,16},{16,32},{32,48},{48,64},{64,80},{80,96},{96,112},{1... | collective-permute-start | bytes 884744 | tf_op jit(solution)/shard_map/ppermute | solution.py:19
  151.1 10.3 %collective-permute-start.8 = (bf16[4,96,384]{2,1,0:T(8,128)(2,1)S(1)}, bf16[4,96,384]{2,1,0:T(8,128)(2,1)S(1)}, u32[]{:S(2)}, u32[]{:S(2)}) collective-permute-start(bf16[4,96,384]{2,1,0:T(8,128)(2,1)S(1)} %collective-permute-done.6), channel_id=1, source_target_pairs={{16,0},{32,16},{48,32},{64,48},{80,64},{96,80},{112,96},{0,112},{1... | collective-permute-start | bytes 884744 | tf_op jit(solution)/shard_map/ppermute | solution.py:19
  161.5 10.5 %copy-start.10 = (f32[96]{0:T(128)S(1)}, f32[96]{0:T(128)}, u32[]{:S(2)}) copy-start(f32[96]{0:T(128)} %param.15) | copy-start | bytes 1156
  161.5 10.7 %copy-start = (bf16[32,96,384]{2,1,0:T(8,128)(2,1)S(1)}, bf16[32,96,384]{2,1,0:T(8,128)(2,1)}, u32[]{:S(2)}) copy-start(bf16[32,96,384]{2,1,0:T(8,128)(2,1)} %all-gather.3.cloned.1.call-done) | copy-start | bytes 7077892
  161.6 10.6 %collective-permute-start.10 = (bf16[3,4,96,384]{3,2,1,0:T(8,128)(2,1)S(1)}, bf16[3,4,96,384]{3,2,1,0:T(8,128)(2,1)}, u32[]{:S(2)}, u32[]{:S(2)}) collective-permute-start(bf16[3,4,96,384]{3,2,1,0:T(8,128)(2,1)S(1)} %pad_maximum_fusion.1.refs_1_), channel_id=1, source_target_pairs={{8,0},{0,8},{9,1},{1,9},{10,2},{2,10},{11,3},{3,11},{12,4},{4,12},... | collective-permute-start | bytes 2654216 | tf_op jit(solution)/shard_map/ppermute | solution.py:19
  166.7 16.9 %all-to-all-start.3 = ((bf16[8,256,96]{1,2,0:T(8,128)(2,1)}), bf16[8,256,96]{1,2,0:T(8,128)(2,1)}, u32[]{:S(2)}, u32[]{:S(2)}) async-start(bf16[8,256,96]{1,2,0:T(8,128)(2,1)} %broadcast_in_dim.53), calls=%async_computation.3 | async-start | bytes 786432 | tf_op jit(solution)/shard_map/all_to_all | solution.py:24
  172.2 1.3 copy-start.1
  183.6 34.1 %all-to-all-start.6 = ((f32[8,96,768]{2,1,0:T(8,128)}), f32[8,96,768]{2,1,0:T(8,128)S(1)}, u32[]{:S(2)}, u32[]{:S(2)}) async-start(f32[8,96,768]{2,1,0:T(8,128)} %shard_map.103), calls=%async_computation.6 | async-start | bytes 4718592 | tf_op jit(solution)/shard_map/all_to_all | solution.py:149
  188.8 1.6 copy-start.3
  190.4 2.4 %copy-start.5 = (bf16[2,512,768]{2,1,0:T(8,128)(2,1)S(1)}, bf16[2,512,768]{2,1,0:T(8,128)(2,1)}, u32[]{:S(2)}) copy-start(bf16[2,512,768]{2,1,0:T(8,128)(2,1)} %copy-done.4) | copy-start | bytes 4718596
Sparse Core Ops, SparseCore 0:
  26.5 45.8 all-gather.2

commit v3 on v2

v3 whole, which is shorter than its diff:
```python
import jax
import jax.numpy as jnp
from jax import lax
from jax.experimental import pallas as pl
from jax.experimental.pallas import tpu as pltpu
from jax.sharding import Mesh, PartitionSpec as P

DAMPING = 0.1
SAMPLED = 768
DP = ("yh", "z", "core")
GROUP = ("yl", "x")
GATHERED, RINGED = 512, 256
NEAR = ((0, 1, -1), (2, -2), (3, -3, 4))


def shift(value, axis, by):
    size = lax.axis_size(axis)
    return lax.ppermute(value, axis, [((i + by) % size, i) for i in range(size)])


def others(block, axis):
    return [shift(block, axis, k) for k in range(1, lax.axis_size(axis))]


def spread(block, axis):
    size = lax.axis_size(axis)
    return lax.all_to_all(jnp.broadcast_to(block[None], (size,) + block.shape), axis, 0, 0, tiled=True)


def after(value, *others):
    return lax.optimization_barrier((value,) + others)[0]


def precondition_kernel(place, *refs):
    gathered, ring = refs[0:2], (refs[2:5], refs[5:8])
    grad, in_eigs, out_eigs, terms, basis, sems = refs[8:]
    z, core = place[0], place[1]
    width = basis.shape[-1]
    copies = []

    def bring(src, target):
        copy = pltpu.make_async_copy(src, target, sems.at[len(copies)])
        copy.start()
        copies.append(copy)

    for side in range(2):
        at = core if side == 0 else 1 - core
        columns = pl.ds(0, GATHERED)
        for k in range(8):
            bring(gathered[side].at[k], basis.at[:, k, at, :, columns])
        columns = pl.ds(GATHERED, RINGED)
        for ref, distances in zip(ring[side], NEAR):
            for k, distance in enumerate(distances):
                bring(ref.at[k], basis.at[:, lax.rem(z + (distance + 8), 8), at, :, columns])
    for copy in copies:
        copy.wait()

    projected = jnp.zeros((grad.shape[0], width), jnp.float32)
    for k in range(8):
        rows = basis[k // 2, (k % 2) * 4 : (k % 2) * 4 + 4].reshape(width, width)
        projected += jnp.dot(
            grad[:, k * width : (k + 1) * width], rows, preferred_element_type=jnp.float32
        )
    denominator = out_eigs[...] * in_eigs[...] + DAMPING
    scaled = (projected / denominator).astype(jnp.bfloat16)
    for k in range(8):
        rows = basis[k // 2, (k % 2) * 4 : (k % 2) * 4 + 4].reshape(width, width)
        terms[k] = lax.dot_general(
            scaled, rows, (((1,), (1,)), ((), ())), preferred_element_type=jnp.float32
        )


def precondition(pieces, grad, in_eigs, out_eigs):
    place = jnp.stack([lax.axis_index("z"), lax.axis_index("core")]).astype(jnp.int32)
    rows = grad.shape[0]
    width = in_eigs.shape[0]
    vmem = pl.BlockSpec(memory_space=pltpu.VMEM)
    return pl.pallas_call(
        precondition_kernel,
        out_shape=jax.ShapeDtypeStruct((8, rows, width), jnp.float32),
        in_specs=[pl.BlockSpec(memory_space=pltpu.SMEM)]
        + [pl.BlockSpec(memory_space=pl.ANY)] * len(pieces)
        + [vmem] * 3,
        out_specs=vmem,
        scratch_shapes=[
            pltpu.VMEM((4, 8, 2, rows, width), jnp.bfloat16),
            pltpu.SemaphoreType.DMA((32,)),
        ],
        compiler_params=pltpu.CompilerParams(vmem_limit_bytes=36 << 20),
        cost_estimate=pl.CostEstimate(
            flops=4 * rows * 8 * width * width, bytes_accessed=24 * width * width, transcendentals=0
        ),
    )(place, *pieces, grad, in_eigs[None, :], out_eigs[:, None])


def shards(activations, out_grads, counts, owners, rotated_grad, basis, input_eigs, output_eigs):
    slots, width = activations.shape
    owned_width = basis.shape[0]
    blocks_per = width // owned_width
    group_count = lax.axis_size("yl") * lax.axis_size("x")

    is_live = lax.broadcasted_iota(jnp.int32, (slots, 1), 0) < counts[0]
    kept = jnp.concatenate([jnp.where(is_live, v, jnp.zeros_like(v)) for v in (activations, out_grads)])
    first = spread(basis[:, :GATHERED], "yh")
    second, *near = lax.optimization_barrier((spread(basis[:, GATHERED:], "yh"), *others(kept, "z")))
    gathered = lax.all_gather(first, "z", axis=0)
    up1, down1 = lax.optimization_barrier((shift(second, "z", 1), shift(second, "z", -1)))
    up2, down2 = lax.optimization_barrier((shift(up1, "z", 1), shift(down1, "z", -1)))
    up3, down3 = lax.optimization_barrier((shift(up2, "z", 1), shift(down2, "z", -1)))
    up4 = shift(up3, "z", 1)
    ring = [jnp.stack(group) for group in ((second, up1, down1), (up2, down2), (up3, down3, up4))]
    gathered = after(gathered, up4)

    kept = jnp.concatenate([kept] + near)
    kept = jnp.concatenate([kept] + others(kept, "yh"))
    kept = after(kept, up4).reshape(-1, 2, slots, width)
    kept = jnp.moveaxis(kept, 1, 0).reshape(2, -1, width)
    both = jnp.concatenate([kept, shift(kept, "core", 1)], axis=1)
    samples = both.shape[1]
    owner_idx = owners[0]
    offset = owner_idx % blocks_per * owned_width
    owned = lax.dynamic_slice_in_dim(both, offset, owned_width, 2)
    pieces = owned.reshape(group_count, 2 * samples // group_count, owned_width)
    pieces = lax.all_to_all(pieces, GROUP, 0, 0, tiled=True)
    piece = lax.dynamic_index_in_dim(pieces, owner_idx // blocks_per, 0, keepdims=False)
    owned = spread(piece, GROUP).reshape(2, samples, owned_width)
    contract_rows = (((0,), (0,)), ((), ()))
    cov_in, cov_out = (
        lax.dot_general(both[k], owned[k], contract_rows, preferred_element_type=jnp.float32)
        / jnp.float32(SAMPLED)
        for k in range(2)
    )

    pieces = [gathered, shift(gathered, "core", 1)]
    pieces += ring + [shift(group, "core", 1) for group in ring]
    terms = precondition(pieces, rotated_grad, input_eigs, output_eigs)
    terms = lax.all_to_all(terms, GROUP, 0, 0, tiled=True)
    preconditioned = jnp.sum(terms, axis=0)
    return (cov_in, cov_out, preconditioned)


def solution(mesh):
    devices = mesh.devices.reshape(4, 8, 2, 2, 4)
    fine = Mesh(devices, DP + GROUP)
    placed = (
        P(DP, GROUP),
        P(DP, GROUP),
        P(DP),
        P(DP),
        P(DP, None),
        P(DP, GROUP),
        P(GROUP),
        P(DP),
    )
    return jax.shard_map(
        shards,
        mesh=fine,
        in_specs=placed,
        out_specs=(P(GROUP, DP), P(GROUP, DP), P(DP, GROUP)),
        check_vma=False,
    )
```

time: 227 us -> 235 us (1.035)
  starting transfers between devices: 66.7 us -> 113 us
  blocking collectives: 64.8 us -> 19 us
  waiting for transfers between devices: 44.6 us -> 55.3 us
  local copies, waits for them, and re-layouts: 17.6 us -> 10.8 us
  other arithmetic: 2.54 us -> 6.63 us
    ppermute x11 -> x22, starting transfers between devices: 39.3 us -> 91.6 us  [shift(): lax.ppermute(value, axis, [((i + by) % size, i) for i in range(size)])]
    all_to_all x2 -> x1, blocking collectives: 64.8 us -> 19 us  [spread(): lax.all_to_all(jnp.broadcast_to(block[None], (size,) + block.shape), axis...]
    ppermute x11 -> x22, waiting for transfers between devices: 7.31 us -> 31.4 us  [shift(): lax.ppermute(value, axis, [((i + by) % size, i) for i in range(size)])]
    all_to_all x3 -> x2, waiting for transfers between devices: 13.3 us -> 0.01 us  [spread(): lax.all_to_all(jnp.broadcast_to(block[None], (size,) + block.shape), axis...]
    all_to_all x3 -> x2, starting transfers between devices: 16.4 us -> 10.2 us  [spread(): lax.all_to_all(jnp.broadcast_to(block[None], (size,) + block.shape), axis...]
    unnamed x27 -> x47, local copies, waits for them, and re-layouts: 9.45 us -> 4.55 us
    another operation x3, other arithmetic: 0.21 us -> 4.13 us  [shards(): jnp.stack(group)]
  transfers between devices with their start and end apart: 17 -> 27, of which waited for: 6 -> 10; matrix products, arithmetic and copies ran while one was open for 8% -> 7% of each run, Pallas kernels for 4% -> 4%
where the time goes in v3:
time: 235 us; the launch traced here: 234 us
  starting transfers between devices  113 us (48%)
  waiting for transfers between devices  55.3 us (24%)
  blocking collectives  19 us (8%)
  between operations  16 us (7%)
  local copies, waits for them, and re-layouts  10.8 us (5%)
  Pallas kernels  10.2 us (4%)
  other arithmetic  6.63 us (3%)
  matrix products  3.46 us (1%)
    ppermute x22, starting transfers between devices, shift(): lax.ppermute(value, axis, [((i + by) % size, i) for i in range(size)])  91.6 us
    ppermute x22, waiting for transfers between devices, shift(): lax.ppermute(value, axis, [((i + by) % size, i) for i in range(size)])  31.4 us
    all_to_all x1, waiting for transfers between devices, shards(): terms = lax.all_to_all(terms, GROUP, 0, 0, tiled=True)  23.9 us
    all_to_all x1, blocking collectives, spread(): lax.all_to_all(jnp.broadcast_to(block[None], (size,) + block.shape), axis...  19 us
    pallas_call x1, Pallas kernels, precondition(): pl.pallas_call(precondition_kernel, out_shape=jax.ShapeDtypeStruct((8, ro...  10.2 us
    all_to_all x2, starting transfers between devices, spread(): lax.all_to_all(jnp.broadcast_to(block[None], (size,) + block.shape), axis...  10.2 us
    all_to_all x1, starting transfers between devices, shards(): terms = lax.all_to_all(terms, GROUP, 0, 0, tiled=True)  5.44 us
    all_to_all x1, starting transfers between devices, shards(): pieces = lax.all_to_all(pieces, GROUP, 0, 0, tiled=True)  5.36 us
  transfers between devices with their start and end apart: 27, of which 10 were waited for; matrix products, arithmetic and copies ran while one was open for 7% of the time, Pallas kernels for 4%

profile of v3, /device:TPU:1, one launch (start us, length us, event | category | flops | bytes accessed | tf_op | source)
XLA Modules:
  0.0 234.1 jit_solution(8166306801564080756)
XLA Ops:
  7.2 0.9 slice.25
  8.2 19.0 %all_to_all.25 = bf16[4,96,512]{2,1,0:T(8,128)(2,1)} all-to-all(bf16[4,96,512]{2,1,0:T(8,128)(2,1)S(1)} %broadcast_in_dim.41), channel_id=1, replica_groups=mesh['yh'=4,'z'=8,'core'=2,'yl'=2,'x'=4] {'yh'}, dimensions={0} | all-to-all | bytes 786432 | tf_op jit(solution)/shard_map/all_to_all | solution.py:27
  27.9 4.8 %all-to-all-start = ((bf16[4,96,256]{2,1,0:T(8,128)(2,1)}), bf16[4,96,256]{2,1,0:T(8,128)(2,1)S(1)}, u32[]{:S(2)}, u32[]{:S(2)}) async-start(bf16[4,96,256]{2,1,0:T(8,128)(2,1)} %broadcast_in_dim.38), calls=%async_computation | async-start | bytes 393216 | tf_op jit(solution)/shard_map/all_to_all | solution.py:27
  33.5 4.1 %collective-permute-start.6 = (bf16[32,768]{1,0:T(8,128)(2,1)S(1)}, bf16[32,768]{1,0:T(8,128)(2,1)S(1)}, u32[]{:S(2)}, u32[]{:S(2)}) collective-permute-start(bf16[32,768]{1,0:T(8,128)(2,1)S(1)} %pad_maximum_fusion.4), channel_id=1, source_target_pairs={{112,0},{0,16},{16,32},{32,48},{48,64},{64,80},{80,96},{96,112},{1... | collective-permute-start | bytes 147464 | tf_op jit(solution)/shard_map/ppermute | solution.py:18
  37.7 5.8 %collective-permute-start.5 = (bf16[32,768]{1,0:T(8,128)(2,1)S(1)}, bf16[32,768]{1,0:T(8,128)(2,1)S(1)}, u32[]{:S(2)}, u32[]{:S(2)}) collective-permute-start(bf16[32,768]{1,0:T(8,128)(2,1)S(1)} %pad_maximum_fusion.4), channel_id=1, source_target_pairs={{96,0},{112,16},{0,32},{16,48},{32,64},{48,80},{64,96},{80,112},{9... | collective-permute-start | bytes 147464 | tf_op jit(solution)/shard_map/ppermute | solution.py:18
  43.5 7.0 %collective-permute-start.4 = (bf16[32,768]{1,0:T(8,128)(2,1)S(1)}, bf16[32,768]{1,0:T(8,128)(2,1)S(1)}, u32[]{:S(2)}, u32[]{:S(2)}) collective-permute-start(bf16[32,768]{1,0:T(8,128)(2,1)S(1)} %pad_maximum_fusion.4), channel_id=1, source_target_pairs={{80,0},{96,16},{112,32},{0,48},{16,64},{32,80},{48,96},{64,112},{8... | collective-permute-start | bytes 147464 | tf_op jit(solution)/shard_map/ppermute | solution.py:18
  50.5 2.8 %collective-permute-start.3 = (bf16[32,768]{1,0:T(8,128)(2,1)S(1)}, bf16[32,768]{1,0:T(8,128)(2,1)S(1)}, u32[]{:S(2)}, u32[]{:S(2)}) collective-permute-start(bf16[32,768]{1,0:T(8,128)(2,1)S(1)} %pad_maximum_fusion.4), channel_id=1, source_target_pairs={{64,0},{80,16},{96,32},{112,48},{0,64},{16,80},{32,96},{48,112},{6... | collective-permute-start | bytes 147464 | tf_op jit(solution)/shard_map/ppermute | solution.py:18
  53.4 6.4 %collective-permute-start.2 = (bf16[32,768]{1,0:T(8,128)(2,1)S(1)}, bf16[32,768]{1,0:T(8,128)(2,1)S(1)}, u32[]{:S(2)}, u32[]{:S(2)}) collective-permute-start(bf16[32,768]{1,0:T(8,128)(2,1)S(1)} %pad_maximum_fusion.4), channel_id=1, source_target_pairs={{48,0},{64,16},{80,32},{96,48},{112,64},{0,80},{16,96},{32,112},{4... | collective-permute-start | bytes 147464 | tf_op jit(solution)/shard_map/ppermute | solution.py:18
  59.8 3.4 %collective-permute-start.1 = (bf16[32,768]{1,0:T(8,128)(2,1)S(1)}, bf16[32,768]{1,0:T(8,128)(2,1)S(1)}, u32[]{:S(2)}, u32[]{:S(2)}) collective-permute-start(bf16[32,768]{1,0:T(8,128)(2,1)S(1)} %pad_maximum_fusion.4), channel_id=1, source_target_pairs={{32,0},{48,16},{64,32},{80,48},{96,64},{112,80},{0,96},{16,112},{3... | collective-permute-start | bytes 147464 | tf_op jit(solution)/shard_map/ppermute | solution.py:18
  63.2 2.2 collective-permute-start
  65.4 2.6 %collective-permute-done.1 = bf16[32,768]{1,0:T(8,128)(2,1)S(1)} collective-permute-done((bf16[32,768]{1,0:T(8,128)(2,1)S(1)}, bf16[32,768]{1,0:T(8,128)(2,1)S(1)}, u32[]{:S(2)}, u32[]{:S(2)}) %collective-permute-start.1) | collective-permute-done | bytes 49184 | tf_op jit(solution)/shard_map/ppermute | solution.py:18
  68.0 2.3 collective-permute-done
  70.3 2.2 collective-permute-start.11
  72.5 4.3 %collective-permute-start.10 = (bf16[4,96,256]{2,1,0:T(8,128)(2,1)S(1)}, bf16[4,96,256]{2,1,0:T(8,128)(2,1)S(1)}, u32[]{:S(2)}, u32[]{:S(2)}) collective-permute-start(bf16[4,96,256]{2,1,0:T(8,128)(2,1)S(1)} %all-to-all-done), channel_id=1, source_target_pairs={{16,0},{32,16},{48,32},{64,48},{80,64},{96,80},{112,96},{0,112},{1... | collective-permute-start | bytes 589832 | tf_op jit(solution)/shard_map/ppermute | solution.py:18
  77.0 6.3 %collective-permute-done.11 = bf16[4,96,256]{2,1,0:T(8,128)(2,1)S(1)} collective-permute-done((bf16[4,96,256]{2,1,0:T(8,128)(2,1)S(1)}, bf16[4,96,256]{2,1,0:T(8,128)(2,1)S(1)}, u32[]{:S(2)}, u32[]{:S(2)}) %collective-permute-start.11) | collective-permute-done | bytes 196640 | tf_op jit(solution)/shard_map/ppermute | solution.py:18
  83.3 1.2 collective-permute-done.10
  84.5 5.4 %collective-permute-start.12 = (bf16[4,96,256]{2,1,0:T(8,128)(2,1)S(1)}, bf16[4,96,256]{2,1,0:T(8,128)(2,1)S(1)}, u32[]{:S(2)}, u32[]{:S(2)}) collective-permute-start(bf16[4,96,256]{2,1,0:T(8,128)(2,1)S(1)} %collective-permute-done.10), channel_id=1, source_target_pairs={{16,0},{32,16},{48,32},{64,48},{80,64},{96,80},{112,96},{0,112},{1... | collective-permute-start | bytes 589832 | tf_op jit(solution)/shard_map/ppermute | solution.py:18
  89.9 1.9 collective-permute-start.13
  92.6 5.6 %collective-permute-start.7 = (bf16[256,768]{1,0:T(8,128)(2,1)}, bf16[256,768]{1,0:T(8,128)(2,1)S(1)}, u32[]{:S(2)}, u32[]{:S(2)}) collective-permute-start(bf16[256,768]{1,0:T(8,128)(2,1)} %copy-done.16), channel_id=1, source_target_pairs={{128,0},{256,128},{384,256},{0,384},{129,1},{257,129},{385,257},{1... | collective-permute-start | bytes 1179656 | tf_op jit(solution)/shard_map/ppermute | solution.py:18
  98.3 4.6 %collective-permute-start.14 = (bf16[4,96,256]{2,1,0:T(8,128)(2,1)S(1)}, bf16[4,96,256]{2,1,0:T(8,128)(2,1)S(1)}, u32[]{:S(2)}, u32[]{:S(2)}) collective-permute-start(bf16[4,96,256]{2,1,0:T(8,128)(2,1)S(1)} %collective-permute-done.12), channel_id=1, source_target_pairs={{16,0},{32,16},{48,32},{64,48},{80,64},{96,80},{112,96},{0,112},{1... | collective-permute-start | bytes 589832 | tf_op jit(solution)/shard_map/ppermute | solution.py:18
  102.9 1.9 collective-permute-start.15
  104.9 5.3 %collective-permute-start.8 = (bf16[256,768]{1,0:T(8,128)(2,1)}, bf16[256,768]{1,0:T(8,128)(2,1)S(1)}, u32[]{:S(2)}, u32[]{:S(2)}) collective-permute-start(bf16[256,768]{1,0:T(8,128)(2,1)} %copy-done.16), channel_id=1, source_target_pairs={{256,0},{384,128},{0,256},{128,384},{257,1},{385,129},{1,257},{129... | collective-permute-start | bytes 1179656 | tf_op jit(solution)/shard_map/ppermute | solution.py:18
  110.2 2.5 %collective-permute-start.9 = (bf16[256,768]{1,0:T(8,128)(2,1)}, bf16[256,768]{1,0:T(8,128)(2,1)S(1)}, u32[]{:S(2)}, u32[]{:S(2)}) collective-permute-start(bf16[256,768]{1,0:T(8,128)(2,1)} %copy-done.16), channel_id=1, source_target_pairs={{384,0},{0,128},{128,256},{256,384},{385,1},{1,129},{129,257},{257... | collective-permute-start | bytes 1179656 | tf_op jit(solution)/shard_map/ppermute | solution.py:18
  112.8 4.6 %collective-permute-start.16 = (bf16[4,96,256]{2,1,0:T(8,128)(2,1)S(1)}, bf16[4,96,256]{2,1,0:T(8,128)(2,1)}, u32[]{:S(2)}, u32[]{:S(2)}) collective-permute-start(bf16[4,96,256]{2,1,0:T(8,128)(2,1)S(1)} %collective-permute-done.14), channel_id=1, source_target_pairs={{16,0},{32,16},{48,32},{64,48},{80,64},{96,80},{112,96},{0,112},{1... | collective-permute-start | bytes 589832 | tf_op jit(solution)/shard_map/ppermute | solution.py:18
  117.4 2.5 %collective-permute-done.16 = bf16[4,96,256]{2,1,0:T(8,128)(2,1)} collective-permute-done((bf16[4,96,256]{2,1,0:T(8,128)(2,1)S(1)}, bf16[4,96,256]{2,1,0:T(8,128)(2,1)}, u32[]{:S(2)}, u32[]{:S(2)}) %collective-permute-start.16) | collective-permute-done | bytes 196640 | tf_op jit(solution)/shard_map/ppermute | solution.py:18
  120.0 8.8 %collective-permute-start.18 = (bf16[8,4,96,512]{3,2,1,0:T(8,128)(2,1)}, bf16[8,4,96,512]{3,2,1,0:T(8,128)(2,1)}, u32[]{:S(2)}, u32[]{:S(2)}) collective-permute-start(bf16[8,4,96,512]{3,2,1,0:T(8,128)(2,1)} %bitcast.44), channel_id=1, source_target_pairs={{8,0},{0,8},{9,1},{1,9},{10,2},{2,10},{11,3},{3,11},{12,4},{4,12},... | collective-permute-start | bytes 9437192 | tf_op jit(solution)/shard_map/ppermute | solution.py:18
  129.5 12.8 %collective-permute-done.9 = bf16[256,768]{1,0:T(8,128)(2,1)S(1)} collective-permute-done((bf16[256,768]{1,0:T(8,128)(2,1)}, bf16[256,768]{1,0:T(8,128)(2,1)S(1)}, u32[]{:S(2)}, u32[]{:S(2)}) %collective-permute-start.9) | collective-permute-done | bytes 393248 | tf_op jit(solution)/shard_map/ppermute | solution.py:18
  142.4 5.5 %collective-permute-start.17 = (bf16[2,512,768]{2,1,0:T(8,128)(2,1)S(1)}, bf16[2,512,768]{2,1,0:T(8,128)(2,1)S(1)}, u32[]{:S(2)}, u32[]{:S(2)}) collective-permute-start(bf16[2,512,768]{2,1,0:T(8,128)(2,1)S(1)} %bitcast.46), channel_id=1, source_target_pairs={{8,0},{0,8},{9,1},{1,9},{10,2},{2,10},{11,3},{3,11},{12,4},{4,12},... | collective-permute-start | bytes 4718600 | tf_op jit(solution)/shard_map/ppermute | solution.py:18
  148.6 2.3 %collective-permute-done.17 = bf16[2,512,768]{2,1,0:T(8,128)(2,1)S(1)} collective-permute-done((bf16[2,512,768]{2,1,0:T(8,128)(2,1)S(1)}, bf16[2,512,768]{2,1,0:T(8,128)(2,1)S(1)}, u32[]{:S(2)}, u32[]{:S(2)}) %collective-permute-start.17) | collective-permute-done | bytes 1572896 | tf_op jit(solution)/shard_map/ppermute | solution.py:18
  150.9 1.4 fusion.14
  152.3 2.0 copy.19
  154.4 5.4 %all-to-all-start.1 = ((bf16[8,256,96]{1,2,0:T(8,128)(2,1)}), bf16[8,256,96]{1,2,0:T(8,128)(2,1)}, u32[]{:S(2)}, u32[]{:S(2)}) async-start(bf16[8,256,96]{1,2,0:T(8,128)(2,1)} %copy.19), calls=%async_computation.1 | async-start | bytes 786432 | tf_op jit(solution)/shard_map/all_to_all | solution.py:124
  159.7 0.9 pad_maximum_fusion.1.refs_2_
  160.6 2.6 %collective-permute-start.19 = (bf16[3,4,96,256]{3,2,1,0:T(8,128)(2,1)}, bf16[3,4,96,256]{3,2,1,0:T(8,128)(2,1)}, u32[]{:S(2)}, u32[]{:S(2)}) collective-permute-start(bf16[3,4,96,256]{3,2,1,0:T(8,128)(2,1)} %pad_maximum_fusion.1.refs_2_), channel_id=1, source_target_pairs={{8,0},{0,8},{9,1},{1,9},{10,2},{2,10},{11,3},{3,11},{12,4},{4,12},... | collective-permute-start | bytes 1769480 | tf_op jit(solution)/shard_map/ppermute | solution.py:18
  163.2 2.2 pad_maximum_fusion.2.refs_4_
  165.4 1.9 collective-permute-start.21
  168.1 0.8 broadcast_in_dim.40
  169.0 5.4 %all-to-all-start.2 = ((bf16[8,256,96]{1,2,0:T(8,128)(2,1)}), bf16[8,256,96]{1,2,0:T(8,128)(2,1)}, u32[]{:S(2)}, u32[]{:S(2)}) async-start(bf16[8,256,96]{1,2,0:T(8,128)(2,1)} %broadcast_in_dim.40), calls=%async_computation.2 | async-start | bytes 786432 | tf_op jit(solution)/shard_map/all_to_all | solution.py:27
  174.4 1.1 pad_maximum_fusion.3.refs_3_
  175.4 2.7 %collective-permute-start.20 = (bf16[2,4,96,256]{3,2,1,0:T(8,128)(2,1)S(1)}, bf16[2,4,96,256]{3,2,1,0:T(8,128)(2,1)}, u32[]{:S(2)}, u32[]{:S(2)}) collective-permute-start(bf16[2,4,96,256]{3,2,1,0:T(8,128)(2,1)S(1)} %pad_maximum_fusion.3.refs_3_), channel_id=1, source_target_pairs={{8,0},{0,8},{9,1},{1,9},{10,2},{2,10},{11,3},{3,11},{12,4},{4,12},... | collective-permute-start | bytes 1179656 | tf_op jit(solution)/shard_map/ppermute | solution.py:18
  179.6 1.3 copy-done.1
  181.7 10.2 %shard_map.103 = f32[8,96,768]{2,1,0:T(8,128)} custom-call(s32[2]{0:T(128)S(1)} %pad_add_fusion.place, bf16[8,4,96,512]{3,2,1,0:T(8,128)(2,1)S(1)} %bitcast.45, bf16[8,4,96,512]{3,2,1,0:T(8,128)(2,1)} %collective-permute-done.18.refs_1_, bf16[3,4,96,256]{3,2,1,0:T(8,128)(2,1)} %pad_maximum_fusion.1.refs_2_, ...), custom_call_target="tpu_custom_call" | custom-call | flops 1811939328 | bytes 14155776 | tf_op jit(solution)/shard_map/pallas_call | solution.py:78
  191.9 5.4 %all-to-all-start.4 = ((f32[8,96,768]{2,1,0:T(8,128)}), f32[8,96,768]{2,1,0:T(8,128)S(1)}, u32[]{:S(2)}, u32[]{:S(2)}) async-start(f32[8,96,768]{2,1,0:T(8,128)} %shard_map.103), calls=%async_computation.4 | async-start | bytes 4718592 | tf_op jit(solution)/shard_map/all_to_all | solution.py:137
  197.4 1.2 slice_bitcast_fusion
  199.0 2.4 %fusion.11 = f32[768,96]{0,1:T(8,128)} fusion(bf16[1024,96]{0,1:T(8,128)(2,1)S(1)} %bitcast.52, bf16[2,512,768]{2,1,0:T(8,128)(2,1)} %copy-done.5, bf16[2,512,768]{2,1,0:T(8,128)(2,1)S(1)} %bitcast.48), kind=kOutput, calls=%fused_computation.12 | convolution fusion | flops 154214400 | bytes 3637248 | tf_op jit(solution)/shard_map/dot_general | solution.py:129
  201.3 1.1 fusion.8
  202.5 23.9 %all-to-all-done.4 = f32[8,96,768]{2,1,0:T(8,128)S(1)} async-done(((f32[8,96,768]{2,1,0:T(8,128)}), f32[8,96,768]{2,1,0:T(8,128)S(1)}, u32[]{:S(2)}, u32[]{:S(2)}) %all-to-all-start.4) | async-done | bytes 2359328 | tf_op jit(solution)/shard_map/all_to_all | solution.py:137
  226.4 0.8 reduce_sum.9
  (83 shorter events, 6.2 us)
Async XLA Ops:
  7.2 20.0 %slice-start = ((bf16[96,768]{1,0:T(8,128)(2,1)}), bf16[96,256]{1,0:T(8,128)(2,1)S(1)}, s32[]{:S(2)}) async-start(bf16[96,768]{1,0:T(8,128)(2,1)} %param.13), calls=%async_computation.6 | async-start | bytes 98304 | tf_op jit(solution)/shard_map/slice | solution.py:105
  7.2 26.2 %copy-start.13 = (bf16[16,768]{1,0:T(8,128)(2,1)S(1)}, bf16[16,768]{1,0:T(8,128)(2,1)}, u32[]{:S(2)}) copy-start(bf16[16,768]{1,0:T(8,128)(2,1)} %param.8) | copy-start | bytes 73732
  7.2 26.3 %copy-start.14 = (bf16[16,768]{1,0:T(8,128)(2,1)S(1)}, bf16[16,768]{1,0:T(8,128)(2,1)}, u32[]{:S(2)}) copy-start(bf16[16,768]{1,0:T(8,128)(2,1)} %param.9) | copy-start | bytes 73732
  7.2 112.8 %all-gather.3.cloned.1.call-start = ((), (), s32[]{:S(2)}) async-start(), calls=%async_computation.5 | async-start | bytes 3538944 | tf_op jit(solution)/shard_map/all_gather | solution.py:106
  27.9 42.4 %all-to-all-start = ((bf16[4,96,256]{2,1,0:T(8,128)(2,1)}), bf16[4,96,256]{2,1,0:T(8,128)(2,1)S(1)}, u32[]{:S(2)}, u32[]{:S(2)}) async-start(bf16[4,96,256]{2,1,0:T(8,128)(2,1)} %broadcast_in_dim.38), calls=%async_computation | async-start | bytes 393216 | tf_op jit(solution)/shard_map/all_to_all | solution.py:27
  33.5 26.2 %collective-permute-start.6 = (bf16[32,768]{1,0:T(8,128)(2,1)S(1)}, bf16[32,768]{1,0:T(8,128)(2,1)S(1)}, u32[]{:S(2)}, u32[]{:S(2)}) collective-permute-start(bf16[32,768]{1,0:T(8,128)(2,1)S(1)} %pad_maximum_fusion.4), channel_id=1, source_target_pairs={{112,0},{0,16},{16,32},{32,48},{48,64},{64,80},{80,96},{96,112},{1... | collective-permute-start | bytes 147464 | tf_op jit(solution)/shard_map/ppermute | solution.py:18
  37.7 25.5 %collective-permute-start.5 = (bf16[32,768]{1,0:T(8,128)(2,1)S(1)}, bf16[32,768]{1,0:T(8,128)(2,1)S(1)}, u32[]{:S(2)}, u32[]{:S(2)}) collective-permute-start(bf16[32,768]{1,0:T(8,128)(2,1)S(1)} %pad_maximum_fusion.4), channel_id=1, source_target_pairs={{96,0},{112,16},{0,32},{16,48},{32,64},{48,80},{64,96},{80,112},{9... | collective-permute-start | bytes 147464 | tf_op jit(solution)/shard_map/ppermute | solution.py:18
  43.5 21.9 %collective-permute-start.4 = (bf16[32,768]{1,0:T(8,128)(2,1)S(1)}, bf16[32,768]{1,0:T(8,128)(2,1)S(1)}, u32[]{:S(2)}, u32[]{:S(2)}) collective-permute-start(bf16[32,768]{1,0:T(8,128)(2,1)S(1)} %pad_maximum_fusion.4), channel_id=1, source_target_pairs={{80,0},{96,16},{112,32},{0,48},{16,64},{32,80},{48,96},{64,112},{8... | collective-permute-start | bytes 147464 | tf_op jit(solution)/shard_map/ppermute | solution.py:18
  50.5 14.9 %collective-permute-start.3 = (bf16[32,768]{1,0:T(8,128)(2,1)S(1)}, bf16[32,768]{1,0:T(8,128)(2,1)S(1)}, u32[]{:S(2)}, u32[]{:S(2)}) collective-permute-start(bf16[32,768]{1,0:T(8,128)(2,1)S(1)} %pad_maximum_fusion.4), channel_id=1, source_target_pairs={{64,0},{80,16},{96,32},{112,48},{0,64},{16,80},{32,96},{48,112},{6... | collective-permute-start | bytes 147464 | tf_op jit(solution)/shard_map/ppermute | solution.py:18
  53.4 12.0 %collective-permute-start.2 = (bf16[32,768]{1,0:T(8,128)(2,1)S(1)}, bf16[32,768]{1,0:T(8,128)(2,1)S(1)}, u32[]{:S(2)}, u32[]{:S(2)}) collective-permute-start(bf16[32,768]{1,0:T(8,128)(2,1)S(1)} %pad_maximum_fusion.4), channel_id=1, source_target_pairs={{48,0},{64,16},{80,32},{96,48},{112,64},{0,80},{16,96},{32,112},{4... | collective-permute-start | bytes 147464 | tf_op jit(solution)/shard_map/ppermute | solution.py:18
  59.8 8.2 %collective-permute-start.1 = (bf16[32,768]{1,0:T(8,128)(2,1)S(1)}, bf16[32,768]{1,0:T(8,128)(2,1)S(1)}, u32[]{:S(2)}, u32[]{:S(2)}) collective-permute-start(bf16[32,768]{1,0:T(8,128)(2,1)S(1)} %pad_maximum_fusion.4), channel_id=1, source_target_pairs={{32,0},{48,16},{64,32},{80,48},{96,64},{112,80},{0,96},{16,112},{3... | collective-permute-start | bytes 147464 | tf_op jit(solution)/shard_map/ppermute | solution.py:18
  63.2 7.1 %collective-permute-start = (bf16[32,768]{1,0:T(8,128)(2,1)S(1)}, bf16[32,768]{1,0:T(8,128)(2,1)S(1)}, u32[]{:S(2)}, u32[]{:S(2)}) collective-permute-start(bf16[32,768]{1,0:T(8,128)(2,1)S(1)} %pad_maximum_fusion.4), channel_id=1, source_target_pairs={{16,0},{32,16},{48,32},{64,48},{80,64},{96,80},{112,96},{0,112},{1... | collective-permute-start | bytes 147464 | tf_op jit(solution)/shard_map/ppermute | solution.py:18
  70.3 13.0 %collective-permute-start.11 = (bf16[4,96,256]{2,1,0:T(8,128)(2,1)S(1)}, bf16[4,96,256]{2,1,0:T(8,128)(2,1)S(1)}, u32[]{:S(2)}, u32[]{:S(2)}) collective-permute-start(bf16[4,96,256]{2,1,0:T(8,128)(2,1)S(1)} %all-to-all-done), channel_id=1, source_target_pairs={{112,0},{0,16},{16,32},{32,48},{48,64},{64,80},{80,96},{96,112},{1... | collective-permute-start | bytes 589832 | tf_op jit(solution)/shard_map/ppermute | solution.py:18
  72.5 12.0 %collective-permute-start.10 = (bf16[4,96,256]{2,1,0:T(8,128)(2,1)S(1)}, bf16[4,96,256]{2,1,0:T(8,128)(2,1)S(1)}, u32[]{:S(2)}, u32[]{:S(2)}) collective-permute-start(bf16[4,96,256]{2,1,0:T(8,128)(2,1)S(1)} %all-to-all-done), channel_id=1, source_target_pairs={{16,0},{32,16},{48,32},{64,48},{80,64},{96,80},{112,96},{0,112},{1... | collective-permute-start | bytes 589832 | tf_op jit(solution)/shard_map/ppermute | solution.py:18
  84.5 18.4 %copy-start.7 = (bf16[4,96,256]{2,1,0:T(8,128)(2,1)}, bf16[4,96,256]{2,1,0:T(8,128)(2,1)S(1)}, u32[]{:S(2)}) copy-start(bf16[4,96,256]{2,1,0:T(8,128)(2,1)S(1)} %collective-permute-done.10) | copy-start | bytes 589828
  84.5 13.8 %collective-permute-start.12 = (bf16[4,96,256]{2,1,0:T(8,128)(2,1)S(1)}, bf16[4,96,256]{2,1,0:T(8,128)(2,1)S(1)}, u32[]{:S(2)}, u32[]{:S(2)}) collective-permute-start(bf16[4,96,256]{2,1,0:T(8,128)(2,1)S(1)} %collective-permute-done.10), channel_id=1, source_target_pairs={{16,0},{32,16},{48,32},{64,48},{80,64},{96,80},{112,96},{0,112},{1... | collective-permute-start | bytes 589832 | tf_op jit(solution)/shard_map/ppermute | solution.py:18
  89.9 8.4 %collective-permute-start.13 = (bf16[4,96,256]{2,1,0:T(8,128)(2,1)S(1)}, bf16[4,96,256]{2,1,0:T(8,128)(2,1)S(1)}, u32[]{:S(2)}, u32[]{:S(2)}) collective-permute-start(bf16[4,96,256]{2,1,0:T(8,128)(2,1)S(1)} %collective-permute-done.11), channel_id=1, source_target_pairs={{112,0},{0,16},{16,32},{32,48},{48,64},{64,80},{80,96},{96,112},{1... | collective-permute-start | bytes 589832 | tf_op jit(solution)/shard_map/ppermute | solution.py:18
  91.9 0.8 copy-start.16
  92.6 24.7 %collective-permute-start.7 = (bf16[256,768]{1,0:T(8,128)(2,1)}, bf16[256,768]{1,0:T(8,128)(2,1)S(1)}, u32[]{:S(2)}, u32[]{:S(2)}) collective-permute-start(bf16[256,768]{1,0:T(8,128)(2,1)} %copy-done.16), channel_id=1, source_target_pairs={{128,0},{256,128},{384,256},{0,384},{129,1},{257,129},{385,257},{1... | collective-permute-start | bytes 1179656 | tf_op jit(solution)/shard_map/ppermute | solution.py:18
  98.3 19.1 %copy-start.11 = (bf16[4,96,256]{2,1,0:T(8,128)(2,1)}, bf16[4,96,256]{2,1,0:T(8,128)(2,1)S(1)}, u32[]{:S(2)}) copy-start(bf16[4,96,256]{2,1,0:T(8,128)(2,1)S(1)} %collective-permute-done.12) | copy-start | bytes 589828
  98.3 19.1 %copy-start.12 = (bf16[4,96,256]{2,1,0:T(8,128)(2,1)}, bf16[4,96,256]{2,1,0:T(8,128)(2,1)S(1)}, u32[]{:S(2)}) copy-start(bf16[4,96,256]{2,1,0:T(8,128)(2,1)S(1)} %collective-permute-done.13) | copy-start | bytes 589828
  98.3 14.4 %collective-permute-start.14 = (bf16[4,96,256]{2,1,0:T(8,128)(2,1)S(1)}, bf16[4,96,256]{2,1,0:T(8,128)(2,1)S(1)}, u32[]{:S(2)}, u32[]{:S(2)}) collective-permute-start(bf16[4,96,256]{2,1,0:T(8,128)(2,1)S(1)} %collective-permute-done.12), channel_id=1, source_target_pairs={{16,0},{32,16},{48,32},{64,48},{80,64},{96,80},{112,96},{0,112},{1... | collective-permute-start | bytes 589832 | tf_op jit(solution)/shard_map/ppermute | solution.py:18
  102.9 9.8 %collective-permute-start.15 = (bf16[4,96,256]{2,1,0:T(8,128)(2,1)S(1)}, bf16[4,96,256]{2,1,0:T(8,128)(2,1)S(1)}, u32[]{:S(2)}, u32[]{:S(2)}) collective-permute-start(bf16[4,96,256]{2,1,0:T(8,128)(2,1)S(1)} %collective-permute-done.13), channel_id=1, source_target_pairs={{112,0},{0,16},{16,32},{32,48},{48,64},{64,80},{80,96},{96,112},{1... | collective-permute-start | bytes 589832 | tf_op jit(solution)/shard_map/ppermute | solution.py:18
  104.9 24.6 %collective-permute-start.8 = (bf16[256,768]{1,0:T(8,128)(2,1)}, bf16[256,768]{1,0:T(8,128)(2,1)S(1)}, u32[]{:S(2)}, u32[]{:S(2)}) collective-permute-start(bf16[256,768]{1,0:T(8,128)(2,1)} %copy-done.16), channel_id=1, source_target_pairs={{256,0},{384,128},{0,256},{128,384},{257,1},{385,129},{1,257},{129... | collective-permute-start | bytes 1179656 | tf_op jit(solution)/shard_map/ppermute | solution.py:18
  110.2 32.0 %collective-permute-start.9 = (bf16[256,768]{1,0:T(8,128)(2,1)}, bf16[256,768]{1,0:T(8,128)(2,1)S(1)}, u32[]{:S(2)}, u32[]{:S(2)}) collective-permute-start(bf16[256,768]{1,0:T(8,128)(2,1)} %copy-done.16), channel_id=1, source_target_pairs={{384,0},{0,128},{128,256},{256,384},{385,1},{1,129},{129,257},{257... | collective-permute-start | bytes 1179656 | tf_op jit(solution)/shard_map/ppermute | solution.py:18
  112.7 29.5 %copy-start.9 = (bf16[4,96,256]{2,1,0:T(8,128)(2,1)}, bf16[4,96,256]{2,1,0:T(8,128)(2,1)S(1)}, u32[]{:S(2)}) copy-start(bf16[4,96,256]{2,1,0:T(8,128)(2,1)S(1)} %collective-permute-done.14) | copy-start | bytes 589828
  112.8 29.5 %copy-start.10 = (bf16[4,96,256]{2,1,0:T(8,128)(2,1)}, bf16[4,96,256]{2,1,0:T(8,128)(2,1)S(1)}, u32[]{:S(2)}) copy-start(bf16[4,96,256]{2,1,0:T(8,128)(2,1)S(1)} %collective-permute-done.15) | copy-start | bytes 589828
  112.8 7.2 %collective-permute-start.16 = (bf16[4,96,256]{2,1,0:T(8,128)(2,1)S(1)}, bf16[4,96,256]{2,1,0:T(8,128)(2,1)}, u32[]{:S(2)}, u32[]{:S(2)}) collective-permute-start(bf16[4,96,256]{2,1,0:T(8,128)(2,1)S(1)} %collective-permute-done.14), channel_id=1, source_target_pairs={{16,0},{32,16},{48,32},{64,48},{80,64},{96,80},{112,96},{0,112},{1... | collective-permute-start | bytes 589832 | tf_op jit(solution)/shard_map/ppermute | solution.py:18
  120.0 59.6 %collective-permute-start.18 = (bf16[8,4,96,512]{3,2,1,0:T(8,128)(2,1)}, bf16[8,4,96,512]{3,2,1,0:T(8,128)(2,1)}, u32[]{:S(2)}, u32[]{:S(2)}) collective-permute-start(bf16[8,4,96,512]{3,2,1,0:T(8,128)(2,1)} %bitcast.44), channel_id=1, source_target_pairs={{8,0},{0,8},{9,1},{1,9},{10,2},{2,10},{11,3},{3,11},{12,4},{4,12},... | collective-permute-start | bytes 9437192 | tf_op jit(solution)/shard_map/ppermute | solution.py:18
  142.4 9.9 %copy-start.3 = (bf16[2,32,16,768]{3,2,1,0:T(8,128)(2,1)}, bf16[2,32,16,768]{3,2,1,0:T(8,128)(2,1)S(1)}, u32[]{:S(2)}) copy-start(bf16[2,32,16,768]{3,2,1,0:T(8,128)(2,1)S(1)} %copy.17) | copy-start | bytes 4718596
  142.4 8.5 %collective-permute-start.17 = (bf16[2,512,768]{2,1,0:T(8,128)(2,1)S(1)}, bf16[2,512,768]{2,1,0:T(8,128)(2,1)S(1)}, u32[]{:S(2)}, u32[]{:S(2)}) collective-permute-start(bf16[2,512,768]{2,1,0:T(8,128)(2,1)S(1)} %bitcast.46), channel_id=1, source_target_pairs={{8,0},{0,8},{9,1},{1,9},{10,2},{2,10},{11,3},{3,11},{12,4},{4,12},... | collective-permute-start | bytes 4718600 | tf_op jit(solution)/shard_map/ppermute | solution.py:18
  150.9 1.4 copy-start.5
  152.3 7.4 %copy-start.8 = (bf16[4,96,256]{2,1,0:T(8,128)(2,1)S(1)}, bf16[4,96,256]{2,1,0:T(8,128)(2,1)}, u32[]{:S(2)}) copy-start(bf16[4,96,256]{2,1,0:T(8,128)(2,1)} %copy-done.7) | copy-start | bytes 589828
  154.4 13.0 %all-to-all-start.1 = ((bf16[8,256,96]{1,2,0:T(8,128)(2,1)}), bf16[8,256,96]{1,2,0:T(8,128)(2,1)}, u32[]{:S(2)}, u32[]{:S(2)}) async-start(bf16[8,256,96]{1,2,0:T(8,128)(2,1)} %copy.19), calls=%async_computation.1 | async-start | bytes 786432 | tf_op jit(solution)/shard_map/all_to_all | solution.py:124
  160.6 18.9 %collective-permute-start.19 = (bf16[3,4,96,256]{3,2,1,0:T(8,128)(2,1)}, bf16[3,4,96,256]{3,2,1,0:T(8,128)(2,1)}, u32[]{:S(2)}, u32[]{:S(2)}) collective-permute-start(bf16[3,4,96,256]{3,2,1,0:T(8,128)(2,1)} %pad_maximum_fusion.1.refs_2_), channel_id=1, source_target_pairs={{8,0},{0,8},{9,1},{1,9},{10,2},{2,10},{11,3},{3,11},{12,4},{4,12},... | collective-permute-start | bytes 1769480 | tf_op jit(solution)/shard_map/ppermute | solution.py:18
  163.2 14.9 %copy-start.15 = (f32[768]{0:T(1024)S(1)}, f32[768]{0:T(1024)}, u32[]{:S(2)}) copy-start(f32[768]{0:T(1024)} %param.14) | copy-start | bytes 9220
  163.2 14.9 %copy-start.17 = (f32[96]{0:T(128)S(1)}, f32[96]{0:T(128)}, u32[]{:S(2)}) copy-start(f32[96]{0:T(128)} %param.15) | copy-start | bytes 1156
  163.2 16.4 %copy-start = (bf16[32,96,512]{2,1,0:T(8,128)(2,1)S(1)}, bf16[32,96,512]{2,1,0:T(8,128)(2,1)}, u32[]{:S(2)}) copy-start(bf16[32,96,512]{2,1,0:T(8,128)(2,1)} %all-gather.3.cloned.1.call-done) | copy-start | bytes 9437188
  165.4 14.2 %collective-permute-start.21 = (bf16[3,4,96,256]{3,2,1,0:T(8,128)(2,1)}, bf16[3,4,96,256]{3,2,1,0:T(8,128)(2,1)}, u32[]{:S(2)}, u32[]{:S(2)}) collective-permute-start(bf16[3,4,96,256]{3,2,1,0:T(8,128)(2,1)} %pad_maximum_fusion.2.refs_4_), channel_id=1, source_target_pairs={{8,0},{0,8},{9,1},{1,9},{10,2},{2,10},{11,3},{3,11},{12,4},{4,12},... | collective-permute-start | bytes 1769480 | tf_op jit(solution)/shard_map/ppermute | solution.py:18
  169.0 23.0 %all-to-all-start.2 = ((bf16[8,256,96]{1,2,0:T(8,128)(2,1)}), bf16[8,256,96]{1,2,0:T(8,128)(2,1)}, u32[]{:S(2)}, u32[]{:S(2)}) async-start(bf16[8,256,96]{1,2,0:T(8,128)(2,1)} %broadcast_in_dim.40), calls=%async_computation.2 | async-start | bytes 786432 | tf_op jit(solution)/shard_map/all_to_all | solution.py:27
  175.4 4.2 %collective-permute-start.20 = (bf16[2,4,96,256]{3,2,1,0:T(8,128)(2,1)S(1)}, bf16[2,4,96,256]{3,2,1,0:T(8,128)(2,1)}, u32[]{:S(2)}, u32[]{:S(2)}) collective-permute-start(bf16[2,4,96,256]{3,2,1,0:T(8,128)(2,1)S(1)} %pad_maximum_fusion.3.refs_3_), channel_id=1, source_target_pairs={{8,0},{0,8},{9,1},{1,9},{10,2},{2,10},{11,3},{3,11},{12,4},{4,12},... | collective-permute-start | bytes 1179656 | tf_op jit(solution)/shard_map/ppermute | solution.py:18
  179.6 1.3 copy-start.1
  180.9 0.8 copy-start.2
  191.9 34.4 %all-to-all-start.4 = ((f32[8,96,768]{2,1,0:T(8,128)}), f32[8,96,768]{2,1,0:T(8,128)S(1)}, u32[]{:S(2)}, u32[]{:S(2)}) async-start(f32[8,96,768]{2,1,0:T(8,128)} %shard_map.103), calls=%async_computation.4 | async-start | bytes 4718592 | tf_op jit(solution)/shard_map/all_to_all | solution.py:137
  197.4 1.6 copy-start.4
  199.0 2.4 %copy-start.6 = (bf16[2,512,768]{2,1,0:T(8,128)(2,1)S(1)}, bf16[2,512,768]{2,1,0:T(8,128)(2,1)}, u32[]{:S(2)}) copy-start(bf16[2,512,768]{2,1,0:T(8,128)(2,1)} %copy-done.5) | copy-start | bytes 4718596
Sparse Core Ops, SparseCore 0:
  27.3 66.0 all-gather.2

commit v4 on v1

v4 whole, which is shorter than its diff:
```python
import jax
import jax.numpy as jnp
from jax import lax
from jax.experimental import pallas as pl
from jax.experimental.pallas import tpu as pltpu
from jax.sharding import Mesh, PartitionSpec as P

DAMPING = 0.1
SAMPLED = 768
DP = ("yh", "z", "core")
GROUP = ("yl", "x")


def shift(value, axis, by):
    size = lax.axis_size(axis)
    return lax.ppermute(value, axis, [((i + by) % size, i) for i in range(size)])


def spread(block, axis):
    size = lax.axis_size(axis)
    return lax.all_to_all(jnp.broadcast_to(block[None], (size,) + block.shape), axis, 0, 0, tiled=True)


def gather_z(block):
    chunks = [block]
    up = down = block
    for step in range(4):
        up = shift(up, "z", 1)
        chunks.append(up)
        if step < 3:
            down = shift(down, "z", -1)
            chunks.append(down)
    return chunks


def precondition_kernel(place, own, other, grad, in_eigs, out_eigs, terms, basis, sems):
    core = place[0]
    rows, width = in_eigs.shape[1], basis.shape[-1]
    steps = basis.shape[0] * 2
    copies = []
    for k in range(steps):
        y, zs = k // 2, pl.ds(k % 2 * 4, 4)
        copies.append(
            [
                pltpu.make_async_copy(src.at[zs, y], basis.at[y, zs, at], sems.at[2 * k + side])
                for side, (src, at) in enumerate(((own, core), (other, 1 - core)))
            ]
        )
    for pair in copies:
        for copy in pair:
            copy.start()

    def block(k):
        return basis[k // 2, k % 2 * 4 : k % 2 * 4 + 4].reshape(rows, width)

    projected = jnp.zeros((grad.shape[0], width), jnp.float32)
    for k in range(steps):
        for copy in copies[k]:
            copy.wait()
        projected += jnp.dot(
            grad[:, k * rows : (k + 1) * rows], block(k), preferred_element_type=jnp.float32
        )
    denominator = out_eigs[...] * in_eigs[...] + DAMPING
    scaled = (projected / denominator).astype(jnp.bfloat16)
    for k in range(steps):
        terms[k] = lax.dot_general(
            scaled, block(k), (((1,), (1,)), ((), ())), preferred_element_type=jnp.float32
        )


def precondition(own, other, grad, in_eigs, out_eigs):
    place = lax.axis_index("core").astype(jnp.int32)[None]
    rows = grad.shape[0]
    width = in_eigs.shape[0]
    anywhere = pl.BlockSpec(memory_space=pl.ANY)
    vmem = pl.BlockSpec(memory_space=pltpu.VMEM)
    return pl.pallas_call(
        precondition_kernel,
        out_shape=jax.ShapeDtypeStruct((8, rows, width), jnp.float32),
        in_specs=[pl.BlockSpec(memory_space=pltpu.SMEM), anywhere, anywhere, vmem, vmem, vmem],
        out_specs=vmem,
        scratch_shapes=[
            pltpu.VMEM((4, 8, 2, rows, width), jnp.bfloat16),
            pltpu.SemaphoreType.DMA((16,)),
        ],
        compiler_params=pltpu.CompilerParams(vmem_limit_bytes=36 << 20),
        cost_estimate=pl.CostEstimate(
            flops=4 * rows * 8 * width * width, bytes_accessed=24 * width * width, transcendentals=0
        ),
    )(place, own, other, grad, in_eigs[None, :], out_eigs[:, None])


def shards(activations, out_grads, counts, owners, rotated_grad, basis, input_eigs, output_eigs):
    slots, width = activations.shape
    owned_width = basis.shape[0]
    blocks_per = width // owned_width
    group_count = lax.axis_size("yl") * lax.axis_size("x")
    is_live = lax.broadcasted_iota(jnp.int32, (slots, 1), 0) < counts[0]
    kept = [jnp.where(is_live, v, jnp.zeros_like(v)) for v in (activations, out_grads)]
    column = spread(jnp.concatenate([basis] + kept), "yh")
    own = lax.all_gather(column[:, :owned_width], "z", axis=0)
    kept = column[:, owned_width:].reshape(-1, 2, slots, width)
    kept = jnp.moveaxis(kept, 1, 0).reshape(2, -1, width)
    kept = jnp.concatenate(gather_z(kept), axis=1)
    both = jnp.concatenate([kept, shift(kept, "core", 1)], axis=1)
    samples = both.shape[1]
    owner_idx = owners[0]
    offset = owner_idx % blocks_per * owned_width
    owned = lax.dynamic_slice_in_dim(both, offset, owned_width, 2)
    pieces = owned.reshape(group_count, 2 * samples // group_count, owned_width)
    pieces = lax.all_to_all(pieces, GROUP, 0, 0, tiled=True)
    piece = lax.dynamic_index_in_dim(pieces, owner_idx // blocks_per, 0, keepdims=False)
    own, piece = lax.optimization_barrier((own, piece))
    owned = spread(piece, GROUP).reshape(2, samples, owned_width)
    contract_rows = (((0,), (0,)), ((), ()))
    cov_in, cov_out = (
        lax.dot_general(both[k], owned[k], contract_rows, preferred_element_type=jnp.float32)
        / jnp.float32(SAMPLED)
        for k in range(2)
    )

    other = shift(own, "core", 1)
    terms = precondition(own, other, rotated_grad, input_eigs, output_eigs)
    terms = lax.all_to_all(terms, GROUP, 0, 0, tiled=True)
    preconditioned = jnp.sum(terms, axis=0)
    return (cov_in, cov_out, preconditioned)


def solution(mesh):
    devices = mesh.devices.reshape(4, 8, 2, 2, 4)
    fine = Mesh(devices, DP + GROUP)
    placed = (
        P(DP, GROUP),
        P(DP, GROUP),
        P(DP),
        P(DP),
        P(DP, None),
        P(DP, GROUP),
        P(GROUP),
        P(DP),
    )
    return jax.shard_map(
        shards,
        mesh=fine,
        in_specs=placed,
        out_specs=(P(GROUP, DP), P(GROUP, DP), P(DP, GROUP)),
        check_vma=False,
    )
```

time: 186 us -> 180 us (0.968)
  blocking collectives: 0 us -> 27.9 us
  waiting for transfers between devices: 66.6 us -> 49.1 us
  starting transfers between devices: 69.4 us -> 56.5 us
  matrix products: 16.3 us -> 5.03 us
  Pallas kernels: 0 us -> 8 us
    all_to_all x0 -> x1, blocking collectives: none -> 27.9 us  [spread(): lax.all_to_all(jnp.broadcast_to(block[None], (size,) + block.shape), axis...]
    all_to_all x1, waiting for transfers between devices: 22.1 us -> 7.32 us  [shards(): pieces = lax.all_to_all(pieces, GROUP, 0, 0, tiled=True)]
    dot_general x1 -> x0, matrix products: 12.7 us -> none  [shards(): lax.dot_general(wide, scaled, (((2,), (1,)), ((), ())), preferred_element...]
    all_gather x1, waiting for transfers between devices: 11.7 us -> 0.01 us  [shards(): own = lax.all_gather(column[:, :owned_width], 'z', axis=0)]
    ppermute x11 -> x9, waiting for transfers between devices: 8.02 us -> 17.9 us  [shift(): lax.ppermute(value, axis, [((i + by) % size, i) for i in range(size)])]
    ppermute x11 -> x9, starting transfers between devices: 54.2 us -> 44.3 us  [shift(): lax.ppermute(value, axis, [((i + by) % size, i) for i in range(size)])]
    pallas_call x0 -> x1, Pallas kernels: none -> 8 us  [precondition(): pl.pallas_call(precondition_kernel, out_shape=jax.ShapeDtypeStruct((8, ro...]
    unnamed x22 -> x16, local copies, waits for them, and re-layouts: 9.75 us -> 7.87 us
  transfers between devices with their start and end apart: 15 -> 13, of which waited for: 9 -> 8; matrix products, arithmetic and copies ran while one was open for 16% -> 9% of each run, Pallas kernels for 0% -> 4%
where the time goes in v4:
time: 180 us; the launch traced here: 179 us
  starting transfers between devices  56.5 us (31%)
  waiting for transfers between devices  49.1 us (27%)
  blocking collectives  27.9 us (16%)
  between operations  15.6 us (9%)
  local copies, waits for them, and re-layouts  14.2 us (8%)
  Pallas kernels  8 us (4%)
  matrix products  5.03 us (3%)
  other arithmetic  2.61 us (1%)
    ppermute x9, starting transfers between devices, shift(): lax.ppermute(value, axis, [((i + by) % size, i) for i in range(size)])  44.3 us
    all_to_all x1, blocking collectives, spread(): lax.all_to_all(jnp.broadcast_to(block[None], (size,) + block.shape), axis...  27.9 us
    all_to_all x1, waiting for transfers between devices, shards(): terms = lax.all_to_all(terms, GROUP, 0, 0, tiled=True)  23.8 us
    ppermute x9, waiting for transfers between devices, shift(): lax.ppermute(value, axis, [((i + by) % size, i) for i in range(size)])  17.9 us
    pallas_call x1, Pallas kernels, precondition(): pl.pallas_call(precondition_kernel, out_shape=jax.ShapeDtypeStruct((8, ro...  8 us
    unnamed x16, local copies, waits for them, and re-layouts  7.87 us
    all_to_all x1, waiting for transfers between devices, shards(): pieces = lax.all_to_all(pieces, GROUP, 0, 0, tiled=True)  7.32 us
    all_to_all x1, starting transfers between devices, shards(): pieces = lax.all_to_all(pieces, GROUP, 0, 0, tiled=True)  5.11 us
  transfers between devices with their start and end apart: 13, of which 8 were waited for; matrix products, arithmetic and copies ran while one was open for 9% of the time, Pallas kernels for 4%

profile of v4, /device:TPU:1, one launch (start us, length us, event | category | flops | bytes accessed | tf_op | source)
XLA Modules:
  0.0 178.9 jit_solution(6084931341061786492)
XLA Ops:
  7.2 0.0 all-gather.3.cloned.1.call-start
  7.9 0.8 broadcast_select_fusion.1
  8.7 0.9 pad_maximum_fusion
  9.6 0.1 broadcast_in_dim.33
  9.7 27.9 %all_to_all.20 = bf16[4,128,768]{2,1,0:T(8,128)(2,1)S(1)} all-to-all(bf16[4,128,768]{2,1,0:T(8,128)(2,1)S(1)} %broadcast_in_dim.33), channel_id=1, replica_groups=mesh['yh'=4,'z'=8,'core'=2,'yl'=2,'x'=4] {'yh'}, dimensions={0} | all-to-all | bytes 1572864 | tf_op jit(solution)/shard_map/all_to_all | solution.py:21
  37.6 0.9 slice.26
  38.5 0.0 all-gather.3.cloned.1.call-update
  38.5 11.0 %collective-permute-start = (bf16[2,64,768]{2,1,0:T(8,128)(2,1)S(1)}, bf16[2,64,768]{2,1,0:T(8,128)(2,1)S(1)}, u32[]{:S(2)}, u32[]{:S(2)}) collective-permute-start(bf16[2,64,768]{2,1,0:T(8,128)(2,1)S(1)} %bitcast.39), channel_id=1, source_target_pairs={{16,0},{32,16},{48,32},{64,48},{80,64},{96,80},{112,96},{0,112},{1... | collective-permute-start | bytes 589832 | tf_op jit(solution)/shard_map/ppermute | solution.py:16
  49.5 1.9 %collective-permute-start.1 = (bf16[2,64,768]{2,1,0:T(8,128)(2,1)S(1)}, bf16[2,64,768]{2,1,0:T(8,128)(2,1)S(1)}, u32[]{:S(2)}, u32[]{:S(2)}) collective-permute-start(bf16[2,64,768]{2,1,0:T(8,128)(2,1)S(1)} %bitcast.40), channel_id=1, source_target_pairs={{112,0},{0,16},{16,32},{32,48},{48,64},{64,80},{80,96},{96,112},{1... | collective-permute-start | bytes 589832 | tf_op jit(solution)/shard_map/ppermute | solution.py:16
  51.5 0.8 constant_dynamic-update-slice_fusion.7
  52.2 0.0 collective-permute-done
  52.3 4.9 %collective-permute-start.2 = (bf16[2,64,768]{2,1,0:T(8,128)(2,1)S(1)}, bf16[2,64,768]{2,1,0:T(8,128)(2,1)S(1)}, u32[]{:S(2)}, u32[]{:S(2)}) collective-permute-start(bf16[2,64,768]{2,1,0:T(8,128)(2,1)S(1)} %collective-permute-done), channel_id=1, source_target_pairs={{16,0},{32,16},{48,32},{64,48},{80,64},{96,80},{112,96},{0,112},{1... | collective-permute-start | bytes 589832 | tf_op jit(solution)/shard_map/ppermute | solution.py:16
  57.1 0.0 collective-permute-done.1
  57.2 1.9 %collective-permute-start.3 = (bf16[2,64,768]{2,1,0:T(8,128)(2,1)S(1)}, bf16[2,64,768]{2,1,0:T(8,128)(2,1)S(1)}, u32[]{:S(2)}, u32[]{:S(2)}) collective-permute-start(bf16[2,64,768]{2,1,0:T(8,128)(2,1)S(1)} %collective-permute-done.1), channel_id=1, source_target_pairs={{112,0},{0,16},{16,32},{32,48},{48,64},{64,80},{80,96},{96,112},{1... | collective-permute-start | bytes 589832 | tf_op jit(solution)/shard_map/ppermute | solution.py:16
  59.1 0.8 constant_dynamic-update-slice_fusion.6
  59.9 0.8 constant_dynamic-update-slice_fusion.5
  60.7 3.0 %collective-permute-done.2 = bf16[2,64,768]{2,1,0:T(8,128)(2,1)S(1)} collective-permute-done((bf16[2,64,768]{2,1,0:T(8,128)(2,1)S(1)}, bf16[2,64,768]{2,1,0:T(8,128)(2,1)S(1)}, u32[]{:S(2)}, u32[]{:S(2)}) %collective-permute-start.2) | collective-permute-done | bytes 196640 | tf_op jit(solution)/shard_map/ppermute | solution.py:16
  63.6 5.4 %collective-permute-start.4 = (bf16[2,64,768]{2,1,0:T(8,128)(2,1)S(1)}, bf16[2,64,768]{2,1,0:T(8,128)(2,1)S(1)}, u32[]{:S(2)}, u32[]{:S(2)}) collective-permute-start(bf16[2,64,768]{2,1,0:T(8,128)(2,1)S(1)} %collective-permute-done.2), channel_id=1, source_target_pairs={{16,0},{32,16},{48,32},{64,48},{80,64},{96,80},{112,96},{0,112},{1... | collective-permute-start | bytes 589832 | tf_op jit(solution)/shard_map/ppermute | solution.py:16
  69.1 0.6 collective-permute-done.3
  69.6 1.9 %collective-permute-start.5 = (bf16[2,64,768]{2,1,0:T(8,128)(2,1)S(1)}, bf16[2,64,768]{2,1,0:T(8,128)(2,1)S(1)}, u32[]{:S(2)}, u32[]{:S(2)}) collective-permute-start(bf16[2,64,768]{2,1,0:T(8,128)(2,1)S(1)} %collective-permute-done.3), channel_id=1, source_target_pairs={{112,0},{0,16},{16,32},{32,48},{48,64},{64,80},{80,96},{96,112},{1... | collective-permute-start | bytes 589832 | tf_op jit(solution)/shard_map/ppermute | solution.py:16
  71.5 0.8 constant_dynamic-update-slice_fusion.4
  72.3 0.8 constant_dynamic-update-slice_fusion.3
  73.1 3.0 %collective-permute-done.4 = bf16[2,64,768]{2,1,0:T(8,128)(2,1)S(1)} collective-permute-done((bf16[2,64,768]{2,1,0:T(8,128)(2,1)S(1)}, bf16[2,64,768]{2,1,0:T(8,128)(2,1)S(1)}, u32[]{:S(2)}, u32[]{:S(2)}) %collective-permute-start.4) | collective-permute-done | bytes 196640 | tf_op jit(solution)/shard_map/ppermute | solution.py:16
  76.1 5.4 %collective-permute-start.6 = (bf16[2,64,768]{2,1,0:T(8,128)(2,1)S(1)}, bf16[2,64,768]{2,1,0:T(8,128)(2,1)S(1)}, u32[]{:S(2)}, u32[]{:S(2)}) collective-permute-start(bf16[2,64,768]{2,1,0:T(8,128)(2,1)S(1)} %collective-permute-done.4), channel_id=1, source_target_pairs={{16,0},{32,16},{48,32},{64,48},{80,64},{96,80},{112,96},{0,112},{1... | collective-permute-start | bytes 589832 | tf_op jit(solution)/shard_map/ppermute | solution.py:16
  81.5 0.8 constant_dynamic-update-slice_fusion.2
  82.3 0.0 collective-permute-done.5
  82.3 0.8 constant_dynamic-update-slice_fusion.1
  83.1 5.3 %collective-permute-done.6 = bf16[2,64,768]{2,1,0:T(8,128)(2,1)S(1)} collective-permute-done((bf16[2,64,768]{2,1,0:T(8,128)(2,1)S(1)}, bf16[2,64,768]{2,1,0:T(8,128)(2,1)S(1)}, u32[]{:S(2)}, u32[]{:S(2)}) %collective-permute-start.6) | collective-permute-done | bytes 196640 | tf_op jit(solution)/shard_map/ppermute | solution.py:16
  88.4 0.8 constant_dynamic-update-slice_fusion
  89.2 8.1 %collective-permute-start.7 = (bf16[2,512,768]{2,1,0:T(8,128)(2,1)}, bf16[2,512,768]{2,1,0:T(8,128)(2,1)S(1)}, u32[]{:S(2)}, u32[]{:S(2)}) collective-permute-start(bf16[2,512,768]{2,1,0:T(8,128)(2,1)} %get-tuple-element.9), channel_id=1, source_target_pairs={{8,0},{0,8},{9,1},{1,9},{10,2},{2,10},{11,3},{3,11},{12,4},{4,12},... | collective-permute-start | bytes 4718600 | tf_op jit(solution)/shard_map/ppermute | solution.py:16
  98.0 2.6 %collective-permute-done.7 = bf16[2,512,768]{2,1,0:T(8,128)(2,1)S(1)} collective-permute-done((bf16[2,512,768]{2,1,0:T(8,128)(2,1)}, bf16[2,512,768]{2,1,0:T(8,128)(2,1)S(1)}, u32[]{:S(2)}, u32[]{:S(2)}) %collective-permute-start.7) | collective-permute-done | bytes 1572896 | tf_op jit(solution)/shard_map/ppermute | solution.py:16
  100.6 1.3 constant_dynamic-update-slice_fusion.8
  101.8 1.5 constant_dynamic-slice_fusion
  103.3 0.9 copy.19
  104.2 5.1 %all-to-all-start.1 = ((bf16[8,256,96]{1,2,0:T(8,128)(2,1)}), bf16[8,256,96]{1,2,0:T(8,128)(2,1)S(1)}, u32[]{:S(2)}, u32[]{:S(2)}) async-start(bf16[8,256,96]{1,2,0:T(8,128)(2,1)} %copy.19), calls=%async_computation.1 | async-start | bytes 786432 | tf_op jit(solution)/shard_map/all_to_all | solution.py:111
  109.4 7.3 %all-to-all-done.1 = bf16[8,256,96]{1,2,0:T(8,128)(2,1)S(1)} async-done(((bf16[8,256,96]{1,2,0:T(8,128)(2,1)}), bf16[8,256,96]{1,2,0:T(8,128)(2,1)S(1)}, u32[]{:S(2)}, u32[]{:S(2)}) %all-to-all-start.1) | async-done | bytes 393248 | tf_op jit(solution)/shard_map/all_to_all | solution.py:111
  116.7 3.7 %collective-permute-start.8 = (bf16[8,4,96,768]{3,2,1,0:T(8,128)(2,1)}, bf16[8,4,96,768]{3,2,1,0:T(8,128)(2,1)}, u32[]{:S(2)}, u32[]{:S(2)}) collective-permute-start(bf16[8,4,96,768]{3,2,1,0:T(8,128)(2,1)} %bitcast.35), channel_id=1, source_target_pairs={{8,0},{0,8},{9,1},{1,9},{10,2},{2,10},{11,3},{3,11},{12,4},{4,12},... | collective-permute-start | bytes 14155784 | tf_op jit(solution)/shard_map/ppermute | solution.py:16
  120.4 0.8 broadcast_in_dim.34
  121.2 3.5 %all-to-all-start.2 = ((bf16[8,256,96]{1,2,0:T(8,128)(2,1)}), bf16[8,256,96]{1,2,0:T(8,128)(2,1)S(1)}, u32[]{:S(2)}, u32[]{:S(2)}) async-start(bf16[8,256,96]{1,2,0:T(8,128)(2,1)} %broadcast_in_dim.34), calls=%async_computation.2 | async-start | bytes 786432 | tf_op jit(solution)/shard_map/all_to_all | solution.py:21
  124.7 0.1 copy.22.out_eigs
  124.8 3.4 %collective-permute-done.8.other = bf16[8,4,96,768]{3,2,1,0:T(8,128)(2,1)} collective-permute-done((bf16[8,4,96,768]{3,2,1,0:T(8,128)(2,1)}, bf16[8,4,96,768]{3,2,1,0:T(8,128)(2,1)}, u32[]{:S(2)}, u32[]{:S(2)}) %collective-permute-start.8) | collective-permute-done | bytes 4718624 | tf_op jit(solution)/shard_map/ppermute | solution.py:16
  128.3 2.3 %copy-done = bf16[32,96,768]{2,1,0:T(8,128)(2,1)S(1)} copy-done((bf16[32,96,768]{2,1,0:T(8,128)(2,1)S(1)}, bf16[32,96,768]{2,1,0:T(8,128)(2,1)}, u32[]{:S(2)}) %copy-start) | copy-done | bytes 4718616
  130.6 8.0 %shard_map.103 = f32[8,96,768]{2,1,0:T(8,128)} custom-call(s32[1]{0:T(128)} %bitcast.10.place, bf16[8,4,96,768]{3,2,1,0:T(8,128)(2,1)S(1)} %bitcast.36, bf16[8,4,96,768]{3,2,1,0:T(8,128)(2,1)} %collective-permute-done.8.other, bf16[96,6144]{1,0:T(8,128)(2,1)S(1)} %copy-done.1, f32[1,768]{1,0:T(1,128)S(1)} %broadcast_in_dim.36.in_eigs, f32[96,1]{1,0:T(8,128)S(1)} %copy.22.out_eigs), custom_call_target="tpu_custom_call" | custom-call | flops 1811939328 | bytes 14155776 | tf_op jit(solution)/shard_map/pallas_call | solution.py:77
  138.6 3.6 %all-to-all-start.3 = ((f32[8,96,768]{2,1,0:T(8,128)}), f32[8,96,768]{2,1,0:T(8,128)S(1)}, u32[]{:S(2)}, u32[]{:S(2)}) async-start(f32[8,96,768]{2,1,0:T(8,128)} %shard_map.103), calls=%async_computation.3 | async-start | bytes 4718592 | tf_op jit(solution)/shard_map/all_to_all | solution.py:124
  142.4 2.5 %fusion.2 = f32[768,96]{0,1:T(8,128)} fusion(bf16[1024,96]{0,1:T(8,128)(2,1)S(1)} %bitcast.42, bf16[2,1024,768]{2,1,0:T(8,128)(2,1)} %constant_dynamic-update-slice_fusion.8), kind=kOutput, calls=%fused_computation.4 | convolution fusion | flops 151068672 | bytes 2064384 | tf_op jit(solution)/shard_map/dot_general | solution.py:117
  144.9 2.5 %fusion.3 = f32[768,96]{0,1:T(8,128)} fusion(bf16[1024,96]{0,1:T(8,128)(2,1)S(1)} %bitcast.43, bf16[2,1024,768]{2,1,0:T(8,128)(2,1)} %constant_dynamic-update-slice_fusion.8), kind=kOutput, calls=%fused_computation.5 | convolution fusion | flops 151068672 | bytes 2064384 | tf_op jit(solution)/shard_map/dot_general | solution.py:117
  147.4 23.8 %all-to-all-done.3 = f32[8,96,768]{2,1,0:T(8,128)S(1)} async-done(((f32[8,96,768]{2,1,0:T(8,128)}), f32[8,96,768]{2,1,0:T(8,128)S(1)}, u32[]{:S(2)}, u32[]{:S(2)}) %all-to-all-start.3) | async-done | bytes 2359328 | tf_op jit(solution)/shard_map/all_to_all | solution.py:124
  171.2 0.8 reduce_sum.9
  (17 shorter events, 0.1 us)
Async XLA Ops:
  7.2 109.5 %all-gather.3.cloned.1.call-start = ((), (), s32[]{:S(2)}) async-start(), calls=%async_computation.4 | async-start | bytes 5308416 | tf_op jit(solution)/shard_map/all_gather | solution.py:101
  38.5 13.7 %collective-permute-start = (bf16[2,64,768]{2,1,0:T(8,128)(2,1)S(1)}, bf16[2,64,768]{2,1,0:T(8,128)(2,1)S(1)}, u32[]{:S(2)}, u32[]{:S(2)}) collective-permute-start(bf16[2,64,768]{2,1,0:T(8,128)(2,1)S(1)} %bitcast.39), channel_id=1, source_target_pairs={{16,0},{32,16},{48,32},{64,48},{80,64},{96,80},{112,96},{0,112},{1... | collective-permute-start | bytes 589832 | tf_op jit(solution)/shard_map/ppermute | solution.py:16
  49.5 7.6 %collective-permute-start.1 = (bf16[2,64,768]{2,1,0:T(8,128)(2,1)S(1)}, bf16[2,64,768]{2,1,0:T(8,128)(2,1)S(1)}, u32[]{:S(2)}, u32[]{:S(2)}) collective-permute-start(bf16[2,64,768]{2,1,0:T(8,128)(2,1)S(1)} %bitcast.40), channel_id=1, source_target_pairs={{112,0},{0,16},{16,32},{32,48},{48,64},{64,80},{80,96},{96,112},{1... | collective-permute-start | bytes 589832 | tf_op jit(solution)/shard_map/ppermute | solution.py:16
  52.3 11.4 %collective-permute-start.2 = (bf16[2,64,768]{2,1,0:T(8,128)(2,1)S(1)}, bf16[2,64,768]{2,1,0:T(8,128)(2,1)S(1)}, u32[]{:S(2)}, u32[]{:S(2)}) collective-permute-start(bf16[2,64,768]{2,1,0:T(8,128)(2,1)S(1)} %collective-permute-done), channel_id=1, source_target_pairs={{16,0},{32,16},{48,32},{64,48},{80,64},{96,80},{112,96},{0,112},{1... | collective-permute-start | bytes 589832 | tf_op jit(solution)/shard_map/ppermute | solution.py:16
  57.2 12.5 %collective-permute-start.3 = (bf16[2,64,768]{2,1,0:T(8,128)(2,1)S(1)}, bf16[2,64,768]{2,1,0:T(8,128)(2,1)S(1)}, u32[]{:S(2)}, u32[]{:S(2)}) collective-permute-start(bf16[2,64,768]{2,1,0:T(8,128)(2,1)S(1)} %collective-permute-done.1), channel_id=1, source_target_pairs={{112,0},{0,16},{16,32},{32,48},{48,64},{64,80},{80,96},{96,112},{1... | collective-permute-start | bytes 589832 | tf_op jit(solution)/shard_map/ppermute | solution.py:16
  63.6 12.4 %collective-permute-start.4 = (bf16[2,64,768]{2,1,0:T(8,128)(2,1)S(1)}, bf16[2,64,768]{2,1,0:T(8,128)(2,1)S(1)}, u32[]{:S(2)}, u32[]{:S(2)}) collective-permute-start(bf16[2,64,768]{2,1,0:T(8,128)(2,1)S(1)} %collective-permute-done.2), channel_id=1, source_target_pairs={{16,0},{32,16},{48,32},{64,48},{80,64},{96,80},{112,96},{0,112},{1... | collective-permute-start | bytes 589832 | tf_op jit(solution)/shard_map/ppermute | solution.py:16
  69.6 12.7 %collective-permute-start.5 = (bf16[2,64,768]{2,1,0:T(8,128)(2,1)S(1)}, bf16[2,64,768]{2,1,0:T(8,128)(2,1)S(1)}, u32[]{:S(2)}, u32[]{:S(2)}) collective-permute-start(bf16[2,64,768]{2,1,0:T(8,128)(2,1)S(1)} %collective-permute-done.3), channel_id=1, source_target_pairs={{112,0},{0,16},{16,32},{32,48},{48,64},{64,80},{80,96},{96,112},{1... | collective-permute-start | bytes 589832 | tf_op jit(solution)/shard_map/ppermute | solution.py:16
  76.1 12.4 %collective-permute-start.6 = (bf16[2,64,768]{2,1,0:T(8,128)(2,1)S(1)}, bf16[2,64,768]{2,1,0:T(8,128)(2,1)S(1)}, u32[]{:S(2)}, u32[]{:S(2)}) collective-permute-start(bf16[2,64,768]{2,1,0:T(8,128)(2,1)S(1)} %collective-permute-done.4), channel_id=1, source_target_pairs={{16,0},{32,16},{48,32},{64,48},{80,64},{96,80},{112,96},{0,112},{1... | collective-permute-start | bytes 589832 | tf_op jit(solution)/shard_map/ppermute | solution.py:16
  89.2 11.4 %collective-permute-start.7 = (bf16[2,512,768]{2,1,0:T(8,128)(2,1)}, bf16[2,512,768]{2,1,0:T(8,128)(2,1)S(1)}, u32[]{:S(2)}, u32[]{:S(2)}) collective-permute-start(bf16[2,512,768]{2,1,0:T(8,128)(2,1)} %get-tuple-element.9), channel_id=1, source_target_pairs={{8,0},{0,8},{9,1},{1,9},{10,2},{2,10},{11,3},{3,11},{12,4},{4,12},... | collective-permute-start | bytes 4718600 | tf_op jit(solution)/shard_map/ppermute | solution.py:16
  100.6 24.1 %copy-start.2 = (f32[768]{0:T(1024)S(1)}, f32[768]{0:T(1024)}, u32[]{:S(2)}) copy-start(f32[768]{0:T(1024)} %param.14) | copy-start | bytes 9220
  100.6 24.2 %copy-start.3 = (f32[96]{0:T(128)S(1)}, f32[96]{0:T(128)}, u32[]{:S(2)}) copy-start(f32[96]{0:T(128)} %param.15) | copy-start | bytes 1156
  100.6 27.7 %copy-start.1 = (bf16[96,6144]{1,0:T(8,128)(2,1)S(1)}, bf16[96,6144]{1,0:T(8,128)(2,1)}, u32[]{:S(2)}) copy-start(bf16[96,6144]{1,0:T(8,128)(2,1)} %grad.1) | copy-start | bytes 3538948
  104.2 12.4 %all-to-all-start.1 = ((bf16[8,256,96]{1,2,0:T(8,128)(2,1)}), bf16[8,256,96]{1,2,0:T(8,128)(2,1)S(1)}, u32[]{:S(2)}, u32[]{:S(2)}) async-start(bf16[8,256,96]{1,2,0:T(8,128)(2,1)} %copy.19), calls=%async_computation.1 | async-start | bytes 786432 | tf_op jit(solution)/shard_map/all_to_all | solution.py:111
  116.7 11.6 %collective-permute-start.8 = (bf16[8,4,96,768]{3,2,1,0:T(8,128)(2,1)}, bf16[8,4,96,768]{3,2,1,0:T(8,128)(2,1)}, u32[]{:S(2)}, u32[]{:S(2)}) collective-permute-start(bf16[8,4,96,768]{3,2,1,0:T(8,128)(2,1)} %bitcast.35), channel_id=1, source_target_pairs={{8,0},{0,8},{9,1},{1,9},{10,2},{2,10},{11,3},{3,11},{12,4},{4,12},... | collective-permute-start | bytes 14155784 | tf_op jit(solution)/shard_map/ppermute | solution.py:16
  121.2 17.4 %all-to-all-start.2 = ((bf16[8,256,96]{1,2,0:T(8,128)(2,1)}), bf16[8,256,96]{1,2,0:T(8,128)(2,1)S(1)}, u32[]{:S(2)}, u32[]{:S(2)}) async-start(bf16[8,256,96]{1,2,0:T(8,128)(2,1)} %broadcast_in_dim.34), calls=%async_computation.2 | async-start | bytes 786432 | tf_op jit(solution)/shard_map/all_to_all | solution.py:21
  128.3 2.3 %copy-start = (bf16[32,96,768]{2,1,0:T(8,128)(2,1)S(1)}, bf16[32,96,768]{2,1,0:T(8,128)(2,1)}, u32[]{:S(2)}) copy-start(bf16[32,96,768]{2,1,0:T(8,128)(2,1)} %all-gather.3.cloned.1.call-done) | copy-start | bytes 14155780
  138.6 32.6 %all-to-all-start.3 = ((f32[8,96,768]{2,1,0:T(8,128)}), f32[8,96,768]{2,1,0:T(8,128)S(1)}, u32[]{:S(2)}, u32[]{:S(2)}) async-start(f32[8,96,768]{2,1,0:T(8,128)} %shard_map.103), calls=%async_computation.3 | async-start | bytes 4718592 | tf_op jit(solution)/shard_map/all_to_all | solution.py:124
Sparse Core Ops, SparseCore 0:
  38.6 75.5 all-gather.2

commit v5 on v4

--- a/solution.py
+++ b/solution.py
@@ -19,18 +19,6 @@
 def spread(block, axis):
     size = lax.axis_size(axis)
     return lax.all_to_all(jnp.broadcast_to(block[None], (size,) + block.shape), axis, 0, 0, tiled=True)
-
-
-def gather_z(block):
-    chunks = [block]
-    up = down = block
-    for step in range(4):
-        up = shift(up, "z", 1)
-        chunks.append(up)
-        if step < 3:
-            down = shift(down, "z", -1)
-            chunks.append(down)
-    return chunks
 
 
 def precondition_kernel(place, own, other, grad, in_eigs, out_eigs, terms, basis, sems):
@@ -96,12 +84,11 @@
     blocks_per = width // owned_width
     group_count = lax.axis_size("yl") * lax.axis_size("x")
     is_live = lax.broadcasted_iota(jnp.int32, (slots, 1), 0) < counts[0]
-    kept = [jnp.where(is_live, v, jnp.zeros_like(v)) for v in (activations, out_grads)]
-    column = spread(jnp.concatenate([basis] + kept), "yh")
-    own = lax.all_gather(column[:, :owned_width], "z", axis=0)
-    kept = column[:, owned_width:].reshape(-1, 2, slots, width)
-    kept = jnp.moveaxis(kept, 1, 0).reshape(2, -1, width)
-    kept = jnp.concatenate(gather_z(kept), axis=1)
+    kept = jnp.concatenate([jnp.where(is_live, v, jnp.zeros_like(v)) for v in (activations, out_grads)])
+    column, kept = lax.optimization_barrier((spread(basis, "yh"), kept))
+    own = lax.all_gather(column, "z", axis=0)
+    kept = spread(spread(kept, "z").reshape(-1, width), "yh")
+    kept = jnp.moveaxis(kept.reshape(-1, 2, slots, width), 1, 0).reshape(2, -1, width)
     both = jnp.concatenate([kept, shift(kept, "core", 1)], axis=1)
     samples = both.shape[1]
     owner_idx = owners[0]

time: 180 us -> 182 us (1.011)
  blocking collectives: 27.9 us -> 58.9 us
  starting transfers between devices: 56.5 us -> 31.1 us
  local copies, waits for them, and re-layouts: 14.2 us -> 7.09 us
  waiting for transfers between devices: 49.1 us -> 52.2 us
    ppermute x9 -> x2, starting transfers between devices: 44.3 us -> 11.6 us  [shift(): lax.ppermute(value, axis, [((i + by) % size, i) for i in range(size)])]
    all_to_all x1 -> x2, blocking collectives: 27.9 us -> 58.9 us  [spread(): lax.all_to_all(jnp.broadcast_to(block[None], (size,) + block.shape), axis...]
    all_to_all x1 -> x2, waiting for transfers between devices: 0.01 us -> 14.9 us  [spread(): lax.all_to_all(jnp.broadcast_to(block[None], (size,) + block.shape), axis...]
    ppermute x9 -> x2, waiting for transfers between devices: 17.9 us -> 5.97 us  [shift(): lax.ppermute(value, axis, [((i + by) % size, i) for i in range(size)])]
    all_to_all x1 -> x2, starting transfers between devices: 3.45 us -> 11.1 us  [spread(): lax.all_to_all(jnp.broadcast_to(block[None], (size,) + block.shape), axis...]
    unnamed x16 -> x15, local copies, waits for them, and re-layouts: 7.87 us -> 3.21 us
    concatenate x2 -> x0, local copies, waits for them, and re-layouts: 2.04 us -> none  [the longest x1 1.26 us: shards(): both = jnp.concatenate([kept, shift(kept, 'core', 1)], axis=1)]
  transfers between devices with their start and end apart: 13 -> 7, of which waited for: 8 -> 5; matrix products, arithmetic and copies ran while one was open for 9% -> 5% of each run, Pallas kernels for 4% -> 4%
where the time goes in v5:
time: 182 us; the launch traced here: 181 us
  blocking collectives  58.9 us (32%)
  waiting for transfers between devices  52.2 us (29%)
  starting transfers between devices  31.1 us (17%)
  between operations  15.5 us (9%)
  Pallas kernels  8 us (4%)
  local copies, waits for them, and re-layouts  7.09 us (4%)
  matrix products  4.48 us (2%)
  other arithmetic  4.09 us (2%)
    all_to_all x2, blocking collectives, spread(): lax.all_to_all(jnp.broadcast_to(block[None], (size,) + block.shape), axis...  58.9 us
    all_to_all x1, waiting for transfers between devices, shards(): terms = lax.all_to_all(terms, GROUP, 0, 0, tiled=True)  24.5 us
    all_to_all x2, waiting for transfers between devices, spread(): lax.all_to_all(jnp.broadcast_to(block[None], (size,) + block.shape), axis...  14.9 us
    ppermute x2, starting transfers between devices, shift(): lax.ppermute(value, axis, [((i + by) % size, i) for i in range(size)])  11.6 us
    all_to_all x2, starting transfers between devices, spread(): lax.all_to_all(jnp.broadcast_to(block[None], (size,) + block.shape), axis...  11.1 us
    pallas_call x1, Pallas kernels, precondition(): pl.pallas_call(precondition_kernel, out_shape=jax.ShapeDtypeStruct((8, ro...  8 us
    all_to_all x1, waiting for transfers between devices, shards(): pieces = lax.all_to_all(pieces, GROUP, 0, 0, tiled=True)  6.88 us
    ppermute x2, waiting for transfers between devices, shift(): lax.ppermute(value, axis, [((i + by) % size, i) for i in range(size)])  5.97 us
  transfers between devices with their start and end apart: 7, of which 5 were waited for; matrix products, arithmetic and copies ran while one was open for 5% of the time, Pallas kernels for 4%

profile of v5, /device:TPU:1, one launch (start us, length us, event | category | flops | bytes accessed | tf_op | source)
XLA Modules:
  0.0 181.4 jit_solution(14240126105072662067)
XLA Ops:
  7.2 0.0 copy-start.4
  7.2 0.0 copy-start.3
  7.2 1.8 broadcast_in_dim.45
  9.0 7.6 %all-to-all-start = ((bf16[4,96,768]{2,1,0:T(8,128)(2,1)}), bf16[4,96,768]{2,1,0:T(8,128)(2,1)S(1)}, u32[]{:S(2)}, u32[]{:S(2)}) async-start(bf16[4,96,768]{2,1,0:T(8,128)(2,1)} %broadcast_in_dim.45), calls=%async_computation | async-start | bytes 1179648 | tf_op jit(solution)/shard_map/all_to_all | solution.py:21
  16.6 0.0 all-gather.3.cloned.1.call-start
  17.3 0.0 copy-done.4
  17.3 0.0 copy-done.3
  17.3 0.1 broadcast_select_fusion.1
  17.4 14.9 %all-to-all-done = bf16[4,96,768]{2,1,0:T(8,128)(2,1)S(1)} async-done(((bf16[4,96,768]{2,1,0:T(8,128)(2,1)}), bf16[4,96,768]{2,1,0:T(8,128)(2,1)S(1)}, u32[]{:S(2)}, u32[]{:S(2)}) %all-to-all-start) | async-done | bytes 589856 | tf_op jit(solution)/shard_map/all_to_all | solution.py:21
  32.3 0.0 copy-start.2
  32.3 0.8 copy-done.2
  33.1 0.0 all-gather.3.cloned.1.call-update
  33.2 21.6 %all_to_all.30 = bf16[8,32,768]{2,1,0:T(8,128)(2,1)S(1)} all-to-all(bf16[8,32,768]{2,1,0:T(8,128)(2,1)S(1)} %broadcast_in_dim.47), channel_id=1, replica_groups=mesh['yh'=4,'z'=8,'core'=2,'yl'=2,'x'=4] {'z'}, dimensions={0} | all-to-all | bytes 786432 | tf_op jit(solution)/shard_map/all_to_all | solution.py:21
  54.7 0.1 broadcast_in_dim.49
  54.8 37.4 %all_to_all.31 = bf16[4,256,768]{2,1,0:T(8,128)(2,1)S(1)} all-to-all(bf16[4,256,768]{2,1,0:T(8,128)(2,1)S(1)} %broadcast_in_dim.49), channel_id=1, replica_groups=mesh['yh'=4,'z'=8,'core'=2,'yl'=2,'x'=4] {'yh'}, dimensions={0} | all-to-all | bytes 3145728 | tf_op jit(solution)/shard_map/all_to_all | solution.py:21
  92.2 0.1 copy.17
  92.3 7.2 %collective-permute-start = (bf16[2,512,768]{2,1,0:T(8,128)(2,1)S(1)}, bf16[2,512,768]{2,1,0:T(8,128)(2,1)}, u32[]{:S(2)}, u32[]{:S(2)}) collective-permute-start(bf16[2,512,768]{2,1,0:T(8,128)(2,1)S(1)} %bitcast.38), channel_id=1, source_target_pairs={{8,0},{0,8},{9,1},{1,9},{10,2},{2,10},{11,3},{3,11},{12,4},{4,12},... | collective-permute-start | bytes 4718600 | tf_op jit(solution)/shard_map/ppermute | solution.py:16
  100.2 2.5 %collective-permute-done = bf16[2,512,768]{2,1,0:T(8,128)(2,1)} collective-permute-done((bf16[2,512,768]{2,1,0:T(8,128)(2,1)S(1)}, bf16[2,512,768]{2,1,0:T(8,128)(2,1)}, u32[]{:S(2)}, u32[]{:S(2)}) %collective-permute-start) | collective-permute-done | bytes 1572896 | tf_op jit(solution)/shard_map/ppermute | solution.py:16
  102.7 1.5 fusion.14
  104.2 0.0 copy-start.5
  104.2 0.0 copy-start.6
  104.2 0.0 copy-start.1
  104.2 1.0 copy.19
  105.2 4.0 %all-to-all-start.3 = ((bf16[8,256,96]{1,2,0:T(8,128)(2,1)}), bf16[8,256,96]{1,2,0:T(8,128)(2,1)S(1)}, u32[]{:S(2)}, u32[]{:S(2)}) async-start(bf16[8,256,96]{1,2,0:T(8,128)(2,1)} %copy.19), calls=%async_computation.3 | async-start | bytes 786432 | tf_op jit(solution)/shard_map/all_to_all | solution.py:98
  109.2 6.9 %all-to-all-done.3 = bf16[8,256,96]{1,2,0:T(8,128)(2,1)S(1)} async-done(((bf16[8,256,96]{1,2,0:T(8,128)(2,1)}), bf16[8,256,96]{1,2,0:T(8,128)(2,1)S(1)}, u32[]{:S(2)}, u32[]{:S(2)}) %all-to-all-start.3) | async-done | bytes 393248 | tf_op jit(solution)/shard_map/all_to_all | solution.py:98
  116.1 0.0 all-gather.3.cloned.1.call-done
  116.1 4.3 %collective-permute-start.1 = (bf16[8,4,96,768]{3,2,1,0:T(8,128)(2,1)}, bf16[8,4,96,768]{3,2,1,0:T(8,128)(2,1)}, u32[]{:S(2)}, u32[]{:S(2)}) collective-permute-start(bf16[8,4,96,768]{3,2,1,0:T(8,128)(2,1)} %bitcast.36), channel_id=1, source_target_pairs={{8,0},{0,8},{9,1},{1,9},{10,2},{2,10},{11,3},{3,11},{12,4},{4,12},... | collective-permute-start | bytes 14155784 | tf_op jit(solution)/shard_map/ppermute | solution.py:16
  120.4 0.8 broadcast_in_dim.50
  121.2 3.5 %all-to-all-start.4 = ((bf16[8,256,96]{1,2,0:T(8,128)(2,1)}), bf16[8,256,96]{1,2,0:T(8,128)(2,1)S(1)}, u32[]{:S(2)}, u32[]{:S(2)}) async-start(bf16[8,256,96]{1,2,0:T(8,128)(2,1)} %broadcast_in_dim.50), calls=%async_computation.4 | async-start | bytes 786432 | tf_op jit(solution)/shard_map/all_to_all | solution.py:21
  124.6 0.0 copy-done.5
  124.7 0.0 copy-done.6
  124.7 0.1 copy.22.out_eigs
  124.8 3.5 %collective-permute-done.1.other = bf16[8,4,96,768]{3,2,1,0:T(8,128)(2,1)} collective-permute-done((bf16[8,4,96,768]{3,2,1,0:T(8,128)(2,1)}, bf16[8,4,96,768]{3,2,1,0:T(8,128)(2,1)}, u32[]{:S(2)}, u32[]{:S(2)}) %collective-permute-start.1) | collective-permute-done | bytes 4718624 | tf_op jit(solution)/shard_map/ppermute | solution.py:16
  128.3 0.0 copy-done.1
  128.3 0.0 copy-start
  128.3 2.3 %copy-done = bf16[32,96,768]{2,1,0:T(8,128)(2,1)S(1)} copy-done((bf16[32,96,768]{2,1,0:T(8,128)(2,1)S(1)}, bf16[32,96,768]{2,1,0:T(8,128)(2,1)}, u32[]{:S(2)}) %copy-start) | copy-done | bytes 4718616
  130.6 8.0 %shard_map.103 = f32[8,96,768]{2,1,0:T(8,128)} custom-call(s32[1]{0:T(128)} %bitcast.11.place, bf16[8,4,96,768]{3,2,1,0:T(8,128)(2,1)S(1)} %bitcast.37, bf16[8,4,96,768]{3,2,1,0:T(8,128)(2,1)} %collective-permute-done.1.other, bf16[96,6144]{1,0:T(8,128)(2,1)S(1)} %copy-done.1, f32[1,768]{1,0:T(1,128)S(1)} %broadcast_in_dim.52.in_eigs, f32[96,1]{1,0:T(8,128)S(1)} %copy.22.out_eigs), custom_call_target="tpu_custom_call" | custom-call | flops 1811939328 | bytes 14155776 | tf_op jit(solution)/shard_map/pallas_call | solution.py:65
  138.6 0.0 all-to-all-done.4
  138.6 4.4 %all-to-all-start.5 = ((f32[8,96,768]{2,1,0:T(8,128)}), f32[8,96,768]{2,1,0:T(8,128)}, u32[]{:S(2)}, u32[]{:S(2)}) async-start(f32[8,96,768]{2,1,0:T(8,128)} %shard_map.103), calls=%async_computation.5 | async-start | bytes 4718592 | tf_op jit(solution)/shard_map/all_to_all | solution.py:111
  143.1 2.2 %fusion.11 = f32[768,96]{0,1:T(8,128)} fusion(bf16[1024,96]{0,1:T(8,128)(2,1)S(1)} %bitcast.45, bf16[2,512,768]{2,1,0:T(8,128)(2,1)} %collective-permute-done, bf16[2,512,768]{2,1,0:T(8,128)(2,1)S(1)} %bitcast.40), kind=kOutput, calls=%fused_computation.12 | convolution fusion | flops 154214400 | bytes 3637248 | tf_op jit(solution)/shard_map/dot_general | solution.py:104
  145.3 2.2 %fusion.8 = f32[768,96]{0,1:T(8,128)} fusion(bf16[1024,96]{0,1:T(8,128)(2,1)S(1)} %bitcast.46, bf16[2,512,768]{2,1,0:T(8,128)(2,1)S(1)} %bitcast.41, bf16[2,512,768]{2,1,0:T(8,128)(2,1)} %collective-permute-done), kind=kOutput, calls=%fused_computation.11 | convolution fusion | flops 154214400 | bytes 3637248 | tf_op jit(solution)/shard_map/dot_general | solution.py:104
  147.6 24.5 %all-to-all-done.5 = f32[8,96,768]{2,1,0:T(8,128)} async-done(((f32[8,96,768]{2,1,0:T(8,128)}), f32[8,96,768]{2,1,0:T(8,128)}, u32[]{:S(2)}, u32[]{:S(2)}) %all-to-all-start.5) | async-done | bytes 2359328 | tf_op jit(solution)/shard_map/all_to_all | solution.py:111
  172.0 2.5 %reduce_sum.9 = f32[96,768]{1,0:T(8,128)} reduce(f32[8,96,768]{2,1,0:T(8,128)} %all-to-all-done.5, f32[]{:T(128)} %constant.48.clone.1), dimensions={0}, to_apply=%region_0.1 | reduce | flops 516096 | bytes 2654212 | tf_op jit(solution)/shard_map/reduce_sum | solution.py:112
  (8 shorter events, 0.1 us)
Async XLA Ops:
  7.2 10.1 %copy-start.4 = (bf16[16,768]{1,0:T(8,128)(2,1)S(1)}, bf16[16,768]{1,0:T(8,128)(2,1)}, u32[]{:S(2)}) copy-start(bf16[16,768]{1,0:T(8,128)(2,1)} %param.9) | copy-start | bytes 73732
  7.2 10.1 %copy-start.3 = (bf16[16,768]{1,0:T(8,128)(2,1)S(1)}, bf16[16,768]{1,0:T(8,128)(2,1)}, u32[]{:S(2)}) copy-start(bf16[16,768]{1,0:T(8,128)(2,1)} %param.8) | copy-start | bytes 73732
  9.0 23.3 %all-to-all-start = ((bf16[4,96,768]{2,1,0:T(8,128)(2,1)}), bf16[4,96,768]{2,1,0:T(8,128)(2,1)S(1)}, u32[]{:S(2)}, u32[]{:S(2)}) async-start(bf16[4,96,768]{2,1,0:T(8,128)(2,1)} %broadcast_in_dim.45), calls=%async_computation | async-start | bytes 1179648 | tf_op jit(solution)/shard_map/all_to_all | solution.py:21
  16.6 99.5 %all-gather.3.cloned.1.call-start = ((), (), s32[]{:S(2)}) async-start(), calls=%async_computation.6 | async-start | bytes 5308416 | tf_op jit(solution)/shard_map/all_gather | solution.py:89
  32.3 0.8 copy-start.2
  92.3 10.4 %collective-permute-start = (bf16[2,512,768]{2,1,0:T(8,128)(2,1)S(1)}, bf16[2,512,768]{2,1,0:T(8,128)(2,1)}, u32[]{:S(2)}, u32[]{:S(2)}) collective-permute-start(bf16[2,512,768]{2,1,0:T(8,128)(2,1)S(1)} %bitcast.38), channel_id=1, source_target_pairs={{8,0},{0,8},{9,1},{1,9},{10,2},{2,10},{11,3},{3,11},{12,4},{4,12},... | collective-permute-start | bytes 4718600 | tf_op jit(solution)/shard_map/ppermute | solution.py:16
  104.2 20.5 %copy-start.5 = (f32[768]{0:T(1024)S(1)}, f32[768]{0:T(1024)}, u32[]{:S(2)}) copy-start(f32[768]{0:T(1024)} %param.14) | copy-start | bytes 9220
  104.2 20.5 %copy-start.6 = (f32[96]{0:T(128)S(1)}, f32[96]{0:T(128)}, u32[]{:S(2)}) copy-start(f32[96]{0:T(128)} %param.15) | copy-start | bytes 1156
  104.2 24.1 %copy-start.1 = (bf16[96,6144]{1,0:T(8,128)(2,1)S(1)}, bf16[96,6144]{1,0:T(8,128)(2,1)}, u32[]{:S(2)}) copy-start(bf16[96,6144]{1,0:T(8,128)(2,1)} %grad.1) | copy-start | bytes 3538948
  105.2 10.9 %all-to-all-start.3 = ((bf16[8,256,96]{1,2,0:T(8,128)(2,1)}), bf16[8,256,96]{1,2,0:T(8,128)(2,1)S(1)}, u32[]{:S(2)}, u32[]{:S(2)}) async-start(bf16[8,256,96]{1,2,0:T(8,128)(2,1)} %copy.19), calls=%async_computation.3 | async-start | bytes 786432 | tf_op jit(solution)/shard_map/all_to_all | solution.py:98
  116.1 12.2 %collective-permute-start.1 = (bf16[8,4,96,768]{3,2,1,0:T(8,128)(2,1)}, bf16[8,4,96,768]{3,2,1,0:T(8,128)(2,1)}, u32[]{:S(2)}, u32[]{:S(2)}) collective-permute-start(bf16[8,4,96,768]{3,2,1,0:T(8,128)(2,1)} %bitcast.36), channel_id=1, source_target_pairs={{8,0},{0,8},{9,1},{1,9},{10,2},{2,10},{11,3},{3,11},{12,4},{4,12},... | collective-permute-start | bytes 14155784 | tf_op jit(solution)/shard_map/ppermute | solution.py:16
  121.2 17.4 %all-to-all-start.4 = ((bf16[8,256,96]{1,2,0:T(8,128)(2,1)}), bf16[8,256,96]{1,2,0:T(8,128)(2,1)S(1)}, u32[]{:S(2)}, u32[]{:S(2)}) async-start(bf16[8,256,96]{1,2,0:T(8,128)(2,1)} %broadcast_in_dim.50), calls=%async_computation.4 | async-start | bytes 786432 | tf_op jit(solution)/shard_map/all_to_all | solution.py:21
  128.3 2.3 %copy-start = (bf16[32,96,768]{2,1,0:T(8,128)(2,1)S(1)}, bf16[32,96,768]{2,1,0:T(8,128)(2,1)}, u32[]{:S(2)}) copy-start(bf16[32,96,768]{2,1,0:T(8,128)(2,1)} %all-gather.3.cloned.1.call-done) | copy-start | bytes 14155780
  138.6 33.4 %all-to-all-start.5 = ((f32[8,96,768]{2,1,0:T(8,128)}), f32[8,96,768]{2,1,0:T(8,128)}, u32[]{:S(2)}, u32[]{:S(2)}) async-start(f32[8,96,768]{2,1,0:T(8,128)} %shard_map.103), calls=%async_computation.5 | async-start | bytes 4718592 | tf_op jit(solution)/shard_map/all_to_all | solution.py:111
Sparse Core Ops, SparseCore 0:
  33.3 67.4 all-gather.2

commit v6 on v5

--- a/solution.py
+++ b/solution.py
@@ -84,11 +84,15 @@
     blocks_per = width // owned_width
     group_count = lax.axis_size("yl") * lax.axis_size("x")
     is_live = lax.broadcasted_iota(jnp.int32, (slots, 1), 0) < counts[0]
-    kept = jnp.concatenate([jnp.where(is_live, v, jnp.zeros_like(v)) for v in (activations, out_grads)])
-    column, kept = lax.optimization_barrier((spread(basis, "yh"), kept))
-    own = lax.all_gather(column, "z", axis=0)
-    kept = spread(spread(kept, "z").reshape(-1, width), "yh")
-    kept = jnp.moveaxis(kept.reshape(-1, 2, slots, width), 1, 0).reshape(2, -1, width)
+    kept_in, kept_out = (jnp.where(is_live, v, jnp.zeros_like(v)) for v in (activations, out_grads))
+    column, kept_out = lax.optimization_barrier(
+        (spread(jnp.concatenate([basis, kept_in]), "yh"), kept_out)
+    )
+    own = lax.all_gather(column[:, :owned_width], "z", axis=0)
+    kept_in, kept_out = lax.optimization_barrier((column[:, owned_width:], spread(kept_out, "z")))
+    kept_out = spread(kept_out.reshape(-1, width), "yh").reshape(-1, width)
+    kept_in = lax.all_gather(kept_in.reshape(-1, width), "z", axis=0, tiled=True)
+    kept = jnp.stack([kept_in, kept_out])
     both = jnp.concatenate([kept, shift(kept, "core", 1)], axis=1)
     samples = both.shape[1]
     owner_idx = owners[0]

time: 182 us -> 178 us (0.978)
  starting transfers between devices: 31.1 us -> 39.1 us
  blocking collectives: 58.9 us -> 51.2 us
  waiting for transfers between devices: 52.2 us -> 46.6 us
    all_to_all x2 -> x1, blocking collectives: 58.9 us -> 25.7 us  [spread(): lax.all_to_all(jnp.broadcast_to(block[None], (size,) + block.shape), axis...]
    all_gather x0 -> x1, blocking collectives: none -> 25.5 us  [shards(): lax.all_gather(kept_in.reshape(-1, width), 'z', axis=0, tiled=True)]
    all_to_all x2 -> x3, starting transfers between devices: 11.1 us -> 17.8 us  [spread(): lax.all_to_all(jnp.broadcast_to(block[None], (size,) + block.shape), axis...]
    all_to_all x2 -> x3, waiting for transfers between devices: 14.9 us -> 8.73 us  [spread(): lax.all_to_all(jnp.broadcast_to(block[None], (size,) + block.shape), axis...]
    unnamed x15 -> x13, local copies, waits for them, and re-layouts: 3.21 us -> 4.03 us
  transfers between devices with their start and end apart: 7 -> 8, of which waited for: 5 -> 5; matrix products, arithmetic and copies ran while one was open for 5% -> 5% of each run, Pallas kernels for 4% -> 5%
where the time goes in v6:
time: 178 us; the launch traced here: 177 us
  blocking collectives  51.2 us (29%)
  waiting for transfers between devices  46.6 us (26%)
  starting transfers between devices  39.1 us (22%)
  between operations  15.5 us (9%)
  local copies, waits for them, and re-layouts  8.72 us (5%)
  Pallas kernels  7.99 us (4%)
  other arithmetic  4.37 us (2%)
  matrix products  3.77 us (2%)
    all_to_all x1, blocking collectives, spread(): lax.all_to_all(jnp.broadcast_to(block[None], (size,) + block.shape), axis...  25.7 us
    all_gather x1, blocking collectives, shards(): lax.all_gather(kept_in.reshape(-1, width), 'z', axis=0, tiled=True)  25.5 us
    all_to_all x1, waiting for transfers between devices, shards(): terms = lax.all_to_all(terms, GROUP, 0, 0, tiled=True)  25.1 us
    all_to_all x3, starting transfers between devices, spread(): lax.all_to_all(jnp.broadcast_to(block[None], (size,) + block.shape), axis...  17.8 us
    ppermute x2, starting transfers between devices, shift(): lax.ppermute(value, axis, [((i + by) % size, i) for i in range(size)])  12.7 us
    all_to_all x3, waiting for transfers between devices, spread(): lax.all_to_all(jnp.broadcast_to(block[None], (size,) + block.shape), axis...  8.73 us
    pallas_call x1, Pallas kernels, precondition(): pl.pallas_call(precondition_kernel, out_shape=jax.ShapeDtypeStruct((8, ro...  7.99 us
    all_to_all x1, waiting for transfers between devices, shards(): pieces = lax.all_to_all(pieces, GROUP, 0, 0, tiled=True)  6.87 us
  transfers between devices with their start and end apart: 8, of which 5 were waited for; matrix products, arithmetic and copies ran while one was open for 5% of the time, Pallas kernels for 5%

profile of v6, /device:TPU:1, one launch (start us, length us, event | category | flops | bytes accessed | tf_op | source)
XLA Modules:
  0.0 177.3 jit_solution(10250177951277347025)
XLA Ops:
  7.2 0.0 all-gather.3.cloned.1.call-start
  7.9 0.8 broadcast_select_fusion
  8.7 0.9 pad_maximum_fusion.2
  9.7 25.7 %all_to_all.30 = bf16[4,112,768]{2,1,0:T(8,128)(2,1)S(1)} all-to-all(bf16[4,112,768]{2,1,0:T(8,128)(2,1)S(1)} %broadcast_in_dim.46), channel_id=1, replica_groups=mesh['yh'=4,'z'=8,'core'=2,'yl'=2,'x'=4] {'yh'}, dimensions={0} | all-to-all | bytes 1376256 | tf_op jit(solution)/shard_map/all_to_all | solution.py:21
  35.4 0.9 slice.22
  36.3 0.0 all-gather.3.cloned.1.call-update
  36.3 0.7 broadcast_in_dim.47
  37.0 10.3 %all-to-all-start.1 = ((bf16[8,16,768]{2,1,0:T(8,128)(2,1)}), bf16[8,16,768]{2,1,0:T(8,128)(2,1)S(1)}, u32[]{:S(2)}, u32[]{:S(2)}) async-start(bf16[8,16,768]{2,1,0:T(8,128)(2,1)} %broadcast_in_dim.47), calls=%async_computation.1 | async-start | bytes 393216 | tf_op jit(solution)/shard_map/all_to_all | solution.py:21
  47.3 8.7 %all-to-all-done.1 = bf16[8,16,768]{2,1,0:T(8,128)(2,1)S(1)} async-done(((bf16[8,16,768]{2,1,0:T(8,128)(2,1)}), bf16[8,16,768]{2,1,0:T(8,128)(2,1)S(1)}, u32[]{:S(2)}, u32[]{:S(2)}) %all-to-all-start.1) | async-done | bytes 196640 | tf_op jit(solution)/shard_map/all_to_all | solution.py:21
  56.0 0.9 broadcast_in_dim.49
  57.0 4.0 %all-to-all-start.2 = ((bf16[4,128,768]{2,1,0:T(8,128)(2,1)}), bf16[4,128,768]{2,1,0:T(8,128)(2,1)S(1)}, u32[]{:S(2)}, u32[]{:S(2)}) async-start(bf16[4,128,768]{2,1,0:T(8,128)(2,1)} %broadcast_in_dim.49), calls=%async_computation.2 | async-start | bytes 1572864 | tf_op jit(solution)/shard_map/all_to_all | solution.py:21
  61.0 25.5 %all_gather.9 = bf16[512,768]{1,0:T(8,128)(2,1)S(1)} all-gather(bf16[64,768]{1,0:T(8,128)(2,1)S(1)} %bitcast.43), channel_id=1, replica_groups=mesh['yh'=4,'z'=8,'core'=2,'yl'=2,'x'=4] {'z'}, dimensions={0}, use_global_device_ids=true | all-gather | bytes 884736 | tf_op jit(solution)/shard_map/all_gather | solution.py:94
  86.5 0.0 all-to-all-done.2
  86.5 0.1 pad_maximum_fusion.1
  86.6 8.4 %collective-permute-start = (bf16[2,512,768]{2,1,0:T(8,128)(2,1)S(1)}, bf16[2,512,768]{2,1,0:T(8,128)(2,1)}, u32[]{:S(2)}, u32[]{:S(2)}) collective-permute-start(bf16[2,512,768]{2,1,0:T(8,128)(2,1)S(1)} %pad_maximum_fusion.1), channel_id=1, source_target_pairs={{8,0},{0,8},{9,1},{1,9},{10,2},{2,10},{11,3},{3,11},{12,4},{4,12},... | collective-permute-start | bytes 4718600 | tf_op jit(solution)/shard_map/ppermute | solution.py:16
  95.7 2.5 %collective-permute-done = bf16[2,512,768]{2,1,0:T(8,128)(2,1)} collective-permute-done((bf16[2,512,768]{2,1,0:T(8,128)(2,1)S(1)}, bf16[2,512,768]{2,1,0:T(8,128)(2,1)}, u32[]{:S(2)}, u32[]{:S(2)}) %collective-permute-start) | collective-permute-done | bytes 1572896 | tf_op jit(solution)/shard_map/ppermute | solution.py:16
  98.2 1.6 pad_maximum_fusion
  99.8 0.0 copy-start.2
  99.8 1.6 copy-done.2
  101.4 0.0 copy-start.4
  101.4 0.0 copy-start.5
  101.4 0.0 copy-start.1
  101.4 0.2 constant_dynamic-slice_fusion
  101.7 1.0 copy.20
  102.6 5.0 %all-to-all-start.3 = ((bf16[8,256,96]{1,2,0:T(8,128)(2,1)}), bf16[8,256,96]{1,2,0:T(8,128)(2,1)S(1)}, u32[]{:S(2)}, u32[]{:S(2)}) async-start(bf16[8,256,96]{1,2,0:T(8,128)(2,1)} %copy.20), calls=%async_computation.3 | async-start | bytes 786432 | tf_op jit(solution)/shard_map/all_to_all | solution.py:102
  107.6 6.9 %all-to-all-done.3 = bf16[8,256,96]{1,2,0:T(8,128)(2,1)S(1)} async-done(((bf16[8,256,96]{1,2,0:T(8,128)(2,1)}), bf16[8,256,96]{1,2,0:T(8,128)(2,1)S(1)}, u32[]{:S(2)}, u32[]{:S(2)}) %all-to-all-start.3) | async-done | bytes 393248 | tf_op jit(solution)/shard_map/all_to_all | solution.py:102
  114.5 0.0 all-gather.3.cloned.1.call-done
  114.5 4.3 %collective-permute-start.1 = (bf16[8,4,96,768]{3,2,1,0:T(8,128)(2,1)}, bf16[8,4,96,768]{3,2,1,0:T(8,128)(2,1)}, u32[]{:S(2)}, u32[]{:S(2)}) collective-permute-start(bf16[8,4,96,768]{3,2,1,0:T(8,128)(2,1)} %bitcast.35), channel_id=1, source_target_pairs={{8,0},{0,8},{9,1},{1,9},{10,2},{2,10},{11,3},{3,11},{12,4},{4,12},... | collective-permute-start | bytes 14155784 | tf_op jit(solution)/shard_map/ppermute | solution.py:16
  118.8 0.8 broadcast_in_dim.50
  119.6 3.5 %all-to-all-start.4 = ((bf16[8,256,96]{1,2,0:T(8,128)(2,1)}), bf16[8,256,96]{1,2,0:T(8,128)(2,1)S(1)}, u32[]{:S(2)}, u32[]{:S(2)}) async-start(bf16[8,256,96]{1,2,0:T(8,128)(2,1)} %broadcast_in_dim.50), calls=%async_computation.4 | async-start | bytes 786432 | tf_op jit(solution)/shard_map/all_to_all | solution.py:21
  123.1 0.0 copy-done.4
  123.1 0.0 copy-done.5
  123.1 0.1 copy.23.out_eigs
  123.2 3.4 %collective-permute-done.1.other = bf16[8,4,96,768]{3,2,1,0:T(8,128)(2,1)} collective-permute-done((bf16[8,4,96,768]{3,2,1,0:T(8,128)(2,1)}, bf16[8,4,96,768]{3,2,1,0:T(8,128)(2,1)}, u32[]{:S(2)}, u32[]{:S(2)}) %collective-permute-start.1) | collective-permute-done | bytes 4718624 | tf_op jit(solution)/shard_map/ppermute | solution.py:16
  126.7 0.0 copy-done.1
  126.7 0.0 copy-start
  126.7 2.3 %copy-done = bf16[32,96,768]{2,1,0:T(8,128)(2,1)S(1)} copy-done((bf16[32,96,768]{2,1,0:T(8,128)(2,1)S(1)}, bf16[32,96,768]{2,1,0:T(8,128)(2,1)}, u32[]{:S(2)}) %copy-start) | copy-done | bytes 4718616
  129.0 8.0 %shard_map.103 = f32[8,96,768]{2,1,0:T(8,128)} custom-call(s32[1]{0:T(128)} %bitcast.11.place, bf16[8,4,96,768]{3,2,1,0:T(8,128)(2,1)S(1)} %bitcast.36, bf16[8,4,96,768]{3,2,1,0:T(8,128)(2,1)} %collective-permute-done.1.other, bf16[96,6144]{1,0:T(8,128)(2,1)S(1)} %copy-done.1, f32[1,768]{1,0:T(1,128)S(1)} %broadcast_in_dim.52.in_eigs, f32[96,1]{1,0:T(8,128)S(1)} %copy.23.out_eigs), custom_call_target="tpu_custom_call" | custom-call | flops 1811939328 | bytes 14155776 | tf_op jit(solution)/shard_map/pallas_call | solution.py:65
  137.0 0.0 all-to-all-done.4
  137.0 3.6 %all-to-all-start.5 = ((f32[8,96,768]{2,1,0:T(8,128)}), f32[8,96,768]{2,1,0:T(8,128)S(1)}, u32[]{:S(2)}, u32[]{:S(2)}) async-start(f32[8,96,768]{2,1,0:T(8,128)} %shard_map.103), calls=%async_computation.5 | async-start | bytes 4718592 | tf_op jit(solution)/shard_map/all_to_all | solution.py:115
  140.7 0.0 copy-start.3
  140.8 2.7 %fusion.3 = f32[768,96]{0,1:T(8,128)} fusion(bf16[1024,96]{0,1:T(8,128)(2,1)S(1)} %bitcast.44, bf16[2,1024,768]{2,1,0:T(8,128)(2,1)} %copy-done.2), kind=kOutput, calls=%fused_computation.7 | convolution fusion | flops 151068672 | bytes 2064384 | tf_op jit(solution)/shard_map/dot_general | solution.py:108
  143.4 0.0 copy-done.3
  143.4 1.1 fusion.2
  144.5 25.1 %all-to-all-done.5 = f32[8,96,768]{2,1,0:T(8,128)S(1)} async-done(((f32[8,96,768]{2,1,0:T(8,128)}), f32[8,96,768]{2,1,0:T(8,128)S(1)}, u32[]{:S(2)}, u32[]{:S(2)}) %all-to-all-start.5) | async-done | bytes 2359328 | tf_op jit(solution)/shard_map/all_to_all | solution.py:115
  169.6 0.8 reduce_sum.9
  (8 shorter events, 0.1 us)
Async XLA Ops:
  7.2 107.3 %all-gather.3.cloned.1.call-start = ((), (), s32[]{:S(2)}) async-start(), calls=%async_computation.6 | async-start | bytes 5308416 | tf_op jit(solution)/shard_map/all_gather | solution.py:91
  37.0 19.0 %all-to-all-start.1 = ((bf16[8,16,768]{2,1,0:T(8,128)(2,1)}), bf16[8,16,768]{2,1,0:T(8,128)(2,1)S(1)}, u32[]{:S(2)}, u32[]{:S(2)}) async-start(bf16[8,16,768]{2,1,0:T(8,128)(2,1)} %broadcast_in_dim.47), calls=%async_computation.1 | async-start | bytes 393216 | tf_op jit(solution)/shard_map/all_to_all | solution.py:21
  57.0 29.5 %all-to-all-start.2 = ((bf16[4,128,768]{2,1,0:T(8,128)(2,1)}), bf16[4,128,768]{2,1,0:T(8,128)(2,1)S(1)}, u32[]{:S(2)}, u32[]{:S(2)}) async-start(bf16[4,128,768]{2,1,0:T(8,128)(2,1)} %broadcast_in_dim.49), calls=%async_computation.2 | async-start | bytes 1572864 | tf_op jit(solution)/shard_map/all_to_all | solution.py:21
  86.6 11.5 %collective-permute-start = (bf16[2,512,768]{2,1,0:T(8,128)(2,1)S(1)}, bf16[2,512,768]{2,1,0:T(8,128)(2,1)}, u32[]{:S(2)}, u32[]{:S(2)}) collective-permute-start(bf16[2,512,768]{2,1,0:T(8,128)(2,1)S(1)} %pad_maximum_fusion.1), channel_id=1, source_target_pairs={{8,0},{0,8},{9,1},{1,9},{10,2},{2,10},{11,3},{3,11},{12,4},{4,12},... | collective-permute-start | bytes 4718600 | tf_op jit(solution)/shard_map/ppermute | solution.py:16
  99.8 1.7 copy-start.2
  101.4 21.7 %copy-start.4 = (f32[768]{0:T(1024)S(1)}, f32[768]{0:T(1024)}, u32[]{:S(2)}) copy-start(f32[768]{0:T(1024)} %param.14) | copy-start | bytes 9220
  101.4 21.7 %copy-start.5 = (f32[96]{0:T(128)S(1)}, f32[96]{0:T(128)}, u32[]{:S(2)}) copy-start(f32[96]{0:T(128)} %param.15) | copy-start | bytes 1156
  101.4 25.2 %copy-start.1 = (bf16[96,6144]{1,0:T(8,128)(2,1)S(1)}, bf16[96,6144]{1,0:T(8,128)(2,1)}, u32[]{:S(2)}) copy-start(bf16[96,6144]{1,0:T(8,128)(2,1)} %grad.1) | copy-start | bytes 3538948
  102.6 11.9 %all-to-all-start.3 = ((bf16[8,256,96]{1,2,0:T(8,128)(2,1)}), bf16[8,256,96]{1,2,0:T(8,128)(2,1)S(1)}, u32[]{:S(2)}, u32[]{:S(2)}) async-start(bf16[8,256,96]{1,2,0:T(8,128)(2,1)} %copy.20), calls=%async_computation.3 | async-start | bytes 786432 | tf_op jit(solution)/shard_map/all_to_all | solution.py:102
  114.5 12.2 %collective-permute-start.1 = (bf16[8,4,96,768]{3,2,1,0:T(8,128)(2,1)}, bf16[8,4,96,768]{3,2,1,0:T(8,128)(2,1)}, u32[]{:S(2)}, u32[]{:S(2)}) collective-permute-start(bf16[8,4,96,768]{3,2,1,0:T(8,128)(2,1)} %bitcast.35), channel_id=1, source_target_pairs={{8,0},{0,8},{9,1},{1,9},{10,2},{2,10},{11,3},{3,11},{12,4},{4,12},... | collective-permute-start | bytes 14155784 | tf_op jit(solution)/shard_map/ppermute | solution.py:16
  119.6 17.4 %all-to-all-start.4 = ((bf16[8,256,96]{1,2,0:T(8,128)(2,1)}), bf16[8,256,96]{1,2,0:T(8,128)(2,1)S(1)}, u32[]{:S(2)}, u32[]{:S(2)}) async-start(bf16[8,256,96]{1,2,0:T(8,128)(2,1)} %broadcast_in_dim.50), calls=%async_computation.4 | async-start | bytes 786432 | tf_op jit(solution)/shard_map/all_to_all | solution.py:21
  126.7 2.3 %copy-start = (bf16[32,96,768]{2,1,0:T(8,128)(2,1)S(1)}, bf16[32,96,768]{2,1,0:T(8,128)(2,1)}, u32[]{:S(2)}) copy-start(bf16[32,96,768]{2,1,0:T(8,128)(2,1)} %all-gather.3.cloned.1.call-done) | copy-start | bytes 14155780
  137.0 32.6 %all-to-all-start.5 = ((f32[8,96,768]{2,1,0:T(8,128)}), f32[8,96,768]{2,1,0:T(8,128)S(1)}, u32[]{:S(2)}, u32[]{:S(2)}) async-start(f32[8,96,768]{2,1,0:T(8,128)} %shard_map.103), calls=%async_computation.5 | async-start | bytes 4718592 | tf_op jit(solution)/shard_map/all_to_all | solution.py:115
  140.7 2.8 %copy-start.3 = (bf16[2,1024,768]{2,1,0:T(8,128)(2,1)S(1)}, bf16[2,1024,768]{2,1,0:T(8,128)(2,1)}, u32[]{:S(2)}) copy-start(bf16[2,1024,768]{2,1,0:T(8,128)(2,1)} %copy-done.2) | copy-start | bytes 9437188
Sparse Core Ops, SparseCore 0:
  36.4 73.2 all-gather.2

commit v7 on v6

--- a/solution.py
+++ b/solution.py
@@ -21,8 +21,8 @@
     return lax.all_to_all(jnp.broadcast_to(block[None], (size,) + block.shape), axis, 0, 0, tiled=True)
 
 
-def precondition_kernel(place, own, other, grad, in_eigs, out_eigs, terms, basis, sems):
-    core = place[0]
+def precondition_kernel(place, own, other, grad, in_eigs, out_eigs, terms, kept, basis, sems):
+    core, member = place[0], place[1]
     rows, width = in_eigs.shape[1], basis.shape[-1]
     steps = basis.shape[0] * 2
     copies = []
@@ -51,27 +51,36 @@
     denominator = out_eigs[...] * in_eigs[...] + DAMPING
     scaled = (projected / denominator).astype(jnp.bfloat16)
     for k in range(steps):
-        terms[k] = lax.dot_general(
+        share = lax.dot_general(
             scaled, block(k), (((1,), (1,)), ((), ())), preferred_element_type=jnp.float32
         )
 
+        @pl.when(member == k)
+        def _():
+            kept[...] = share
+
+        terms[k] = jnp.where(member == k, 0.0, share).astype(terms.dtype)
+
 
 def precondition(own, other, grad, in_eigs, out_eigs):
-    place = lax.axis_index("core").astype(jnp.int32)[None]
+    place = jnp.stack([lax.axis_index("core"), lax.axis_index(GROUP)]).astype(jnp.int32)
     rows = grad.shape[0]
     width = in_eigs.shape[0]
     anywhere = pl.BlockSpec(memory_space=pl.ANY)
     vmem = pl.BlockSpec(memory_space=pltpu.VMEM)
     return pl.pallas_call(
         precondition_kernel,
-        out_shape=jax.ShapeDtypeStruct((8, rows, width), jnp.float32),
+        out_shape=(
+            jax.ShapeDtypeStruct((8, rows, width), jnp.bfloat16),
+            jax.ShapeDtypeStruct((rows, width), jnp.float32),
+        ),
         in_specs=[pl.BlockSpec(memory_space=pltpu.SMEM), anywhere, anywhere, vmem, vmem, vmem],
-        out_specs=vmem,
+        out_specs=(vmem, vmem),
         scratch_shapes=[
             pltpu.VMEM((4, 8, 2, rows, width), jnp.bfloat16),
             pltpu.SemaphoreType.DMA((16,)),
         ],
-        compiler_params=pltpu.CompilerParams(vmem_limit_bytes=36 << 20),
+        compiler_params=pltpu.CompilerParams(vmem_limit_bytes=58 << 20),
         cost_estimate=pl.CostEstimate(
             flops=4 * rows * 8 * width * width, bytes_accessed=24 * width * width, transcendentals=0
         ),
@@ -111,9 +120,9 @@
     )
 
     other = shift(own, "core", 1)
-    terms = precondition(own, other, rotated_grad, input_eigs, output_eigs)
+    terms, own_term = precondition(own, other, rotated_grad, input_eigs, output_eigs)
     terms = lax.all_to_all(terms, GROUP, 0, 0, tiled=True)
-    preconditioned = jnp.sum(terms, axis=0)
+    preconditioned = own_term + jnp.sum(terms.astype(jnp.float32), axis=0)
     return (cov_in, cov_out, preconditioned)
 
 

time: 178 us -> 166 us (0.933)
  waiting for transfers between devices: 46.6 us -> 32.1 us
  Pallas kernels: 7.99 us -> 11.2 us
    all_to_all x1, waiting for transfers between devices: 25.1 us -> 12.4 us  [shards(): terms = lax.all_to_all(terms, GROUP, 0, 0, tiled=True)]
    pallas_call x1, Pallas kernels: 7.99 us -> 11.2 us  [precondition(): pl.pallas_call(precondition_kernel, out_shape=(jax.ShapeDtypeStruct((8, r...]
    unnamed x13 -> x11, local copies, waits for them, and re-layouts: 4.03 us -> 1.7 us
    ppermute x2, waiting for transfers between devices: 5.92 us -> 4.11 us  [shift(): lax.ppermute(value, axis, [((i + by) % size, i) for i in range(size)])]
  transfers between devices with their start and end apart: 8 -> 8, of which waited for: 5 -> 5; matrix products, arithmetic and copies ran while one was open for 5% -> 7% of each run, Pallas kernels for 5% -> 7%
where the time goes in v7:
time: 166 us
  blocking collectives  51.2 us (31%)
  starting transfers between devices  39.1 us (24%)
  waiting for transfers between devices  32.1 us (19%)
  between operations  15.5 us (9%)
  Pallas kernels  11.2 us (7%)
  local copies, waits for them, and re-layouts  7.54 us (5%)
  other arithmetic  5.1 us (3%)
  matrix products  3.77 us (2%)
    all_to_all x1, blocking collectives, spread(): lax.all_to_all(jnp.broadcast_to(block[None], (size,) + block.shape), axis...  25.7 us
    all_gather x1, blocking collectives, shards(): lax.all_gather(kept_in.reshape(-1, width), 'z', axis=0, tiled=True)  25.5 us
    all_to_all x3, starting transfers between devices, spread(): lax.all_to_all(jnp.broadcast_to(block[None], (size,) + block.shape), axis...  17.8 us
    ppermute x2, starting transfers between devices, shift(): lax.ppermute(value, axis, [((i + by) % size, i) for i in range(size)])  12.7 us
    all_to_all x1, waiting for transfers between devices, shards(): terms = lax.all_to_all(terms, GROUP, 0, 0, tiled=True)  12.4 us
    pallas_call x1, Pallas kernels, precondition(): pl.pallas_call(precondition_kernel, out_shape=(jax.ShapeDtypeStruct((8, r...  11.2 us
    all_to_all x3, waiting for transfers between devices, spread(): lax.all_to_all(jnp.broadcast_to(block[None], (size,) + block.shape), axis...  8.73 us
    all_to_all x1, waiting for transfers between devices, shards(): pieces = lax.all_to_all(pieces, GROUP, 0, 0, tiled=True)  6.87 us
  transfers between devices with their start and end apart: 8, of which 5 were waited for; matrix products, arithmetic and copies ran while one was open for 7% of the time, Pallas kernels for 7%

profile of v7, /device:TPU:1, one launch (start us, length us, event | category | flops | bytes accessed | tf_op | source)
XLA Modules:
  0.0 165.6 jit_solution(11172909277395001564)
XLA Ops:
  7.2 0.0 all-gather.3.cloned.1.call-start
  7.9 0.8 broadcast_select_fusion
  8.7 0.9 pad_maximum_fusion.2
  9.7 25.7 %all_to_all.30 = bf16[4,112,768]{2,1,0:T(8,128)(2,1)S(1)} all-to-all(bf16[4,112,768]{2,1,0:T(8,128)(2,1)S(1)} %broadcast_in_dim.43), channel_id=1, replica_groups=mesh['yh'=4,'z'=8,'core'=2,'yl'=2,'x'=4] {'yh'}, dimensions={0} | all-to-all | bytes 1376256 | tf_op jit(solution)/shard_map/all_to_all | solution.py:21
  35.4 0.9 slice.22
  36.3 0.0 all-gather.3.cloned.1.call-update
  36.3 0.7 broadcast_in_dim.44
  37.0 10.3 %all-to-all-start.1 = ((bf16[8,16,768]{2,1,0:T(8,128)(2,1)}), bf16[8,16,768]{2,1,0:T(8,128)(2,1)S(1)}, u32[]{:S(2)}, u32[]{:S(2)}) async-start(bf16[8,16,768]{2,1,0:T(8,128)(2,1)} %broadcast_in_dim.44), calls=%async_computation.1 | async-start | bytes 393216 | tf_op jit(solution)/shard_map/all_to_all | solution.py:21
  47.3 8.7 %all-to-all-done.1 = bf16[8,16,768]{2,1,0:T(8,128)(2,1)S(1)} async-done(((bf16[8,16,768]{2,1,0:T(8,128)(2,1)}), bf16[8,16,768]{2,1,0:T(8,128)(2,1)S(1)}, u32[]{:S(2)}, u32[]{:S(2)}) %all-to-all-start.1) | async-done | bytes 196640 | tf_op jit(solution)/shard_map/all_to_all | solution.py:21
  56.0 0.9 broadcast_in_dim.46
  57.0 4.0 %all-to-all-start.2 = ((bf16[4,128,768]{2,1,0:T(8,128)(2,1)}), bf16[4,128,768]{2,1,0:T(8,128)(2,1)S(1)}, u32[]{:S(2)}, u32[]{:S(2)}) async-start(bf16[4,128,768]{2,1,0:T(8,128)(2,1)} %broadcast_in_dim.46), calls=%async_computation.2 | async-start | bytes 1572864 | tf_op jit(solution)/shard_map/all_to_all | solution.py:21
  61.0 25.5 %all_gather.9 = bf16[512,768]{1,0:T(8,128)(2,1)S(1)} all-gather(bf16[64,768]{1,0:T(8,128)(2,1)S(1)} %bitcast.44), channel_id=1, replica_groups=mesh['yh'=4,'z'=8,'core'=2,'yl'=2,'x'=4] {'z'}, dimensions={0}, use_global_device_ids=true | all-gather | bytes 884736 | tf_op jit(solution)/shard_map/all_gather | solution.py:103
  86.5 0.0 all-to-all-done.2
  86.5 0.1 pad_maximum_fusion.1
  86.6 8.4 %collective-permute-start = (bf16[2,512,768]{2,1,0:T(8,128)(2,1)S(1)}, bf16[2,512,768]{2,1,0:T(8,128)(2,1)}, u32[]{:S(2)}, u32[]{:S(2)}) collective-permute-start(bf16[2,512,768]{2,1,0:T(8,128)(2,1)S(1)} %pad_maximum_fusion.1), channel_id=1, source_target_pairs={{8,0},{0,8},{9,1},{1,9},{10,2},{2,10},{11,3},{3,11},{12,4},{4,12},... | collective-permute-start | bytes 4718600 | tf_op jit(solution)/shard_map/ppermute | solution.py:16
  95.7 2.5 %collective-permute-done = bf16[2,512,768]{2,1,0:T(8,128)(2,1)} collective-permute-done((bf16[2,512,768]{2,1,0:T(8,128)(2,1)S(1)}, bf16[2,512,768]{2,1,0:T(8,128)(2,1)}, u32[]{:S(2)}, u32[]{:S(2)}) %collective-permute-start) | collective-permute-done | bytes 1572896 | tf_op jit(solution)/shard_map/ppermute | solution.py:16
  98.2 1.6 pad_maximum_fusion
  99.8 0.0 copy-start
  99.8 1.6 copy-done
  101.4 0.0 copy-start.3
  101.4 0.0 copy-start.4
  101.4 0.2 constant_dynamic-slice_fusion
  101.7 1.0 copy.20
  102.6 5.0 %all-to-all-start.3 = ((bf16[8,256,96]{1,2,0:T(8,128)(2,1)}), bf16[8,256,96]{1,2,0:T(8,128)(2,1)S(1)}, u32[]{:S(2)}, u32[]{:S(2)}) async-start(bf16[8,256,96]{1,2,0:T(8,128)(2,1)} %copy.20), calls=%async_computation.3 | async-start | bytes 786432 | tf_op jit(solution)/shard_map/all_to_all | solution.py:111
  107.6 6.9 %all-to-all-done.3 = bf16[8,256,96]{1,2,0:T(8,128)(2,1)S(1)} async-done(((bf16[8,256,96]{1,2,0:T(8,128)(2,1)}), bf16[8,256,96]{1,2,0:T(8,128)(2,1)S(1)}, u32[]{:S(2)}, u32[]{:S(2)}) %all-to-all-start.3) | async-done | bytes 393248 | tf_op jit(solution)/shard_map/all_to_all | solution.py:111
  114.5 0.0 all-gather.3.cloned.1.call-done
  114.5 4.3 %collective-permute-start.1 = (bf16[8,4,96,768]{3,2,1,0:T(8,128)(2,1)}, bf16[8,4,96,768]{3,2,1,0:T(8,128)(2,1)}, u32[]{:S(2)}, u32[]{:S(2)}) collective-permute-start(bf16[8,4,96,768]{3,2,1,0:T(8,128)(2,1)} %bitcast.40), channel_id=1, source_target_pairs={{8,0},{0,8},{9,1},{1,9},{10,2},{2,10},{11,3},{3,11},{12,4},{4,12},... | collective-permute-start | bytes 14155784 | tf_op jit(solution)/shard_map/ppermute | solution.py:16
  118.8 0.8 broadcast_in_dim.47
  119.6 3.5 %all-to-all-start.4 = ((bf16[8,256,96]{1,2,0:T(8,128)(2,1)}), bf16[8,256,96]{1,2,0:T(8,128)(2,1)S(1)}, u32[]{:S(2)}, u32[]{:S(2)}) async-start(bf16[8,256,96]{1,2,0:T(8,128)(2,1)} %broadcast_in_dim.47), calls=%async_computation.4 | async-start | bytes 786432 | tf_op jit(solution)/shard_map/all_to_all | solution.py:21
  123.1 0.0 copy-done.3
  123.1 0.6 broadcast_in_dim.48.in_eigs
  123.6 0.0 copy-done.4
  123.6 0.7 copy.23.out_eigs
  124.4 0.7 pad_add_fusion.place
  125.0 1.6 collective-permute-done.1.other
  126.7 11.2 %shard_map.103 = (bf16[8,96,768]{2,1,0:T(8,128)(2,1)}, f32[96,768]{1,0:T(8,128)}) custom-call(s32[2]{0:T(128)} %pad_add_fusion.place, bf16[8,4,96,768]{3,2,1,0:T(8,128)(2,1)} %bitcast.41, bf16[8,4,96,768]{3,2,1,0:T(8,128)(2,1)} %collective-permute-done.1.other, bf16[96,6144]{1,0:T(8,128)(2,1)} %grad.1, f32[1,768]{1,0:T(1,128)} %broadcast_in_dim.48.in_eigs, ...), custom_call_target="tpu_custom_call" | custom-call | flops 1811939328 | bytes 14155776 | tf_op jit(solution)/shard_map/pallas_call | solution.py:71
  137.9 0.0 all-to-all-done.4
  137.9 3.6 %all-to-all-start.5 = ((bf16[8,96,768]{2,1,0:T(8,128)(2,1)}), bf16[8,96,768]{2,1,0:T(8,128)(2,1)S(1)}, u32[]{:S(2)}, u32[]{:S(2)}) async-start(bf16[8,96,768]{2,1,0:T(8,128)(2,1)} %get-tuple-element.18), calls=%async_computation.5 | async-start | bytes 2359296 | tf_op jit(solution)/shard_map/all_to_all | solution.py:124
  141.5 0.0 copy-start.1
  141.6 0.0 copy-start.2
  141.6 2.7 %fusion.3 = f32[768,96]{0,1:T(8,128)} fusion(bf16[1024,96]{0,1:T(8,128)(2,1)S(1)} %bitcast.45, bf16[2,1024,768]{2,1,0:T(8,128)(2,1)} %copy-done), kind=kOutput, calls=%fused_computation.8 | convolution fusion | flops 151068672 | bytes 2064384 | tf_op jit(solution)/shard_map/dot_general | solution.py:117
  144.3 0.0 copy-done.1
  144.3 1.1 fusion.2
  145.4 12.4 %all-to-all-done.5 = bf16[8,96,768]{2,1,0:T(8,128)(2,1)S(1)} async-done(((bf16[8,96,768]{2,1,0:T(8,128)(2,1)}), bf16[8,96,768]{2,1,0:T(8,128)(2,1)S(1)}, u32[]{:S(2)}, u32[]{:S(2)}) %all-to-all-start.5) | async-done | bytes 1179680 | tf_op jit(solution)/shard_map/all_to_all | solution.py:124
  157.8 0.2 convert_reduce_fusion
  158.0 0.0 copy-done.2
  158.0 0.7 add.22
  (7 shorter events, 0.1 us)
Async XLA Ops:
  7.2 107.3 %all-gather.3.cloned.1.call-start = ((), (), s32[]{:S(2)}) async-start(), calls=%async_computation.6 | async-start | bytes 5308416 | tf_op jit(solution)/shard_map/all_gather | solution.py:100
  37.0 19.0 %all-to-all-start.1 = ((bf16[8,16,768]{2,1,0:T(8,128)(2,1)}), bf16[8,16,768]{2,1,0:T(8,128)(2,1)S(1)}, u32[]{:S(2)}, u32[]{:S(2)}) async-start(bf16[8,16,768]{2,1,0:T(8,128)(2,1)} %broadcast_in_dim.44), calls=%async_computation.1 | async-start | bytes 393216 | tf_op jit(solution)/shard_map/all_to_all | solution.py:21
  57.0 29.5 %all-to-all-start.2 = ((bf16[4,128,768]{2,1,0:T(8,128)(2,1)}), bf16[4,128,768]{2,1,0:T(8,128)(2,1)S(1)}, u32[]{:S(2)}, u32[]{:S(2)}) async-start(bf16[4,128,768]{2,1,0:T(8,128)(2,1)} %broadcast_in_dim.46), calls=%async_computation.2 | async-start | bytes 1572864 | tf_op jit(solution)/shard_map/all_to_all | solution.py:21
  86.6 11.5 %collective-permute-start = (bf16[2,512,768]{2,1,0:T(8,128)(2,1)S(1)}, bf16[2,512,768]{2,1,0:T(8,128)(2,1)}, u32[]{:S(2)}, u32[]{:S(2)}) collective-permute-start(bf16[2,512,768]{2,1,0:T(8,128)(2,1)S(1)} %pad_maximum_fusion.1), channel_id=1, source_target_pairs={{8,0},{0,8},{9,1},{1,9},{10,2},{2,10},{11,3},{3,11},{12,4},{4,12},... | collective-permute-start | bytes 4718600 | tf_op jit(solution)/shard_map/ppermute | solution.py:16
  99.8 1.7 %copy-start = (bf16[2,1024,768]{2,1,0:T(8,128)(2,1)}, bf16[2,1024,768]{2,1,0:T(8,128)(2,1)S(1)}, u32[]{:S(2)}) copy-start(bf16[2,1024,768]{2,1,0:T(8,128)(2,1)S(1)} %pad_maximum_fusion) | copy-start | bytes 9437188
  101.4 21.6 %copy-start.3 = (f32[768]{0:T(1024)S(1)}, f32[768]{0:T(1024)}, u32[]{:S(2)}) copy-start(f32[768]{0:T(1024)} %param.14) | copy-start | bytes 9220
  101.4 22.2 %copy-start.4 = (f32[96]{0:T(128)S(1)}, f32[96]{0:T(128)}, u32[]{:S(2)}) copy-start(f32[96]{0:T(128)} %param.15) | copy-start | bytes 1156
  102.6 11.9 %all-to-all-start.3 = ((bf16[8,256,96]{1,2,0:T(8,128)(2,1)}), bf16[8,256,96]{1,2,0:T(8,128)(2,1)S(1)}, u32[]{:S(2)}, u32[]{:S(2)}) async-start(bf16[8,256,96]{1,2,0:T(8,128)(2,1)} %copy.20), calls=%async_computation.3 | async-start | bytes 786432 | tf_op jit(solution)/shard_map/all_to_all | solution.py:111
  114.5 12.2 %collective-permute-start.1 = (bf16[8,4,96,768]{3,2,1,0:T(8,128)(2,1)}, bf16[8,4,96,768]{3,2,1,0:T(8,128)(2,1)}, u32[]{:S(2)}, u32[]{:S(2)}) collective-permute-start(bf16[8,4,96,768]{3,2,1,0:T(8,128)(2,1)} %bitcast.40), channel_id=1, source_target_pairs={{8,0},{0,8},{9,1},{1,9},{10,2},{2,10},{11,3},{3,11},{12,4},{4,12},... | collective-permute-start | bytes 14155784 | tf_op jit(solution)/shard_map/ppermute | solution.py:16
  119.6 18.3 %all-to-all-start.4 = ((bf16[8,256,96]{1,2,0:T(8,128)(2,1)}), bf16[8,256,96]{1,2,0:T(8,128)(2,1)S(1)}, u32[]{:S(2)}, u32[]{:S(2)}) async-start(bf16[8,256,96]{1,2,0:T(8,128)(2,1)} %broadcast_in_dim.47), calls=%async_computation.4 | async-start | bytes 786432 | tf_op jit(solution)/shard_map/all_to_all | solution.py:21
  137.9 19.9 %all-to-all-start.5 = ((bf16[8,96,768]{2,1,0:T(8,128)(2,1)}), bf16[8,96,768]{2,1,0:T(8,128)(2,1)S(1)}, u32[]{:S(2)}, u32[]{:S(2)}) async-start(bf16[8,96,768]{2,1,0:T(8,128)(2,1)} %get-tuple-element.18), calls=%async_computation.5 | async-start | bytes 2359296 | tf_op jit(solution)/shard_map/all_to_all | solution.py:124
  141.5 2.8 %copy-start.1 = (bf16[2,1024,768]{2,1,0:T(8,128)(2,1)S(1)}, bf16[2,1024,768]{2,1,0:T(8,128)(2,1)}, u32[]{:S(2)}) copy-start(bf16[2,1024,768]{2,1,0:T(8,128)(2,1)} %copy-done) | copy-start | bytes 9437188
  141.6 16.4 %copy-start.2 = (f32[96,768]{1,0:T(8,128)S(1)}, f32[96,768]{1,0:T(8,128)}, u32[]{:S(2)}) copy-start(f32[96,768]{1,0:T(8,128)} %get-tuple-element.17) | copy-start | bytes 884740
Sparse Core Ops, SparseCore 0:
  36.4 73.2 all-gather.2

commit v8 on v7

--- a/solution.py
+++ b/solution.py
@@ -101,22 +101,26 @@
     kept_in, kept_out = lax.optimization_barrier((column[:, owned_width:], spread(kept_out, "z")))
     kept_out = spread(kept_out.reshape(-1, width), "yh").reshape(-1, width)
     kept_in = lax.all_gather(kept_in.reshape(-1, width), "z", axis=0, tiled=True)
-    kept = jnp.stack([kept_in, kept_out])
-    both = jnp.concatenate([kept, shift(kept, "core", 1)], axis=1)
-    samples = both.shape[1]
+    theirs = shift(jnp.stack([kept_in, kept_out]), "core", 1)
+    samples = [(kept_in, theirs[0]), (kept_out, theirs[1])]
     owner_idx = owners[0]
     offset = owner_idx % blocks_per * owned_width
-    owned = lax.dynamic_slice_in_dim(both, offset, owned_width, 2)
-    pieces = owned.reshape(group_count, 2 * samples // group_count, owned_width)
-    pieces = lax.all_to_all(pieces, GROUP, 0, 0, tiled=True)
-    piece = lax.dynamic_index_in_dim(pieces, owner_idx // blocks_per, 0, keepdims=False)
+    owned = jnp.concatenate(
+        [lax.dynamic_slice_in_dim(v, offset, owned_width, 1) for pair in samples for v in pair]
+    )
+    pieces = owned.reshape(group_count, -1, owned_width)
+    arrived = lax.all_to_all(pieces, GROUP, 0, 0, tiled=True)
+    piece = lax.dynamic_index_in_dim(arrived, owner_idx // blocks_per, 0, keepdims=False)
     own, piece = lax.optimization_barrier((own, piece))
-    owned = spread(piece, GROUP).reshape(2, samples, owned_width)
+    owned = spread(piece, GROUP).reshape(2, 2, -1, owned_width)
     contract_rows = (((0,), (0,)), ((), ()))
     cov_in, cov_out = (
-        lax.dot_general(both[k], owned[k], contract_rows, preferred_element_type=jnp.float32)
+        sum(
+            lax.dot_general(v, part, contract_rows, preferred_element_type=jnp.float32)
+            for v, part in zip(pair, parts)
+        )
         / jnp.float32(SAMPLED)
-        for k in range(2)
+        for pair, parts in zip(samples, owned)
     )
 
     other = shift(own, "core", 1)

time: 166 us -> 170 us (1.024)
  other arithmetic: 5.1 us -> 6.87 us
    dot_general x2 -> x4, matrix products: 3.77 us -> 2.48 us  [shards(): lax.dot_general(v, part, contract_rows, preferred_element_type=jnp.float32)]
    broadcast_in_dim x4 -> x5, local copies, waits for them, and re-layouts: 2.46 us -> 3.48 us  [spread(): jnp.broadcast_to(block[None], (size,) + block.shape)]
  transfers between devices with their start and end apart: 8 -> 8, of which waited for: 5 -> 5; matrix products, arithmetic and copies ran while one was open for 7% -> 8% of each run, Pallas kernels for 7% -> 7%
where the time goes in v8:
time: 170 us; the launch traced here: 169 us
  blocking collectives  51.2 us (30%)
  starting transfers between devices  39.9 us (23%)
  waiting for transfers between devices  32.6 us (19%)
  between operations  15.5 us (9%)
  Pallas kernels  11.2 us (7%)
  local copies, waits for them, and re-layouts  9.17 us (5%)
  other arithmetic  6.87 us (4%)
  matrix products  2.48 us (1%)
    all_to_all x1, blocking collectives, spread(): lax.all_to_all(jnp.broadcast_to(block[None], (size,) + block.shape), axis...  25.7 us
    all_gather x1, blocking collectives, shards(): lax.all_gather(kept_in.reshape(-1, width), 'z', axis=0, tiled=True)  25.5 us
    all_to_all x3, starting transfers between devices, spread(): lax.all_to_all(jnp.broadcast_to(block[None], (size,) + block.shape), axis...  17.8 us
    all_to_all x1, waiting for transfers between devices, shards(): terms = lax.all_to_all(terms, GROUP, 0, 0, tiled=True)  13.9 us
    ppermute x2, starting transfers between devices, shift(): lax.ppermute(value, axis, [((i + by) % size, i) for i in range(size)])  12.7 us
    pallas_call x1, Pallas kernels, precondition(): pl.pallas_call(precondition_kernel, out_shape=(jax.ShapeDtypeStruct((8, r...  11.2 us
    all_to_all x3, waiting for transfers between devices, spread(): lax.all_to_all(jnp.broadcast_to(block[None], (size,) + block.shape), axis...  8.73 us
    all_to_all x1, waiting for transfers between devices, shards(): arrived = lax.all_to_all(pieces, GROUP, 0, 0, tiled=True)  6.88 us
  transfers between devices with their start and end apart: 8, of which 5 were waited for; matrix products, arithmetic and copies ran while one was open for 8% of the time, Pallas kernels for 7%

profile of v8, /device:TPU:1, one launch (start us, length us, event | category | flops | bytes accessed | tf_op | source)
XLA Modules:
  0.0 168.9 jit_solution(11170904983435987965)
XLA Ops:
  7.2 0.0 all-gather.3.cloned.1.call-start
  7.9 0.8 broadcast_select_fusion
  8.7 0.9 pad_maximum_fusion.2
  9.7 25.7 %all_to_all.30 = bf16[4,112,768]{2,1,0:T(8,128)(2,1)S(1)} all-to-all(bf16[4,112,768]{2,1,0:T(8,128)(2,1)S(1)} %broadcast_in_dim.43), channel_id=1, replica_groups=mesh['yh'=4,'z'=8,'core'=2,'yl'=2,'x'=4] {'yh'}, dimensions={0} | all-to-all | bytes 1376256 | tf_op jit(solution)/shard_map/all_to_all | solution.py:21
  35.4 0.9 slice.23
  36.3 0.0 all-gather.3.cloned.1.call-update
  36.3 0.7 broadcast_in_dim.44
  37.0 10.3 %all-to-all-start.1 = ((bf16[8,16,768]{2,1,0:T(8,128)(2,1)}), bf16[8,16,768]{2,1,0:T(8,128)(2,1)S(1)}, u32[]{:S(2)}, u32[]{:S(2)}) async-start(bf16[8,16,768]{2,1,0:T(8,128)(2,1)} %broadcast_in_dim.44), calls=%async_computation.1 | async-start | bytes 393216 | tf_op jit(solution)/shard_map/all_to_all | solution.py:21
  47.3 8.7 %all-to-all-done.1 = bf16[8,16,768]{2,1,0:T(8,128)(2,1)S(1)} async-done(((bf16[8,16,768]{2,1,0:T(8,128)(2,1)}), bf16[8,16,768]{2,1,0:T(8,128)(2,1)S(1)}, u32[]{:S(2)}, u32[]{:S(2)}) %all-to-all-start.1) | async-done | bytes 196640 | tf_op jit(solution)/shard_map/all_to_all | solution.py:21
  56.0 0.2 copy.29
  56.2 1.0 broadcast_in_dim.46
  57.2 4.0 %all-to-all-start.2 = ((bf16[4,128,768]{1,2,0:T(8,128)(2,1)}), bf16[4,128,768]{1,2,0:T(8,128)(2,1)S(1)}, u32[]{:S(2)}, u32[]{:S(2)}) async-start(bf16[4,128,768]{1,2,0:T(8,128)(2,1)} %broadcast_in_dim.46), calls=%async_computation.2 | async-start | bytes 1572864 | tf_op jit(solution)/shard_map/all_to_all | solution.py:21
  61.2 25.5 %all_gather.9 = bf16[512,768]{1,0:T(8,128)(2,1)S(1)} all-gather(bf16[64,768]{1,0:T(8,128)(2,1)S(1)} %bitcast.55), channel_id=1, replica_groups=mesh['yh'=4,'z'=8,'core'=2,'yl'=2,'x'=4] {'z'}, dimensions={0}, use_global_device_ids=true | all-gather | bytes 884736 | tf_op jit(solution)/shard_map/all_gather | solution.py:103
  86.7 0.0 all-to-all-done.2
  86.7 0.3 copy.30
  86.9 1.3 pad_maximum_fusion
  88.3 8.4 %collective-permute-start = (bf16[2,512,768]{2,1,0:T(8,128)(2,1)}, bf16[2,512,768]{2,1,0:T(8,128)(2,1)S(1)}, u32[]{:S(2)}, u32[]{:S(2)}) collective-permute-start(bf16[2,512,768]{2,1,0:T(8,128)(2,1)} %pad_maximum_fusion), channel_id=1, source_target_pairs={{8,0},{0,8},{9,1},{1,9},{10,2},{2,10},{11,3},{3,11},{12,4},{4,12},... | collective-permute-start | bytes 4718600 | tf_op jit(solution)/shard_map/ppermute | solution.py:16
  97.4 0.1 constant_dynamic-slice_fusion.1
  97.5 0.1 constant_dynamic-slice_fusion
  97.6 2.3 %collective-permute-done = bf16[2,512,768]{2,1,0:T(8,128)(2,1)S(1)} collective-permute-done((bf16[2,512,768]{2,1,0:T(8,128)(2,1)}, bf16[2,512,768]{2,1,0:T(8,128)(2,1)S(1)}, u32[]{:S(2)}, u32[]{:S(2)}) %collective-permute-start) | collective-permute-done | bytes 1572896 | tf_op jit(solution)/shard_map/ppermute | solution.py:16
  99.9 0.1 fusion.6
  100.0 0.1 dynamic-slice_bitcast_fusion
  100.2 0.9 pad_maximum_fusion.1
  101.1 0.0 copy-start.1
  101.1 2.0 %copy.33 = bf16[8,256,96]{1,2,0:T(8,128)(2,1)} copy(bf16[8,256,96]{2,1,0:T(8,128)(2,1)} %bitcast.53) | data formatting | bytes 786432 | tf_op jit(solution)/shard_map/reshape | solution.py:111
  103.1 5.1 %all-to-all-start.3 = ((bf16[8,256,96]{1,2,0:T(8,128)(2,1)}), bf16[8,256,96]{1,2,0:T(8,128)(2,1)S(1)}, u32[]{:S(2)}, u32[]{:S(2)}) async-start(bf16[8,256,96]{1,2,0:T(8,128)(2,1)} %copy.33), calls=%async_computation.3 | async-start | bytes 786432 | tf_op jit(solution)/shard_map/all_to_all | solution.py:112
  108.2 6.9 %all-to-all-done.3 = bf16[8,256,96]{1,2,0:T(8,128)(2,1)S(1)} async-done(((bf16[8,256,96]{1,2,0:T(8,128)(2,1)}), bf16[8,256,96]{1,2,0:T(8,128)(2,1)S(1)}, u32[]{:S(2)}, u32[]{:S(2)}) %all-to-all-start.3) | async-done | bytes 393248 | tf_op jit(solution)/shard_map/all_to_all | solution.py:112
  115.1 0.6 dynamic-slice_bitcast_fusion.2
  115.7 4.3 %collective-permute-start.1 = (bf16[8,4,96,768]{3,2,1,0:T(8,128)(2,1)}, bf16[8,4,96,768]{3,2,1,0:T(8,128)(2,1)}, u32[]{:S(2)}, u32[]{:S(2)}) collective-permute-start(bf16[8,4,96,768]{3,2,1,0:T(8,128)(2,1)} %bitcast.51), channel_id=1, source_target_pairs={{8,0},{0,8},{9,1},{1,9},{10,2},{2,10},{11,3},{3,11},{12,4},{4,12},... | collective-permute-start | bytes 14155784 | tf_op jit(solution)/shard_map/ppermute | solution.py:16
  120.1 1.6 broadcast_in_dim.47
  121.6 3.5 %all-to-all-start.4 = ((bf16[8,256,96]{1,2,0:T(8,128)(2,1)}), bf16[8,256,96]{1,2,0:T(8,128)(2,1)S(1)}, u32[]{:S(2)}, u32[]{:S(2)}) async-start(bf16[8,256,96]{1,2,0:T(8,128)(2,1)} %broadcast_in_dim.47), calls=%async_computation.4 | async-start | bytes 786432 | tf_op jit(solution)/shard_map/all_to_all | solution.py:21
  125.1 0.0 copy-done.1
  125.1 0.6 broadcast_in_dim.48.in_eigs
  125.7 0.0 copy-done.2
  125.7 0.7 copy.38.out_eigs
  126.4 0.7 pad_add_fusion.place
  127.1 0.8 collective-permute-done.1.other
  127.9 11.2 %shard_map.103 = (bf16[8,96,768]{2,1,0:T(8,128)(2,1)}, f32[96,768]{1,0:T(8,128)}) custom-call(s32[2]{0:T(128)} %pad_add_fusion.place, bf16[8,4,96,768]{3,2,1,0:T(8,128)(2,1)} %bitcast.52, bf16[8,4,96,768]{3,2,1,0:T(8,128)(2,1)} %collective-permute-done.1.other, bf16[96,6144]{1,0:T(8,128)(2,1)} %grad.1, f32[1,768]{1,0:T(1,128)} %broadcast_in_dim.48.in_eigs, ...), custom_call_target="tpu_custom_call" | custom-call | flops 1811939328 | bytes 14155776 | tf_op jit(solution)/shard_map/pallas_call | solution.py:71
  139.2 0.0 all-to-all-done.4
  139.2 4.3 %all-to-all-start.5 = ((bf16[8,96,768]{2,1,0:T(8,128)(2,1)}), bf16[8,96,768]{2,1,0:T(8,128)(2,1)}, u32[]{:S(2)}, u32[]{:S(2)}) async-start(bf16[8,96,768]{2,1,0:T(8,128)(2,1)} %get-tuple-element.18), calls=%async_computation.5 | async-start | bytes 2359296 | tf_op jit(solution)/shard_map/all_to_all | solution.py:128
  143.5 0.3 fusion.8
  143.8 0.3 fusion.7
  144.1 1.0 fusion.1
  145.0 1.0 fusion
  146.0 13.9 %all-to-all-done.5 = bf16[8,96,768]{2,1,0:T(8,128)(2,1)} async-done(((bf16[8,96,768]{2,1,0:T(8,128)(2,1)}), bf16[8,96,768]{2,1,0:T(8,128)(2,1)}, u32[]{:S(2)}, u32[]{:S(2)}) %all-to-all-start.5) | async-done | bytes 1179680 | tf_op jit(solution)/shard_map/all_to_all | solution.py:128
  159.9 1.5 convert_reduce_fusion
  161.3 0.0 copy-done
  161.4 0.7 add.33
  (11 shorter events, 0.1 us)
Async XLA Ops:
  7.2 108.6 %all-gather.3.cloned.1.call-start = ((), (), s32[]{:S(2)}) async-start(), calls=%async_computation.6 | async-start | bytes 5308416 | tf_op jit(solution)/shard_map/all_gather | solution.py:100
  37.0 19.0 %all-to-all-start.1 = ((bf16[8,16,768]{2,1,0:T(8,128)(2,1)}), bf16[8,16,768]{2,1,0:T(8,128)(2,1)S(1)}, u32[]{:S(2)}, u32[]{:S(2)}) async-start(bf16[8,16,768]{2,1,0:T(8,128)(2,1)} %broadcast_in_dim.44), calls=%async_computation.1 | async-start | bytes 393216 | tf_op jit(solution)/shard_map/all_to_all | solution.py:21
  57.2 29.5 %all-to-all-start.2 = ((bf16[4,128,768]{1,2,0:T(8,128)(2,1)}), bf16[4,128,768]{1,2,0:T(8,128)(2,1)S(1)}, u32[]{:S(2)}, u32[]{:S(2)}) async-start(bf16[4,128,768]{1,2,0:T(8,128)(2,1)} %broadcast_in_dim.46), calls=%async_computation.2 | async-start | bytes 1572864 | tf_op jit(solution)/shard_map/all_to_all | solution.py:21
  88.3 11.6 %collective-permute-start = (bf16[2,512,768]{2,1,0:T(8,128)(2,1)}, bf16[2,512,768]{2,1,0:T(8,128)(2,1)S(1)}, u32[]{:S(2)}, u32[]{:S(2)}) collective-permute-start(bf16[2,512,768]{2,1,0:T(8,128)(2,1)} %pad_maximum_fusion), channel_id=1, source_target_pairs={{8,0},{0,8},{9,1},{1,9},{10,2},{2,10},{11,3},{3,11},{12,4},{4,12},... | collective-permute-start | bytes 4718600 | tf_op jit(solution)/shard_map/ppermute | solution.py:16
  101.1 24.0 %copy-start.1 = (f32[768]{0:T(1024)S(1)}, f32[768]{0:T(1024)}, u32[]{:S(2)}) copy-start(f32[768]{0:T(1024)} %param.14) | copy-start | bytes 9220
  101.1 24.6 %copy-start.2 = (f32[96]{0:T(128)S(1)}, f32[96]{0:T(128)}, u32[]{:S(2)}) copy-start(f32[96]{0:T(128)} %param.15) | copy-start | bytes 1156
  103.1 12.0 %all-to-all-start.3 = ((bf16[8,256,96]{1,2,0:T(8,128)(2,1)}), bf16[8,256,96]{1,2,0:T(8,128)(2,1)S(1)}, u32[]{:S(2)}, u32[]{:S(2)}) async-start(bf16[8,256,96]{1,2,0:T(8,128)(2,1)} %copy.33), calls=%async_computation.3 | async-start | bytes 786432 | tf_op jit(solution)/shard_map/all_to_all | solution.py:112
  115.7 12.2 %collective-permute-start.1 = (bf16[8,4,96,768]{3,2,1,0:T(8,128)(2,1)}, bf16[8,4,96,768]{3,2,1,0:T(8,128)(2,1)}, u32[]{:S(2)}, u32[]{:S(2)}) collective-permute-start(bf16[8,4,96,768]{3,2,1,0:T(8,128)(2,1)} %bitcast.51), channel_id=1, source_target_pairs={{8,0},{0,8},{9,1},{1,9},{10,2},{2,10},{11,3},{3,11},{12,4},{4,12},... | collective-permute-start | bytes 14155784 | tf_op jit(solution)/shard_map/ppermute | solution.py:16
  121.6 17.5 %all-to-all-start.4 = ((bf16[8,256,96]{1,2,0:T(8,128)(2,1)}), bf16[8,256,96]{1,2,0:T(8,128)(2,1)S(1)}, u32[]{:S(2)}, u32[]{:S(2)}) async-start(bf16[8,256,96]{1,2,0:T(8,128)(2,1)} %broadcast_in_dim.47), calls=%async_computation.4 | async-start | bytes 786432 | tf_op jit(solution)/shard_map/all_to_all | solution.py:21
  139.2 20.7 %all-to-all-start.5 = ((bf16[8,96,768]{2,1,0:T(8,128)(2,1)}), bf16[8,96,768]{2,1,0:T(8,128)(2,1)}, u32[]{:S(2)}, u32[]{:S(2)}) async-start(bf16[8,96,768]{2,1,0:T(8,128)(2,1)} %get-tuple-element.18), calls=%async_computation.5 | async-start | bytes 2359296 | tf_op jit(solution)/shard_map/all_to_all | solution.py:128
  145.0 16.3 %copy-start = (f32[96,768]{1,0:T(8,128)S(1)}, f32[96,768]{1,0:T(8,128)}, u32[]{:S(2)}) copy-start(f32[96,768]{1,0:T(8,128)} %get-tuple-element.17) | copy-start | bytes 884740
Sparse Core Ops, SparseCore 0:
  36.4 73.2 all-gather.2

commit v9 on v8

--- a/solution.py
+++ b/solution.py
@@ -94,33 +94,39 @@
     group_count = lax.axis_size("yl") * lax.axis_size("x")
     is_live = lax.broadcasted_iota(jnp.int32, (slots, 1), 0) < counts[0]
     kept_in, kept_out = (jnp.where(is_live, v, jnp.zeros_like(v)) for v in (activations, out_grads))
-    column, kept_out = lax.optimization_barrier(
-        (spread(jnp.concatenate([basis, kept_in]), "yh"), kept_out)
+    column, kept_out, partner = lax.optimization_barrier(
+        (spread(jnp.concatenate([basis, kept_in]), "yh"), kept_out, shift(owners, "core", 1))
     )
+    owner_pair = owners[0], partner[0]
     own = lax.all_gather(column[:, :owned_width], "z", axis=0)
     kept_in, kept_out = lax.optimization_barrier((column[:, owned_width:], spread(kept_out, "z")))
     kept_out = spread(kept_out.reshape(-1, width), "yh").reshape(-1, width)
     kept_in = lax.all_gather(kept_in.reshape(-1, width), "z", axis=0, tiled=True)
-    theirs = shift(jnp.stack([kept_in, kept_out]), "core", 1)
-    samples = [(kept_in, theirs[0]), (kept_out, theirs[1])]
-    owner_idx = owners[0]
-    offset = owner_idx % blocks_per * owned_width
-    owned = jnp.concatenate(
-        [lax.dynamic_slice_in_dim(v, offset, owned_width, 1) for pair in samples for v in pair]
+    samples = jnp.stack([kept_in, kept_out])
+    pieces = []
+    for idx in owner_pair:
+        offset = idx % blocks_per * owned_width
+        columns = [lax.dynamic_slice_in_dim(v, offset, owned_width, 1) for v in (kept_in, kept_out)]
+        pieces.append(jnp.concatenate(columns).reshape(group_count, -1, owned_width))
+    arrived = lax.all_to_all(jnp.concatenate(pieces, axis=1), GROUP, 0, 0, tiled=True)
+    rows = pieces[0].shape[1]
+    piece, for_other = (
+        lax.dynamic_slice(arrived, (idx // blocks_per, k * rows, 0), (1, rows, owned_width))[0]
+        for k, idx in enumerate(owner_pair)
     )
-    pieces = owned.reshape(group_count, -1, owned_width)
-    arrived = lax.all_to_all(pieces, GROUP, 0, 0, tiled=True)
-    piece = lax.dynamic_index_in_dim(arrived, owner_idx // blocks_per, 0, keepdims=False)
-    own, piece = lax.optimization_barrier((own, piece))
-    owned = spread(piece, GROUP).reshape(2, 2, -1, owned_width)
+    own, piece, for_other = lax.optimization_barrier((own, piece, for_other))
+    piece = jnp.concatenate([piece, shift(for_other, "core", 1)])
+    owned = spread(piece, GROUP).reshape(group_count, 2, rows, owned_width)
+    owned = jnp.moveaxis(owned, 1, 0).reshape(2, 2, -1, owned_width)
+    theirs = shift(samples, "core", 1)
     contract_rows = (((0,), (0,)), ((), ()))
     cov_in, cov_out = (
-        sum(
-            lax.dot_general(v, part, contract_rows, preferred_element_type=jnp.float32)
-            for v, part in zip(pair, parts)
+        (
+            lax.dot_general(mine, owned[0, k], contract_rows, preferred_element_type=jnp.float32)
+            + lax.dot_general(theirs[k], owned[1, k], contract_rows, preferred_element_type=jnp.float32)
         )
         / jnp.float32(SAMPLED)
-        for pair, parts in zip(samples, owned)
+        for k, mine in enumerate((kept_in, kept_out))
     )
 
     other = shift(own, "core", 1)

time: 170 us -> 174 us (1.024)
  blocking collectives: 51.2 us -> 25.6 us
  waiting for transfers between devices: 32.6 us -> 49.8 us
  starting transfers between devices: 39.9 us -> 48.5 us
  matrix products: 2.48 us -> 4.79 us
  between operations: 15.5 us -> 17.8 us
  other arithmetic: 6.87 us -> 4.71 us
    all_to_all x1 -> x0, blocking collectives: 25.7 us -> none  [spread(): lax.all_to_all(jnp.broadcast_to(block[None], (size,) + block.shape), axis...]
    all_to_all x3 -> x4, waiting for transfers between devices: 8.73 us -> 20.6 us  [spread(): lax.all_to_all(jnp.broadcast_to(block[None], (size,) + block.shape), axis...]
    all_to_all x3 -> x4, starting transfers between devices: 17.8 us -> 27.4 us  [spread(): lax.all_to_all(jnp.broadcast_to(block[None], (size,) + block.shape), axis...]
    all_gather x1, waiting for transfers between devices: 0.01 us -> 7.69 us  [shards(): own = lax.all_gather(column[:, :owned_width], 'z', axis=0)]
    all_to_all x1, waiting for transfers between devices: 13.9 us -> 8.8 us  [shards(): terms = lax.all_to_all(terms, GROUP, 0, 0, tiled=True)]
    ppermute x2 -> x4, waiting for transfers between devices: 3.13 us -> 6.69 us  [shift(): lax.ppermute(value, axis, [((i + by) % size, i) for i in range(size)])]
    dot_general x4, matrix products: 2.48 us -> 4.79 us  [the longest x2 4.27 us: shards(): lax.dot_general(theirs[k], owned[1, k], contract_rows, preferred_element_...]
    ppermute x2 -> x4, starting transfers between devices: 12.7 us -> 11.7 us  [shift(): lax.ppermute(value, axis, [((i + by) % size, i) for i in range(size)])]
  transfers between devices with their start and end apart: 8 -> 11, of which waited for: 5 -> 7; matrix products, arithmetic and copies ran while one was open for 8% -> 9% of each run, Pallas kernels for 7% -> 7%
where the time goes in v9:
time: 174 us; the launch traced here: 173 us
  waiting for transfers between devices  49.8 us (29%)
  starting transfers between devices  48.5 us (28%)
  blocking collectives  25.6 us (15%)
  between operations  17.8 us (10%)
  Pallas kernels  11.2 us (6%)
  local copies, waits for them, and re-layouts  10.3 us (6%)
  matrix products  4.79 us (3%)
  other arithmetic  4.71 us (3%)
    all_to_all x4, starting transfers between devices, spread(): lax.all_to_all(jnp.broadcast_to(block[None], (size,) + block.shape), axis...  27.4 us
    all_gather x1, blocking collectives, shards(): lax.all_gather(kept_in.reshape(-1, width), 'z', axis=0, tiled=True)  25.6 us
    all_to_all x4, waiting for transfers between devices, spread(): lax.all_to_all(jnp.broadcast_to(block[None], (size,) + block.shape), axis...  20.6 us
    ppermute x4, starting transfers between devices, shift(): lax.ppermute(value, axis, [((i + by) % size, i) for i in range(size)])  11.7 us
    pallas_call x1, Pallas kernels, precondition(): pl.pallas_call(precondition_kernel, out_shape=(jax.ShapeDtypeStruct((8, r...  11.2 us
    all_to_all x1, waiting for transfers between devices, shards(): terms = lax.all_to_all(terms, GROUP, 0, 0, tiled=True)  8.8 us
    all_gather x1, waiting for transfers between devices, shards(): own = lax.all_gather(column[:, :owned_width], 'z', axis=0)  7.69 us
    ppermute x4, waiting for transfers between devices, shift(): lax.ppermute(value, axis, [((i + by) % size, i) for i in range(size)])  6.69 us
  transfers between devices with their start and end apart: 11, of which 7 were waited for; matrix products, arithmetic and copies ran while one was open for 9% of the time, Pallas kernels for 7%

profile of v9, /device:TPU:1, one launch (start us, length us, event | category | flops | bytes accessed | tf_op | source)
XLA Modules:
  0.0 172.8 jit_solution(12786525355532056080)
XLA Ops:
  7.8 0.8 broadcast_select_fusion
  8.7 0.9 pad_maximum_fusion.4
  9.6 0.9 broadcast_in_dim.43
  10.5 7.6 %all-to-all-start = ((bf16[4,112,768]{2,1,0:T(8,128)(2,1)}), bf16[4,112,768]{2,1,0:T(8,128)(2,1)S(1)}, u32[]{:S(2)}, u32[]{:S(2)}) async-start(bf16[4,112,768]{2,1,0:T(8,128)(2,1)} %broadcast_in_dim.43), calls=%async_computation | async-start | bytes 1376256 | tf_op jit(solution)/shard_map/all_to_all | solution.py:21
  18.1 4.7 %collective-permute-start = (s32[1]{0:T(128)}, s32[1]{0:T(128)}, u32[]{:S(2)}, u32[]{:S(2)}) collective-permute-start(s32[1]{0:T(128)} %param.11), channel_id=1, source_target_pairs={{8,0},{0,8},{9,1},{1,9},{10,2},{2,10},{11,3},{3,11},{12,4},{4,12},... | collective-permute-start | bytes 20 | tf_op jit(solution)/shard_map/ppermute | solution.py:16
  22.8 1.1 collective-permute-done
  23.9 11.9 %all-to-all-done = bf16[4,112,768]{2,1,0:T(8,128)(2,1)S(1)} async-done(((bf16[4,112,768]{2,1,0:T(8,128)(2,1)}), bf16[4,112,768]{2,1,0:T(8,128)(2,1)S(1)}, u32[]{:S(2)}, u32[]{:S(2)}) %all-to-all-start) | async-done | bytes 688160 | tf_op jit(solution)/shard_map/all_to_all | solution.py:21
  35.8 0.9 slice.25
  36.7 0.7 broadcast_in_dim.44
  37.4 10.0 %all-to-all-start.1 = ((bf16[8,16,768]{2,1,0:T(8,128)(2,1)}), bf16[8,16,768]{2,1,0:T(8,128)(2,1)S(1)}, u32[]{:S(2)}, u32[]{:S(2)}) async-start(bf16[8,16,768]{2,1,0:T(8,128)(2,1)} %broadcast_in_dim.44), calls=%async_computation.1 | async-start | bytes 393216 | tf_op jit(solution)/shard_map/all_to_all | solution.py:21
  47.5 8.7 %all-to-all-done.1 = bf16[8,16,768]{2,1,0:T(8,128)(2,1)S(1)} async-done(((bf16[8,16,768]{2,1,0:T(8,128)(2,1)}), bf16[8,16,768]{2,1,0:T(8,128)(2,1)S(1)}, u32[]{:S(2)}, u32[]{:S(2)}) %all-to-all-start.1) | async-done | bytes 196640 | tf_op jit(solution)/shard_map/all_to_all | solution.py:21
  56.1 0.2 copy.33
  56.3 1.0 broadcast_in_dim.46
  57.3 5.0 %all-to-all-start.2 = ((bf16[4,128,768]{1,2,0:T(8,128)(2,1)}), bf16[4,128,768]{1,2,0:T(8,128)(2,1)S(1)}, u32[]{:S(2)}, u32[]{:S(2)}) async-start(bf16[4,128,768]{1,2,0:T(8,128)(2,1)} %broadcast_in_dim.46), calls=%async_computation.2 | async-start | bytes 1572864 | tf_op jit(solution)/shard_map/all_to_all | solution.py:21
  64.7 25.6 %all_gather.9 = bf16[512,768]{1,0:T(8,128)(2,1)S(1)} all-gather(bf16[64,768]{1,0:T(8,128)(2,1)S(1)} %bitcast.60), channel_id=1, replica_groups=mesh['yh'=4,'z'=8,'core'=2,'yl'=2,'x'=4] {'z'}, dimensions={0}, use_global_device_ids=true | all-gather | bytes 884736 | tf_op jit(solution)/shard_map/all_gather | solution.py:104
  90.3 0.1 constant_dynamic-slice_fusion.3
  90.4 0.3 copy.34
  90.7 0.2 constant_dynamic-slice_fusion.2
  90.9 0.1 pad_maximum_fusion.2
  91.0 0.2 copy.41
  91.2 0.2 copy.42
  91.4 0.8 copy.37
  92.3 4.0 %all-to-all-start.3 = ((bf16[8,256,96]{1,2,0:T(8,128)(2,1)}), bf16[8,256,96]{1,2,0:T(8,128)(2,1)S(1)}, u32[]{:S(2)}, u32[]{:S(2)}) async-start(bf16[8,256,96]{1,2,0:T(8,128)(2,1)} %copy.37), calls=%async_computation.3 | async-start | bytes 786432 | tf_op jit(solution)/shard_map/all_to_all | solution.py:111
  96.9 6.0 %all-to-all-done.3 = bf16[8,256,96]{1,2,0:T(8,128)(2,1)S(1)} async-done(((bf16[8,256,96]{1,2,0:T(8,128)(2,1)}), bf16[8,256,96]{1,2,0:T(8,128)(2,1)S(1)}, u32[]{:S(2)}, u32[]{:S(2)}) %all-to-all-start.3) | async-done | bytes 393248 | tf_op jit(solution)/shard_map/all_to_all | solution.py:111
  102.9 7.7 %all-gather.3.cloned.1.call-done = bf16[32,96,768]{2,1,0:T(8,128)(2,1)} async-done(((bf16[4,96,768]{2,1,0:T(8,128)(2,1)}), bf16[32,96,768]{2,1,0:T(8,128)(2,1)}) %all-gather.3.cloned.1.call-update) | async-done | bytes 4718608 | tf_op jit(solution)/shard_map/all_gather | solution.py:101
  110.6 2.6 %collective-permute-start.3 = (bf16[8,4,96,768]{3,2,1,0:T(8,128)(2,1)}, bf16[8,4,96,768]{3,2,1,0:T(8,128)(2,1)}, u32[]{:S(2)}, u32[]{:S(2)}) collective-permute-start(bf16[8,4,96,768]{3,2,1,0:T(8,128)(2,1)} %bitcast.54), channel_id=1, source_target_pairs={{8,0},{0,8},{9,1},{1,9},{10,2},{2,10},{11,3},{3,11},{12,4},{4,12},... | collective-permute-start | bytes 14155784 | tf_op jit(solution)/shard_map/ppermute | solution.py:16
  113.1 1.9 %collective-permute-start.1 = (bf16[128,96]{0,1:T(8,128)(2,1)S(1)}, bf16[128,96]{0,1:T(8,128)(2,1)S(1)}, u32[]{:S(2)}, u32[]{:S(2)}) collective-permute-start(bf16[128,96]{0,1:T(8,128)(2,1)S(1)} %get-tuple-element.19), channel_id=1, source_target_pairs={{8,0},{0,8},{9,1},{1,9},{10,2},{2,10},{11,3},{3,11},{12,4},{4,12},... | collective-permute-start | bytes 73736 | tf_op jit(solution)/shard_map/ppermute | solution.py:16
  115.1 5.6 %collective-permute-done.1 = bf16[128,96]{0,1:T(8,128)(2,1)S(1)} collective-permute-done((bf16[128,96]{0,1:T(8,128)(2,1)S(1)}, bf16[128,96]{0,1:T(8,128)(2,1)S(1)}, u32[]{:S(2)}, u32[]{:S(2)}) %collective-permute-start.1) | collective-permute-done | bytes 24608 | tf_op jit(solution)/shard_map/ppermute | solution.py:16
  120.7 0.8 broadcast_in_dim.47
  121.5 4.7 %all-to-all-start.4 = ((bf16[8,256,96]{1,2,0:T(8,128)(2,1)}), bf16[8,256,96]{1,2,0:T(8,128)(2,1)S(1)}, u32[]{:S(2)}, u32[]{:S(2)}) async-start(bf16[8,256,96]{1,2,0:T(8,128)(2,1)} %broadcast_in_dim.47), calls=%async_computation.4 | async-start | bytes 786432 | tf_op jit(solution)/shard_map/all_to_all | solution.py:21
  126.2 0.6 broadcast_in_dim.48.in_eigs
  126.8 0.7 copy.40.out_eigs
  127.5 0.6 pad_add_fusion.place
  128.1 1.3 pad_maximum_fusion
  129.4 2.6 %collective-permute-start.2 = (bf16[2,512,768]{2,1,0:T(8,128)(2,1)}, bf16[2,512,768]{2,1,0:T(8,128)(2,1)}, u32[]{:S(2)}, u32[]{:S(2)}) collective-permute-start(bf16[2,512,768]{2,1,0:T(8,128)(2,1)} %pad_maximum_fusion), channel_id=1, source_target_pairs={{8,0},{0,8},{9,1},{1,9},{10,2},{2,10},{11,3},{3,11},{12,4},{4,12},... | collective-permute-start | bytes 4718600 | tf_op jit(solution)/shard_map/ppermute | solution.py:16
  132.0 11.2 %shard_map.103 = (bf16[8,96,768]{2,1,0:T(8,128)(2,1)}, f32[96,768]{1,0:T(8,128)}) custom-call(s32[2]{0:T(128)} %pad_add_fusion.place, bf16[8,4,96,768]{3,2,1,0:T(8,128)(2,1)} %bitcast.55, bf16[8,4,96,768]{3,2,1,0:T(8,128)(2,1)} %collective-permute-done.3.other, bf16[96,6144]{1,0:T(8,128)(2,1)} %grad.1, f32[1,768]{1,0:T(1,128)} %broadcast_in_dim.48.in_eigs, ...), custom_call_target="tpu_custom_call" | custom-call | flops 1811939328 | bytes 14155776 | tf_op jit(solution)/shard_map/pallas_call | solution.py:71
  143.2 5.4 %all-to-all-start.5 = ((bf16[8,96,768]{2,1,0:T(8,128)(2,1)}), bf16[8,96,768]{2,1,0:T(8,128)(2,1)S(1)}, u32[]{:S(2)}, u32[]{:S(2)}) async-start(bf16[8,96,768]{2,1,0:T(8,128)(2,1)} %get-tuple-element.22), calls=%async_computation.5 | async-start | bytes 2359296 | tf_op jit(solution)/shard_map/all_to_all | solution.py:134
  148.7 0.1 reshape.37
  148.8 1.0 copy.38
  149.8 1.1 reshape.38
  150.9 0.6 fusion.12
  151.5 0.3 fusion.4
  151.7 0.3 fusion.9
  152.0 2.1 %fusion.1 = f32[768,96]{0,1:T(8,128)} fusion(f32[768,96]{0,1:T(8,128)S(1)} %fusion.4, bf16[2,512,768]{2,1,0:T(8,128)(2,1)} %collective-permute-done.2, bf16[1,1,512,96]{2,1,3,0:T(2,128)(2,1)S(1)} %get-tuple-element.27), kind=kOutput, calls=%fused_computation.5 | convolution fusion | flops 75644928 | bytes 1474560 | tf_op jit(solution)/shard_map/dot_general | solution.py:126
  154.1 2.2 %fusion = f32[768,96]{0,1:T(8,128)} fusion(f32[768,96]{0,1:T(8,128)S(1)} %fusion.9, bf16[2,512,768]{2,1,0:T(8,128)(2,1)} %collective-permute-done.2, bf16[1,1,512,96]{2,1,3,0:T(2,128)(2,1)S(1)} %get-tuple-element.29), kind=kOutput, calls=%fused_computation.4 | convolution fusion | flops 75644928 | bytes 1474560 | tf_op jit(solution)/shard_map/dot_general | solution.py:126
  156.3 8.8 %all-to-all-done.5 = bf16[8,96,768]{2,1,0:T(8,128)(2,1)S(1)} async-done(((bf16[8,96,768]{2,1,0:T(8,128)(2,1)}), bf16[8,96,768]{2,1,0:T(8,128)(2,1)S(1)}, u32[]{:S(2)}, u32[]{:S(2)}) %all-to-all-start.5) | async-done | bytes 1179680 | tf_op jit(solution)/shard_map/all_to_all | solution.py:134
  165.1 0.2 convert_reduce_fusion
  165.2 0.7 add.44
  (17 shorter events, 0.1 us)
Async XLA Ops:
  10.5 25.3 %all-to-all-start = ((bf16[4,112,768]{2,1,0:T(8,128)(2,1)}), bf16[4,112,768]{2,1,0:T(8,128)(2,1)S(1)}, u32[]{:S(2)}, u32[]{:S(2)}) async-start(bf16[4,112,768]{2,1,0:T(8,128)(2,1)} %broadcast_in_dim.43), calls=%async_computation | async-start | bytes 1376256 | tf_op jit(solution)/shard_map/all_to_all | solution.py:21
  18.1 92.5 %all-gather.3.cloned.1.call-start = ((), (), s32[]{:S(2)}) async-start(), calls=%async_computation.6 | async-start | bytes 5308416 | tf_op jit(solution)/shard_map/all_gather | solution.py:101
  18.1 5.8 %collective-permute-start = (s32[1]{0:T(128)}, s32[1]{0:T(128)}, u32[]{:S(2)}, u32[]{:S(2)}) collective-permute-start(s32[1]{0:T(128)} %param.11), channel_id=1, source_target_pairs={{8,0},{0,8},{9,1},{1,9},{10,2},{2,10},{11,3},{3,11},{12,4},{4,12},... | collective-permute-start | bytes 20 | tf_op jit(solution)/shard_map/ppermute | solution.py:16
  37.4 18.7 %all-to-all-start.1 = ((bf16[8,16,768]{2,1,0:T(8,128)(2,1)}), bf16[8,16,768]{2,1,0:T(8,128)(2,1)S(1)}, u32[]{:S(2)}, u32[]{:S(2)}) async-start(bf16[8,16,768]{2,1,0:T(8,128)(2,1)} %broadcast_in_dim.44), calls=%async_computation.1 | async-start | bytes 393216 | tf_op jit(solution)/shard_map/all_to_all | solution.py:21
  57.3 33.1 %all-to-all-start.2 = ((bf16[4,128,768]{1,2,0:T(8,128)(2,1)}), bf16[4,128,768]{1,2,0:T(8,128)(2,1)S(1)}, u32[]{:S(2)}, u32[]{:S(2)}) async-start(bf16[4,128,768]{1,2,0:T(8,128)(2,1)} %broadcast_in_dim.46), calls=%async_computation.2 | async-start | bytes 1572864 | tf_op jit(solution)/shard_map/all_to_all | solution.py:21
  91.4 34.8 %copy-start.1 = (f32[768]{0:T(1024)S(1)}, f32[768]{0:T(1024)}, u32[]{:S(2)}) copy-start(f32[768]{0:T(1024)} %param.14) | copy-start | bytes 9220
  91.4 35.4 %copy-start.2 = (f32[96]{0:T(128)S(1)}, f32[96]{0:T(128)}, u32[]{:S(2)}) copy-start(f32[96]{0:T(128)} %param.15) | copy-start | bytes 1156
  92.3 10.6 %all-to-all-start.3 = ((bf16[8,256,96]{1,2,0:T(8,128)(2,1)}), bf16[8,256,96]{1,2,0:T(8,128)(2,1)S(1)}, u32[]{:S(2)}, u32[]{:S(2)}) async-start(bf16[8,256,96]{1,2,0:T(8,128)(2,1)} %copy.37), calls=%async_computation.3 | async-start | bytes 786432 | tf_op jit(solution)/shard_map/all_to_all | solution.py:111
  110.6 21.4 %collective-permute-start.3 = (bf16[8,4,96,768]{3,2,1,0:T(8,128)(2,1)}, bf16[8,4,96,768]{3,2,1,0:T(8,128)(2,1)}, u32[]{:S(2)}, u32[]{:S(2)}) collective-permute-start(bf16[8,4,96,768]{3,2,1,0:T(8,128)(2,1)} %bitcast.54), channel_id=1, source_target_pairs={{8,0},{0,8},{9,1},{1,9},{10,2},{2,10},{11,3},{3,11},{12,4},{4,12},... | collective-permute-start | bytes 14155784 | tf_op jit(solution)/shard_map/ppermute | solution.py:16
  113.1 7.5 %collective-permute-start.1 = (bf16[128,96]{0,1:T(8,128)(2,1)S(1)}, bf16[128,96]{0,1:T(8,128)(2,1)S(1)}, u32[]{:S(2)}, u32[]{:S(2)}) collective-permute-start(bf16[128,96]{0,1:T(8,128)(2,1)S(1)} %get-tuple-element.19), channel_id=1, source_target_pairs={{8,0},{0,8},{9,1},{1,9},{10,2},{2,10},{11,3},{3,11},{12,4},{4,12},... | collective-permute-start | bytes 73736 | tf_op jit(solution)/shard_map/ppermute | solution.py:16
  121.5 21.8 %all-to-all-start.4 = ((bf16[8,256,96]{1,2,0:T(8,128)(2,1)}), bf16[8,256,96]{1,2,0:T(8,128)(2,1)S(1)}, u32[]{:S(2)}, u32[]{:S(2)}) async-start(bf16[8,256,96]{1,2,0:T(8,128)(2,1)} %broadcast_in_dim.47), calls=%async_computation.4 | async-start | bytes 786432 | tf_op jit(solution)/shard_map/all_to_all | solution.py:21
  129.4 22.6 %collective-permute-start.2 = (bf16[2,512,768]{2,1,0:T(8,128)(2,1)}, bf16[2,512,768]{2,1,0:T(8,128)(2,1)}, u32[]{:S(2)}, u32[]{:S(2)}) collective-permute-start(bf16[2,512,768]{2,1,0:T(8,128)(2,1)} %pad_maximum_fusion), channel_id=1, source_target_pairs={{8,0},{0,8},{9,1},{1,9},{10,2},{2,10},{11,3},{3,11},{12,4},{4,12},... | collective-permute-start | bytes 4718600 | tf_op jit(solution)/shard_map/ppermute | solution.py:16
  143.2 21.8 %all-to-all-start.5 = ((bf16[8,96,768]{2,1,0:T(8,128)(2,1)}), bf16[8,96,768]{2,1,0:T(8,128)(2,1)S(1)}, u32[]{:S(2)}, u32[]{:S(2)}) async-start(bf16[8,96,768]{2,1,0:T(8,128)(2,1)} %get-tuple-element.22), calls=%async_computation.5 | async-start | bytes 2359296 | tf_op jit(solution)/shard_map/all_to_all | solution.py:134
  154.1 11.1 %copy-start = (f32[96,768]{1,0:T(8,128)S(1)}, f32[96,768]{1,0:T(8,128)}, u32[]{:S(2)}) copy-start(f32[96,768]{1,0:T(8,128)} %get-tuple-element.21) | copy-start | bytes 884740
Sparse Core Ops, SparseCore 0:
  36.8 73.6 all-gather.2

commit v10 on v9

--- a/solution.py
+++ b/solution.py
@@ -102,7 +102,6 @@
     kept_in, kept_out = lax.optimization_barrier((column[:, owned_width:], spread(kept_out, "z")))
     kept_out = spread(kept_out.reshape(-1, width), "yh").reshape(-1, width)
     kept_in = lax.all_gather(kept_in.reshape(-1, width), "z", axis=0, tiled=True)
-    samples = jnp.stack([kept_in, kept_out])
     pieces = []
     for idx in owner_pair:
         offset = idx % blocks_per * owned_width
@@ -114,16 +113,22 @@
         lax.dynamic_slice(arrived, (idx // blocks_per, k * rows, 0), (1, rows, owned_width))[0]
         for k, idx in enumerate(owner_pair)
     )
-    own, piece, for_other = lax.optimization_barrier((own, piece, for_other))
-    piece = jnp.concatenate([piece, shift(for_other, "core", 1)])
-    owned = spread(piece, GROUP).reshape(group_count, 2, rows, owned_width)
-    owned = jnp.moveaxis(owned, 1, 0).reshape(2, 2, -1, owned_width)
-    theirs = shift(samples, "core", 1)
+    theirs = shift(jnp.stack([kept_in, kept_out]), "core", 1)
+    own, piece, for_other, theirs = lax.optimization_barrier((own, piece, for_other, theirs))
+    core = lax.axis_index("core")
+    shares = jnp.stack([jnp.where(core == k, piece, for_other) for k in range(2)])
+    shares = jnp.broadcast_to(shares[:, None], (2, group_count) + piece.shape)
+    owned = lax.all_to_all(
+        shares.reshape((-1,) + piece.shape), ("core",) + GROUP, 0, 0, tiled=True
+    ).reshape(2, 2, -1, owned_width)
+    owned_mine, owned_theirs = (
+        lax.dynamic_index_in_dim(owned, k, 0, keepdims=False) for k in (core, 1 - core)
+    )
     contract_rows = (((0,), (0,)), ((), ()))
     cov_in, cov_out = (
         (
-            lax.dot_general(mine, owned[0, k], contract_rows, preferred_element_type=jnp.float32)
-            + lax.dot_general(theirs[k], owned[1, k], contract_rows, preferred_element_type=jnp.float32)
+            lax.dot_general(mine, owned_mine[k], contract_rows, preferred_element_type=jnp.float32)
+            + lax.dot_general(theirs[k], owned_theirs[k], contract_rows, preferred_element_type=jnp.float32)
         )
         / jnp.float32(SAMPLED)
         for k, mine in enumerate((kept_in, kept_out))

time: 174 us -> 170 us (0.977)
  waiting for transfers between devices: 49.8 us -> 39.8 us
  local copies, waits for them, and re-layouts: 10.3 us -> 14 us
  other arithmetic: 4.71 us -> 7.22 us
  matrix products: 4.79 us -> 2.47 us
    all_gather x1, waiting for transfers between devices: 7.69 us -> 0.01 us  [shards(): own = lax.all_gather(column[:, :owned_width], 'z', axis=0)]
    ppermute x4 -> x3, waiting for transfers between devices: 6.69 us -> 1.85 us  [shift(): lax.ppermute(value, axis, [((i + by) % size, i) for i in range(size)])]
    all_to_all x4 -> x3, starting transfers between devices: 27.4 us -> 22.6 us  [spread(): lax.all_to_all(jnp.broadcast_to(block[None], (size,) + block.shape), axis...]
    ppermute x4 -> x3, starting transfers between devices: 11.7 us -> 15.9 us  [shift(): lax.ppermute(value, axis, [((i + by) % size, i) for i in range(size)])]
    all_to_all x0 -> x1, starting transfers between devices: none -> 3.45 us  [shards(): lax.all_to_all(shares.reshape((-1,) + piece.shape), ('core',) + GROUP, 0,...]
    dot_general x4, matrix products: 4.79 us -> 2.47 us  [the longest x2 1.95 us: shards(): lax.dot_general(theirs[k], owned_theirs[k], contract_rows, preferred_elem...]
    reshape x2, local copies, waits for them, and re-layouts: 0.35 us -> 2.62 us  [shards(): jnp.concatenate(columns).reshape(group_count, -1, owned_width)]
    broadcast_in_dim x5 -> x4, local copies, waits for them, and re-layouts: 3.54 us -> 2.79 us  [spread(): jnp.broadcast_to(block[None], (size,) + block.shape)]
  transfers between devices with their start and end apart: 11 -> 10, of which waited for: 7 -> 6; matrix products, arithmetic and copies ran while one was open for 9% -> 11% of each run, Pallas kernels for 7% -> 7%
where the time goes in v10:
time: 170 us; the launch traced here: 168 us
  starting transfers between devices  50.2 us (30%)
  waiting for transfers between devices  39.8 us (23%)
  blocking collectives  25.6 us (15%)
  between operations  18 us (11%)
  local copies, waits for them, and re-layouts  14 us (8%)
  Pallas kernels  11.2 us (7%)
  other arithmetic  7.22 us (4%)
  matrix products  2.47 us (1%)
    all_gather x1, blocking collectives, shards(): lax.all_gather(kept_in.reshape(-1, width), 'z', axis=0, tiled=True)  25.6 us
    all_to_all x3, starting transfers between devices, spread(): lax.all_to_all(jnp.broadcast_to(block[None], (size,) + block.shape), axis...  22.6 us
    all_to_all x3, waiting for transfers between devices, spread(): lax.all_to_all(jnp.broadcast_to(block[None], (size,) + block.shape), axis...  20.8 us
    ppermute x3, starting transfers between devices, shift(): lax.ppermute(value, axis, [((i + by) % size, i) for i in range(size)])  15.9 us
    pallas_call x1, Pallas kernels, precondition(): pl.pallas_call(precondition_kernel, out_shape=(jax.ShapeDtypeStruct((8, r...  11.2 us
    all_to_all x1, waiting for transfers between devices, shards(): terms = lax.all_to_all(terms, GROUP, 0, 0, tiled=True)  10.3 us
    all_to_all x1, waiting for transfers between devices, shards(): lax.all_to_all(jnp.concatenate(pieces, axis=1), GROUP, 0, 0, tiled=True)  6.86 us
    all_to_all x1, starting transfers between devices, shards(): terms = lax.all_to_all(terms, GROUP, 0, 0, tiled=True)  4.11 us
  transfers between devices with their start and end apart: 10, of which 6 were waited for; matrix products, arithmetic and copies ran while one was open for 11% of the time, Pallas kernels for 7%

profile of v10, /device:TPU:1, one launch (start us, length us, event | category | flops | bytes accessed | tf_op | source)
XLA Modules:
  0.0 168.5 jit_solution(9255804977653310399)
XLA Ops:
  7.8 0.8 broadcast_select_fusion
  8.7 0.9 pad_maximum_fusion.4
  9.6 0.9 broadcast_in_dim.43
  10.5 7.6 %all-to-all-start = ((bf16[4,112,768]{2,1,0:T(8,128)(2,1)}), bf16[4,112,768]{2,1,0:T(8,128)(2,1)S(1)}, u32[]{:S(2)}, u32[]{:S(2)}) async-start(bf16[4,112,768]{2,1,0:T(8,128)(2,1)} %broadcast_in_dim.43), calls=%async_computation | async-start | bytes 1376256 | tf_op jit(solution)/shard_map/all_to_all | solution.py:21
  18.1 4.7 %collective-permute-start = (s32[1]{0:T(128)}, s32[1]{0:T(128)}, u32[]{:S(2)}, u32[]{:S(2)}) collective-permute-start(s32[1]{0:T(128)} %param.11), channel_id=1, source_target_pairs={{8,0},{0,8},{9,1},{1,9},{10,2},{2,10},{11,3},{3,11},{12,4},{4,12},... | collective-permute-start | bytes 20 | tf_op jit(solution)/shard_map/ppermute | solution.py:16
  22.8 0.9 collective-permute-done
  23.8 12.1 %all-to-all-done = bf16[4,112,768]{2,1,0:T(8,128)(2,1)S(1)} async-done(((bf16[4,112,768]{2,1,0:T(8,128)(2,1)}), bf16[4,112,768]{2,1,0:T(8,128)(2,1)S(1)}, u32[]{:S(2)}, u32[]{:S(2)}) %all-to-all-start) | async-done | bytes 688160 | tf_op jit(solution)/shard_map/all_to_all | solution.py:21
  35.8 0.9 slice.29
  36.7 0.7 broadcast_in_dim.44
  37.4 10.0 %all-to-all-start.1 = ((bf16[8,16,768]{2,1,0:T(8,128)(2,1)}), bf16[8,16,768]{2,1,0:T(8,128)(2,1)S(1)}, u32[]{:S(2)}, u32[]{:S(2)}) async-start(bf16[8,16,768]{2,1,0:T(8,128)(2,1)} %broadcast_in_dim.44), calls=%async_computation.1 | async-start | bytes 393216 | tf_op jit(solution)/shard_map/all_to_all | solution.py:21
  47.5 8.7 %all-to-all-done.1 = bf16[8,16,768]{2,1,0:T(8,128)(2,1)S(1)} async-done(((bf16[8,16,768]{2,1,0:T(8,128)(2,1)}), bf16[8,16,768]{2,1,0:T(8,128)(2,1)S(1)}, u32[]{:S(2)}, u32[]{:S(2)}) %all-to-all-start.1) | async-done | bytes 196640 | tf_op jit(solution)/shard_map/all_to_all | solution.py:21
  56.3 1.0 broadcast_in_dim.46
  57.3 5.0 %all-to-all-start.2 = ((bf16[4,128,768]{1,2,0:T(8,128)(2,1)}), bf16[4,128,768]{1,2,0:T(8,128)(2,1)S(1)}, u32[]{:S(2)}, u32[]{:S(2)}) async-start(bf16[4,128,768]{1,2,0:T(8,128)(2,1)} %broadcast_in_dim.46), calls=%async_computation.2 | async-start | bytes 1572864 | tf_op jit(solution)/shard_map/all_to_all | solution.py:21
  62.3 25.6 %all_gather.9 = bf16[512,768]{1,0:T(8,128)(2,1)S(1)} all-gather(bf16[64,768]{1,0:T(8,128)(2,1)S(1)} %bitcast.60), channel_id=1, replica_groups=mesh['yh'=4,'z'=8,'core'=2,'yl'=2,'x'=4] {'z'}, dimensions={0}, use_global_device_ids=true | all-gather | bytes 884736 | tf_op jit(solution)/shard_map/all_gather | solution.py:104
  87.9 0.3 copy.24
  88.2 1.3 pad_maximum_fusion
  89.5 7.7 %collective-permute-start.1 = (bf16[2,512,768]{2,1,0:T(8,128)(2,1)}, bf16[2,512,768]{2,1,0:T(8,128)(2,1)S(1)}, u32[]{:S(2)}, u32[]{:S(2)}) collective-permute-start(bf16[2,512,768]{2,1,0:T(8,128)(2,1)} %pad_maximum_fusion), channel_id=1, source_target_pairs={{8,0},{0,8},{9,1},{1,9},{10,2},{2,10},{11,3},{3,11},{12,4},{4,12},... | collective-permute-start | bytes 4718600 | tf_op jit(solution)/shard_map/ppermute | solution.py:16
  99.7 0.2 constant_dynamic-slice_fusion.7
  99.9 0.2 constant_dynamic-slice_fusion.6
  100.1 0.8 pad_maximum_fusion.2
  100.9 1.8 %copy.31 = bf16[8,128,96]{1,0,2:T(8,128)(2,1)} copy(bf16[8,128,96]{2,1,0:T(8,128)(2,1)} %bitcast.58) | data formatting | bytes 393216 | tf_op jit(solution)/shard_map/reshape | solution.py:109
  102.7 0.8 copy.32
  103.5 1.1 pad_maximum_fusion.1
  104.6 0.8 copy.27
  105.4 4.0 %all-to-all-start.3 = ((bf16[8,256,96]{1,2,0:T(8,128)(2,1)}), bf16[8,256,96]{1,2,0:T(8,128)(2,1)S(1)}, u32[]{:S(2)}, u32[]{:S(2)}) async-start(bf16[8,256,96]{1,2,0:T(8,128)(2,1)} %copy.27), calls=%async_computation.3 | async-start | bytes 786432 | tf_op jit(solution)/shard_map/all_to_all | solution.py:110
  110.1 6.9 %all-to-all-done.3 = bf16[8,256,96]{1,2,0:T(8,128)(2,1)S(1)} async-done(((bf16[8,256,96]{1,2,0:T(8,128)(2,1)}), bf16[8,256,96]{1,2,0:T(8,128)(2,1)S(1)}, u32[]{:S(2)}, u32[]{:S(2)}) %all-to-all-start.3) | async-done | bytes 393248 | tf_op jit(solution)/shard_map/all_to_all | solution.py:110
  117.0 0.6 dynamic-slice_bitcast_fusion
  117.6 3.6 %collective-permute-start.2 = (bf16[8,4,96,768]{3,2,1,0:T(8,128)(2,1)}, bf16[8,4,96,768]{3,2,1,0:T(8,128)(2,1)}, u32[]{:S(2)}, u32[]{:S(2)}) collective-permute-start(bf16[8,4,96,768]{3,2,1,0:T(8,128)(2,1)} %bitcast.54), channel_id=1, source_target_pairs={{8,0},{0,8},{9,1},{1,9},{10,2},{2,10},{11,3},{3,11},{12,4},{4,12},... | collective-permute-start | bytes 14155784 | tf_op jit(solution)/shard_map/ppermute | solution.py:16
  121.2 0.8 select_bitcast_fusion.1
  121.9 0.8 broadcast_in_dim.47
  122.8 3.4 %all-to-all-start.4 = ((bf16[16,128,96]{1,2,0:T(8,128)(2,1)}), bf16[16,128,96]{1,2,0:T(8,128)(2,1)S(1)}, u32[]{:S(2)}, u32[]{:S(2)}) async-start(bf16[16,128,96]{1,2,0:T(8,128)(2,1)} %bitcast.56), calls=%async_computation.4 | async-start | bytes 786432 | tf_op jit(solution)/shard_map/all_to_all | solution.py:121
  126.2 0.6 broadcast_in_dim.48.in_eigs
  126.8 0.7 copy.30.out_eigs
  127.5 0.6 pad_add_fusion.place
  128.1 0.9 collective-permute-done.2.other
  129.0 11.2 %shard_map.103 = (bf16[8,96,768]{2,1,0:T(8,128)(2,1)}, f32[96,768]{1,0:T(8,128)}) custom-call(s32[2]{0:T(128)} %pad_add_fusion.place, bf16[8,4,96,768]{3,2,1,0:T(8,128)(2,1)} %bitcast.55, bf16[8,4,96,768]{3,2,1,0:T(8,128)(2,1)} %collective-permute-done.2.other, bf16[96,6144]{1,0:T(8,128)(2,1)} %grad.1, f32[1,768]{1,0:T(1,128)} %broadcast_in_dim.48.in_eigs, ...), custom_call_target="tpu_custom_call" | custom-call | flops 1811939328 | bytes 14155776 | tf_op jit(solution)/shard_map/pallas_call | solution.py:71
  140.2 4.1 %all-to-all-start.5 = ((bf16[8,96,768]{2,1,0:T(8,128)(2,1)}), bf16[8,96,768]{2,1,0:T(8,128)(2,1)S(1)}, u32[]{:S(2)}, u32[]{:S(2)}) async-start(bf16[8,96,768]{2,1,0:T(8,128)(2,1)} %get-tuple-element.24), calls=%async_computation.5 | async-start | bytes 2359296 | tf_op jit(solution)/shard_map/all_to_all | solution.py:139
  144.3 0.9 copy.29
  145.3 1.1 reshape.46
  146.4 0.6 constant_dynamic-slice_fusion.2
  147.1 0.3 fusion.8
  147.3 0.3 fusion.13
  147.6 0.9 copy-done.1
  148.5 1.0 fusion.1
  149.4 1.0 fusion
  150.4 10.3 %all-to-all-done.5 = bf16[8,96,768]{2,1,0:T(8,128)(2,1)S(1)} async-done(((bf16[8,96,768]{2,1,0:T(8,128)(2,1)}), bf16[8,96,768]{2,1,0:T(8,128)(2,1)S(1)}, u32[]{:S(2)}, u32[]{:S(2)}) %all-to-all-start.5) | async-done | bytes 1179680 | tf_op jit(solution)/shard_map/all_to_all | solution.py:139
  160.7 0.2 convert_reduce_fusion
  160.9 0.7 add.54
  (19 shorter events, 0.2 us)
Async XLA Ops:
  10.5 25.3 %all-to-all-start = ((bf16[4,112,768]{2,1,0:T(8,128)(2,1)}), bf16[4,112,768]{2,1,0:T(8,128)(2,1)S(1)}, u32[]{:S(2)}, u32[]{:S(2)}) async-start(bf16[4,112,768]{2,1,0:T(8,128)(2,1)} %broadcast_in_dim.43), calls=%async_computation | async-start | bytes 1376256 | tf_op jit(solution)/shard_map/all_to_all | solution.py:21
  18.1 99.4 %all-gather.3.cloned.1.call-start = ((), (), s32[]{:S(2)}) async-start(), calls=%async_computation.6 | async-start | bytes 5308416 | tf_op jit(solution)/shard_map/all_gather | solution.py:101
  18.1 5.6 %collective-permute-start = (s32[1]{0:T(128)}, s32[1]{0:T(128)}, u32[]{:S(2)}, u32[]{:S(2)}) collective-permute-start(s32[1]{0:T(128)} %param.11), channel_id=1, source_target_pairs={{8,0},{0,8},{9,1},{1,9},{10,2},{2,10},{11,3},{3,11},{12,4},{4,12},... | collective-permute-start | bytes 20 | tf_op jit(solution)/shard_map/ppermute | solution.py:16
  37.4 18.7 %all-to-all-start.1 = ((bf16[8,16,768]{2,1,0:T(8,128)(2,1)}), bf16[8,16,768]{2,1,0:T(8,128)(2,1)S(1)}, u32[]{:S(2)}, u32[]{:S(2)}) async-start(bf16[8,16,768]{2,1,0:T(8,128)(2,1)} %broadcast_in_dim.44), calls=%async_computation.1 | async-start | bytes 393216 | tf_op jit(solution)/shard_map/all_to_all | solution.py:21
  57.3 30.6 %all-to-all-start.2 = ((bf16[4,128,768]{1,2,0:T(8,128)(2,1)}), bf16[4,128,768]{1,2,0:T(8,128)(2,1)S(1)}, u32[]{:S(2)}, u32[]{:S(2)}) async-start(bf16[4,128,768]{1,2,0:T(8,128)(2,1)} %broadcast_in_dim.46), calls=%async_computation.2 | async-start | bytes 1572864 | tf_op jit(solution)/shard_map/all_to_all | solution.py:21
  89.5 28.0 %collective-permute-start.1 = (bf16[2,512,768]{2,1,0:T(8,128)(2,1)}, bf16[2,512,768]{2,1,0:T(8,128)(2,1)S(1)}, u32[]{:S(2)}, u32[]{:S(2)}) collective-permute-start(bf16[2,512,768]{2,1,0:T(8,128)(2,1)} %pad_maximum_fusion), channel_id=1, source_target_pairs={{8,0},{0,8},{9,1},{1,9},{10,2},{2,10},{11,3},{3,11},{12,4},{4,12},... | collective-permute-start | bytes 4718600 | tf_op jit(solution)/shard_map/ppermute | solution.py:16
  104.6 21.6 %copy-start.3 = (f32[768]{0:T(1024)S(1)}, f32[768]{0:T(1024)}, u32[]{:S(2)}) copy-start(f32[768]{0:T(1024)} %param.14) | copy-start | bytes 9220
  104.6 22.2 %copy-start.4 = (f32[96]{0:T(128)S(1)}, f32[96]{0:T(128)}, u32[]{:S(2)}) copy-start(f32[96]{0:T(128)} %param.15) | copy-start | bytes 1156
  105.4 11.5 %all-to-all-start.3 = ((bf16[8,256,96]{1,2,0:T(8,128)(2,1)}), bf16[8,256,96]{1,2,0:T(8,128)(2,1)S(1)}, u32[]{:S(2)}, u32[]{:S(2)}) async-start(bf16[8,256,96]{1,2,0:T(8,128)(2,1)} %copy.27), calls=%async_computation.3 | async-start | bytes 786432 | tf_op jit(solution)/shard_map/all_to_all | solution.py:110
  117.6 22.6 %copy-start = (bf16[2,512,768]{2,1,0:T(8,128)(2,1)}, bf16[2,512,768]{2,1,0:T(8,128)(2,1)S(1)}, u32[]{:S(2)}) copy-start(bf16[2,512,768]{2,1,0:T(8,128)(2,1)S(1)} %collective-permute-done.1) | copy-start | bytes 4718596
  117.6 11.4 %collective-permute-start.2 = (bf16[8,4,96,768]{3,2,1,0:T(8,128)(2,1)}, bf16[8,4,96,768]{3,2,1,0:T(8,128)(2,1)}, u32[]{:S(2)}, u32[]{:S(2)}) collective-permute-start(bf16[8,4,96,768]{3,2,1,0:T(8,128)(2,1)} %bitcast.54), channel_id=1, source_target_pairs={{8,0},{0,8},{9,1},{1,9},{10,2},{2,10},{11,3},{3,11},{12,4},{4,12},... | collective-permute-start | bytes 14155784 | tf_op jit(solution)/shard_map/ppermute | solution.py:16
  122.8 17.5 %all-to-all-start.4 = ((bf16[16,128,96]{1,2,0:T(8,128)(2,1)}), bf16[16,128,96]{1,2,0:T(8,128)(2,1)S(1)}, u32[]{:S(2)}, u32[]{:S(2)}) async-start(bf16[16,128,96]{1,2,0:T(8,128)(2,1)} %bitcast.56), calls=%async_computation.4 | async-start | bytes 786432 | tf_op jit(solution)/shard_map/all_to_all | solution.py:121
  140.2 20.5 %all-to-all-start.5 = ((bf16[8,96,768]{2,1,0:T(8,128)(2,1)}), bf16[8,96,768]{2,1,0:T(8,128)(2,1)S(1)}, u32[]{:S(2)}, u32[]{:S(2)}) async-start(bf16[8,96,768]{2,1,0:T(8,128)(2,1)} %get-tuple-element.24), calls=%async_computation.5 | async-start | bytes 2359296 | tf_op jit(solution)/shard_map/all_to_all | solution.py:139
  147.1 1.4 copy-start.1
  149.4 11.4 %copy-start.2 = (f32[96,768]{1,0:T(8,128)S(1)}, f32[96,768]{1,0:T(8,128)}, u32[]{:S(2)}) copy-start(f32[96,768]{1,0:T(8,128)} %get-tuple-element.23) | copy-start | bytes 884740
Sparse Core Ops, SparseCore 0:
  36.9 73.6 all-gather.2

commit v11 on v10

--- a/solution.py
+++ b/solution.py
@@ -80,7 +80,7 @@
             pltpu.VMEM((4, 8, 2, rows, width), jnp.bfloat16),
             pltpu.SemaphoreType.DMA((16,)),
         ],
-        compiler_params=pltpu.CompilerParams(vmem_limit_bytes=58 << 20),
+        compiler_params=pltpu.CompilerParams(vmem_limit_bytes=20 << 20),
         cost_estimate=pl.CostEstimate(
             flops=4 * rows * 8 * width * width, bytes_accessed=24 * width * width, transcendentals=0
         ),

time: 170 us -> 166 us (0.976)
  other arithmetic: 7.22 us -> 4.25 us
  local copies, waits for them, and re-layouts: 14 us -> 11.4 us
  matrix products: 2.47 us -> 4.74 us
    ppermute x3, waiting for transfers between devices: 1.85 us -> 4.28 us  [shift(): lax.ppermute(value, axis, [((i + by) % size, i) for i in range(size)])]
    reshape x2, local copies, waits for them, and re-layouts: 2.62 us -> 0.35 us  [shards(): jnp.concatenate(columns).reshape(group_count, -1, owned_width)]
    dot_general x2, matrix products: 1.95 us -> 4.22 us  [shards(): lax.dot_general(theirs[k], owned_theirs[k], contract_rows, preferred_elem...]
  transfers between devices with their start and end apart: 10 -> 10, of which waited for: 6 -> 6; matrix products, arithmetic and copies ran while one was open for 11% -> 8% of each run, Pallas kernels for 7% -> 6%
where the time goes in v11:
time: 166 us; the launch traced here: 164 us
  starting transfers between devices  49.6 us (30%)
  waiting for transfers between devices  40.7 us (25%)
  blocking collectives  25.6 us (15%)
  between operations  18.4 us (11%)
  local copies, waits for them, and re-layouts  11.4 us (7%)
  Pallas kernels  9.71 us (6%)
  matrix products  4.74 us (3%)
  other arithmetic  4.25 us (3%)
    all_gather x1, blocking collectives, shards(): lax.all_gather(kept_in.reshape(-1, width), 'z', axis=0, tiled=True)  25.6 us
    all_to_all x3, starting transfers between devices, spread(): lax.all_to_all(jnp.broadcast_to(block[None], (size,) + block.shape), axis...  22.6 us
    all_to_all x3, waiting for transfers between devices, spread(): lax.all_to_all(jnp.broadcast_to(block[None], (size,) + block.shape), axis...  20.8 us
    ppermute x3, starting transfers between devices, shift(): lax.ppermute(value, axis, [((i + by) % size, i) for i in range(size)])  16 us
    pallas_call x1, Pallas kernels, precondition(): pl.pallas_call(precondition_kernel, out_shape=(jax.ShapeDtypeStruct((8, r...  9.71 us
    all_to_all x1, waiting for transfers between devices, shards(): terms = lax.all_to_all(terms, GROUP, 0, 0, tiled=True)  8.86 us
    all_to_all x1, waiting for transfers between devices, shards(): lax.all_to_all(jnp.concatenate(pieces, axis=1), GROUP, 0, 0, tiled=True)  6.79 us
    ppermute x3, waiting for transfers between devices, shift(): lax.ppermute(value, axis, [((i + by) % size, i) for i in range(size)])  4.28 us
  transfers between devices with their start and end apart: 10, of which 6 were waited for; matrix products, arithmetic and copies ran while one was open for 8% of the time, Pallas kernels for 6%

profile of v11, /device:TPU:1, one launch (start us, length us, event | category | flops | bytes accessed | tf_op | source)
XLA Modules:
  0.0 164.4 jit_solution(11622904342475384614)
XLA Ops:
  7.8 0.8 broadcast_select_fusion
  8.7 0.9 pad_maximum_fusion.4
  9.6 0.9 broadcast_in_dim.43
  10.5 7.6 %all-to-all-start = ((bf16[4,112,768]{2,1,0:T(8,128)(2,1)}), bf16[4,112,768]{2,1,0:T(8,128)(2,1)S(1)}, u32[]{:S(2)}, u32[]{:S(2)}) async-start(bf16[4,112,768]{2,1,0:T(8,128)(2,1)} %broadcast_in_dim.43), calls=%async_computation | async-start | bytes 1376256 | tf_op jit(solution)/shard_map/all_to_all | solution.py:21
  18.1 4.7 %collective-permute-start = (s32[1]{0:T(128)}, s32[1]{0:T(128)}, u32[]{:S(2)}, u32[]{:S(2)}) collective-permute-start(s32[1]{0:T(128)} %param.11), channel_id=1, source_target_pairs={{8,0},{0,8},{9,1},{1,9},{10,2},{2,10},{11,3},{3,11},{12,4},{4,12},... | collective-permute-start | bytes 20 | tf_op jit(solution)/shard_map/ppermute | solution.py:16
  22.8 0.9 collective-permute-done
  23.7 12.1 %all-to-all-done = bf16[4,112,768]{2,1,0:T(8,128)(2,1)S(1)} async-done(((bf16[4,112,768]{2,1,0:T(8,128)(2,1)}), bf16[4,112,768]{2,1,0:T(8,128)(2,1)S(1)}, u32[]{:S(2)}, u32[]{:S(2)}) %all-to-all-start) | async-done | bytes 688160 | tf_op jit(solution)/shard_map/all_to_all | solution.py:21
  35.8 0.9 slice.29
  36.7 0.0 all-gather.3.cloned.1.call-update
  36.7 0.7 broadcast_in_dim.44
  37.4 10.0 %all-to-all-start.1 = ((bf16[8,16,768]{2,1,0:T(8,128)(2,1)}), bf16[8,16,768]{2,1,0:T(8,128)(2,1)S(1)}, u32[]{:S(2)}, u32[]{:S(2)}) async-start(bf16[8,16,768]{2,1,0:T(8,128)(2,1)} %broadcast_in_dim.44), calls=%async_computation.1 | async-start | bytes 393216 | tf_op jit(solution)/shard_map/all_to_all | solution.py:21
  47.5 8.7 %all-to-all-done.1 = bf16[8,16,768]{2,1,0:T(8,128)(2,1)S(1)} async-done(((bf16[8,16,768]{2,1,0:T(8,128)(2,1)}), bf16[8,16,768]{2,1,0:T(8,128)(2,1)S(1)}, u32[]{:S(2)}, u32[]{:S(2)}) %all-to-all-start.1) | async-done | bytes 196640 | tf_op jit(solution)/shard_map/all_to_all | solution.py:21
  56.1 0.2 copy.23
  56.3 1.0 broadcast_in_dim.46
  57.3 5.0 %all-to-all-start.2 = ((bf16[4,128,768]{1,2,0:T(8,128)(2,1)}), bf16[4,128,768]{1,2,0:T(8,128)(2,1)S(1)}, u32[]{:S(2)}, u32[]{:S(2)}) async-start(bf16[4,128,768]{1,2,0:T(8,128)(2,1)} %broadcast_in_dim.46), calls=%async_computation.2 | async-start | bytes 1572864 | tf_op jit(solution)/shard_map/all_to_all | solution.py:21
  62.3 25.6 %all_gather.9 = bf16[512,768]{1,0:T(8,128)(2,1)S(1)} all-gather(bf16[64,768]{1,0:T(8,128)(2,1)S(1)} %bitcast.59), channel_id=1, replica_groups=mesh['yh'=4,'z'=8,'core'=2,'yl'=2,'x'=4] {'z'}, dimensions={0}, use_global_device_ids=true | all-gather | bytes 884736 | tf_op jit(solution)/shard_map/all_gather | solution.py:104
  87.9 0.3 copy.24
  88.2 1.3 pad_maximum_fusion
  89.5 7.7 %collective-permute-start.1 = (bf16[2,512,768]{2,1,0:T(8,128)(2,1)}, bf16[2,512,768]{2,1,0:T(8,128)(2,1)}, u32[]{:S(2)}, u32[]{:S(2)}) collective-permute-start(bf16[2,512,768]{2,1,0:T(8,128)(2,1)} %pad_maximum_fusion), channel_id=1, source_target_pairs={{8,0},{0,8},{9,1},{1,9},{10,2},{2,10},{11,3},{3,11},{12,4},{4,12},... | collective-permute-start | bytes 4718600 | tf_op jit(solution)/shard_map/ppermute | solution.py:16
  100.0 0.2 constant_dynamic-slice_fusion.7
  100.2 0.2 constant_dynamic-slice_fusion.6
  100.3 0.1 pad_maximum_fusion.2
  100.4 0.2 copy.31
  100.6 0.2 copy.32
  100.8 0.0 copy-start.2
  100.9 0.8 copy.27
  101.7 4.0 %all-to-all-start.3 = ((bf16[8,256,96]{1,2,0:T(8,128)(2,1)}), bf16[8,256,96]{1,2,0:T(8,128)(2,1)S(1)}, u32[]{:S(2)}, u32[]{:S(2)}) async-start(bf16[8,256,96]{1,2,0:T(8,128)(2,1)} %copy.27), calls=%async_computation.3 | async-start | bytes 786432 | tf_op jit(solution)/shard_map/all_to_all | solution.py:110
  106.4 6.8 %all-to-all-done.3 = bf16[8,256,96]{1,2,0:T(8,128)(2,1)S(1)} async-done(((bf16[8,256,96]{1,2,0:T(8,128)(2,1)}), bf16[8,256,96]{1,2,0:T(8,128)(2,1)S(1)}, u32[]{:S(2)}, u32[]{:S(2)}) %all-to-all-start.3) | async-done | bytes 393248 | tf_op jit(solution)/shard_map/all_to_all | solution.py:110
  113.2 0.0 all-gather.3.cloned.1.call-done
  113.3 3.5 %collective-permute-start.2 = (bf16[8,4,96,768]{3,2,1,0:T(8,128)(2,1)}, bf16[8,4,96,768]{3,2,1,0:T(8,128)(2,1)}, u32[]{:S(2)}, u32[]{:S(2)}) collective-permute-start(bf16[8,4,96,768]{3,2,1,0:T(8,128)(2,1)} %bitcast.50), channel_id=1, source_target_pairs={{8,0},{0,8},{9,1},{1,9},{10,2},{2,10},{11,3},{3,11},{12,4},{4,12},... | collective-permute-start | bytes 14155784 | tf_op jit(solution)/shard_map/ppermute | solution.py:16
  116.9 0.8 broadcast_in_dim.47
  117.7 3.4 %all-to-all-start.4 = ((bf16[16,128,96]{1,2,0:T(8,128)(2,1)}), bf16[16,128,96]{1,2,0:T(8,128)(2,1)S(1)}, u32[]{:S(2)}, u32[]{:S(2)}) async-start(bf16[16,128,96]{1,2,0:T(8,128)(2,1)} %bitcast.15), calls=%async_computation.4 | async-start | bytes 786432 | tf_op jit(solution)/shard_map/all_to_all | solution.py:121
  121.1 0.1 copy.30.out_eigs
  121.3 0.1 pad_add_fusion.place
  121.3 3.3 %collective-permute-done.2.other = bf16[8,4,96,768]{3,2,1,0:T(8,128)(2,1)} collective-permute-done((bf16[8,4,96,768]{3,2,1,0:T(8,128)(2,1)}, bf16[8,4,96,768]{3,2,1,0:T(8,128)(2,1)}, u32[]{:S(2)}, u32[]{:S(2)}) %collective-permute-start.2) | collective-permute-done | bytes 4718624 | tf_op jit(solution)/shard_map/ppermute | solution.py:16
  124.7 2.3 %copy-done = bf16[32,96,768]{2,1,0:T(8,128)(2,1)S(1)} copy-done((bf16[32,96,768]{2,1,0:T(8,128)(2,1)S(1)}, bf16[32,96,768]{2,1,0:T(8,128)(2,1)}, u32[]{:S(2)}) %copy-start) | copy-done | bytes 4718616
  127.0 9.7 %shard_map.103 = (bf16[8,96,768]{2,1,0:T(8,128)(2,1)}, f32[96,768]{1,0:T(8,128)S(1)}) custom-call(s32[2]{0:T(128)S(1)} %pad_add_fusion.place, bf16[8,4,96,768]{3,2,1,0:T(8,128)(2,1)S(1)} %bitcast.51, bf16[8,4,96,768]{3,2,1,0:T(8,128)(2,1)} %collective-permute-done.2.other, bf16[96,6144]{1,0:T(8,128)(2,1)S(1)} %copy-done.1, ...), custom_call_target="tpu_custom_call" | custom-call | flops 1811939328 | bytes 14155776 | tf_op jit(solution)/shard_map/pallas_call | solution.py:71
  136.7 3.6 %all-to-all-start.5 = ((bf16[8,96,768]{2,1,0:T(8,128)(2,1)}), bf16[8,96,768]{2,1,0:T(8,128)(2,1)S(1)}, u32[]{:S(2)}, u32[]{:S(2)}) async-start(bf16[8,96,768]{2,1,0:T(8,128)(2,1)} %get-tuple-element.24), calls=%async_computation.5 | async-start | bytes 2359296 | tf_op jit(solution)/shard_map/all_to_all | solution.py:139
  140.3 0.9 copy.29
  141.2 1.1 reshape.46
  142.4 0.6 constant_dynamic-slice_fusion.2
  143.0 0.3 fusion.8
  143.3 0.3 fusion.13
  143.6 2.1 %fusion.1 = f32[768,96]{0,1:T(8,128)} fusion(f32[768,96]{0,1:T(8,128)S(1)} %fusion.8, bf16[2,512,768]{2,1,0:T(8,128)(2,1)} %collective-permute-done.1, bf16[1,1,512,96]{2,1,0,3:T(2,128)(2,1)S(1)} %get-tuple-element.29), kind=kOutput, calls=%fused_computation.5 | convolution fusion | flops 75644928 | bytes 1474560 | tf_op jit(solution)/shard_map/dot_general | solution.py:131
  145.7 2.1 %fusion = f32[768,96]{0,1:T(8,128)} fusion(f32[768,96]{0,1:T(8,128)S(1)} %fusion.13, bf16[2,512,768]{2,1,0:T(8,128)(2,1)} %collective-permute-done.1, bf16[1,1,512,96]{2,1,0,3:T(2,128)(2,1)S(1)} %get-tuple-element.30), kind=kOutput, calls=%fused_computation.4 | convolution fusion | flops 75644928 | bytes 1474560 | tf_op jit(solution)/shard_map/dot_general | solution.py:131
  147.8 8.9 %all-to-all-done.5 = bf16[8,96,768]{2,1,0:T(8,128)(2,1)S(1)} async-done(((bf16[8,96,768]{2,1,0:T(8,128)(2,1)}), bf16[8,96,768]{2,1,0:T(8,128)(2,1)S(1)}, u32[]{:S(2)}, u32[]{:S(2)}) %all-to-all-start.5) | async-done | bytes 1179680 | tf_op jit(solution)/shard_map/all_to_all | solution.py:139
  156.6 0.2 convert_reduce_fusion
  156.8 0.7 add.54
  (17 shorter events, 0.1 us)
Async XLA Ops:
  10.5 25.3 %all-to-all-start = ((bf16[4,112,768]{2,1,0:T(8,128)(2,1)}), bf16[4,112,768]{2,1,0:T(8,128)(2,1)S(1)}, u32[]{:S(2)}, u32[]{:S(2)}) async-start(bf16[4,112,768]{2,1,0:T(8,128)(2,1)} %broadcast_in_dim.43), calls=%async_computation | async-start | bytes 1376256 | tf_op jit(solution)/shard_map/all_to_all | solution.py:21
  18.1 95.1 %all-gather.3.cloned.1.call-start = ((), (), s32[]{:S(2)}) async-start(), calls=%async_computation.6 | async-start | bytes 5308416 | tf_op jit(solution)/shard_map/all_gather | solution.py:101
  18.1 5.6 %collective-permute-start = (s32[1]{0:T(128)}, s32[1]{0:T(128)}, u32[]{:S(2)}, u32[]{:S(2)}) collective-permute-start(s32[1]{0:T(128)} %param.11), channel_id=1, source_target_pairs={{8,0},{0,8},{9,1},{1,9},{10,2},{2,10},{11,3},{3,11},{12,4},{4,12},... | collective-permute-start | bytes 20 | tf_op jit(solution)/shard_map/ppermute | solution.py:16
  37.4 18.7 %all-to-all-start.1 = ((bf16[8,16,768]{2,1,0:T(8,128)(2,1)}), bf16[8,16,768]{2,1,0:T(8,128)(2,1)S(1)}, u32[]{:S(2)}, u32[]{:S(2)}) async-start(bf16[8,16,768]{2,1,0:T(8,128)(2,1)} %broadcast_in_dim.44), calls=%async_computation.1 | async-start | bytes 393216 | tf_op jit(solution)/shard_map/all_to_all | solution.py:21
  57.3 30.6 %all-to-all-start.2 = ((bf16[4,128,768]{1,2,0:T(8,128)(2,1)}), bf16[4,128,768]{1,2,0:T(8,128)(2,1)S(1)}, u32[]{:S(2)}, u32[]{:S(2)}) async-start(bf16[4,128,768]{1,2,0:T(8,128)(2,1)} %broadcast_in_dim.46), calls=%async_computation.2 | async-start | bytes 1572864 | tf_op jit(solution)/shard_map/all_to_all | solution.py:21
  89.5 23.7 %collective-permute-start.1 = (bf16[2,512,768]{2,1,0:T(8,128)(2,1)}, bf16[2,512,768]{2,1,0:T(8,128)(2,1)}, u32[]{:S(2)}, u32[]{:S(2)}) collective-permute-start(bf16[2,512,768]{2,1,0:T(8,128)(2,1)} %pad_maximum_fusion), channel_id=1, source_target_pairs={{8,0},{0,8},{9,1},{1,9},{10,2},{2,10},{11,3},{3,11},{12,4},{4,12},... | collective-permute-start | bytes 4718600 | tf_op jit(solution)/shard_map/ppermute | solution.py:16
  100.8 20.3 %copy-start.2 = (f32[768]{0:T(1024)S(1)}, f32[768]{0:T(1024)}, u32[]{:S(2)}) copy-start(f32[768]{0:T(1024)} %param.14) | copy-start | bytes 9220
  100.9 20.3 %copy-start.3 = (f32[96]{0:T(128)S(1)}, f32[96]{0:T(128)}, u32[]{:S(2)}) copy-start(f32[96]{0:T(128)} %param.15) | copy-start | bytes 1156
  100.9 23.8 %copy-start.1 = (bf16[96,6144]{1,0:T(8,128)(2,1)S(1)}, bf16[96,6144]{1,0:T(8,128)(2,1)}, u32[]{:S(2)}) copy-start(bf16[96,6144]{1,0:T(8,128)(2,1)} %grad.1) | copy-start | bytes 3538948
  101.7 11.5 %all-to-all-start.3 = ((bf16[8,256,96]{1,2,0:T(8,128)(2,1)}), bf16[8,256,96]{1,2,0:T(8,128)(2,1)S(1)}, u32[]{:S(2)}, u32[]{:S(2)}) async-start(bf16[8,256,96]{1,2,0:T(8,128)(2,1)} %copy.27), calls=%async_computation.3 | async-start | bytes 786432 | tf_op jit(solution)/shard_map/all_to_all | solution.py:110
  113.3 11.4 %collective-permute-start.2 = (bf16[8,4,96,768]{3,2,1,0:T(8,128)(2,1)}, bf16[8,4,96,768]{3,2,1,0:T(8,128)(2,1)}, u32[]{:S(2)}, u32[]{:S(2)}) collective-permute-start(bf16[8,4,96,768]{3,2,1,0:T(8,128)(2,1)} %bitcast.50), channel_id=1, source_target_pairs={{8,0},{0,8},{9,1},{1,9},{10,2},{2,10},{11,3},{3,11},{12,4},{4,12},... | collective-permute-start | bytes 14155784 | tf_op jit(solution)/shard_map/ppermute | solution.py:16
  117.7 19.1 %all-to-all-start.4 = ((bf16[16,128,96]{1,2,0:T(8,128)(2,1)}), bf16[16,128,96]{1,2,0:T(8,128)(2,1)S(1)}, u32[]{:S(2)}, u32[]{:S(2)}) async-start(bf16[16,128,96]{1,2,0:T(8,128)(2,1)} %bitcast.15), calls=%async_computation.4 | async-start | bytes 786432 | tf_op jit(solution)/shard_map/all_to_all | solution.py:121
  124.7 2.3 %copy-start = (bf16[32,96,768]{2,1,0:T(8,128)(2,1)S(1)}, bf16[32,96,768]{2,1,0:T(8,128)(2,1)}, u32[]{:S(2)}) copy-start(bf16[32,96,768]{2,1,0:T(8,128)(2,1)} %all-gather.3.cloned.1.call-done) | copy-start | bytes 14155780
  136.7 19.9 %all-to-all-start.5 = ((bf16[8,96,768]{2,1,0:T(8,128)(2,1)}), bf16[8,96,768]{2,1,0:T(8,128)(2,1)S(1)}, u32[]{:S(2)}, u32[]{:S(2)}) async-start(bf16[8,96,768]{2,1,0:T(8,128)(2,1)} %get-tuple-element.24), calls=%async_computation.5 | async-start | bytes 2359296 | tf_op jit(solution)/shard_map/all_to_all | solution.py:139
Sparse Core Ops, SparseCore 0:
  36.9 73.6 all-gather.2

commit v12 on v11

--- a/solution.py
+++ b/solution.py
@@ -66,7 +66,7 @@
     place = jnp.stack([lax.axis_index("core"), lax.axis_index(GROUP)]).astype(jnp.int32)
     rows = grad.shape[0]
     width = in_eigs.shape[0]
-    anywhere = pl.BlockSpec(memory_space=pl.ANY)
+    hbm = pl.BlockSpec(memory_space=pltpu.HBM)
     vmem = pl.BlockSpec(memory_space=pltpu.VMEM)
     return pl.pallas_call(
         precondition_kernel,
@@ -74,13 +74,13 @@
             jax.ShapeDtypeStruct((8, rows, width), jnp.bfloat16),
             jax.ShapeDtypeStruct((rows, width), jnp.float32),
         ),
-        in_specs=[pl.BlockSpec(memory_space=pltpu.SMEM), anywhere, anywhere, vmem, vmem, vmem],
+        in_specs=[pl.BlockSpec(memory_space=pltpu.SMEM), hbm, hbm, vmem, vmem, vmem],
         out_specs=(vmem, vmem),
         scratch_shapes=[
             pltpu.VMEM((4, 8, 2, rows, width), jnp.bfloat16),
             pltpu.SemaphoreType.DMA((16,)),
         ],
-        compiler_params=pltpu.CompilerParams(vmem_limit_bytes=20 << 20),
+        compiler_params=pltpu.CompilerParams(vmem_limit_bytes=50 << 20),
         cost_estimate=pl.CostEstimate(
             flops=4 * rows * 8 * width * width, bytes_accessed=24 * width * width, transcendentals=0
         ),
@@ -94,24 +94,26 @@
     group_count = lax.axis_size("yl") * lax.axis_size("x")
     is_live = lax.broadcasted_iota(jnp.int32, (slots, 1), 0) < counts[0]
     kept_in, kept_out = (jnp.where(is_live, v, jnp.zeros_like(v)) for v in (activations, out_grads))
-    column, kept_out, partner = lax.optimization_barrier(
-        (spread(jnp.concatenate([basis, kept_in]), "yh"), kept_out, shift(owners, "core", 1))
+    owner_pair = [
+        (lax.rem(idx, blocks_per) * owned_width, lax.div(idx, blocks_per))
+        for idx in (owners[0], shift(owners, "core", 1)[0])
+    ]
+    column, kept_out, owner_pair = lax.optimization_barrier(
+        (spread(jnp.concatenate([basis, kept_in]), "yh"), kept_out, owner_pair)
     )
-    owner_pair = owners[0], partner[0]
     own = lax.all_gather(column[:, :owned_width], "z", axis=0)
     kept_in, kept_out = lax.optimization_barrier((column[:, owned_width:], spread(kept_out, "z")))
     kept_out = spread(kept_out.reshape(-1, width), "yh").reshape(-1, width)
     kept_in = lax.all_gather(kept_in.reshape(-1, width), "z", axis=0, tiled=True)
     pieces = []
-    for idx in owner_pair:
-        offset = idx % blocks_per * owned_width
+    for offset, _ in owner_pair:
         columns = [lax.dynamic_slice_in_dim(v, offset, owned_width, 1) for v in (kept_in, kept_out)]
         pieces.append(jnp.concatenate(columns).reshape(group_count, -1, owned_width))
     arrived = lax.all_to_all(jnp.concatenate(pieces, axis=1), GROUP, 0, 0, tiled=True)
     rows = pieces[0].shape[1]
     piece, for_other = (
-        lax.dynamic_slice(arrived, (idx // blocks_per, k * rows, 0), (1, rows, owned_width))[0]
-        for k, idx in enumerate(owner_pair)
+        lax.dynamic_slice(arrived, (root, k * rows, 0), (1, rows, owned_width))[0]
+        for k, (_, root) in enumerate(owner_pair)
     )
     theirs = shift(jnp.stack([kept_in, kept_out]), "core", 1)
     own, piece, for_other, theirs = lax.optimization_barrier((own, piece, for_other, theirs))

time: 166 us -> 161 us (0.970)
  waiting for transfers between devices: 40.7 us -> 38.1 us
  local copies, waits for them, and re-layouts: 11.4 us -> 9.05 us
    unnamed x8 -> x6, local copies, waits for them, and re-layouts: 2.36 us -> 0.02 us
    all_to_all x3, waiting for transfers between devices: 20.8 us -> 18.7 us  [spread(): lax.all_to_all(jnp.broadcast_to(block[None], (size,) + block.shape), axis...]
  transfers between devices with their start and end apart: 10 -> 10, of which waited for: 6 -> 7; matrix products, arithmetic and copies ran while one was open for 8% -> 8% of each run, Pallas kernels for 6% -> 6%
where the time goes in v12:
time: 161 us; the launch traced here: 160 us
  starting transfers between devices  50.6 us (31%)
  waiting for transfers between devices  38.1 us (24%)
  blocking collectives  25.6 us (16%)
  between operations  17.6 us (11%)
  Pallas kernels  10.3 us (6%)
  local copies, waits for them, and re-layouts  9.05 us (6%)
  matrix products  4.74 us (3%)
  other arithmetic  4.26 us (3%)
    all_gather x1, blocking collectives, shards(): lax.all_gather(kept_in.reshape(-1, width), 'z', axis=0, tiled=True)  25.6 us
    all_to_all x3, starting transfers between devices, spread(): lax.all_to_all(jnp.broadcast_to(block[None], (size,) + block.shape), axis...  22.6 us
    all_to_all x3, waiting for transfers between devices, spread(): lax.all_to_all(jnp.broadcast_to(block[None], (size,) + block.shape), axis...  18.7 us
    ppermute x3, starting transfers between devices, shift(): lax.ppermute(value, axis, [((i + by) % size, i) for i in range(size)])  15.9 us
    pallas_call x1, Pallas kernels, precondition(): pl.pallas_call(precondition_kernel, out_shape=(jax.ShapeDtypeStruct((8, r...  10.3 us
    all_to_all x1, waiting for transfers between devices, shards(): terms = lax.all_to_all(terms, GROUP, 0, 0, tiled=True)  8.91 us
    all_to_all x1, waiting for transfers between devices, shards(): lax.all_to_all(jnp.concatenate(pieces, axis=1), GROUP, 0, 0, tiled=True)  7.51 us
    dot_general x2, matrix products, shards(): lax.dot_general(theirs[k], owned_theirs[k], contract_rows, preferred_elem...  4.22 us
  transfers between devices with their start and end apart: 10, of which 7 were waited for; matrix products, arithmetic and copies ran while one was open for 8% of the time, Pallas kernels for 6%

profile of v12, /device:TPU:1, one launch (start us, length us, event | category | flops | bytes accessed | tf_op | source)
XLA Modules:
  0.0 160.2 jit_solution(13559399310198921747)
XLA Ops:
  7.8 0.8 broadcast_select_fusion
  8.7 0.9 pad_maximum_fusion.4
  9.6 0.9 broadcast_in_dim.43
  10.5 7.6 %all-to-all-start = ((bf16[4,112,768]{2,1,0:T(8,128)(2,1)}), bf16[4,112,768]{2,1,0:T(8,128)(2,1)S(1)}, u32[]{:S(2)}, u32[]{:S(2)}) async-start(bf16[4,112,768]{2,1,0:T(8,128)(2,1)} %broadcast_in_dim.43), calls=%async_computation | async-start | bytes 1376256 | tf_op jit(solution)/shard_map/all_to_all | solution.py:21
  18.1 4.7 %collective-permute-start = (s32[1]{0:T(128)}, s32[1]{0:T(128)}, u32[]{:S(2)}, u32[]{:S(2)}) collective-permute-start(s32[1]{0:T(128)} %param.11), channel_id=1, source_target_pairs={{8,0},{0,8},{9,1},{1,9},{10,2},{2,10},{11,3},{3,11},{12,4},{4,12},... | collective-permute-start | bytes 20 | tf_op jit(solution)/shard_map/ppermute | solution.py:16
  23.5 0.3 collective-permute-done
  25.8 10.0 %all-to-all-done = bf16[4,112,768]{2,1,0:T(8,128)(2,1)S(1)} async-done(((bf16[4,112,768]{2,1,0:T(8,128)(2,1)}), bf16[4,112,768]{2,1,0:T(8,128)(2,1)S(1)}, u32[]{:S(2)}, u32[]{:S(2)}) %all-to-all-start) | async-done | bytes 688160 | tf_op jit(solution)/shard_map/all_to_all | solution.py:21
  35.8 0.9 slice.29
  36.7 0.0 all-gather.3.cloned.1.call-update
  36.7 0.7 broadcast_in_dim.44
  37.4 10.0 %all-to-all-start.1 = ((bf16[8,16,768]{2,1,0:T(8,128)(2,1)}), bf16[8,16,768]{2,1,0:T(8,128)(2,1)S(1)}, u32[]{:S(2)}, u32[]{:S(2)}) async-start(bf16[8,16,768]{2,1,0:T(8,128)(2,1)} %broadcast_in_dim.44), calls=%async_computation.1 | async-start | bytes 393216 | tf_op jit(solution)/shard_map/all_to_all | solution.py:21
  47.5 8.7 %all-to-all-done.1 = bf16[8,16,768]{2,1,0:T(8,128)(2,1)S(1)} async-done(((bf16[8,16,768]{2,1,0:T(8,128)(2,1)}), bf16[8,16,768]{2,1,0:T(8,128)(2,1)S(1)}, u32[]{:S(2)}, u32[]{:S(2)}) %all-to-all-start.1) | async-done | bytes 196640 | tf_op jit(solution)/shard_map/all_to_all | solution.py:21
  56.1 0.2 copy.23
  56.3 1.0 broadcast_in_dim.46
  57.3 5.0 %all-to-all-start.2 = ((bf16[4,128,768]{1,2,0:T(8,128)(2,1)}), bf16[4,128,768]{1,2,0:T(8,128)(2,1)S(1)}, u32[]{:S(2)}, u32[]{:S(2)}) async-start(bf16[4,128,768]{1,2,0:T(8,128)(2,1)} %broadcast_in_dim.46), calls=%async_computation.2 | async-start | bytes 1572864 | tf_op jit(solution)/shard_map/all_to_all | solution.py:21
  62.3 25.6 %all_gather.9 = bf16[512,768]{1,0:T(8,128)(2,1)S(1)} all-gather(bf16[64,768]{1,0:T(8,128)(2,1)S(1)} %bitcast.58), channel_id=1, replica_groups=mesh['yh'=4,'z'=8,'core'=2,'yl'=2,'x'=4] {'z'}, dimensions={0}, use_global_device_ids=true | all-gather | bytes 884736 | tf_op jit(solution)/shard_map/all_gather | solution.py:107
  87.9 0.3 copy.24
  88.1 1.3 pad_maximum_fusion
  89.5 7.7 %collective-permute-start.1 = (bf16[2,512,768]{2,1,0:T(8,128)(2,1)}, bf16[2,512,768]{2,1,0:T(8,128)(2,1)}, u32[]{:S(2)}, u32[]{:S(2)}) collective-permute-start(bf16[2,512,768]{2,1,0:T(8,128)(2,1)} %pad_maximum_fusion), channel_id=1, source_target_pairs={{8,0},{0,8},{9,1},{1,9},{10,2},{2,10},{11,3},{3,11},{12,4},{4,12},... | collective-permute-start | bytes 4718600 | tf_op jit(solution)/shard_map/ppermute | solution.py:16
  97.2 0.2 constant_dynamic-slice_fusion.7
  97.4 0.2 constant_dynamic-slice_fusion.6
  97.6 0.1 pad_maximum_fusion.2
  97.7 0.2 copy.31
  97.9 0.2 copy.32
  98.1 0.0 copy-start.2
  98.1 0.0 copy-start
  98.1 0.8 copy.27
  99.0 4.0 %all-to-all-start.3 = ((bf16[8,256,96]{1,2,0:T(8,128)(2,1)}), bf16[8,256,96]{1,2,0:T(8,128)(2,1)S(1)}, u32[]{:S(2)}, u32[]{:S(2)}) async-start(bf16[8,256,96]{1,2,0:T(8,128)(2,1)} %copy.27), calls=%async_computation.3 | async-start | bytes 786432 | tf_op jit(solution)/shard_map/all_to_all | solution.py:112
  103.0 7.5 %all-to-all-done.3 = bf16[8,256,96]{1,2,0:T(8,128)(2,1)S(1)} async-done(((bf16[8,256,96]{1,2,0:T(8,128)(2,1)}), bf16[8,256,96]{1,2,0:T(8,128)(2,1)S(1)}, u32[]{:S(2)}, u32[]{:S(2)}) %all-to-all-start.3) | async-done | bytes 393248 | tf_op jit(solution)/shard_map/all_to_all | solution.py:112
  110.5 0.1 all-gather.3.cloned.1.call-done
  110.6 3.5 %collective-permute-start.2 = (bf16[8,4,96,768]{3,2,1,0:T(8,128)(2,1)}, bf16[8,4,96,768]{3,2,1,0:T(8,128)(2,1)}, u32[]{:S(2)}, u32[]{:S(2)}) collective-permute-start(bf16[8,4,96,768]{3,2,1,0:T(8,128)(2,1)} %bitcast.53), channel_id=1, source_target_pairs={{8,0},{0,8},{9,1},{1,9},{10,2},{2,10},{11,3},{3,11},{12,4},{4,12},... | collective-permute-start | bytes 14155784 | tf_op jit(solution)/shard_map/ppermute | solution.py:16
  114.1 0.8 broadcast_in_dim.47
  114.9 4.2 %all-to-all-start.4 = ((bf16[16,128,96]{1,2,0:T(8,128)(2,1)}), bf16[16,128,96]{1,2,0:T(8,128)(2,1)S(1)}, u32[]{:S(2)}, u32[]{:S(2)}) async-start(bf16[16,128,96]{1,2,0:T(8,128)(2,1)} %bitcast.15), calls=%async_computation.4 | async-start | bytes 786432 | tf_op jit(solution)/shard_map/all_to_all | solution.py:123
  119.2 0.1 copy.30.out_eigs
  119.3 0.1 pad_add_fusion.place
  119.3 2.6 %collective-permute-done.2.other = bf16[8,4,96,768]{3,2,1,0:T(8,128)(2,1)} collective-permute-done((bf16[8,4,96,768]{3,2,1,0:T(8,128)(2,1)}, bf16[8,4,96,768]{3,2,1,0:T(8,128)(2,1)}, u32[]{:S(2)}, u32[]{:S(2)}) %collective-permute-start.2) | collective-permute-done | bytes 4718624 | tf_op jit(solution)/shard_map/ppermute | solution.py:16
  122.0 10.3 %shard_map.103 = (bf16[8,96,768]{2,1,0:T(8,128)(2,1)}, f32[96,768]{1,0:T(8,128)S(1)}) custom-call(s32[2]{0:T(128)S(1)} %pad_add_fusion.place, bf16[8,4,96,768]{3,2,1,0:T(8,128)(2,1)} %bitcast.54, bf16[8,4,96,768]{3,2,1,0:T(8,128)(2,1)} %collective-permute-done.2.other, bf16[96,6144]{1,0:T(8,128)(2,1)S(1)} %copy-done, f32[1,768]{1,0:T(1,128)S(1)} %broadcast_in_dim.48.in_eigs, ...), custom_call_target="tpu_custom_call" | custom-call | flops 1811939328 | bytes 14155776 | tf_op jit(solution)/shard_map/pallas_call | solution.py:71
  132.3 3.8 %all-to-all-start.5 = ((bf16[8,96,768]{2,1,0:T(8,128)(2,1)}), bf16[8,96,768]{2,1,0:T(8,128)(2,1)S(1)}, u32[]{:S(2)}, u32[]{:S(2)}) async-start(bf16[8,96,768]{2,1,0:T(8,128)(2,1)} %get-tuple-element.30), calls=%async_computation.5 | async-start | bytes 2359296 | tf_op jit(solution)/shard_map/all_to_all | solution.py:141
  136.1 0.9 copy.29
  137.0 1.1 reshape.46
  138.2 0.6 constant_dynamic-slice_fusion.2
  138.8 0.3 fusion.8
  139.1 0.3 fusion.13
  139.3 2.1 %fusion.1 = f32[768,96]{0,1:T(8,128)} fusion(f32[768,96]{0,1:T(8,128)S(1)} %fusion.8, bf16[2,512,768]{2,1,0:T(8,128)(2,1)} %collective-permute-done.1, bf16[1,1,512,96]{2,1,0,3:T(2,128)(2,1)S(1)} %get-tuple-element.35), kind=kOutput, calls=%fused_computation.5 | convolution fusion | flops 75644928 | bytes 1474560 | tf_op jit(solution)/shard_map/dot_general | solution.py:133
  141.5 2.1 %fusion = f32[768,96]{0,1:T(8,128)} fusion(f32[768,96]{0,1:T(8,128)S(1)} %fusion.13, bf16[2,512,768]{2,1,0:T(8,128)(2,1)} %collective-permute-done.1, bf16[1,1,512,96]{2,1,0,3:T(2,128)(2,1)S(1)} %get-tuple-element.36), kind=kOutput, calls=%fused_computation.4 | convolution fusion | flops 75644928 | bytes 1474560 | tf_op jit(solution)/shard_map/dot_general | solution.py:133
  143.6 8.9 %all-to-all-done.5 = bf16[8,96,768]{2,1,0:T(8,128)(2,1)S(1)} async-done(((bf16[8,96,768]{2,1,0:T(8,128)(2,1)}), bf16[8,96,768]{2,1,0:T(8,128)(2,1)S(1)}, u32[]{:S(2)}, u32[]{:S(2)}) %all-to-all-start.5) | async-done | bytes 1179680 | tf_op jit(solution)/shard_map/all_to_all | solution.py:141
  152.5 0.2 convert_reduce_fusion
  152.6 0.7 add.43
  (15 shorter events, 0.1 us)
Async XLA Ops:
  10.5 25.3 %all-to-all-start = ((bf16[4,112,768]{2,1,0:T(8,128)(2,1)}), bf16[4,112,768]{2,1,0:T(8,128)(2,1)S(1)}, u32[]{:S(2)}, u32[]{:S(2)}) async-start(bf16[4,112,768]{2,1,0:T(8,128)(2,1)} %broadcast_in_dim.43), calls=%async_computation | async-start | bytes 1376256 | tf_op jit(solution)/shard_map/all_to_all | solution.py:21
  18.1 92.5 %all-gather.3.cloned.1.call-start = ((), (), s32[]{:S(2)}) async-start(), calls=%async_computation.6 | async-start | bytes 5308416 | tf_op jit(solution)/shard_map/all_gather | solution.py:104
  18.1 5.6 %collective-permute-start = (s32[1]{0:T(128)}, s32[1]{0:T(128)}, u32[]{:S(2)}, u32[]{:S(2)}) collective-permute-start(s32[1]{0:T(128)} %param.11), channel_id=1, source_target_pairs={{8,0},{0,8},{9,1},{1,9},{10,2},{2,10},{11,3},{3,11},{12,4},{4,12},... | collective-permute-start | bytes 20 | tf_op jit(solution)/shard_map/ppermute | solution.py:16
  37.4 18.7 %all-to-all-start.1 = ((bf16[8,16,768]{2,1,0:T(8,128)(2,1)}), bf16[8,16,768]{2,1,0:T(8,128)(2,1)S(1)}, u32[]{:S(2)}, u32[]{:S(2)}) async-start(bf16[8,16,768]{2,1,0:T(8,128)(2,1)} %broadcast_in_dim.44), calls=%async_computation.1 | async-start | bytes 393216 | tf_op jit(solution)/shard_map/all_to_all | solution.py:21
  57.3 30.5 %all-to-all-start.2 = ((bf16[4,128,768]{1,2,0:T(8,128)(2,1)}), bf16[4,128,768]{1,2,0:T(8,128)(2,1)S(1)}, u32[]{:S(2)}, u32[]{:S(2)}) async-start(bf16[4,128,768]{1,2,0:T(8,128)(2,1)} %broadcast_in_dim.46), calls=%async_computation.2 | async-start | bytes 1572864 | tf_op jit(solution)/shard_map/all_to_all | solution.py:21
  89.5 21.0 %collective-permute-start.1 = (bf16[2,512,768]{2,1,0:T(8,128)(2,1)}, bf16[2,512,768]{2,1,0:T(8,128)(2,1)}, u32[]{:S(2)}, u32[]{:S(2)}) collective-permute-start(bf16[2,512,768]{2,1,0:T(8,128)(2,1)} %pad_maximum_fusion), channel_id=1, source_target_pairs={{8,0},{0,8},{9,1},{1,9},{10,2},{2,10},{11,3},{3,11},{12,4},{4,12},... | collective-permute-start | bytes 4718600 | tf_op jit(solution)/shard_map/ppermute | solution.py:16
  98.1 21.0 %copy-start.1 = (f32[768]{0:T(1024)S(1)}, f32[768]{0:T(1024)}, u32[]{:S(2)}) copy-start(f32[768]{0:T(1024)} %param.14) | copy-start | bytes 9220
  98.1 21.1 %copy-start.2 = (f32[96]{0:T(128)S(1)}, f32[96]{0:T(128)}, u32[]{:S(2)}) copy-start(f32[96]{0:T(128)} %param.15) | copy-start | bytes 1156
  98.1 23.8 %copy-start = (bf16[96,6144]{1,0:T(8,128)(2,1)S(1)}, bf16[96,6144]{1,0:T(8,128)(2,1)}, u32[]{:S(2)}) copy-start(bf16[96,6144]{1,0:T(8,128)(2,1)} %grad.1) | copy-start | bytes 3538948
  99.0 11.5 %all-to-all-start.3 = ((bf16[8,256,96]{1,2,0:T(8,128)(2,1)}), bf16[8,256,96]{1,2,0:T(8,128)(2,1)S(1)}, u32[]{:S(2)}, u32[]{:S(2)}) async-start(bf16[8,256,96]{1,2,0:T(8,128)(2,1)} %copy.27), calls=%async_computation.3 | async-start | bytes 786432 | tf_op jit(solution)/shard_map/all_to_all | solution.py:112
  110.6 11.4 %collective-permute-start.2 = (bf16[8,4,96,768]{3,2,1,0:T(8,128)(2,1)}, bf16[8,4,96,768]{3,2,1,0:T(8,128)(2,1)}, u32[]{:S(2)}, u32[]{:S(2)}) collective-permute-start(bf16[8,4,96,768]{3,2,1,0:T(8,128)(2,1)} %bitcast.53), channel_id=1, source_target_pairs={{8,0},{0,8},{9,1},{1,9},{10,2},{2,10},{11,3},{3,11},{12,4},{4,12},... | collective-permute-start | bytes 14155784 | tf_op jit(solution)/shard_map/ppermute | solution.py:16
  114.9 17.4 %all-to-all-start.4 = ((bf16[16,128,96]{1,2,0:T(8,128)(2,1)}), bf16[16,128,96]{1,2,0:T(8,128)(2,1)S(1)}, u32[]{:S(2)}, u32[]{:S(2)}) async-start(bf16[16,128,96]{1,2,0:T(8,128)(2,1)} %bitcast.15), calls=%async_computation.4 | async-start | bytes 786432 | tf_op jit(solution)/shard_map/all_to_all | solution.py:123
  132.3 20.2 %all-to-all-start.5 = ((bf16[8,96,768]{2,1,0:T(8,128)(2,1)}), bf16[8,96,768]{2,1,0:T(8,128)(2,1)S(1)}, u32[]{:S(2)}, u32[]{:S(2)}) async-start(bf16[8,96,768]{2,1,0:T(8,128)(2,1)} %get-tuple-element.30), calls=%async_computation.5 | async-start | bytes 2359296 | tf_op jit(solution)/shard_map/all_to_all | solution.py:141
Sparse Core Ops, SparseCore 0:
  36.8 73.6 all-gather.2

commit v13 on v12

--- a/solution.py
+++ b/solution.py
@@ -115,8 +115,10 @@
         lax.dynamic_slice(arrived, (root, k * rows, 0), (1, rows, owned_width))[0]
         for k, (_, root) in enumerate(owner_pair)
     )
-    theirs = shift(jnp.stack([kept_in, kept_out]), "core", 1)
-    own, piece, for_other, theirs = lax.optimization_barrier((own, piece, for_other, theirs))
+    own, piece, for_other, samples = lax.optimization_barrier(
+        (own, piece, for_other, (kept_in, kept_out))
+    )
+    theirs = shift(jnp.stack(samples), "core", 1)
     core = lax.axis_index("core")
     shares = jnp.stack([jnp.where(core == k, piece, for_other) for k in range(2)])
     shares = jnp.broadcast_to(shares[:, None], (2, group_count) + piece.shape)

time: 161 us -> 163 us (1.012)
  waiting for transfers between devices: 38.1 us -> 44.6 us
  starting transfers between devices: 50.6 us -> 46.4 us
    all_gather x1, waiting for transfers between devices: 0.07 us -> 10.1 us  [shards(): own = lax.all_gather(column[:, :owned_width], 'z', axis=0)]
    ppermute x3, starting transfers between devices: 15.9 us -> 9.25 us  [shift(): lax.ppermute(value, axis, [((i + by) % size, i) for i in range(size)])]
    ppermute x3, waiting for transfers between devices: 2.87 us -> 0.28 us  [shift(): lax.ppermute(value, axis, [((i + by) % size, i) for i in range(size)])]
  transfers between devices with their start and end apart: 10 -> 10, of which waited for: 7 -> 6; matrix products, arithmetic and copies ran while one was open for 8% -> 8% of each run, Pallas kernels for 6% -> 6%
where the time goes in v13:
time: 163 us
  starting transfers between devices  46.4 us (28%)
  waiting for transfers between devices  44.6 us (27%)
  blocking collectives  25.6 us (16%)
  between operations  17.6 us (11%)
  Pallas kernels  10.4 us (6%)
  local copies, waits for them, and re-layouts  9.03 us (6%)
  matrix products  4.74 us (3%)
  other arithmetic  4.21 us (3%)
    all_gather x1, blocking collectives, shards(): lax.all_gather(kept_in.reshape(-1, width), 'z', axis=0, tiled=True)  25.6 us
    all_to_all x3, starting transfers between devices, spread(): lax.all_to_all(jnp.broadcast_to(block[None], (size,) + block.shape), axis...  22.6 us
    all_to_all x3, waiting for transfers between devices, spread(): lax.all_to_all(jnp.broadcast_to(block[None], (size,) + block.shape), axis...  18.7 us
    pallas_call x1, Pallas kernels, precondition(): pl.pallas_call(precondition_kernel, out_shape=(jax.ShapeDtypeStruct((8, r...  10.4 us
    all_gather x1, waiting for transfers between devices, shards(): own = lax.all_gather(column[:, :owned_width], 'z', axis=0)  10.1 us
    ppermute x3, starting transfers between devices, shift(): lax.ppermute(value, axis, [((i + by) % size, i) for i in range(size)])  9.25 us
    all_to_all x1, waiting for transfers between devices, shards(): terms = lax.all_to_all(terms, GROUP, 0, 0, tiled=True)  8.93 us
    all_to_all x1, waiting for transfers between devices, shards(): lax.all_to_all(jnp.concatenate(pieces, axis=1), GROUP, 0, 0, tiled=True)  6.6 us
  transfers between devices with their start and end apart: 10, of which 6 were waited for; matrix products, arithmetic and copies ran while one was open for 8% of the time, Pallas kernels for 6%

profile of v13, /device:TPU:1, one launch (start us, length us, event | category | flops | bytes accessed | tf_op | source)
XLA Modules:
  0.0 162.6 jit_solution(1846325254647616693)
XLA Ops:
  7.8 0.8 broadcast_select_fusion
  8.7 0.9 pad_maximum_fusion.4
  9.6 0.9 broadcast_in_dim.43
  10.5 7.6 %all-to-all-start = ((bf16[4,112,768]{2,1,0:T(8,128)(2,1)}), bf16[4,112,768]{2,1,0:T(8,128)(2,1)S(1)}, u32[]{:S(2)}, u32[]{:S(2)}) async-start(bf16[4,112,768]{2,1,0:T(8,128)(2,1)} %broadcast_in_dim.43), calls=%async_computation | async-start | bytes 1376256 | tf_op jit(solution)/shard_map/all_to_all | solution.py:21
  18.1 4.7 %collective-permute-start = (s32[1]{0:T(128)}, s32[1]{0:T(128)}, u32[]{:S(2)}, u32[]{:S(2)}) collective-permute-start(s32[1]{0:T(128)} %param.11), channel_id=1, source_target_pairs={{8,0},{0,8},{9,1},{1,9},{10,2},{2,10},{11,3},{3,11},{12,4},{4,12},... | collective-permute-start | bytes 20 | tf_op jit(solution)/shard_map/ppermute | solution.py:16
  23.5 0.3 collective-permute-done
  25.8 10.0 %all-to-all-done = bf16[4,112,768]{2,1,0:T(8,128)(2,1)S(1)} async-done(((bf16[4,112,768]{2,1,0:T(8,128)(2,1)}), bf16[4,112,768]{2,1,0:T(8,128)(2,1)S(1)}, u32[]{:S(2)}, u32[]{:S(2)}) %all-to-all-start) | async-done | bytes 688160 | tf_op jit(solution)/shard_map/all_to_all | solution.py:21
  35.8 0.9 slice.29
  36.7 0.0 all-gather.3.cloned.1.call-update
  36.7 0.7 broadcast_in_dim.44
  37.4 10.0 %all-to-all-start.1 = ((bf16[8,16,768]{2,1,0:T(8,128)(2,1)}), bf16[8,16,768]{2,1,0:T(8,128)(2,1)S(1)}, u32[]{:S(2)}, u32[]{:S(2)}) async-start(bf16[8,16,768]{2,1,0:T(8,128)(2,1)} %broadcast_in_dim.44), calls=%async_computation.1 | async-start | bytes 393216 | tf_op jit(solution)/shard_map/all_to_all | solution.py:21
  47.5 8.7 %all-to-all-done.1 = bf16[8,16,768]{2,1,0:T(8,128)(2,1)S(1)} async-done(((bf16[8,16,768]{2,1,0:T(8,128)(2,1)}), bf16[8,16,768]{2,1,0:T(8,128)(2,1)S(1)}, u32[]{:S(2)}, u32[]{:S(2)}) %all-to-all-start.1) | async-done | bytes 196640 | tf_op jit(solution)/shard_map/all_to_all | solution.py:21
  56.1 0.2 copy.23
  56.3 1.0 broadcast_in_dim.46
  57.3 5.0 %all-to-all-start.2 = ((bf16[4,128,768]{1,2,0:T(8,128)(2,1)}), bf16[4,128,768]{1,2,0:T(8,128)(2,1)S(1)}, u32[]{:S(2)}, u32[]{:S(2)}) async-start(bf16[4,128,768]{1,2,0:T(8,128)(2,1)} %broadcast_in_dim.46), calls=%async_computation.2 | async-start | bytes 1572864 | tf_op jit(solution)/shard_map/all_to_all | solution.py:21
  62.3 25.6 %all_gather.9 = bf16[512,768]{1,0:T(8,128)(2,1)S(1)} all-gather(bf16[64,768]{1,0:T(8,128)(2,1)S(1)} %bitcast.58), channel_id=1, replica_groups=mesh['yh'=4,'z'=8,'core'=2,'yl'=2,'x'=4] {'z'}, dimensions={0}, use_global_device_ids=true | all-gather | bytes 884736 | tf_op jit(solution)/shard_map/all_gather | solution.py:107
  87.9 0.1 constant_dynamic-slice_fusion.7
  88.0 0.0 all-to-all-done.2
  88.0 0.3 copy.24
  88.3 0.2 constant_dynamic-slice_fusion.6
  88.5 0.1 pad_maximum_fusion.2
  88.6 0.2 copy.30
  88.8 0.2 copy.31
  89.0 0.0 copy-start.1
  89.0 0.0 copy-start.2
  89.0 0.8 copy.27
  89.8 4.0 %all-to-all-start.3 = ((bf16[8,256,96]{1,2,0:T(8,128)(2,1)}), bf16[8,256,96]{1,2,0:T(8,128)(2,1)S(1)}, u32[]{:S(2)}, u32[]{:S(2)}) async-start(bf16[8,256,96]{1,2,0:T(8,128)(2,1)} %copy.27), calls=%async_computation.3 | async-start | bytes 786432 | tf_op jit(solution)/shard_map/all_to_all | solution.py:112
  93.9 6.6 %all-to-all-done.3 = bf16[8,256,96]{1,2,0:T(8,128)(2,1)S(1)} async-done(((bf16[8,256,96]{1,2,0:T(8,128)(2,1)}), bf16[8,256,96]{1,2,0:T(8,128)(2,1)S(1)}, u32[]{:S(2)}, u32[]{:S(2)}) %all-to-all-start.3) | async-done | bytes 393248 | tf_op jit(solution)/shard_map/all_to_all | solution.py:112
  100.5 10.1 %all-gather.3.cloned.1.call-done = bf16[32,96,768]{2,1,0:T(8,128)(2,1)} async-done(((bf16[4,96,768]{2,1,0:T(8,128)(2,1)}), bf16[32,96,768]{2,1,0:T(8,128)(2,1)}) %all-gather.3.cloned.1.call-update) | async-done | bytes 4718608 | tf_op jit(solution)/shard_map/all_gather | solution.py:104
  110.6 2.6 %collective-permute-start.2 = (bf16[8,4,96,768]{3,2,1,0:T(8,128)(2,1)}, bf16[8,4,96,768]{3,2,1,0:T(8,128)(2,1)}, u32[]{:S(2)}, u32[]{:S(2)}) collective-permute-start(bf16[8,4,96,768]{3,2,1,0:T(8,128)(2,1)} %bitcast.53), channel_id=1, source_target_pairs={{8,0},{0,8},{9,1},{1,9},{10,2},{2,10},{11,3},{3,11},{12,4},{4,12},... | collective-permute-start | bytes 14155784 | tf_op jit(solution)/shard_map/ppermute | solution.py:16
  113.2 0.8 broadcast_in_dim.47
  114.0 5.1 %all-to-all-start.4 = ((bf16[16,128,96]{1,2,0:T(8,128)(2,1)}), bf16[16,128,96]{1,2,0:T(8,128)(2,1)S(1)}, u32[]{:S(2)}, u32[]{:S(2)}) async-start(bf16[16,128,96]{1,2,0:T(8,128)(2,1)} %bitcast.13), calls=%async_computation.4 | async-start | bytes 786432 | tf_op jit(solution)/shard_map/all_to_all | solution.py:125
  119.2 0.1 copy.29.out_eigs
  119.3 0.1 pad_add_fusion.place
  119.3 1.3 pad_maximum_fusion
  120.6 2.0 %collective-permute-start.1 = (bf16[2,512,768]{2,1,0:T(8,128)(2,1)}, bf16[2,512,768]{2,1,0:T(8,128)(2,1)}, u32[]{:S(2)}, u32[]{:S(2)}) collective-permute-start(bf16[2,512,768]{2,1,0:T(8,128)(2,1)} %pad_maximum_fusion), channel_id=1, source_target_pairs={{8,0},{0,8},{9,1},{1,9},{10,2},{2,10},{11,3},{3,11},{12,4},{4,12},... | collective-permute-start | bytes 4718600 | tf_op jit(solution)/shard_map/ppermute | solution.py:16
  122.7 10.4 %shard_map.103 = (bf16[8,96,768]{2,1,0:T(8,128)(2,1)}, f32[96,768]{1,0:T(8,128)S(1)}) custom-call(s32[2]{0:T(128)S(1)} %pad_add_fusion.place, bf16[8,4,96,768]{3,2,1,0:T(8,128)(2,1)} %bitcast.54, bf16[8,4,96,768]{3,2,1,0:T(8,128)(2,1)} %collective-permute-done.2.other, bf16[96,6144]{1,0:T(8,128)(2,1)S(1)} %copy-done, f32[1,768]{1,0:T(1,128)S(1)} %broadcast_in_dim.48.in_eigs, ...), custom_call_target="tpu_custom_call" | custom-call | flops 1811939328 | bytes 14155776 | tf_op jit(solution)/shard_map/pallas_call | solution.py:71
  133.1 5.3 %all-to-all-start.5 = ((bf16[8,96,768]{2,1,0:T(8,128)(2,1)}), bf16[8,96,768]{2,1,0:T(8,128)(2,1)S(1)}, u32[]{:S(2)}, u32[]{:S(2)}) async-start(bf16[8,96,768]{2,1,0:T(8,128)(2,1)} %get-tuple-element.32), calls=%async_computation.5 | async-start | bytes 2359296 | tf_op jit(solution)/shard_map/all_to_all | solution.py:143
  138.4 0.9 copy.28
  139.3 1.1 reshape.46
  140.5 0.6 constant_dynamic-slice_fusion.2
  141.1 0.3 fusion.9
  141.4 0.3 fusion.4
  141.7 2.1 %fusion.1 = f32[768,96]{0,1:T(8,128)} fusion(f32[768,96]{0,1:T(8,128)S(1)} %fusion.4, bf16[2,512,768]{2,1,0:T(8,128)(2,1)} %collective-permute-done.1, bf16[1,1,512,96]{2,1,0,3:T(2,128)(2,1)S(1)} %get-tuple-element.37), kind=kOutput, calls=%fused_computation.5 | convolution fusion | flops 75644928 | bytes 1474560 | tf_op jit(solution)/shard_map/dot_general | solution.py:135
  143.8 2.1 %fusion = f32[768,96]{0,1:T(8,128)} fusion(f32[768,96]{0,1:T(8,128)S(1)} %fusion.9, bf16[2,512,768]{2,1,0:T(8,128)(2,1)} %collective-permute-done.1, bf16[1,1,512,96]{2,1,0,3:T(2,128)(2,1)S(1)} %get-tuple-element.38), kind=kOutput, calls=%fused_computation.4 | convolution fusion | flops 75644928 | bytes 1474560 | tf_op jit(solution)/shard_map/dot_general | solution.py:135
  145.9 8.9 %all-to-all-done.5 = bf16[8,96,768]{2,1,0:T(8,128)(2,1)S(1)} async-done(((bf16[8,96,768]{2,1,0:T(8,128)(2,1)}), bf16[8,96,768]{2,1,0:T(8,128)(2,1)S(1)}, u32[]{:S(2)}, u32[]{:S(2)}) %all-to-all-start.5) | async-done | bytes 1179680 | tf_op jit(solution)/shard_map/all_to_all | solution.py:143
  154.8 0.2 convert_reduce_fusion
  155.0 0.7 add.43
  (15 shorter events, 0.1 us)
Async XLA Ops:
  10.5 25.3 %all-to-all-start = ((bf16[4,112,768]{2,1,0:T(8,128)(2,1)}), bf16[4,112,768]{2,1,0:T(8,128)(2,1)S(1)}, u32[]{:S(2)}, u32[]{:S(2)}) async-start(bf16[4,112,768]{2,1,0:T(8,128)(2,1)} %broadcast_in_dim.43), calls=%async_computation | async-start | bytes 1376256 | tf_op jit(solution)/shard_map/all_to_all | solution.py:21
  18.1 92.5 %all-gather.3.cloned.1.call-start = ((), (), s32[]{:S(2)}) async-start(), calls=%async_computation.6 | async-start | bytes 5308416 | tf_op jit(solution)/shard_map/all_gather | solution.py:104
  18.1 5.6 %collective-permute-start = (s32[1]{0:T(128)}, s32[1]{0:T(128)}, u32[]{:S(2)}, u32[]{:S(2)}) collective-permute-start(s32[1]{0:T(128)} %param.11), channel_id=1, source_target_pairs={{8,0},{0,8},{9,1},{1,9},{10,2},{2,10},{11,3},{3,11},{12,4},{4,12},... | collective-permute-start | bytes 20 | tf_op jit(solution)/shard_map/ppermute | solution.py:16
  37.4 18.7 %all-to-all-start.1 = ((bf16[8,16,768]{2,1,0:T(8,128)(2,1)}), bf16[8,16,768]{2,1,0:T(8,128)(2,1)S(1)}, u32[]{:S(2)}, u32[]{:S(2)}) async-start(bf16[8,16,768]{2,1,0:T(8,128)(2,1)} %broadcast_in_dim.44), calls=%async_computation.1 | async-start | bytes 393216 | tf_op jit(solution)/shard_map/all_to_all | solution.py:21
  57.3 30.7 %all-to-all-start.2 = ((bf16[4,128,768]{1,2,0:T(8,128)(2,1)}), bf16[4,128,768]{1,2,0:T(8,128)(2,1)S(1)}, u32[]{:S(2)}, u32[]{:S(2)}) async-start(bf16[4,128,768]{1,2,0:T(8,128)(2,1)} %broadcast_in_dim.46), calls=%async_computation.2 | async-start | bytes 1572864 | tf_op jit(solution)/shard_map/all_to_all | solution.py:21
  89.0 30.1 %copy-start.1 = (f32[768]{0:T(1024)S(1)}, f32[768]{0:T(1024)}, u32[]{:S(2)}) copy-start(f32[768]{0:T(1024)} %param.14) | copy-start | bytes 9220
  89.0 30.1 %copy-start.2 = (f32[96]{0:T(128)S(1)}, f32[96]{0:T(128)}, u32[]{:S(2)}) copy-start(f32[96]{0:T(128)} %param.15) | copy-start | bytes 1156
  89.8 10.6 %all-to-all-start.3 = ((bf16[8,256,96]{1,2,0:T(8,128)(2,1)}), bf16[8,256,96]{1,2,0:T(8,128)(2,1)S(1)}, u32[]{:S(2)}, u32[]{:S(2)}) async-start(bf16[8,256,96]{1,2,0:T(8,128)(2,1)} %copy.27), calls=%async_computation.3 | async-start | bytes 786432 | tf_op jit(solution)/shard_map/all_to_all | solution.py:112
  110.6 12.1 %collective-permute-start.2 = (bf16[8,4,96,768]{3,2,1,0:T(8,128)(2,1)}, bf16[8,4,96,768]{3,2,1,0:T(8,128)(2,1)}, u32[]{:S(2)}, u32[]{:S(2)}) collective-permute-start(bf16[8,4,96,768]{3,2,1,0:T(8,128)(2,1)} %bitcast.53), channel_id=1, source_target_pairs={{8,0},{0,8},{9,1},{1,9},{10,2},{2,10},{11,3},{3,11},{12,4},{4,12},... | collective-permute-start | bytes 14155784 | tf_op jit(solution)/shard_map/ppermute | solution.py:16
  114.0 19.1 %all-to-all-start.4 = ((bf16[16,128,96]{1,2,0:T(8,128)(2,1)}), bf16[16,128,96]{1,2,0:T(8,128)(2,1)S(1)}, u32[]{:S(2)}, u32[]{:S(2)}) async-start(bf16[16,128,96]{1,2,0:T(8,128)(2,1)} %bitcast.13), calls=%async_computation.4 | async-start | bytes 786432 | tf_op jit(solution)/shard_map/all_to_all | solution.py:125
  119.3 3.3 %copy-start = (bf16[96,6144]{1,0:T(8,128)(2,1)S(1)}, bf16[96,6144]{1,0:T(8,128)(2,1)}, u32[]{:S(2)}) copy-start(bf16[96,6144]{1,0:T(8,128)(2,1)} %grad.1) | copy-start | bytes 3538948
  120.6 21.0 %collective-permute-start.1 = (bf16[2,512,768]{2,1,0:T(8,128)(2,1)}, bf16[2,512,768]{2,1,0:T(8,128)(2,1)}, u32[]{:S(2)}, u32[]{:S(2)}) collective-permute-start(bf16[2,512,768]{2,1,0:T(8,128)(2,1)} %pad_maximum_fusion), channel_id=1, source_target_pairs={{8,0},{0,8},{9,1},{1,9},{10,2},{2,10},{11,3},{3,11},{12,4},{4,12},... | collective-permute-start | bytes 4718600 | tf_op jit(solution)/shard_map/ppermute | solution.py:16
  133.1 21.7 %all-to-all-start.5 = ((bf16[8,96,768]{2,1,0:T(8,128)(2,1)}), bf16[8,96,768]{2,1,0:T(8,128)(2,1)S(1)}, u32[]{:S(2)}, u32[]{:S(2)}) async-start(bf16[8,96,768]{2,1,0:T(8,128)(2,1)} %get-tuple-element.32), calls=%async_computation.5 | async-start | bytes 2359296 | tf_op jit(solution)/shard_map/all_to_all | solution.py:143
Sparse Core Ops, SparseCore 0:
  36.8 73.6 all-gather.2

commit v14 on v12

--- a/solution.py
+++ b/solution.py
@@ -93,13 +93,16 @@
     blocks_per = width // owned_width
     group_count = lax.axis_size("yl") * lax.axis_size("x")
     is_live = lax.broadcasted_iota(jnp.int32, (slots, 1), 0) < counts[0]
-    kept_in, kept_out = (jnp.where(is_live, v, jnp.zeros_like(v)) for v in (activations, out_grads))
+    kept_out = jnp.where(is_live, out_grads, jnp.zeros_like(out_grads))
+    joined = jnp.concatenate([basis, activations])
+    row = lax.broadcasted_iota(jnp.int32, (joined.shape[0], 1), 0)
+    joined = jnp.where(row < owned_width + counts[0], joined, jnp.zeros_like(joined))
     owner_pair = [
         (lax.rem(idx, blocks_per) * owned_width, lax.div(idx, blocks_per))
         for idx in (owners[0], shift(owners, "core", 1)[0])
     ]
     column, kept_out, owner_pair = lax.optimization_barrier(
-        (spread(jnp.concatenate([basis, kept_in]), "yh"), kept_out, owner_pair)
+        (spread(joined, "yh"), kept_out, owner_pair)
     )
     own = lax.all_gather(column[:, :owned_width], "z", axis=0)
     kept_in, kept_out = lax.optimization_barrier((column[:, owned_width:], spread(kept_out, "z")))

time: 161 us -> 160 us (level)
  transfers between devices with their start and end apart: 10 -> 10, of which waited for: 7 -> 7; matrix products, arithmetic and copies ran while one was open for 8% -> 9% of each run, Pallas kernels for 6% -> 6%
where the time goes in v14:
time: 160 us
  starting transfers between devices  50.6 us (32%)
  waiting for transfers between devices  38 us (24%)
  blocking collectives  25.6 us (16%)
  between operations  17.6 us (11%)
  Pallas kernels  10.3 us (6%)
  local copies, waits for them, and re-layouts  9.07 us (6%)
  matrix products  4.74 us (3%)
  other arithmetic  3.61 us (2%)
    all_gather x1, blocking collectives, shards(): lax.all_gather(kept_in.reshape(-1, width), 'z', axis=0, tiled=True)  25.6 us
    all_to_all x3, starting transfers between devices, spread(): lax.all_to_all(jnp.broadcast_to(block[None], (size,) + block.shape), axis...  22.6 us
    all_to_all x3, waiting for transfers between devices, spread(): lax.all_to_all(jnp.broadcast_to(block[None], (size,) + block.shape), axis...  18.7 us
    ppermute x3, starting transfers between devices, shift(): lax.ppermute(value, axis, [((i + by) % size, i) for i in range(size)])  15.9 us
    pallas_call x1, Pallas kernels, precondition(): pl.pallas_call(precondition_kernel, out_shape=(jax.ShapeDtypeStruct((8, r...  10.3 us
    all_to_all x1, waiting for transfers between devices, shards(): terms = lax.all_to_all(terms, GROUP, 0, 0, tiled=True)  8.9 us
    all_to_all x1, waiting for transfers between devices, shards(): lax.all_to_all(jnp.concatenate(pieces, axis=1), GROUP, 0, 0, tiled=True)  7.52 us
    dot_general x2, matrix products, shards(): lax.dot_general(theirs[k], owned_theirs[k], contract_rows, preferred_elem...  4.22 us
  transfers between devices with their start and end apart: 10, of which 7 were waited for; matrix products, arithmetic and copies ran while one was open for 9% of the time, Pallas kernels for 6%

profile of v14, /device:TPU:1, one launch (start us, length us, event | category | flops | bytes accessed | tf_op | source)
XLA Modules:
  0.0 159.5 jit_solution(9280467525964078612)
XLA Ops:
  7.8 1.0 maximum_select_fusion
  8.9 0.9 broadcast_in_dim.55
  9.8 7.6 %all-to-all-start = ((bf16[4,112,768]{2,1,0:T(8,128)(2,1)}), bf16[4,112,768]{2,1,0:T(8,128)(2,1)S(1)}, u32[]{:S(2)}, u32[]{:S(2)}) async-start(bf16[4,112,768]{2,1,0:T(8,128)(2,1)} %broadcast_in_dim.55), calls=%async_computation | async-start | bytes 1376256 | tf_op jit(solution)/shard_map/all_to_all | solution.py:21
  17.4 4.7 %collective-permute-start = (s32[1]{0:T(128)}, s32[1]{0:T(128)}, u32[]{:S(2)}, u32[]{:S(2)}) collective-permute-start(s32[1]{0:T(128)} %param.11), channel_id=1, source_target_pairs={{8,0},{0,8},{9,1},{1,9},{10,2},{2,10},{11,3},{3,11},{12,4},{4,12},... | collective-permute-start | bytes 20 | tf_op jit(solution)/shard_map/ppermute | solution.py:16
  22.8 0.1 broadcast_select_fusion
  22.9 0.2 collective-permute-done
  25.1 10.0 %all-to-all-done = bf16[4,112,768]{2,1,0:T(8,128)(2,1)S(1)} async-done(((bf16[4,112,768]{2,1,0:T(8,128)(2,1)}), bf16[4,112,768]{2,1,0:T(8,128)(2,1)S(1)}, u32[]{:S(2)}, u32[]{:S(2)}) %all-to-all-start) | async-done | bytes 688160 | tf_op jit(solution)/shard_map/all_to_all | solution.py:21
  35.1 0.9 slice.29
  36.0 0.0 all-gather.3.cloned.1.call-update
  36.0 0.7 broadcast_in_dim.58
  36.7 10.0 %all-to-all-start.1 = ((bf16[8,16,768]{2,1,0:T(8,128)(2,1)}), bf16[8,16,768]{2,1,0:T(8,128)(2,1)S(1)}, u32[]{:S(2)}, u32[]{:S(2)}) async-start(bf16[8,16,768]{2,1,0:T(8,128)(2,1)} %broadcast_in_dim.58), calls=%async_computation.1 | async-start | bytes 393216 | tf_op jit(solution)/shard_map/all_to_all | solution.py:21
  46.8 8.7 %all-to-all-done.1 = bf16[8,16,768]{2,1,0:T(8,128)(2,1)S(1)} async-done(((bf16[8,16,768]{2,1,0:T(8,128)(2,1)}), bf16[8,16,768]{2,1,0:T(8,128)(2,1)S(1)}, u32[]{:S(2)}, u32[]{:S(2)}) %all-to-all-start.1) | async-done | bytes 196640 | tf_op jit(solution)/shard_map/all_to_all | solution.py:21
  55.4 0.2 copy.23
  55.6 1.0 broadcast_in_dim.60
  56.6 5.0 %all-to-all-start.2 = ((bf16[4,128,768]{1,2,0:T(8,128)(2,1)}), bf16[4,128,768]{1,2,0:T(8,128)(2,1)S(1)}, u32[]{:S(2)}, u32[]{:S(2)}) async-start(bf16[4,128,768]{1,2,0:T(8,128)(2,1)} %broadcast_in_dim.60), calls=%async_computation.2 | async-start | bytes 1572864 | tf_op jit(solution)/shard_map/all_to_all | solution.py:21
  61.6 25.6 %all_gather.9 = bf16[512,768]{1,0:T(8,128)(2,1)S(1)} all-gather(bf16[64,768]{1,0:T(8,128)(2,1)S(1)} %bitcast.59), channel_id=1, replica_groups=mesh['yh'=4,'z'=8,'core'=2,'yl'=2,'x'=4] {'z'}, dimensions={0}, use_global_device_ids=true | all-gather | bytes 884736 | tf_op jit(solution)/shard_map/all_gather | solution.py:110
  87.1 0.3 copy.24
  87.4 1.3 pad_maximum_fusion
  88.8 7.7 %collective-permute-start.1 = (bf16[2,512,768]{2,1,0:T(8,128)(2,1)}, bf16[2,512,768]{2,1,0:T(8,128)(2,1)}, u32[]{:S(2)}, u32[]{:S(2)}) collective-permute-start(bf16[2,512,768]{2,1,0:T(8,128)(2,1)} %pad_maximum_fusion), channel_id=1, source_target_pairs={{8,0},{0,8},{9,1},{1,9},{10,2},{2,10},{11,3},{3,11},{12,4},{4,12},... | collective-permute-start | bytes 4718600 | tf_op jit(solution)/shard_map/ppermute | solution.py:16
  96.5 0.2 constant_dynamic-slice_fusion.7
  96.7 0.2 constant_dynamic-slice_fusion.6
  96.9 0.1 pad_maximum_fusion.2
  97.0 0.2 copy.31
  97.2 0.2 copy.32
  97.4 0.0 copy-start.3
  97.4 0.0 copy-start
  97.4 0.8 copy.27
  98.3 4.0 %all-to-all-start.3 = ((bf16[8,256,96]{1,2,0:T(8,128)(2,1)}), bf16[8,256,96]{1,2,0:T(8,128)(2,1)S(1)}, u32[]{:S(2)}, u32[]{:S(2)}) async-start(bf16[8,256,96]{1,2,0:T(8,128)(2,1)} %copy.27), calls=%async_computation.3 | async-start | bytes 786432 | tf_op jit(solution)/shard_map/all_to_all | solution.py:115
  102.3 7.5 %all-to-all-done.3 = bf16[8,256,96]{1,2,0:T(8,128)(2,1)S(1)} async-done(((bf16[8,256,96]{1,2,0:T(8,128)(2,1)}), bf16[8,256,96]{1,2,0:T(8,128)(2,1)S(1)}, u32[]{:S(2)}, u32[]{:S(2)}) %all-to-all-start.3) | async-done | bytes 393248 | tf_op jit(solution)/shard_map/all_to_all | solution.py:115
  109.8 0.1 all-gather.3.cloned.1.call-done
  109.9 3.5 %collective-permute-start.2 = (bf16[8,4,96,768]{3,2,1,0:T(8,128)(2,1)}, bf16[8,4,96,768]{3,2,1,0:T(8,128)(2,1)}, u32[]{:S(2)}, u32[]{:S(2)}) collective-permute-start(bf16[8,4,96,768]{3,2,1,0:T(8,128)(2,1)} %bitcast.54), channel_id=1, source_target_pairs={{8,0},{0,8},{9,1},{1,9},{10,2},{2,10},{11,3},{3,11},{12,4},{4,12},... | collective-permute-start | bytes 14155784 | tf_op jit(solution)/shard_map/ppermute | solution.py:16
  113.4 0.8 broadcast_in_dim.61
  114.2 4.2 %all-to-all-start.4 = ((bf16[16,128,96]{1,2,0:T(8,128)(2,1)}), bf16[16,128,96]{1,2,0:T(8,128)(2,1)S(1)}, u32[]{:S(2)}, u32[]{:S(2)}) async-start(bf16[16,128,96]{1,2,0:T(8,128)(2,1)} %bitcast.15), calls=%async_computation.4 | async-start | bytes 786432 | tf_op jit(solution)/shard_map/all_to_all | solution.py:126
  118.5 0.1 copy.30.out_eigs
  118.6 0.1 pad_add_fusion.place
  118.6 2.6 %collective-permute-done.2.other = bf16[8,4,96,768]{3,2,1,0:T(8,128)(2,1)} collective-permute-done((bf16[8,4,96,768]{3,2,1,0:T(8,128)(2,1)}, bf16[8,4,96,768]{3,2,1,0:T(8,128)(2,1)}, u32[]{:S(2)}, u32[]{:S(2)}) %collective-permute-start.2) | collective-permute-done | bytes 4718624 | tf_op jit(solution)/shard_map/ppermute | solution.py:16
  121.3 10.3 %shard_map.103 = (bf16[8,96,768]{2,1,0:T(8,128)(2,1)}, f32[96,768]{1,0:T(8,128)S(1)}) custom-call(s32[2]{0:T(128)S(1)} %pad_add_fusion.place, bf16[8,4,96,768]{3,2,1,0:T(8,128)(2,1)} %bitcast.55, bf16[8,4,96,768]{3,2,1,0:T(8,128)(2,1)} %collective-permute-done.2.other, bf16[96,6144]{1,0:T(8,128)(2,1)S(1)} %copy-done, f32[1,768]{1,0:T(1,128)S(1)} %broadcast_in_dim.62.in_eigs, ...), custom_call_target="tpu_custom_call" | custom-call | flops 1811939328 | bytes 14155776 | tf_op jit(solution)/shard_map/pallas_call | solution.py:71
  131.6 3.8 %all-to-all-start.5 = ((bf16[8,96,768]{2,1,0:T(8,128)(2,1)}), bf16[8,96,768]{2,1,0:T(8,128)(2,1)S(1)}, u32[]{:S(2)}, u32[]{:S(2)}) async-start(bf16[8,96,768]{2,1,0:T(8,128)(2,1)} %get-tuple-element.30), calls=%async_computation.5 | async-start | bytes 2359296 | tf_op jit(solution)/shard_map/all_to_all | solution.py:144
  135.4 0.9 copy.29
  136.3 1.1 reshape.77
  137.4 0.6 constant_dynamic-slice_fusion.2
  138.1 0.3 fusion.8
  138.4 0.3 fusion.13
  138.6 2.1 %fusion.1 = f32[768,96]{0,1:T(8,128)} fusion(f32[768,96]{0,1:T(8,128)S(1)} %fusion.8, bf16[2,512,768]{2,1,0:T(8,128)(2,1)} %collective-permute-done.1, bf16[1,1,512,96]{2,1,0,3:T(2,128)(2,1)S(1)} %get-tuple-element.35), kind=kOutput, calls=%fused_computation.5 | convolution fusion | flops 75644928 | bytes 1474560 | tf_op jit(solution)/shard_map/dot_general | solution.py:136
  140.7 2.1 %fusion = f32[768,96]{0,1:T(8,128)} fusion(f32[768,96]{0,1:T(8,128)S(1)} %fusion.13, bf16[2,512,768]{2,1,0:T(8,128)(2,1)} %collective-permute-done.1, bf16[1,1,512,96]{2,1,0,3:T(2,128)(2,1)S(1)} %get-tuple-element.36), kind=kOutput, calls=%fused_computation.4 | convolution fusion | flops 75644928 | bytes 1474560 | tf_op jit(solution)/shard_map/dot_general | solution.py:136
  142.8 8.9 %all-to-all-done.5 = bf16[8,96,768]{2,1,0:T(8,128)(2,1)S(1)} async-done(((bf16[8,96,768]{2,1,0:T(8,128)(2,1)}), bf16[8,96,768]{2,1,0:T(8,128)(2,1)S(1)}, u32[]{:S(2)}, u32[]{:S(2)}) %all-to-all-start.5) | async-done | bytes 1179680 | tf_op jit(solution)/shard_map/all_to_all | solution.py:144
  151.8 0.2 convert_reduce_fusion
  151.9 0.7 add.47
  (18 shorter events, 0.1 us)
Async XLA Ops:
  7.2 15.6 %copy-start.1 = (bf16[16,768]{1,0:T(8,128)(2,1)S(1)}, bf16[16,768]{1,0:T(8,128)(2,1)}, u32[]{:S(2)}) copy-start(bf16[16,768]{1,0:T(8,128)(2,1)} %param.9) | copy-start | bytes 73732
  9.8 25.3 %all-to-all-start = ((bf16[4,112,768]{2,1,0:T(8,128)(2,1)}), bf16[4,112,768]{2,1,0:T(8,128)(2,1)S(1)}, u32[]{:S(2)}, u32[]{:S(2)}) async-start(bf16[4,112,768]{2,1,0:T(8,128)(2,1)} %broadcast_in_dim.55), calls=%async_computation | async-start | bytes 1376256 | tf_op jit(solution)/shard_map/all_to_all | solution.py:21
  17.4 92.5 %all-gather.3.cloned.1.call-start = ((), (), s32[]{:S(2)}) async-start(), calls=%async_computation.6 | async-start | bytes 5308416 | tf_op jit(solution)/shard_map/all_gather | solution.py:107
  17.4 5.6 %collective-permute-start = (s32[1]{0:T(128)}, s32[1]{0:T(128)}, u32[]{:S(2)}, u32[]{:S(2)}) collective-permute-start(s32[1]{0:T(128)} %param.11), channel_id=1, source_target_pairs={{8,0},{0,8},{9,1},{1,9},{10,2},{2,10},{11,3},{3,11},{12,4},{4,12},... | collective-permute-start | bytes 20 | tf_op jit(solution)/shard_map/ppermute | solution.py:16
  36.7 18.7 %all-to-all-start.1 = ((bf16[8,16,768]{2,1,0:T(8,128)(2,1)}), bf16[8,16,768]{2,1,0:T(8,128)(2,1)S(1)}, u32[]{:S(2)}, u32[]{:S(2)}) async-start(bf16[8,16,768]{2,1,0:T(8,128)(2,1)} %broadcast_in_dim.58), calls=%async_computation.1 | async-start | bytes 393216 | tf_op jit(solution)/shard_map/all_to_all | solution.py:21
  56.6 30.5 %all-to-all-start.2 = ((bf16[4,128,768]{1,2,0:T(8,128)(2,1)}), bf16[4,128,768]{1,2,0:T(8,128)(2,1)S(1)}, u32[]{:S(2)}, u32[]{:S(2)}) async-start(bf16[4,128,768]{1,2,0:T(8,128)(2,1)} %broadcast_in_dim.60), calls=%async_computation.2 | async-start | bytes 1572864 | tf_op jit(solution)/shard_map/all_to_all | solution.py:21
  88.8 21.0 %collective-permute-start.1 = (bf16[2,512,768]{2,1,0:T(8,128)(2,1)}, bf16[2,512,768]{2,1,0:T(8,128)(2,1)}, u32[]{:S(2)}, u32[]{:S(2)}) collective-permute-start(bf16[2,512,768]{2,1,0:T(8,128)(2,1)} %pad_maximum_fusion), channel_id=1, source_target_pairs={{8,0},{0,8},{9,1},{1,9},{10,2},{2,10},{11,3},{3,11},{12,4},{4,12},... | collective-permute-start | bytes 4718600 | tf_op jit(solution)/shard_map/ppermute | solution.py:16
  97.4 21.0 %copy-start.2 = (f32[768]{0:T(1024)S(1)}, f32[768]{0:T(1024)}, u32[]{:S(2)}) copy-start(f32[768]{0:T(1024)} %param.14) | copy-start | bytes 9220
  97.4 21.0 %copy-start.3 = (f32[96]{0:T(128)S(1)}, f32[96]{0:T(128)}, u32[]{:S(2)}) copy-start(f32[96]{0:T(128)} %param.15) | copy-start | bytes 1156
  97.4 23.8 %copy-start = (bf16[96,6144]{1,0:T(8,128)(2,1)S(1)}, bf16[96,6144]{1,0:T(8,128)(2,1)}, u32[]{:S(2)}) copy-start(bf16[96,6144]{1,0:T(8,128)(2,1)} %grad.1) | copy-start | bytes 3538948
  98.3 11.5 %all-to-all-start.3 = ((bf16[8,256,96]{1,2,0:T(8,128)(2,1)}), bf16[8,256,96]{1,2,0:T(8,128)(2,1)S(1)}, u32[]{:S(2)}, u32[]{:S(2)}) async-start(bf16[8,256,96]{1,2,0:T(8,128)(2,1)} %copy.27), calls=%async_computation.3 | async-start | bytes 786432 | tf_op jit(solution)/shard_map/all_to_all | solution.py:115
  109.9 11.4 %collective-permute-start.2 = (bf16[8,4,96,768]{3,2,1,0:T(8,128)(2,1)}, bf16[8,4,96,768]{3,2,1,0:T(8,128)(2,1)}, u32[]{:S(2)}, u32[]{:S(2)}) collective-permute-start(bf16[8,4,96,768]{3,2,1,0:T(8,128)(2,1)} %bitcast.54), channel_id=1, source_target_pairs={{8,0},{0,8},{9,1},{1,9},{10,2},{2,10},{11,3},{3,11},{12,4},{4,12},... | collective-permute-start | bytes 14155784 | tf_op jit(solution)/shard_map/ppermute | solution.py:16
  114.2 17.4 %all-to-all-start.4 = ((bf16[16,128,96]{1,2,0:T(8,128)(2,1)}), bf16[16,128,96]{1,2,0:T(8,128)(2,1)S(1)}, u32[]{:S(2)}, u32[]{:S(2)}) async-start(bf16[16,128,96]{1,2,0:T(8,128)(2,1)} %bitcast.15), calls=%async_computation.4 | async-start | bytes 786432 | tf_op jit(solution)/shard_map/all_to_all | solution.py:126
  131.6 20.1 %all-to-all-start.5 = ((bf16[8,96,768]{2,1,0:T(8,128)(2,1)}), bf16[8,96,768]{2,1,0:T(8,128)(2,1)S(1)}, u32[]{:S(2)}, u32[]{:S(2)}) async-start(bf16[8,96,768]{2,1,0:T(8,128)(2,1)} %get-tuple-element.30), calls=%async_computation.5 | async-start | bytes 2359296 | tf_op jit(solution)/shard_map/all_to_all | solution.py:144
Sparse Core Ops, SparseCore 0:
  36.1 73.6 all-gather.2

commit v15 on v14

--- a/solution.py
+++ b/solution.py
@@ -21,7 +21,7 @@
     return lax.all_to_all(jnp.broadcast_to(block[None], (size,) + block.shape), axis, 0, 0, tiled=True)
 
 
-def precondition_kernel(place, own, other, grad, in_eigs, out_eigs, terms, kept, basis, sems):
+def precondition_kernel(place, own, other, grad, in_eigs, out_eigs, terms, kept, basis, staged, sems):
     core, member = place[0], place[1]
     rows, width = in_eigs.shape[1], basis.shape[-1]
     steps = basis.shape[0] * 2
@@ -50,6 +50,7 @@
         )
     denominator = out_eigs[...] * in_eigs[...] + DAMPING
     scaled = (projected / denominator).astype(jnp.bfloat16)
+    sent = []
     for k in range(steps):
         share = lax.dot_general(
             scaled, block(k), (((1,), (1,)), ((), ())), preferred_element_type=jnp.float32
@@ -59,7 +60,11 @@
         def _():
             kept[...] = share
 
-        terms[k] = jnp.where(member == k, 0.0, share).astype(terms.dtype)
+        staged[k] = jnp.where(member == k, 0.0, share).astype(staged.dtype)
+        sent.append(pltpu.make_async_copy(staged.at[k], terms.at[k], sems.at[2 * steps + k]))
+        sent[k].start()
+    for copy in sent:
+        copy.wait()
 
 
 def precondition(own, other, grad, in_eigs, out_eigs):
@@ -75,10 +80,11 @@
             jax.ShapeDtypeStruct((rows, width), jnp.float32),
         ),
         in_specs=[pl.BlockSpec(memory_space=pltpu.SMEM), hbm, hbm, vmem, vmem, vmem],
-        out_specs=(vmem, vmem),
+        out_specs=(hbm, vmem),
         scratch_shapes=[
             pltpu.VMEM((4, 8, 2, rows, width), jnp.bfloat16),
-            pltpu.SemaphoreType.DMA((16,)),
+            pltpu.VMEM((8, rows, width), jnp.bfloat16),
+            pltpu.SemaphoreType.DMA((24,)),
         ],
         compiler_params=pltpu.CompilerParams(vmem_limit_bytes=50 << 20),
         cost_estimate=pl.CostEstimate(
@@ -142,7 +148,9 @@
     other = shift(own, "core", 1)
     terms, own_term = precondition(own, other, rotated_grad, input_eigs, output_eigs)
     terms = lax.all_to_all(terms, GROUP, 0, 0, tiled=True)
-    preconditioned = own_term + jnp.sum(terms.astype(jnp.float32), axis=0)
+    preconditioned = own_term
+    for k in range(group_count):
+        preconditioned += terms[k].astype(jnp.float32)
     return (cov_in, cov_out, preconditioned)
 
 

time: 160 us -> 160 us (level)
  no operation moved by 1% of the time
where the time goes in v15:
time: 160 us; the launch traced here: 159 us
  starting transfers between devices  50.6 us (32%)
  waiting for transfers between devices  38.1 us (24%)
  blocking collectives  25.6 us (16%)
  between operations  17.5 us (11%)
  Pallas kernels  10.1 us (6%)
  local copies, waits for them, and re-layouts  9.06 us (6%)
  matrix products  4.74 us (3%)
  other arithmetic  3.57 us (2%)
    all_gather x1, blocking collectives, shards(): lax.all_gather(kept_in.reshape(-1, width), 'z', axis=0, tiled=True)  25.6 us
    all_to_all x3, starting transfers between devices, spread(): lax.all_to_all(jnp.broadcast_to(block[None], (size,) + block.shape), axis...  22.6 us
    all_to_all x3, waiting for transfers between devices, spread(): lax.all_to_all(jnp.broadcast_to(block[None], (size,) + block.shape), axis...  18.7 us
    ppermute x3, starting transfers between devices, shift(): lax.ppermute(value, axis, [((i + by) % size, i) for i in range(size)])  15.9 us
    pallas_call x1, Pallas kernels, precondition(): pl.pallas_call(precondition_kernel, out_shape=(jax.ShapeDtypeStruct((8, r...  10.1 us
    all_to_all x1, waiting for transfers between devices, shards(): terms = lax.all_to_all(terms, GROUP, 0, 0, tiled=True)  8.89 us
    all_to_all x1, waiting for transfers between devices, shards(): lax.all_to_all(jnp.concatenate(pieces, axis=1), GROUP, 0, 0, tiled=True)  7.51 us
    dot_general x2, matrix products, shards(): lax.dot_general(theirs[k], owned_theirs[k], contract_rows, preferred_elem...  4.22 us
  transfers between devices with their start and end apart: 10, of which 7 were waited for; matrix products, arithmetic and copies ran while one was open for 9% of the time, Pallas kernels for 6%

profile of v15, /device:TPU:1, one launch (start us, length us, event | category | flops | bytes accessed | tf_op | source)
XLA Modules:
  0.0 159.3 jit_solution(725020320783400530)
XLA Ops:
  7.8 1.0 maximum_select_fusion
  8.9 0.9 broadcast_in_dim.55
  9.8 7.6 %all-to-all-start = ((bf16[4,112,768]{2,1,0:T(8,128)(2,1)}), bf16[4,112,768]{2,1,0:T(8,128)(2,1)S(1)}, u32[]{:S(2)}, u32[]{:S(2)}) async-start(bf16[4,112,768]{2,1,0:T(8,128)(2,1)} %broadcast_in_dim.55), calls=%async_computation | async-start | bytes 1376256 | tf_op jit(solution)/shard_map/all_to_all | solution.py:21
  17.4 4.7 %collective-permute-start = (s32[1]{0:T(128)}, s32[1]{0:T(128)}, u32[]{:S(2)}, u32[]{:S(2)}) collective-permute-start(s32[1]{0:T(128)} %param.11), channel_id=1, source_target_pairs={{8,0},{0,8},{9,1},{1,9},{10,2},{2,10},{11,3},{3,11},{12,4},{4,12},... | collective-permute-start | bytes 20 | tf_op jit(solution)/shard_map/ppermute | solution.py:16
  22.8 0.1 broadcast_select_fusion
  22.9 0.3 collective-permute-done
  25.1 10.0 %all-to-all-done = bf16[4,112,768]{2,1,0:T(8,128)(2,1)S(1)} async-done(((bf16[4,112,768]{2,1,0:T(8,128)(2,1)}), bf16[4,112,768]{2,1,0:T(8,128)(2,1)S(1)}, u32[]{:S(2)}, u32[]{:S(2)}) %all-to-all-start) | async-done | bytes 688160 | tf_op jit(solution)/shard_map/all_to_all | solution.py:21
  35.1 0.9 slice.53
  36.0 0.0 all-gather.3.cloned.1.call-update
  36.0 0.7 broadcast_in_dim.58
  36.7 10.0 %all-to-all-start.1 = ((bf16[8,16,768]{2,1,0:T(8,128)(2,1)}), bf16[8,16,768]{2,1,0:T(8,128)(2,1)S(1)}, u32[]{:S(2)}, u32[]{:S(2)}) async-start(bf16[8,16,768]{2,1,0:T(8,128)(2,1)} %broadcast_in_dim.58), calls=%async_computation.1 | async-start | bytes 393216 | tf_op jit(solution)/shard_map/all_to_all | solution.py:21
  46.8 8.7 %all-to-all-done.1 = bf16[8,16,768]{2,1,0:T(8,128)(2,1)S(1)} async-done(((bf16[8,16,768]{2,1,0:T(8,128)(2,1)}), bf16[8,16,768]{2,1,0:T(8,128)(2,1)S(1)}, u32[]{:S(2)}, u32[]{:S(2)}) %all-to-all-start.1) | async-done | bytes 196640 | tf_op jit(solution)/shard_map/all_to_all | solution.py:21
  55.4 0.2 copy.23
  55.6 1.0 broadcast_in_dim.60
  56.6 5.0 %all-to-all-start.2 = ((bf16[4,128,768]{1,2,0:T(8,128)(2,1)}), bf16[4,128,768]{1,2,0:T(8,128)(2,1)S(1)}, u32[]{:S(2)}, u32[]{:S(2)}) async-start(bf16[4,128,768]{1,2,0:T(8,128)(2,1)} %broadcast_in_dim.60), calls=%async_computation.2 | async-start | bytes 1572864 | tf_op jit(solution)/shard_map/all_to_all | solution.py:21
  61.6 25.6 %all_gather.9 = bf16[512,768]{1,0:T(8,128)(2,1)S(1)} all-gather(bf16[64,768]{1,0:T(8,128)(2,1)S(1)} %bitcast.99), channel_id=1, replica_groups=mesh['yh'=4,'z'=8,'core'=2,'yl'=2,'x'=4] {'z'}, dimensions={0}, use_global_device_ids=true | all-gather | bytes 884736 | tf_op jit(solution)/shard_map/all_gather | solution.py:116
  87.2 0.3 copy.24
  87.5 1.3 pad_maximum_fusion
  88.8 7.7 %collective-permute-start.1 = (bf16[2,512,768]{2,1,0:T(8,128)(2,1)}, bf16[2,512,768]{2,1,0:T(8,128)(2,1)}, u32[]{:S(2)}, u32[]{:S(2)}) collective-permute-start(bf16[2,512,768]{2,1,0:T(8,128)(2,1)} %pad_maximum_fusion), channel_id=1, source_target_pairs={{8,0},{0,8},{9,1},{1,9},{10,2},{2,10},{11,3},{3,11},{12,4},{4,12},... | collective-permute-start | bytes 4718600 | tf_op jit(solution)/shard_map/ppermute | solution.py:16
  96.5 0.2 constant_dynamic-slice_fusion.7
  96.7 0.2 constant_dynamic-slice_fusion.6
  96.9 0.1 pad_maximum_fusion.2
  97.0 0.2 copy.31
  97.2 0.2 copy.32
  97.4 0.0 copy-start.2
  97.4 0.0 copy-start.3
  97.4 0.0 copy-start
  97.4 0.8 copy.27
  98.2 4.0 %all-to-all-start.3 = ((bf16[8,256,96]{1,2,0:T(8,128)(2,1)}), bf16[8,256,96]{1,2,0:T(8,128)(2,1)S(1)}, u32[]{:S(2)}, u32[]{:S(2)}) async-start(bf16[8,256,96]{1,2,0:T(8,128)(2,1)} %copy.27), calls=%async_computation.3 | async-start | bytes 786432 | tf_op jit(solution)/shard_map/all_to_all | solution.py:121
  102.3 7.5 %all-to-all-done.3 = bf16[8,256,96]{1,2,0:T(8,128)(2,1)S(1)} async-done(((bf16[8,256,96]{1,2,0:T(8,128)(2,1)}), bf16[8,256,96]{1,2,0:T(8,128)(2,1)S(1)}, u32[]{:S(2)}, u32[]{:S(2)}) %all-to-all-start.3) | async-done | bytes 393248 | tf_op jit(solution)/shard_map/all_to_all | solution.py:121
  109.8 0.1 all-gather.3.cloned.1.call-done
  109.9 3.5 %collective-permute-start.2 = (bf16[8,4,96,768]{3,2,1,0:T(8,128)(2,1)}, bf16[8,4,96,768]{3,2,1,0:T(8,128)(2,1)}, u32[]{:S(2)}, u32[]{:S(2)}) collective-permute-start(bf16[8,4,96,768]{3,2,1,0:T(8,128)(2,1)} %bitcast.94), channel_id=1, source_target_pairs={{8,0},{0,8},{9,1},{1,9},{10,2},{2,10},{11,3},{3,11},{12,4},{4,12},... | collective-permute-start | bytes 14155784 | tf_op jit(solution)/shard_map/ppermute | solution.py:16
  113.4 0.8 broadcast_in_dim.61
  114.2 4.2 %all-to-all-start.4 = ((bf16[16,128,96]{1,2,0:T(8,128)(2,1)}), bf16[16,128,96]{1,2,0:T(8,128)(2,1)S(1)}, u32[]{:S(2)}, u32[]{:S(2)}) async-start(bf16[16,128,96]{1,2,0:T(8,128)(2,1)} %bitcast.15), calls=%async_computation.4 | async-start | bytes 786432 | tf_op jit(solution)/shard_map/all_to_all | solution.py:132
  118.5 0.1 copy.30.out_eigs
  118.6 0.1 pad_add_fusion.place
  118.7 2.6 %collective-permute-done.2.other = bf16[8,4,96,768]{3,2,1,0:T(8,128)(2,1)} collective-permute-done((bf16[8,4,96,768]{3,2,1,0:T(8,128)(2,1)}, bf16[8,4,96,768]{3,2,1,0:T(8,128)(2,1)}, u32[]{:S(2)}, u32[]{:S(2)}) %collective-permute-start.2) | collective-permute-done | bytes 4718624 | tf_op jit(solution)/shard_map/ppermute | solution.py:16
  121.2 10.1 %shard_map.103 = (bf16[8,96,768]{2,1,0:T(8,128)(2,1)}, f32[96,768]{1,0:T(8,128)S(1)}) custom-call(s32[2]{0:T(128)S(1)} %pad_add_fusion.place, bf16[8,4,96,768]{3,2,1,0:T(8,128)(2,1)} %bitcast.95, bf16[8,4,96,768]{3,2,1,0:T(8,128)(2,1)} %collective-permute-done.2.other, bf16[96,6144]{1,0:T(8,128)(2,1)S(1)} %copy-done, f32[1,768]{1,0:T(1,128)S(1)} %broadcast_in_dim.62.in_eigs, ...), custom_call_target="tpu_custom_call" | custom-call | flops 1811939328 | bytes 14155776 | tf_op jit(solution)/shard_map/pallas_call | solution.py:76
  131.4 3.8 %all-to-all-start.5 = ((bf16[8,96,768]{2,1,0:T(8,128)(2,1)}), bf16[8,96,768]{2,1,0:T(8,128)(2,1)S(1)}, u32[]{:S(2)}, u32[]{:S(2)}) async-start(bf16[8,96,768]{2,1,0:T(8,128)(2,1)} %get-tuple-element.30), calls=%async_computation.5 | async-start | bytes 2359296 | tf_op jit(solution)/shard_map/all_to_all | solution.py:150
  135.2 0.9 copy.29
  136.1 1.1 reshape.93
  137.3 0.6 constant_dynamic-slice_fusion.2
  137.9 0.3 fusion.8
  138.2 0.3 fusion.13
  138.4 2.1 %fusion.1 = f32[768,96]{0,1:T(8,128)} fusion(f32[768,96]{0,1:T(8,128)S(1)} %fusion.8, bf16[2,512,768]{2,1,0:T(8,128)(2,1)} %collective-permute-done.1, bf16[1,1,512,96]{2,1,0,3:T(2,128)(2,1)S(1)} %get-tuple-element.35), kind=kOutput, calls=%fused_computation.4 | convolution fusion | flops 75644928 | bytes 1474560 | tf_op jit(solution)/shard_map/dot_general | solution.py:142
  140.6 2.1 %fusion = f32[768,96]{0,1:T(8,128)} fusion(f32[768,96]{0,1:T(8,128)S(1)} %fusion.13, bf16[2,512,768]{2,1,0:T(8,128)(2,1)} %collective-permute-done.1, bf16[1,1,512,96]{2,1,0,3:T(2,128)(2,1)S(1)} %get-tuple-element.36), kind=kOutput, calls=%fused_computation.3 | convolution fusion | flops 75644928 | bytes 1474560 | tf_op jit(solution)/shard_map/dot_general | solution.py:142
  142.7 8.9 %all-to-all-done.5 = bf16[8,96,768]{2,1,0:T(8,128)(2,1)S(1)} async-done(((bf16[8,96,768]{2,1,0:T(8,128)(2,1)}), bf16[8,96,768]{2,1,0:T(8,128)(2,1)S(1)}, u32[]{:S(2)}, u32[]{:S(2)}) %all-to-all-start.5) | async-done | bytes 1179680 | tf_op jit(solution)/shard_map/all_to_all | solution.py:150
  151.6 0.9 convert_add_fusion
  (17 shorter events, 0.1 us)
Async XLA Ops:
  7.2 15.6 %copy-start.1 = (bf16[16,768]{1,0:T(8,128)(2,1)S(1)}, bf16[16,768]{1,0:T(8,128)(2,1)}, u32[]{:S(2)}) copy-start(bf16[16,768]{1,0:T(8,128)(2,1)} %param.9) | copy-start | bytes 73732
  9.8 25.3 %all-to-all-start = ((bf16[4,112,768]{2,1,0:T(8,128)(2,1)}), bf16[4,112,768]{2,1,0:T(8,128)(2,1)S(1)}, u32[]{:S(2)}, u32[]{:S(2)}) async-start(bf16[4,112,768]{2,1,0:T(8,128)(2,1)} %broadcast_in_dim.55), calls=%async_computation | async-start | bytes 1376256 | tf_op jit(solution)/shard_map/all_to_all | solution.py:21
  17.4 92.5 %all-gather.3.cloned.1.call-start = ((), (), s32[]{:S(2)}) async-start(), calls=%async_computation.6 | async-start | bytes 5308416 | tf_op jit(solution)/shard_map/all_gather | solution.py:113
  17.4 5.8 %collective-permute-start = (s32[1]{0:T(128)}, s32[1]{0:T(128)}, u32[]{:S(2)}, u32[]{:S(2)}) collective-permute-start(s32[1]{0:T(128)} %param.11), channel_id=1, source_target_pairs={{8,0},{0,8},{9,1},{1,9},{10,2},{2,10},{11,3},{3,11},{12,4},{4,12},... | collective-permute-start | bytes 20 | tf_op jit(solution)/shard_map/ppermute | solution.py:16
  36.7 18.7 %all-to-all-start.1 = ((bf16[8,16,768]{2,1,0:T(8,128)(2,1)}), bf16[8,16,768]{2,1,0:T(8,128)(2,1)S(1)}, u32[]{:S(2)}, u32[]{:S(2)}) async-start(bf16[8,16,768]{2,1,0:T(8,128)(2,1)} %broadcast_in_dim.58), calls=%async_computation.1 | async-start | bytes 393216 | tf_op jit(solution)/shard_map/all_to_all | solution.py:21
  56.6 30.6 %all-to-all-start.2 = ((bf16[4,128,768]{1,2,0:T(8,128)(2,1)}), bf16[4,128,768]{1,2,0:T(8,128)(2,1)S(1)}, u32[]{:S(2)}, u32[]{:S(2)}) async-start(bf16[4,128,768]{1,2,0:T(8,128)(2,1)} %broadcast_in_dim.60), calls=%async_computation.2 | async-start | bytes 1572864 | tf_op jit(solution)/shard_map/all_to_all | solution.py:21
  88.8 21.0 %collective-permute-start.1 = (bf16[2,512,768]{2,1,0:T(8,128)(2,1)}, bf16[2,512,768]{2,1,0:T(8,128)(2,1)}, u32[]{:S(2)}, u32[]{:S(2)}) collective-permute-start(bf16[2,512,768]{2,1,0:T(8,128)(2,1)} %pad_maximum_fusion), channel_id=1, source_target_pairs={{8,0},{0,8},{9,1},{1,9},{10,2},{2,10},{11,3},{3,11},{12,4},{4,12},... | collective-permute-start | bytes 4718600 | tf_op jit(solution)/shard_map/ppermute | solution.py:16
  97.4 21.1 %copy-start.2 = (f32[768]{0:T(1024)S(1)}, f32[768]{0:T(1024)}, u32[]{:S(2)}) copy-start(f32[768]{0:T(1024)} %param.14) | copy-start | bytes 9220
  97.4 21.1 %copy-start.3 = (f32[96]{0:T(128)S(1)}, f32[96]{0:T(128)}, u32[]{:S(2)}) copy-start(f32[96]{0:T(128)} %param.15) | copy-start | bytes 1156
  97.4 23.8 %copy-start = (bf16[96,6144]{1,0:T(8,128)(2,1)S(1)}, bf16[96,6144]{1,0:T(8,128)(2,1)}, u32[]{:S(2)}) copy-start(bf16[96,6144]{1,0:T(8,128)(2,1)} %grad.1) | copy-start | bytes 3538948
  98.2 11.6 %all-to-all-start.3 = ((bf16[8,256,96]{1,2,0:T(8,128)(2,1)}), bf16[8,256,96]{1,2,0:T(8,128)(2,1)S(1)}, u32[]{:S(2)}, u32[]{:S(2)}) async-start(bf16[8,256,96]{1,2,0:T(8,128)(2,1)} %copy.27), calls=%async_computation.3 | async-start | bytes 786432 | tf_op jit(solution)/shard_map/all_to_all | solution.py:121
  109.9 11.4 %collective-permute-start.2 = (bf16[8,4,96,768]{3,2,1,0:T(8,128)(2,1)}, bf16[8,4,96,768]{3,2,1,0:T(8,128)(2,1)}, u32[]{:S(2)}, u32[]{:S(2)}) collective-permute-start(bf16[8,4,96,768]{3,2,1,0:T(8,128)(2,1)} %bitcast.94), channel_id=1, source_target_pairs={{8,0},{0,8},{9,1},{1,9},{10,2},{2,10},{11,3},{3,11},{12,4},{4,12},... | collective-permute-start | bytes 14155784 | tf_op jit(solution)/shard_map/ppermute | solution.py:16
  114.2 17.2 %all-to-all-start.4 = ((bf16[16,128,96]{1,2,0:T(8,128)(2,1)}), bf16[16,128,96]{1,2,0:T(8,128)(2,1)S(1)}, u32[]{:S(2)}, u32[]{:S(2)}) async-start(bf16[16,128,96]{1,2,0:T(8,128)(2,1)} %bitcast.15), calls=%async_computation.4 | async-start | bytes 786432 | tf_op jit(solution)/shard_map/all_to_all | solution.py:132
  131.4 20.2 %all-to-all-start.5 = ((bf16[8,96,768]{2,1,0:T(8,128)(2,1)}), bf16[8,96,768]{2,1,0:T(8,128)(2,1)S(1)}, u32[]{:S(2)}, u32[]{:S(2)}) async-start(bf16[8,96,768]{2,1,0:T(8,128)(2,1)} %get-tuple-element.30), calls=%async_computation.5 | async-start | bytes 2359296 | tf_op jit(solution)/shard_map/all_to_all | solution.py:150
Sparse Core Ops, SparseCore 0:
  36.2 73.6 all-gather.2

commit v16 on v14

--- a/solution.py
+++ b/solution.py
@@ -142,7 +142,9 @@
     other = shift(own, "core", 1)
     terms, own_term = precondition(own, other, rotated_grad, input_eigs, output_eigs)
     terms = lax.all_to_all(terms, GROUP, 0, 0, tiled=True)
-    preconditioned = own_term + jnp.sum(terms.astype(jnp.float32), axis=0)
+    preconditioned = own_term
+    for k in range(group_count):
+        preconditioned += terms[k].astype(jnp.float32)
     return (cov_in, cov_out, preconditioned)
 
 

time: 160 us -> 160 us (level)
  no operation moved by 1% of the time
where the time goes in v16:
time: 160 us; the launch traced here: 159 us
  starting transfers between devices  50.6 us (32%)
  waiting for transfers between devices  38.1 us (24%)
  blocking collectives  25.6 us (16%)
  between operations  17.5 us (11%)
  Pallas kernels  10.4 us (6%)
  local copies, waits for them, and re-layouts  9.08 us (6%)
  matrix products  4.74 us (3%)
  other arithmetic  3.57 us (2%)
    all_gather x1, blocking collectives, shards(): lax.all_gather(kept_in.reshape(-1, width), 'z', axis=0, tiled=True)  25.6 us
    all_to_all x3, starting transfers between devices, spread(): lax.all_to_all(jnp.broadcast_to(block[None], (size,) + block.shape), axis...  22.6 us
    all_to_all x3, waiting for transfers between devices, spread(): lax.all_to_all(jnp.broadcast_to(block[None], (size,) + block.shape), axis...  18.7 us
    ppermute x3, starting transfers between devices, shift(): lax.ppermute(value, axis, [((i + by) % size, i) for i in range(size)])  15.9 us
    pallas_call x1, Pallas kernels, precondition(): pl.pallas_call(precondition_kernel, out_shape=(jax.ShapeDtypeStruct((8, r...  10.4 us
    all_to_all x1, waiting for transfers between devices, shards(): terms = lax.all_to_all(terms, GROUP, 0, 0, tiled=True)  8.9 us
    all_to_all x1, waiting for transfers between devices, shards(): lax.all_to_all(jnp.concatenate(pieces, axis=1), GROUP, 0, 0, tiled=True)  7.52 us
    dot_general x2, matrix products, shards(): lax.dot_general(theirs[k], owned_theirs[k], contract_rows, preferred_elem...  4.22 us
  transfers between devices with their start and end apart: 10, of which 7 were waited for; matrix products, arithmetic and copies ran while one was open for 9% of the time, Pallas kernels for 6%

profile of v16, /device:TPU:1, one launch (start us, length us, event | category | flops | bytes accessed | tf_op | source)
XLA Modules:
  0.0 159.5 jit_solution(286654160796999298)
XLA Ops:
  7.8 1.0 maximum_select_fusion
  8.9 0.9 broadcast_in_dim.55
  9.8 7.6 %all-to-all-start = ((bf16[4,112,768]{2,1,0:T(8,128)(2,1)}), bf16[4,112,768]{2,1,0:T(8,128)(2,1)S(1)}, u32[]{:S(2)}, u32[]{:S(2)}) async-start(bf16[4,112,768]{2,1,0:T(8,128)(2,1)} %broadcast_in_dim.55), calls=%async_computation | async-start | bytes 1376256 | tf_op jit(solution)/shard_map/all_to_all | solution.py:21
  17.4 4.7 %collective-permute-start = (s32[1]{0:T(128)}, s32[1]{0:T(128)}, u32[]{:S(2)}, u32[]{:S(2)}) collective-permute-start(s32[1]{0:T(128)} %param.11), channel_id=1, source_target_pairs={{8,0},{0,8},{9,1},{1,9},{10,2},{2,10},{11,3},{3,11},{12,4},{4,12},... | collective-permute-start | bytes 20 | tf_op jit(solution)/shard_map/ppermute | solution.py:16
  22.8 0.1 broadcast_select_fusion
  22.9 0.3 collective-permute-done
  25.1 10.0 %all-to-all-done = bf16[4,112,768]{2,1,0:T(8,128)(2,1)S(1)} async-done(((bf16[4,112,768]{2,1,0:T(8,128)(2,1)}), bf16[4,112,768]{2,1,0:T(8,128)(2,1)S(1)}, u32[]{:S(2)}, u32[]{:S(2)}) %all-to-all-start) | async-done | bytes 688160 | tf_op jit(solution)/shard_map/all_to_all | solution.py:21
  35.1 0.9 slice.53
  36.0 0.0 all-gather.3.cloned.1.call-update
  36.0 0.7 broadcast_in_dim.58
  36.7 10.0 %all-to-all-start.1 = ((bf16[8,16,768]{2,1,0:T(8,128)(2,1)}), bf16[8,16,768]{2,1,0:T(8,128)(2,1)S(1)}, u32[]{:S(2)}, u32[]{:S(2)}) async-start(bf16[8,16,768]{2,1,0:T(8,128)(2,1)} %broadcast_in_dim.58), calls=%async_computation.1 | async-start | bytes 393216 | tf_op jit(solution)/shard_map/all_to_all | solution.py:21
  46.8 8.7 %all-to-all-done.1 = bf16[8,16,768]{2,1,0:T(8,128)(2,1)S(1)} async-done(((bf16[8,16,768]{2,1,0:T(8,128)(2,1)}), bf16[8,16,768]{2,1,0:T(8,128)(2,1)S(1)}, u32[]{:S(2)}, u32[]{:S(2)}) %all-to-all-start.1) | async-done | bytes 196640 | tf_op jit(solution)/shard_map/all_to_all | solution.py:21
  55.4 0.2 copy.23
  55.6 1.0 broadcast_in_dim.60
  56.6 5.0 %all-to-all-start.2 = ((bf16[4,128,768]{1,2,0:T(8,128)(2,1)}), bf16[4,128,768]{1,2,0:T(8,128)(2,1)S(1)}, u32[]{:S(2)}, u32[]{:S(2)}) async-start(bf16[4,128,768]{1,2,0:T(8,128)(2,1)} %broadcast_in_dim.60), calls=%async_computation.2 | async-start | bytes 1572864 | tf_op jit(solution)/shard_map/all_to_all | solution.py:21
  61.6 25.6 %all_gather.9 = bf16[512,768]{1,0:T(8,128)(2,1)S(1)} all-gather(bf16[64,768]{1,0:T(8,128)(2,1)S(1)} %bitcast.99), channel_id=1, replica_groups=mesh['yh'=4,'z'=8,'core'=2,'yl'=2,'x'=4] {'z'}, dimensions={0}, use_global_device_ids=true | all-gather | bytes 884736 | tf_op jit(solution)/shard_map/all_gather | solution.py:110
  87.2 0.3 copy.24
  87.5 1.3 pad_maximum_fusion
  88.8 7.7 %collective-permute-start.1 = (bf16[2,512,768]{2,1,0:T(8,128)(2,1)}, bf16[2,512,768]{2,1,0:T(8,128)(2,1)}, u32[]{:S(2)}, u32[]{:S(2)}) collective-permute-start(bf16[2,512,768]{2,1,0:T(8,128)(2,1)} %pad_maximum_fusion), channel_id=1, source_target_pairs={{8,0},{0,8},{9,1},{1,9},{10,2},{2,10},{11,3},{3,11},{12,4},{4,12},... | collective-permute-start | bytes 4718600 | tf_op jit(solution)/shard_map/ppermute | solution.py:16
  96.5 0.2 constant_dynamic-slice_fusion.7
  96.7 0.2 constant_dynamic-slice_fusion.6
  96.9 0.1 pad_maximum_fusion.2
  97.0 0.2 copy.31
  97.2 0.2 copy.32
  97.4 0.0 copy-start.2
  97.4 0.0 copy-start.3
  97.4 0.0 copy-start
  97.4 0.8 copy.27
  98.2 4.0 %all-to-all-start.3 = ((bf16[8,256,96]{1,2,0:T(8,128)(2,1)}), bf16[8,256,96]{1,2,0:T(8,128)(2,1)S(1)}, u32[]{:S(2)}, u32[]{:S(2)}) async-start(bf16[8,256,96]{1,2,0:T(8,128)(2,1)} %copy.27), calls=%async_computation.3 | async-start | bytes 786432 | tf_op jit(solution)/shard_map/all_to_all | solution.py:115
  102.3 7.5 %all-to-all-done.3 = bf16[8,256,96]{1,2,0:T(8,128)(2,1)S(1)} async-done(((bf16[8,256,96]{1,2,0:T(8,128)(2,1)}), bf16[8,256,96]{1,2,0:T(8,128)(2,1)S(1)}, u32[]{:S(2)}, u32[]{:S(2)}) %all-to-all-start.3) | async-done | bytes 393248 | tf_op jit(solution)/shard_map/all_to_all | solution.py:115
  109.8 0.1 all-gather.3.cloned.1.call-done
  109.9 3.5 %collective-permute-start.2 = (bf16[8,4,96,768]{3,2,1,0:T(8,128)(2,1)}, bf16[8,4,96,768]{3,2,1,0:T(8,128)(2,1)}, u32[]{:S(2)}, u32[]{:S(2)}) collective-permute-start(bf16[8,4,96,768]{3,2,1,0:T(8,128)(2,1)} %bitcast.94), channel_id=1, source_target_pairs={{8,0},{0,8},{9,1},{1,9},{10,2},{2,10},{11,3},{3,11},{12,4},{4,12},... | collective-permute-start | bytes 14155784 | tf_op jit(solution)/shard_map/ppermute | solution.py:16
  113.4 0.8 broadcast_in_dim.61
  114.2 4.2 %all-to-all-start.4 = ((bf16[16,128,96]{1,2,0:T(8,128)(2,1)}), bf16[16,128,96]{1,2,0:T(8,128)(2,1)S(1)}, u32[]{:S(2)}, u32[]{:S(2)}) async-start(bf16[16,128,96]{1,2,0:T(8,128)(2,1)} %bitcast.15), calls=%async_computation.4 | async-start | bytes 786432 | tf_op jit(solution)/shard_map/all_to_all | solution.py:126
  118.5 0.1 copy.30.out_eigs
  118.6 0.1 pad_add_fusion.place
  118.7 2.6 %collective-permute-done.2.other = bf16[8,4,96,768]{3,2,1,0:T(8,128)(2,1)} collective-permute-done((bf16[8,4,96,768]{3,2,1,0:T(8,128)(2,1)}, bf16[8,4,96,768]{3,2,1,0:T(8,128)(2,1)}, u32[]{:S(2)}, u32[]{:S(2)}) %collective-permute-start.2) | collective-permute-done | bytes 4718624 | tf_op jit(solution)/shard_map/ppermute | solution.py:16
  121.3 10.4 %shard_map.103 = (bf16[8,96,768]{2,1,0:T(8,128)(2,1)}, f32[96,768]{1,0:T(8,128)S(1)}) custom-call(s32[2]{0:T(128)S(1)} %pad_add_fusion.place, bf16[8,4,96,768]{3,2,1,0:T(8,128)(2,1)} %bitcast.95, bf16[8,4,96,768]{3,2,1,0:T(8,128)(2,1)} %collective-permute-done.2.other, bf16[96,6144]{1,0:T(8,128)(2,1)S(1)} %copy-done, f32[1,768]{1,0:T(1,128)S(1)} %broadcast_in_dim.62.in_eigs, ...), custom_call_target="tpu_custom_call" | custom-call | flops 1811939328 | bytes 14155776 | tf_op jit(solution)/shard_map/pallas_call | solution.py:71
  131.6 3.8 %all-to-all-start.5 = ((bf16[8,96,768]{2,1,0:T(8,128)(2,1)}), bf16[8,96,768]{2,1,0:T(8,128)(2,1)S(1)}, u32[]{:S(2)}, u32[]{:S(2)}) async-start(bf16[8,96,768]{2,1,0:T(8,128)(2,1)} %get-tuple-element.30), calls=%async_computation.5 | async-start | bytes 2359296 | tf_op jit(solution)/shard_map/all_to_all | solution.py:144
  135.4 0.9 copy.29
  136.3 1.1 reshape.93
  137.5 0.6 constant_dynamic-slice_fusion.2
  138.1 0.3 fusion.8
  138.4 0.3 fusion.13
  138.7 2.1 %fusion.1 = f32[768,96]{0,1:T(8,128)} fusion(f32[768,96]{0,1:T(8,128)S(1)} %fusion.8, bf16[2,512,768]{2,1,0:T(8,128)(2,1)} %collective-permute-done.1, bf16[1,1,512,96]{2,1,0,3:T(2,128)(2,1)S(1)} %get-tuple-element.35), kind=kOutput, calls=%fused_computation.4 | convolution fusion | flops 75644928 | bytes 1474560 | tf_op jit(solution)/shard_map/dot_general | solution.py:136
  140.8 2.1 %fusion = f32[768,96]{0,1:T(8,128)} fusion(f32[768,96]{0,1:T(8,128)S(1)} %fusion.13, bf16[2,512,768]{2,1,0:T(8,128)(2,1)} %collective-permute-done.1, bf16[1,1,512,96]{2,1,0,3:T(2,128)(2,1)S(1)} %get-tuple-element.36), kind=kOutput, calls=%fused_computation.3 | convolution fusion | flops 75644928 | bytes 1474560 | tf_op jit(solution)/shard_map/dot_general | solution.py:136
  142.9 8.9 %all-to-all-done.5 = bf16[8,96,768]{2,1,0:T(8,128)(2,1)S(1)} async-done(((bf16[8,96,768]{2,1,0:T(8,128)(2,1)}), bf16[8,96,768]{2,1,0:T(8,128)(2,1)S(1)}, u32[]{:S(2)}, u32[]{:S(2)}) %all-to-all-start.5) | async-done | bytes 1179680 | tf_op jit(solution)/shard_map/all_to_all | solution.py:144
  151.8 0.9 convert_add_fusion
  (17 shorter events, 0.1 us)
Async XLA Ops:
  7.2 15.6 %copy-start.1 = (bf16[16,768]{1,0:T(8,128)(2,1)S(1)}, bf16[16,768]{1,0:T(8,128)(2,1)}, u32[]{:S(2)}) copy-start(bf16[16,768]{1,0:T(8,128)(2,1)} %param.9) | copy-start | bytes 73732
  9.8 25.3 %all-to-all-start = ((bf16[4,112,768]{2,1,0:T(8,128)(2,1)}), bf16[4,112,768]{2,1,0:T(8,128)(2,1)S(1)}, u32[]{:S(2)}, u32[]{:S(2)}) async-start(bf16[4,112,768]{2,1,0:T(8,128)(2,1)} %broadcast_in_dim.55), calls=%async_computation | async-start | bytes 1376256 | tf_op jit(solution)/shard_map/all_to_all | solution.py:21
  17.4 92.5 %all-gather.3.cloned.1.call-start = ((), (), s32[]{:S(2)}) async-start(), calls=%async_computation.6 | async-start | bytes 5308416 | tf_op jit(solution)/shard_map/all_gather | solution.py:107
  17.4 5.8 %collective-permute-start = (s32[1]{0:T(128)}, s32[1]{0:T(128)}, u32[]{:S(2)}, u32[]{:S(2)}) collective-permute-start(s32[1]{0:T(128)} %param.11), channel_id=1, source_target_pairs={{8,0},{0,8},{9,1},{1,9},{10,2},{2,10},{11,3},{3,11},{12,4},{4,12},... | collective-permute-start | bytes 20 | tf_op jit(solution)/shard_map/ppermute | solution.py:16
  36.7 18.7 %all-to-all-start.1 = ((bf16[8,16,768]{2,1,0:T(8,128)(2,1)}), bf16[8,16,768]{2,1,0:T(8,128)(2,1)S(1)}, u32[]{:S(2)}, u32[]{:S(2)}) async-start(bf16[8,16,768]{2,1,0:T(8,128)(2,1)} %broadcast_in_dim.58), calls=%async_computation.1 | async-start | bytes 393216 | tf_op jit(solution)/shard_map/all_to_all | solution.py:21
  56.6 30.6 %all-to-all-start.2 = ((bf16[4,128,768]{1,2,0:T(8,128)(2,1)}), bf16[4,128,768]{1,2,0:T(8,128)(2,1)S(1)}, u32[]{:S(2)}, u32[]{:S(2)}) async-start(bf16[4,128,768]{1,2,0:T(8,128)(2,1)} %broadcast_in_dim.60), calls=%async_computation.2 | async-start | bytes 1572864 | tf_op jit(solution)/shard_map/all_to_all | solution.py:21
  88.8 21.0 %collective-permute-start.1 = (bf16[2,512,768]{2,1,0:T(8,128)(2,1)}, bf16[2,512,768]{2,1,0:T(8,128)(2,1)}, u32[]{:S(2)}, u32[]{:S(2)}) collective-permute-start(bf16[2,512,768]{2,1,0:T(8,128)(2,1)} %pad_maximum_fusion), channel_id=1, source_target_pairs={{8,0},{0,8},{9,1},{1,9},{10,2},{2,10},{11,3},{3,11},{12,4},{4,12},... | collective-permute-start | bytes 4718600 | tf_op jit(solution)/shard_map/ppermute | solution.py:16
  97.4 21.0 %copy-start.2 = (f32[768]{0:T(1024)S(1)}, f32[768]{0:T(1024)}, u32[]{:S(2)}) copy-start(f32[768]{0:T(1024)} %param.14) | copy-start | bytes 9220
  97.4 21.0 %copy-start.3 = (f32[96]{0:T(128)S(1)}, f32[96]{0:T(128)}, u32[]{:S(2)}) copy-start(f32[96]{0:T(128)} %param.15) | copy-start | bytes 1156
  97.4 23.8 %copy-start = (bf16[96,6144]{1,0:T(8,128)(2,1)S(1)}, bf16[96,6144]{1,0:T(8,128)(2,1)}, u32[]{:S(2)}) copy-start(bf16[96,6144]{1,0:T(8,128)(2,1)} %grad.1) | copy-start | bytes 3538948
  98.2 11.6 %all-to-all-start.3 = ((bf16[8,256,96]{1,2,0:T(8,128)(2,1)}), bf16[8,256,96]{1,2,0:T(8,128)(2,1)S(1)}, u32[]{:S(2)}, u32[]{:S(2)}) async-start(bf16[8,256,96]{1,2,0:T(8,128)(2,1)} %copy.27), calls=%async_computation.3 | async-start | bytes 786432 | tf_op jit(solution)/shard_map/all_to_all | solution.py:115
  109.9 11.4 %collective-permute-start.2 = (bf16[8,4,96,768]{3,2,1,0:T(8,128)(2,1)}, bf16[8,4,96,768]{3,2,1,0:T(8,128)(2,1)}, u32[]{:S(2)}, u32[]{:S(2)}) collective-permute-start(bf16[8,4,96,768]{3,2,1,0:T(8,128)(2,1)} %bitcast.94), channel_id=1, source_target_pairs={{8,0},{0,8},{9,1},{1,9},{10,2},{2,10},{11,3},{3,11},{12,4},{4,12},... | collective-permute-start | bytes 14155784 | tf_op jit(solution)/shard_map/ppermute | solution.py:16
  114.2 17.4 %all-to-all-start.4 = ((bf16[16,128,96]{1,2,0:T(8,128)(2,1)}), bf16[16,128,96]{1,2,0:T(8,128)(2,1)S(1)}, u32[]{:S(2)}, u32[]{:S(2)}) async-start(bf16[16,128,96]{1,2,0:T(8,128)(2,1)} %bitcast.15), calls=%async_computation.4 | async-start | bytes 786432 | tf_op jit(solution)/shard_map/all_to_all | solution.py:126
  131.6 20.1 %all-to-all-start.5 = ((bf16[8,96,768]{2,1,0:T(8,128)(2,1)}), bf16[8,96,768]{2,1,0:T(8,128)(2,1)S(1)}, u32[]{:S(2)}, u32[]{:S(2)}) async-start(bf16[8,96,768]{2,1,0:T(8,128)(2,1)} %get-tuple-element.30), calls=%async_computation.5 | async-start | bytes 2359296 | tf_op jit(solution)/shard_map/all_to_all | solution.py:144
Sparse Core Ops, SparseCore 0:
  36.2 73.6 all-gather.2
